TPU v7x, 32 devices: a whole 2x2x4 slice. The times are simulated.
32 devices in a mesh: dp: 4 (over x, core), seq: 8 (over z, y).
Axes of the slice: x: 2, y: 2, z: 4, core: 2. Of those that a mesh axis runs over, the one named last changes fastest.
Arguments:
- decoder_in: bfloat16 [2, 32, 512, 768], P(None, ('dp', 'seq')), may hold values from -6 to 6
- memory: bfloat16 [2, 32, 1024, 768], P(None, ('dp', 'seq')), may hold values from -6 to 6
- doc_offsets: int32 [2, 4, 8], P(None, 'dp'), may hold values from 256 to 511, as said below
- self_query: bfloat16 [768, 768], P(('dp', 'seq')), may hold values from -0.0546875 to 0.0546875
- self_key: bfloat16 [768, 768], P(('dp', 'seq')), may hold values from -0.21875 to 0.21875
- self_value: bfloat16 [768, 768], P(('dp', 'seq')), may hold values from -0.21875 to 0.21875
- self_out: bfloat16 [768, 768], P(('dp', 'seq')), may hold values from -0.625 to 0.625
- cross_query: bfloat16 [768, 768], P(('dp', 'seq')), may hold values from -0.0546875 to 0.0546875
- cross_key: bfloat16 [768, 768], P(('dp', 'seq')), may hold values from -0.21875 to 0.21875
- cross_value: bfloat16 [768, 768], P(('dp', 'seq')), may hold values from -0.21875 to 0.21875
- cross_out: bfloat16 [768, 768], P(('dp', 'seq')), may hold values from -0.625 to 0.625
- ffn_gate: bfloat16 [768, 2048], P(('dp', 'seq')), may hold values from -0.21875 to 0.21875
- ffn_up: bfloat16 [768, 2048], P(('dp', 'seq')), may hold values from -0.21875 to 0.21875
- ffn_down: bfloat16 [2048, 768], P(('dp', 'seq')), may hold values from -0.125 to 0.125
- norm_self: bfloat16 [768], P(('dp', 'seq')), may hold values from 0.5 to 1.5
- norm_cross: bfloat16 [768], P(('dp', 'seq')), may hold values from 0.5 to 1.5
- norm_ffn: bfloat16 [768], P(('dp', 'seq')), may hold values from 0.5 to 1.5
- bias_table: bfloat16 [12, 32], replicated, may hold values from -4 to 4
- cotangent: bfloat16 [2, 32, 512, 768], P(None, ('dp', 'seq')), may hold values from -6 to 6
Outputs:
- out_layer: bfloat16 [2, 32, 512, 768], P(None, ('dp', 'seq'))
- grad_decoder: bfloat16 [2, 32, 512, 768], P(None, ('dp', 'seq'))
- grad_memory: bfloat16 [2, 32, 1024, 768], P(None, ('dp', 'seq'))
- grad_self_query: float32 [768, 768], P(('dp', 'seq'))
- grad_self_key: float32 [768, 768], P(('dp', 'seq'))
- grad_self_value: float32 [768, 768], P(('dp', 'seq'))
- grad_self_out: float32 [768, 768], P(('dp', 'seq'))
- grad_cross_query: float32 [768, 768], P(('dp', 'seq'))
- grad_cross_key: float32 [768, 768], P(('dp', 'seq'))
- grad_cross_value: float32 [768, 768], P(('dp', 'seq'))
- grad_cross_out: float32 [768, 768], P(('dp', 'seq'))
- grad_ffn_gate: float32 [768, 2048], P(('dp', 'seq'))
- grad_ffn_up: float32 [768, 2048], P(('dp', 'seq'))
- grad_ffn_down: float32 [2048, 768], P(('dp', 'seq'))
- grad_norm_self: float32 [768], P(('dp', 'seq'))
- grad_norm_cross: float32 [768], P(('dp', 'seq'))
- grad_norm_ffn: float32 [768], P(('dp', 'seq'))
- grad_bias_table: float32 [12, 32], replicated
Inputs may be any that keep to these rules, and one draw needn't show every extreme that they name: Within a group the memory row blocks form one stream; the slots of row block s before doc_offsets[m, g, s] belong to the document of target s - 1 (padding for s = 0), the rest to the document of target s.
All inputs are finite; a program needn't handle non-finite values.
Results may differ from a plain program's by a relative error of at most 0.029.
The roundings to bfloat16 on the way count: a program that leaves them out, or rounds other values in their place, can miss the bound.
Values may be sent and summed in bfloat16 or wider, within the bound.
No kernel may reach another device: no remote copies, remote signals or barrier semaphores. Data moves between devices by JAX's collectives and lax.ppermute only.
A program may use at most 256 MiB of HBM per device.

v0:
```python
import math

import jax
import jax.numpy as jnp
from jax import lax
from jax.sharding import PartitionSpec as P

D = 768
HEADS = 12
HEAD_DIM = 64
BUCKETS = 32
REACH = 128
TGT_LEN = 512
MEM_DEV = 1024
MICRO = 2


NORM_EPS = 1e-06
MASKED = -1e30


def shortened(x):

    def short(part):
        return part.astype(jnp.bfloat16) if part.dtype == jnp.float32 else part

    return jax.tree.map(short, x)


def passed_along(block, axis, distance):
    devices = range(lax.axis_size(axis))
    route = [(i - distance, i) for i in devices if i - distance in devices]
    return lax.ppermute(block, axis, route)


def bucket_limits(buckets, reach):
    exact_count = buckets // 2
    limits = []
    for target in range(exact_count + 1, buckets):
        distance = exact_count
        while (
            exact_count
            + int(
                math.log(distance / exact_count)
                / math.log(reach / exact_count)
                * (buckets - exact_count)
            )
            < target
        ):
            distance += 1
        limits.append(distance)
    return limits


def distance_buckets(length, buckets, reach):
    distance = jnp.arange(length, dtype=jnp.int32)
    exact_count = buckets // 2
    far_bucket = jnp.full((length,), exact_count, jnp.int32)
    for threshold in bucket_limits(buckets, reach):
        far_bucket = far_bucket + (distance >= threshold).astype(jnp.int32)
    return jnp.where(distance < exact_count, distance, far_bucket)


def distance_grid(by_distance):
    heads_count, length = by_distance.shape
    first = by_distance[:, :1]
    wrapped = jnp.concatenate(
        [first, jnp.broadcast_to(first, (heads_count, length - 1)), by_distance[:, 1:][:, ::-1]],
        axis=1,
    )
    period = 2 * length - 1
    tiled = jnp.broadcast_to(wrapped[:, None, :], (heads_count, length, period)).reshape(
        heads_count, length * period
    )
    skewed = tiled[:, : length * (period - 1)].reshape(heads_count, length, period - 1)
    return skewed[:, :, :length]


def norm_rows(values, gain):
    inverse = lax.rsqrt(jnp.mean(values * values, axis=-1, keepdims=True) + NORM_EPS)
    return values * inverse * gain


def gated_units(gate_pre, up_pre):
    return jax.nn.gelu(gate_pre, approximate=True) * up_pre


def project(rows, weight):
    return jnp.dot(rows, weight, preferred_element_type=jnp.float32)


def project_back(grads, weight):
    return jnp.einsum("lo,io->li", grads, weight, preferred_element_type=jnp.float32)


def weight_grad(rows, grads):
    return jnp.einsum("li,lo->io", rows, grads, preferred_element_type=jnp.float32)


def split_heads(matrix):
    return matrix.reshape(matrix.shape[0], HEADS, HEAD_DIM).transpose(1, 0, 2)


def join_heads(stacked):
    return stacked.transpose(1, 0, 2).reshape(stacked.shape[1], HEADS * HEAD_DIM)


def distance_sums(grid):
    length = grid.shape[0]
    flipped = grid[:, ::-1]
    padded = jnp.concatenate([flipped, jnp.zeros((length, length), jnp.float32)], axis=1).reshape(
        -1
    )
    skewed = padded[: length * (2 * length - 1)].reshape(length, 2 * length - 1)
    return jnp.sum(skewed, axis=0)[length - 1 :]


def head_scores(query_h, key_h, bias_h, valid):
    raw_scores = jnp.einsum("qe,ke->qk", query_h, key_h, preferred_element_type=jnp.float32)
    return jnp.where(valid, raw_scores + bias_h, MASKED)


def head_forward(query_h, key_h, value_h, bias_h, valid):
    scores = head_scores(query_h, key_h, bias_h, valid)
    top_score = jnp.max(scores, axis=-1, keepdims=True)
    weights = jnp.exp(scores - top_score)
    row_total = jnp.sum(weights, axis=-1, keepdims=True)
    probs = weights / row_total
    mixed = jnp.einsum(
        "qk,ke->qe", probs.astype(jnp.bfloat16), value_h, preferred_element_type=jnp.float32
    )
    return (mixed.astype(jnp.bfloat16), (top_score + jnp.log(row_total))[:, 0])


def head_backward(query_h, key_h, value_h, bias_h, valid, log_total, grad_mixed):
    scores = head_scores(query_h, key_h, bias_h, valid)
    probs = jnp.exp(scores - log_total[:, None])
    grad_probs = jnp.einsum("qe,ke->qk", grad_mixed, value_h, preferred_element_type=jnp.float32)
    grad_value = jnp.einsum(
        "qk,qe->ke", probs.astype(jnp.bfloat16), grad_mixed, preferred_element_type=jnp.float32
    )
    centre = jnp.sum(probs * grad_probs, axis=-1, keepdims=True)
    grad_scores = probs * (grad_probs - centre)
    grad_rounded = grad_scores.astype(jnp.bfloat16)
    grad_query = jnp.einsum("qk,ke->qe", grad_rounded, key_h, preferred_element_type=jnp.float32)
    grad_key = jnp.einsum("qk,qe->ke", grad_rounded, query_h, preferred_element_type=jnp.float32)
    return (grad_query, grad_key, grad_value, grad_scores)


def self_forward(query_all, key_all, value_all, self_bias, causal):

    def one_head(packed):
        query_h, key_h, value_h, bias_h = packed
        return head_forward(query_h, key_h, value_h, bias_h, causal)

    return lax.map(one_head, (query_all, key_all, value_all, self_bias))


def cross_forward(query_all, key_all, value_all, valid):

    def one_head(packed):
        query_h, key_h, value_h = packed
        return head_forward(query_h, key_h, value_h, 0.0, valid)

    return lax.map(one_head, (query_all, key_all, value_all))


def self_backward(
    query_all, key_all, value_all, self_bias, causal, log_totals, grad_all, distance_hot
):

    def one_head(packed):
        query_h, key_h, value_h, bias_h, log_total, grad_mixed = packed
        grad_query, grad_key, grad_value, grad_scores = head_backward(
            query_h, key_h, value_h, bias_h, causal, log_total, grad_mixed
        )
        table_row = jnp.dot(
            distance_sums(grad_scores), distance_hot, precision=lax.Precision.HIGHEST
        )
        return (grad_query, grad_key, grad_value, table_row)

    return lax.map(one_head, (query_all, key_all, value_all, self_bias, log_totals, grad_all))


def cross_backward(query_all, key_all, value_all, valid, log_totals, grad_all):

    def one_head(packed):
        query_h, key_h, value_h, log_total, grad_mixed = packed
        grad_query, grad_key, grad_value, grad_scores = head_backward(
            query_h, key_h, value_h, 0.0, valid, log_total, grad_mixed
        )
        return (grad_query, grad_key, grad_value)

    return lax.map(one_head, (query_all, key_all, value_all, log_totals, grad_all))


def key_masks(offsets_row, position):
    quarter_rows = MEM_DEV // 4
    half_rows = MEM_DEV // 2
    shard_ids = jnp.arange(offsets_row.shape[0], dtype=jnp.int32)
    own_start = jnp.sum(jnp.where(shard_ids == position, offsets_row, 0))
    next_start = jnp.sum(jnp.where(shard_ids == position + 1, offsets_row, 0))
    own_valid = jnp.arange(quarter_rows, MEM_DEV, dtype=jnp.int32) >= own_start
    next_valid = jnp.arange(half_rows, dtype=jnp.int32) < next_start
    return jnp.concatenate([own_valid, next_valid])[None, :]


def fetch_weights(
    self_query,
    self_key,
    self_value,
    self_out,
    cross_query,
    cross_key,
    cross_value,
    cross_out,
    ffn_gate,
    ffn_up,
    ffn_down,
    norm_self,
    norm_cross,
    norm_ffn,
):
    return (
        lax.all_gather(shortened(self_query), ("dp", "seq"), axis=0, tiled=True).astype(
            self_query.dtype
        ),
        lax.all_gather(shortened(self_key), ("dp", "seq"), axis=0, tiled=True).astype(
            self_key.dtype
        ),
        lax.all_gather(shortened(self_value), ("dp", "seq"), axis=0, tiled=True).astype(
            self_value.dtype
        ),
        lax.all_gather(shortened(self_out), ("dp", "seq"), axis=0, tiled=True).astype(
            self_out.dtype
        ),
        lax.all_gather(shortened(cross_query), ("dp", "seq"), axis=0, tiled=True).astype(
            cross_query.dtype
        ),
        lax.all_gather(shortened(cross_key), ("dp", "seq"), axis=0, tiled=True).astype(
            cross_key.dtype
        ),
        lax.all_gather(shortened(cross_value), ("dp", "seq"), axis=0, tiled=True).astype(
            cross_value.dtype
        ),
        lax.all_gather(shortened(cross_out), ("dp", "seq"), axis=0, tiled=True).astype(
            cross_out.dtype
        ),
        lax.all_gather(shortened(ffn_gate), ("dp", "seq"), axis=0, tiled=True).astype(
            ffn_gate.dtype
        ),
        lax.all_gather(shortened(ffn_up), ("dp", "seq"), axis=0, tiled=True).astype(ffn_up.dtype),
        lax.all_gather(shortened(ffn_down), ("dp", "seq"), axis=0, tiled=True).astype(
            ffn_down.dtype
        ),
        lax.all_gather(shortened(norm_self), ("dp", "seq"), axis=0, tiled=True).astype(
            norm_self.dtype
        ),
        lax.all_gather(shortened(norm_cross), ("dp", "seq"), axis=0, tiled=True).astype(
            norm_cross.dtype
        ),
        lax.all_gather(shortened(norm_ffn), ("dp", "seq"), axis=0, tiled=True).astype(
            norm_ffn.dtype
        ),
    )


def reduce_grads(grads, table_grad):
    (
        g_self_query,
        g_self_key,
        g_self_value,
        g_self_out,
        g_cross_query,
        g_cross_key,
        g_cross_value,
        g_cross_out,
        g_ffn_gate,
        g_ffn_up,
        g_ffn_down,
        g_norm_self,
        g_norm_cross,
        g_norm_ffn,
    ) = grads
    shares = (
        lax.psum_scatter(g_self_query, ("dp", "seq"), scatter_dimension=0, tiled=True),
        lax.psum_scatter(g_self_key, ("dp", "seq"), scatter_dimension=0, tiled=True),
        lax.psum_scatter(g_self_value, ("dp", "seq"), scatter_dimension=0, tiled=True),
        lax.psum_scatter(g_self_out, ("dp", "seq"), scatter_dimension=0, tiled=True),
        lax.psum_scatter(g_cross_query, ("dp", "seq"), scatter_dimension=0, tiled=True),
        lax.psum_scatter(g_cross_key, ("dp", "seq"), scatter_dimension=0, tiled=True),
        lax.psum_scatter(g_cross_value, ("dp", "seq"), scatter_dimension=0, tiled=True),
        lax.psum_scatter(g_cross_out, ("dp", "seq"), scatter_dimension=0, tiled=True),
        lax.psum_scatter(g_ffn_gate, ("dp", "seq"), scatter_dimension=0, tiled=True),
        lax.psum_scatter(g_ffn_up, ("dp", "seq"), scatter_dimension=0, tiled=True),
        lax.psum_scatter(g_ffn_down, ("dp", "seq"), scatter_dimension=0, tiled=True),
        lax.psum_scatter(g_norm_self, ("dp", "seq"), scatter_dimension=0, tiled=True),
        lax.psum_scatter(g_norm_cross, ("dp", "seq"), scatter_dimension=0, tiled=True),
        lax.psum_scatter(g_norm_ffn, ("dp", "seq"), scatter_dimension=0, tiled=True),
    )
    table_sum = lax.psum(table_grad, ("dp", "seq"))
    return (tuple(shares), table_sum)


def micro_step(weights, rows_in, memory_rows, valid, self_bias, causal, distance_hot, cot_rows):
    (
        self_query,
        self_key,
        self_value,
        self_out,
        cross_query,
        cross_key,
        cross_value,
        cross_out,
        ffn_gate,
        ffn_up,
        ffn_down,
        norm_self,
        norm_cross,
        norm_ffn,
    ) = weights
    quarter_rows = MEM_DEV // 4
    half_rows = MEM_DEV // 2
    own_count = MEM_DEV - quarter_rows
    rows_f = rows_in.astype(jnp.float32)
    normed_one, norm_back_one = jax.vjp(norm_rows, rows_f, norm_self.astype(jnp.float32))
    input_one = normed_one.astype(jnp.bfloat16)
    query_one = split_heads(project(input_one, self_query).astype(jnp.bfloat16))
    key_one = split_heads(project(input_one, self_key).astype(jnp.bfloat16))
    value_one = split_heads(project(input_one, self_value).astype(jnp.bfloat16))
    mixed_one, lse_one = self_forward(query_one, key_one, value_one, self_bias, causal)
    attn_one = join_heads(mixed_one)
    after_self = rows_f + project(attn_one, self_out)
    normed_two, norm_back_two = jax.vjp(norm_rows, after_self, norm_cross.astype(jnp.float32))
    input_two = normed_two.astype(jnp.bfloat16)
    query_two = split_heads(project(input_two, cross_query).astype(jnp.bfloat16))
    memory_keys = project(memory_rows, cross_key).astype(jnp.bfloat16)
    memory_values = project(memory_rows, cross_value).astype(jnp.bfloat16)
    next_keys, next_values = passed_along(
        (memory_keys[:half_rows], memory_values[:half_rows]), "seq", -1
    )
    key_two = split_heads(jnp.concatenate([memory_keys[quarter_rows:], next_keys], axis=0))
    value_two = split_heads(jnp.concatenate([memory_values[quarter_rows:], next_values], axis=0))
    mixed_two, lse_two = cross_forward(query_two, key_two, value_two, valid)
    attn_two = join_heads(mixed_two)
    after_cross = after_self + project(attn_two, cross_out)
    normed_three, norm_back_three = jax.vjp(norm_rows, after_cross, norm_ffn.astype(jnp.float32))
    input_three = normed_three.astype(jnp.bfloat16)
    gate_pre = project(input_three, ffn_gate)
    up_pre = project(input_three, ffn_up)
    activated, gated_back = jax.vjp(gated_units, gate_pre, up_pre)
    hidden = activated.astype(jnp.bfloat16)
    layer_out = after_cross + project(hidden, ffn_down)
    grad_out = cot_rows.astype(jnp.float32)
    grad_branch = grad_out.astype(jnp.bfloat16)
    grad_hidden = project_back(grad_branch, ffn_down)
    grad_ffn_down = weight_grad(hidden, grad_branch)
    grad_gate_full, grad_up_full = gated_back(grad_hidden)
    grad_gate_low = grad_gate_full.astype(jnp.bfloat16)
    grad_up_low = grad_up_full.astype(jnp.bfloat16)
    grad_input_three = project_back(grad_gate_low, ffn_gate) + project_back(grad_up_low, ffn_up)
    grad_ffn_gate = weight_grad(input_three, grad_gate_low)
    grad_ffn_up = weight_grad(input_three, grad_up_low)
    grad_cross_rows, grad_norm_ffn = norm_back_three(grad_input_three)
    grad_after_cross = grad_out + grad_cross_rows
    grad_branch_two = grad_after_cross.astype(jnp.bfloat16)
    grad_attn_two = project_back(grad_branch_two, cross_out).astype(jnp.bfloat16)
    grad_cross_out = weight_grad(attn_two, grad_branch_two)
    grad_query_two, grad_key_two, grad_value_two = cross_backward(
        query_two, key_two, value_two, valid, lse_two, split_heads(grad_attn_two)
    )
    grad_query_low = join_heads(grad_query_two).astype(jnp.bfloat16)
    grad_keys_all = join_heads(grad_key_two)
    grad_values_all = join_heads(grad_value_two)
    prev_keys, prev_values = passed_along(
        (shortened(grad_keys_all[own_count:]), shortened(grad_values_all[own_count:])), "seq", 1
    )
    head_zeros = jnp.zeros((quarter_rows, D), jnp.float32)
    tail_zeros = jnp.zeros((MEM_DEV - half_rows, D), jnp.float32)
    grad_memory_keys = (
        jnp.concatenate([head_zeros, grad_keys_all[:own_count]], axis=0)
        + jnp.concatenate([prev_keys, tail_zeros], axis=0)
    ).astype(jnp.bfloat16)
    grad_memory_values = (
        jnp.concatenate([head_zeros, grad_values_all[:own_count]], axis=0)
        + jnp.concatenate([prev_values, tail_zeros], axis=0)
    ).astype(jnp.bfloat16)
    grad_memory = project_back(grad_memory_keys, cross_key) + project_back(
        grad_memory_values, cross_value
    )
    grad_cross_key = weight_grad(memory_rows, grad_memory_keys)
    grad_cross_value = weight_grad(memory_rows, grad_memory_values)
    grad_input_two = project_back(grad_query_low, cross_query)
    grad_cross_query = weight_grad(input_two, grad_query_low)
    grad_self_rows, grad_norm_cross = norm_back_two(grad_input_two)
    grad_after_self = grad_after_cross + grad_self_rows
    grad_branch_one = grad_after_self.astype(jnp.bfloat16)
    grad_attn_one = project_back(grad_branch_one, self_out).astype(jnp.bfloat16)
    grad_self_out = weight_grad(attn_one, grad_branch_one)
    grad_query_one, grad_key_one, grad_value_one, table_rows = self_backward(
        query_one,
        key_one,
        value_one,
        self_bias,
        causal,
        lse_one,
        split_heads(grad_attn_one),
        distance_hot,
    )
    query_low = join_heads(grad_query_one).astype(jnp.bfloat16)
    key_low = join_heads(grad_key_one).astype(jnp.bfloat16)
    value_low = join_heads(grad_value_one).astype(jnp.bfloat16)
    grad_input_one = (
        project_back(query_low, self_query)
        + project_back(key_low, self_key)
        + project_back(value_low, self_value)
    )
    grad_self_query = weight_grad(input_one, query_low)
    grad_self_key = weight_grad(input_one, key_low)
    grad_self_value = weight_grad(input_one, value_low)
    grad_rows, grad_norm_self = norm_back_one(grad_input_one)
    grad_decoder = grad_after_self + grad_rows
    grads = (
        grad_self_query,
        grad_self_key,
        grad_self_value,
        grad_self_out,
        grad_cross_query,
        grad_cross_key,
        grad_cross_value,
        grad_cross_out,
        grad_ffn_gate,
        grad_ffn_up,
        grad_ffn_down,
        grad_norm_self,
        grad_norm_cross,
        grad_norm_ffn,
    )
    return (
        layer_out.astype(jnp.bfloat16),
        grad_decoder.astype(jnp.bfloat16),
        grad_memory.astype(jnp.bfloat16),
        grads,
        table_rows,
    )


def local(
    decoder_in,
    memory,
    doc_offsets,
    self_query,
    self_key,
    self_value,
    self_out,
    cross_query,
    cross_key,
    cross_value,
    cross_out,
    ffn_gate,
    ffn_up,
    ffn_down,
    norm_self,
    norm_cross,
    norm_ffn,
    bias_table,
    cotangent,
):
    position = lax.axis_index("seq")
    distance_bucket = distance_buckets(TGT_LEN, BUCKETS, REACH)
    distance_hot = (
        distance_bucket[:, None] == jnp.arange(BUCKETS, dtype=jnp.int32)[None, :]
    ).astype(jnp.float32)
    by_distance = jnp.einsum(
        "hb,nb->hn", bias_table.astype(jnp.float32), distance_hot, precision=lax.Precision.HIGHEST
    )
    self_bias = distance_grid(by_distance)
    positions = jnp.arange(TGT_LEN, dtype=jnp.int32)
    causal = positions[:, None] >= positions[None, :]
    outputs = []
    grad_inputs = []
    grad_memories = []
    for micro_index in range(MICRO):
        weights_now = fetch_weights(
            self_query,
            self_key,
            self_value,
            self_out,
            cross_query,
            cross_key,
            cross_value,
            cross_out,
            ffn_gate,
            ffn_up,
            ffn_down,
            norm_self,
            norm_cross,
            norm_ffn,
        )
        valid = key_masks(doc_offsets[micro_index, 0], position)
        layer_out, grad_decoder, grad_memory, step_grads, step_table = micro_step(
            weights_now,
            decoder_in[micro_index, 0],
            memory[micro_index, 0],
            valid,
            self_bias,
            causal,
            distance_hot,
            cotangent[micro_index, 0],
        )
        outputs.append(layer_out)
        grad_inputs.append(grad_decoder)
        grad_memories.append(grad_memory)
        piece_grads, piece_table = reduce_grads(step_grads, step_table)
        if micro_index == 0:
            kept_grads, kept_table = (piece_grads, piece_table)
        else:
            kept_grads = jax.tree.map(lambda first, second: first + second, kept_grads, piece_grads)
            kept_table = kept_table + piece_table
    stacked_out = jnp.stack(outputs)[:, None]
    stacked_inputs = jnp.stack(grad_inputs)[:, None]
    stacked_memory = jnp.stack(grad_memories)[:, None]
    return (stacked_out, stacked_inputs, stacked_memory) + tuple(kept_grads) + (kept_table,)


def solution(mesh):
    in_specs = (
        P(None, ("dp", "seq"), None, None),
        P(None, ("dp", "seq"), None, None),
        P(None, "dp", None),
        P(("dp", "seq"), None),
        P(("dp", "seq"), None),
        P(("dp", "seq"), None),
        P(("dp", "seq"), None),
        P(("dp", "seq"), None),
        P(("dp", "seq"), None),
        P(("dp", "seq"), None),
        P(("dp", "seq"), None),
        P(("dp", "seq"), None),
        P(("dp", "seq"), None),
        P(("dp", "seq"), None),
        P(("dp", "seq")),
        P(("dp", "seq")),
        P(("dp", "seq")),
        P(),
        P(None, ("dp", "seq"), None, None),
    )
    out_specs = (
        P(None, ("dp", "seq"), None, None),
        P(None, ("dp", "seq"), None, None),
        P(None, ("dp", "seq"), None, None),
        P(("dp", "seq"), None),
        P(("dp", "seq"), None),
        P(("dp", "seq"), None),
        P(("dp", "seq"), None),
        P(("dp", "seq"), None),
        P(("dp", "seq"), None),
        P(("dp", "seq"), None),
        P(("dp", "seq"), None),
        P(("dp", "seq"), None),
        P(("dp", "seq"), None),
        P(("dp", "seq"), None),
        P(("dp", "seq")),
        P(("dp", "seq")),
        P(("dp", "seq")),
        P(),
    )
    return jax.shard_map(local, mesh=mesh, in_specs=in_specs, out_specs=out_specs, check_vma=False)
```

profile of v0, /device:TPU:0, one launch (start us, length us, event | category | flops | bytes accessed | tf_op | source)
XLA Modules:
  0.0 2545.7 jit_solution(17809724556050053931)
XLA Ops:
  18.1 42.1 %all-reduce.17 = (bf16[768]{0:T(1024)(128)(2,1)S(1)}, bf16[768]{0:T(1024)(128)(2,1)S(1)}, bf16[768]{0:T(1024)(128)(2,1)S(1)}) all-reduce(bf16[768]{0:T(1024)(128)(2,1)S(1)} %dynamic-update-slice, bf16[768]{0:T(1024)(128)(2,1)S(1)} %dynamic-update-slice.1, ...), channel_id=1, replica_groups=mesh['dp'=4,'seq'=8] {'dp','seq'}, use_global_device_ids=true, to_apply=%add.10 | all-reduce | flops 2304 | bytes 9216
  60.8 11.6 broadcast_in_dim.207
  72.4 38.2 %reshape.524 = f32[12,523776]{1,0:T(8,128)} reshape(f32[12,512,1023]{2,1,0:T(8,128)} %broadcast_in_dim.207) | data formatting | bytes 50282496 | tf_op jit(solution)/shard_map/reshape | solution.py:72
  110.6 22.6 slice.156
  133.2 55.1 %reshape.525 = f32[12,512,1022]{2,1,0:T(8,128)} reshape(f32[12,523264]{1,0:T(8,128)} %slice.156) | data formatting | bytes 50233344 | tf_op jit(solution)/shard_map/reshape | solution.py:75
  188.3 10.7 slice.157
  199.0 12.8 copy.175
  239.9 51.9 %all-gather.16.cloned.1.call-done = bf16[768,768]{1,0:T(8,128)(2,1)} async-done(((bf16[24,768]{1,0:T(8,128)(2,1)}), bf16[768,768]{1,0:T(8,128)(2,1)}) %all-gather.16.cloned.1.call-update) | async-done | bytes 1179664 | tf_op jit(solution)/shard_map/all_gather | solution.py:231
  295.9 39.1 %while.117 = (s32[]{:T(128)}, bf16[12,512,64]{1,2,0:T(8,128)(2,1)S(1)}, f32[12,512]{1,0:T(8,128)S(1)}, bf16[12,512,64]{2,1,0:T(8,128)(2,1)}, bf16[12,512,64]{2,1...) while((s32[]{:T(128)}, ...), condition=%wide.region_17.18_spmd.clone, body=%wide.region_14.17_spmd.clone.sunk | while | flops 69500416 | bytes 4676201 | solution.py:156
  335.0 12.7 all-gather.18.cloned.1.call-done
  350.2 53.6 %all-gather.20.cloned.1.call-done = bf16[768,768]{1,0:T(8,128)(2,1)} async-done(((bf16[24,768]{1,0:T(8,128)(2,1)}), bf16[768,768]{1,0:T(8,128)(2,1)}) %all-gather.20.cloned.1.call-update) | async-done | bytes 1179664 | tf_op jit(solution)/shard_map/all_gather | solution.py:237
  438.4 45.8 %while.116 = (s32[]{:T(128)}, bf16[12,512,64]{1,2,0:T(8,128)(2,1)}, f32[12,512]{1,0:T(8,128)S(1)}, bf16[12,512,64]{2,1,0:T(8,128)(2,1)}, bf16[12,512,64]{2,1,0:T...) while((s32[]{:T(128)}, bf16[12,512,64]{1,2,0:T(8,128)(2,1)}, ...), condition=%wide.region_4.5_spmd.clone, body=%wide.region_1.0_spmd.clone.sunk | while | flops 69500416 | bytes 4676201 | solution.py:156
  501.8 4.8 copy.194
  513.3 4.8 copy.195
  518.2 47.8 %while.113 = (s32[]{:T(128)}, bf16[12,512,64]{1,2,0:T(8,128)(2,1)S(1)}, f32[12,512]{1,0:T(8,128)S(1)}, pred[1,1280]{1,0:T(4,128)(4,1)S(1)}, bf16[12,512,64]{2,1,...) while((s32[]{:T(128)}, ...), condition=%wide.region_24.25_spmd, body=%wide.region_21.24_spmd.sunk | while | flops 172391936 | bytes 8742770 | solution.py:165
  573.2 4.9 copy.181
  584.6 4.7 copy.182
  590.3 54.9 %while.112 = (s32[]{:T(128)}, bf16[12,512,64]{1,2,0:T(8,128)(2,1)}, f32[12,512]{1,0:T(8,128)S(1)}, pred[1,1280]{1,0:T(4,128)(4,1)S(1)}, bf16[12,512,64]{2,1,0:T(...) while((s32[]{:T(128)}, bf16[12,512,64]{1,2,0:T(8,128)(2,1)}, ...), condition=%wide.region_11.12_spmd, body=%wide.region_8.11_spmd.sunk | while | flops 172391936 | bytes 8742770 | solution.py:165
  650.3 5.9 fusion.331
  656.2 5.8 fusion.332
  662.0 9.2 multiply_convert_fusion.3
  682.1 6.6 multiply_convert_fusion.2
  703.0 111.7 %while.115 = (s32[]{:T(128)}, bf16[12,512,64]{1,2,0:T(8,128)(2,1)S(1)}, f32[12,1280,64]{1,2,0:T(8,128)}, f32[12,1280,64]{1,2,0:T(8,128)}, pred[1,1280]{1,0:T(4,1...) while((s32[]{:T(128)}, ...), condition=%wide.region_39.40_spmd, body=%wide.region_37.39_spmd.sunk | while | flops 424672768 | bytes 21842816 | solution.py:194
  823.4 111.9 %while.114 = (s32[]{:T(128)}, bf16[12,512,64]{1,2,0:T(8,128)(2,1)S(1)}, f32[12,1280,64]{1,2,0:T(8,128)}, f32[12,1280,64]{1,2,0:T(8,128)}, pred[1,1280]{1,0:T(4,1...) while((s32[]{:T(128)}, ...), condition=%wide.region_29.30_spmd, body=%wide.region_27.29_spmd.sunk | while | flops 424672768 | bytes 21842816 | solution.py:194
  948.7 182.1 %while.119 = (s32[]{:T(128)}, bf16[12,512,64]{1,2,0:T(8,128)(2,1)}, bf16[12,512,64]{1,2,0:T(8,128)(2,1)}, bf16[12,512,64]{1,2,0:T(8,128)(2,1)S(1)}, f32[12,32]{1...) while((s32[]{:T(128)}, bf16[12,512,64]{1,2,0:T(8,128)(2,1)}, ...), condition=%wide.region_44.45_spmd.clone, body=%wide.region_41.44_spmd.clone.sunk | while | flops 171407360 | bytes 29513756 | solution.py:182
  1137.8 189.9 %while.118 = (s32[]{:T(128)}, bf16[12,512,64]{1,2,0:T(8,128)(2,1)}, bf16[12,512,64]{1,2,0:T(8,128)(2,1)}, bf16[12,512,64]{1,2,0:T(8,128)(2,1)}, f32[12,32]{1,0:T...) while((s32[]{:T(128)}, bf16[12,512,64]{1,2,0:T(8,128)(2,1)}, ...), condition=%wide.region_34.35_spmd.clone, body=%wide.region_31.34_spmd.clone.sunk | while | flops 171407360 | bytes 29513756 | solution.py:182
  1361.0 6.5 collective-permute-start.6
  1369.1 5.1 collective-permute-start.4
  1376.3 9.1 collective-permute-done.6
  1386.8 18.6 collective-permute-done.4
  1413.0 6.6 collective-permute-start.7
  1421.1 5.6 collective-permute-start.5
  1428.8 9.3 collective-permute-done.7
  1439.5 13.1 collective-permute-done.5
  1463.3 4.6 convolution_add_fusion.6
  1471.7 4.7 convolution_add_fusion.5
  1481.5 4.6 convolution_add_fusion.4
  1500.2 47.9 %all-reduce.16 = (f32[768]{0:T(1024)S(1)}, f32[768]{0:T(1024)S(1)}, f32[768]{0:T(1024)S(1)}, f32[12,32]{1,0:T(8,128)}) all-reduce(f32[768]{0:T(1024)S(1)} %add.607, f32[768]{0:T(1024)S(1)} %add.608, f32[768]{0:T(1024)S(1)} %add.609, f32[12,32]{1,0:T(8,128)S(1)} %add.595), channel_id=27, replica_groups=mesh['dp'=4,'seq'=8] {'dp','seq'}, use_global_device_ids=true, to_apply=%region_69.70.clone | all-reduce | flops 2688 | bytes 21504
  1549.8 4.9 fusion.245
  1572.0 84.7 %reduce-scatter.20.cloned.1.call-done = f32[24,768]{1,0:T(8,128)} async-done(((f32[768,768]{1,0:T(8,128)}), f32[24,768]{1,0:T(8,128)}) %reduce-scatter.20.cloned.1.call-update) | async-done | bytes 73744 | tf_op jit(solution)/shard_map/reduce_scatter | solution.py:288
  1656.7 104.6 %reduce-scatter.22.cloned.1.call-done = f32[24,768]{1,0:T(8,128)} async-done(((f32[768,768]{1,0:T(8,128)}), f32[24,768]{1,0:T(8,128)}) %reduce-scatter.22.cloned.1.call-update) | async-done | bytes 73744 | tf_op jit(solution)/shard_map/reduce_scatter | solution.py:289
  1761.3 103.8 %reduce-scatter.24.cloned.1.call-done = f32[24,768]{1,0:T(8,128)} async-done(((f32[768,768]{1,0:T(8,128)}), f32[24,768]{1,0:T(8,128)}) %reduce-scatter.24.cloned.1.call-update) | async-done | bytes 73744 | tf_op jit(solution)/shard_map/reduce_scatter | solution.py:290
  1865.0 104.7 %reduce-scatter.26.cloned.1.call-done = f32[24,768]{1,0:T(8,128)} async-done(((f32[768,768]{1,0:T(8,128)}), f32[24,768]{1,0:T(8,128)}) %reduce-scatter.26.cloned.1.call-update) | async-done | bytes 73744 | tf_op jit(solution)/shard_map/reduce_scatter | solution.py:293
  1969.7 103.7 %reduce-scatter.34.cloned.1.call-done = f32[24,768]{1,0:T(8,128)} async-done(((f32[768,768]{1,0:T(8,128)}), f32[24,768]{1,0:T(8,128)}) %reduce-scatter.34.cloned.1.call-update) | async-done | bytes 73744
  2073.4 104.8 %reduce-scatter.36.cloned.1.call-done = f32[24,768]{1,0:T(8,128)} async-done(((f32[768,768]{1,0:T(8,128)}), f32[24,768]{1,0:T(8,128)}) %reduce-scatter.36.cloned.1.call-update) | async-done | bytes 73744
  2178.2 119.6 %reduce-scatter.28.cloned.1.call-done = f32[24,2048]{1,0:T(8,128)} async-done(((f32[768,2048]{1,0:T(8,128)}), f32[24,2048]{1,0:T(8,128)}) %reduce-scatter.28.cloned.1.call-update) | async-done | bytes 196624 | tf_op jit(solution)/shard_map/reduce_scatter | solution.py:294
  2297.8 121.0 %reduce-scatter.30.cloned.1.call-done = f32[24,2048]{1,0:T(8,128)} async-done(((f32[768,2048]{1,0:T(8,128)}), f32[24,2048]{1,0:T(8,128)}) %reduce-scatter.30.cloned.1.call-update) | async-done | bytes 196624 | tf_op jit(solution)/shard_map/reduce_scatter | solution.py:295
  2418.7 120.0 %reduce-scatter.32.cloned.1.call-done = f32[64,768]{1,0:T(8,128)} async-done(((f32[2048,768]{1,0:T(8,128)}), f32[64,768]{1,0:T(8,128)}) %reduce-scatter.32.cloned.1.call-update) | async-done | bytes 196624 | tf_op jit(solution)/shard_map/reduce_scatter | solution.py:296
  (1319 shorter events, 1059.4 us)
Async XLA Ops:
  7.2 208.1 %all-gather.22.cloned.1.call-start = ((), (), s32[]{:S(2)}) async-start(), calls=%async_computation.16 | async-start | bytes 1216512 | tf_op jit(solution)/shard_map/all_gather | solution.py:240
  8.0 211.4 %all-gather.24.cloned.1.call-start = ((), (), s32[]{:S(2)}) async-start(), calls=%async_computation.17 | async-start | bytes 1216512 | tf_op jit(solution)/shard_map/all_gather | solution.py:243
  8.7 221.8 %all-gather.12.cloned.1.call-start = ((), (), s32[]{:S(2)}) async-start(), calls=%async_computation.11 | async-start | bytes 1216512 | tf_op jit(solution)/shard_map/all_gather | solution.py:225
  9.5 226.5 %all-gather.14.cloned.1.call-start = ((), (), s32[]{:S(2)}) async-start(), calls=%async_computation.12 | async-start | bytes 1216512 | tf_op jit(solution)/shard_map/all_gather | solution.py:228
  10.0 281.8 %all-gather.16.cloned.1.call-start = ((), (), s32[]{:S(2)}) async-start(), calls=%async_computation.13 | async-start | bytes 1216512 | tf_op jit(solution)/shard_map/all_gather | solution.py:231
  10.6 337.1 %all-gather.18.cloned.1.call-start = ((), (), s32[]{:S(2)}) async-start(), calls=%async_computation.14 | async-start | bytes 1216512 | tf_op jit(solution)/shard_map/all_gather | solution.py:234
  11.2 392.5 %all-gather.20.cloned.1.call-start = ((), (), s32[]{:S(2)}) async-start(), calls=%async_computation.15 | async-start | bytes 1216512 | tf_op jit(solution)/shard_map/all_gather | solution.py:237
  11.9 633.3 %all-gather.26.cloned.1.call-start = ((), (), s32[]{:S(2)}) async-start(), calls=%async_computation.18 | async-start | bytes 1216512 | tf_op jit(solution)/shard_map/all_gather | solution.py:246
  12.7 637.6 %all-gather.28.cloned.1.call-start = ((), (), s32[]{:S(2)}) async-start(), calls=%async_computation.19 | async-start | bytes 3244032 | tf_op jit(solution)/shard_map/all_gather | solution.py:249
  13.4 642.8 %all-gather.30.cloned.1.call-start = ((), (), s32[]{:S(2)}) async-start(), calls=%async_computation.20 | async-start | bytes 3244032 | tf_op jit(solution)/shard_map/all_gather | solution.py:252
  14.0 648.0 %all-gather.32.cloned.1.call-start = ((), (), s32[]{:S(2)}) async-start(), calls=%async_computation.21 | async-start | bytes 3244032 | tf_op jit(solution)/shard_map/all_gather | solution.py:253
  14.8 1557.2 %reduce-scatter.16.cloned.1.call-start = ((), (), s32[]{:S(2)}) async-start(), calls=%async_computation.22 | async-start | bytes 2433024 | tf_op jit(solution)/shard_map/reduce_scatter | solution.py:286
  17.4 42.9 %copy-start.80 = (f32[512]{0:T(512)}, f32[512]{0:T(512)S(1)}, u32[]{:S(2)}) copy-start(f32[512]{0:T(512)S(1)} %get-tuple-element.841) | copy-start | bytes 6148
  17.4 196.5 %copy-start.78 = (f32[512]{0:T(512)}, f32[512]{0:T(512)S(1)}, u32[]{:S(2)}) copy-start(f32[512]{0:T(512)S(1)} %get-tuple-element.840) | copy-start | bytes 6148
  17.4 274.5 %copy-start.70 = (f32[512]{0:T(512)}, f32[512]{0:T(512)S(1)}, u32[]{:S(2)}) copy-start(f32[512]{0:T(512)S(1)} %fusion.287) | copy-start | bytes 6148
  60.3 369.4 %copy-start.64 = (f32[768]{0:T(1024)}, f32[768]{0:T(1024)S(1)}, u32[]{:S(2)}) copy-start(f32[768]{0:T(1024)S(1)} %convert_element_type.507) | copy-start | bytes 9220
  199.0 16.3 copy-start.93
  213.9 273.0 %copy-start.66 = (f32[768]{0:T(1024)}, f32[768]{0:T(1024)S(1)}, u32[]{:S(2)}) copy-start(f32[768]{0:T(1024)S(1)} %convert_element_type.527) | copy-start | bytes 9220
  213.9 215.8 %copy-start.72 = (f32[512]{0:T(512)}, f32[512]{0:T(512)S(1)}, u32[]{:S(2)}) copy-start(f32[512]{0:T(512)S(1)} %fusion.284) | copy-start | bytes 6148
  334.9 15.2 copy-start.68
  350.1 56.7 %copy-start.84 = (f32[512]{0:T(512)}, f32[512]{0:T(512)S(1)}, u32[]{:S(2)}) copy-start(f32[512]{0:T(512)S(1)} %get-tuple-element.1030) | copy-start | bytes 6148
  350.1 297.7 %copy-start.4 = (f32[512,768]{1,0:T(8,128)}, f32[512,768]{1,0:T(8,128)S(1)}, u32[]{:S(2)}) copy-start(f32[512,768]{1,0:T(8,128)S(1)} %get-tuple-element.1031) | copy-start | bytes 4718596
  350.2 56.6 %copy-start.76 = (f32[512]{0:T(512)}, f32[512]{0:T(512)S(1)}, u32[]{:S(2)}) copy-start(f32[512]{0:T(512)S(1)} %fusion.288) | copy-start | bytes 6148
  411.6 83.5 %collective-permute-start.2 = (bf16[512,768]{1,0:T(8,128)(2,1)}, bf16[512,768]{1,0:T(8,128)(2,1)}, u32[]{:S(2)}, u32[]{:S(2)}) collective-permute-start(bf16[512,768]{1,0:T(8,128)(2,1)} %slice.163), channel_id=1, source_target_pairs={{1,0},{2,1},{3,2},{4,3},{5,4},{6,5},{7,6},{9,8},{10,9},{11,10},{12... | collective-permute-start | bytes 2359304 | tf_op jit(solution)/shard_map/ppermute | solution.py:33
  412.9 93.8 %collective-permute-start.3 = (bf16[512,768]{1,0:T(8,128)(2,1)}, bf16[512,768]{1,0:T(8,128)(2,1)}, u32[]{:S(2)}, u32[]{:S(2)}) collective-permute-start(bf16[512,768]{1,0:T(8,128)(2,1)} %slice.165), channel_id=1, source_target_pairs={{1,0},{2,1},{3,2},{4,3},{5,4},{6,5},{7,6},{9,8},{10,9},{11,10},{12... | collective-permute-start | bytes 2359304 | tf_op jit(solution)/shard_map/ppermute | solution.py:33
  492.5 73.5 %collective-permute-start = (bf16[512,768]{1,0:T(8,128)(2,1)}, bf16[512,768]{1,0:T(8,128)(2,1)}, u32[]{:S(2)}, u32[]{:S(2)}) collective-permute-start(bf16[512,768]{1,0:T(8,128)(2,1)} %slice.159), channel_id=1, source_target_pairs={{1,0},{2,1},{3,2},{4,3},{5,4},{6,5},{7,6},{9,8},{10,9},{11,10},{12... | collective-permute-start | bytes 2359304 | tf_op jit(solution)/shard_map/ppermute | solution.py:33
  493.8 84.3 %collective-permute-start.1 = (bf16[512,768]{1,0:T(8,128)(2,1)}, bf16[512,768]{1,0:T(8,128)(2,1)}, u32[]{:S(2)}, u32[]{:S(2)}) collective-permute-start(bf16[512,768]{1,0:T(8,128)(2,1)} %slice.161), channel_id=1, source_target_pairs={{1,0},{2,1},{3,2},{4,3},{5,4},{6,5},{7,6},{9,8},{10,9},{11,10},{12... | collective-permute-start | bytes 2359304 | tf_op jit(solution)/shard_map/ppermute | solution.py:33
  590.3 54.9 %copy-start.8 = (f32[512,768]{1,0:T(8,128)S(1)}, f32[512,768]{1,0:T(8,128)}, u32[]{:S(2)}) copy-start(f32[512,768]{1,0:T(8,128)} %copy-done.7) | copy-start | bytes 4718596
  1130.9 210.9 %copy-start.25 = (bf16[12,512,64]{1,2,0:T(8,128)(2,1)}, bf16[12,512,64]{1,2,0:T(8,128)(2,1)S(1)}, u32[]{:S(2)}) copy-start(bf16[12,512,64]{1,2,0:T(8,128)(2,1)S(1)} %get-tuple-element.443) | copy-start | bytes 2359300
  1137.8 189.9 %copy-start.65 = (f32[768]{0:T(1024)S(1)}, f32[768]{0:T(1024)}, u32[]{:S(2)}) copy-start(f32[768]{0:T(1024)} %copy-done.64) | copy-start | bytes 9220
  1137.8 189.9 %copy-start.73 = (f32[512]{0:T(512)S(1)}, f32[512]{0:T(512)}, u32[]{:S(2)}) copy-start(f32[512]{0:T(512)} %copy-done.72) | copy-start | bytes 6148
  1333.8 238.2 %reduce-scatter.18.cloned.1.call-start = ((), (), s32[]{:S(2)}) async-start(), calls=%async_computation.23 | async-start | bytes 2433024 | tf_op jit(solution)/shard_map/reduce_scatter | solution.py:287
  1339.6 317.1 %reduce-scatter.20.cloned.1.call-start = ((), (), s32[]{:S(2)}) async-start(), calls=%async_computation.24 | async-start | bytes 2433024 | tf_op jit(solution)/shard_map/reduce_scatter | solution.py:288
  1344.2 417.1 %reduce-scatter.22.cloned.1.call-start = ((), (), s32[]{:S(2)}) async-start(), calls=%async_computation.25 | async-start | bytes 2433024 | tf_op jit(solution)/shard_map/reduce_scatter | solution.py:289
  1349.1 516.0 %reduce-scatter.24.cloned.1.call-start = ((), (), s32[]{:S(2)}) async-start(), calls=%async_computation.26 | async-start | bytes 2433024 | tf_op jit(solution)/shard_map/reduce_scatter | solution.py:290
  1354.5 615.2 %reduce-scatter.26.cloned.1.call-start = ((), (), s32[]{:S(2)}) async-start(), calls=%async_computation.27 | async-start | bytes 2433024 | tf_op jit(solution)/shard_map/reduce_scatter | solution.py:293
  1359.4 714.0 %reduce-scatter.34.cloned.1.call-start = ((), (), s32[]{:S(2)}) async-start(), calls=%async_computation.31 | async-start | bytes 2433024
  1361.0 24.4 collective-permute-start.6
  1369.1 36.4 %collective-permute-start.4 = (bf16[512,768]{0,1:T(8,128)(2,1)S(1)}, bf16[512,768]{0,1:T(8,128)(2,1)S(1)}, u32[]{:S(2)}, u32[]{:S(2)}) collective-permute-start(bf16[512,768]{0,1:T(8,128)(2,1)S(1)} %bitcast.792), channel_id=1, source_target_pairs={{0,1},{1,2},{2,3},{3,4},{4,5},{5,6},{6,7},{8,9},{9,10},{10,11},{11... | collective-permute-start | bytes 2359304 | tf_op jit(solution)/shard_map/ppermute | solution.py:33
  1376.3 29.2 %copy-start.47 = (f32[768,12,64]{0,2,1:T(8,128)}, f32[768,12,64]{0,2,1:T(8,128)S(1)}, u32[]{:S(2)}) copy-start(f32[768,12,64]{0,2,1:T(8,128)S(1)} %slice.166) | copy-start | bytes 7077892
  1411.5 766.7 %reduce-scatter.36.cloned.1.call-start = ((), (), s32[]{:S(2)}) async-start(), calls=%async_computation.32 | async-start | bytes 2433024
  1413.0 25.0 collective-permute-start.7
  1421.1 31.5 %collective-permute-start.5 = (bf16[512,768]{0,1:T(8,128)(2,1)S(1)}, bf16[512,768]{0,1:T(8,128)(2,1)S(1)}, u32[]{:S(2)}, u32[]{:S(2)}) collective-permute-start(bf16[512,768]{0,1:T(8,128)(2,1)S(1)} %bitcast.793), channel_id=1, source_target_pairs={{0,1},{1,2},{2,3},{3,4},{4,5},{5,6},{6,7},{8,9},{9,10},{10,11},{11... | collective-permute-start | bytes 2359304 | tf_op jit(solution)/shard_map/ppermute | solution.py:33
  1428.8 23.9 copy-start.51
  1458.6 839.2 %reduce-scatter.28.cloned.1.call-start = ((), (), s32[]{:S(2)}) async-start(), calls=%async_computation.28 | async-start | bytes 6488064 | tf_op jit(solution)/shard_map/reduce_scatter | solution.py:294
  1468.0 950.7 %reduce-scatter.30.cloned.1.call-start = ((), (), s32[]{:S(2)}) async-start(), calls=%async_computation.29 | async-start | bytes 6488064 | tf_op jit(solution)/shard_map/reduce_scatter | solution.py:295
  1476.4 1062.3 %reduce-scatter.32.cloned.1.call-start = ((), (), s32[]{:S(2)}) async-start(), calls=%async_computation.30 | async-start | bytes 6488064 | tf_op jit(solution)/shard_map/reduce_scatter | solution.py:296
  1570.0 968.7 %copy-start.1 = (bf16[12,32]{1,0:T(8,128)(2,1)S(1)}, bf16[12,32]{1,0:T(8,128)(2,1)}, u32[]{:S(2)}) copy-start(bf16[12,32]{1,0:T(8,128)(2,1)} %param.52) | copy-start | bytes 2308
  (103 other events, 369.2 us)
Sparse Core Ops, SparseCore 0:
  11.0 56.9 all-gather.21
  70.9 53.1 all-gather.23
  127.0 53.0 all-gather.11
  182.9 53.0 all-gather.13
  238.7 53.0 all-gather.15
  294.6 53.0 all-gather.17
  350.6 53.0 all-gather.19
  406.6 54.4 all-gather.25
  464.1 65.6 all-gather.27
  532.6 59.3 all-gather.29
  594.9 57.9 all-gather.31
  1333.9 113.6 reduce-scatter.15
  1454.3 98.4 reduce-scatter.17
  1558.5 98.0 reduce-scatter.19
  1663.2 98.0 reduce-scatter.21
  1767.0 97.9 reduce-scatter.23
  1871.6 98.0 reduce-scatter.25
  1975.4 97.9 reduce-scatter.33
  2080.1 98.0 reduce-scatter.35
  2184.2 113.4 reduce-scatter.27
  2304.9 113.7 reduce-scatter.29
  2424.9 113.7 reduce-scatter.31
where the time goes:
time: 2570 us; the launch traced here: 2550 us
  waiting for transfers between devices  1140 us (44%)
  matrix products  760 us (30%)
  local copies, waits for them, and re-layouts  440 us (17%)
  blocking collectives  90 us (4%)
  other arithmetic  61.4 us (2%)
  starting transfers between devices  30.6 us (1%)
    unnamed x24, waiting for transfers between devices  216 us
    dot_general x96, matrix products, head_scores(): jnp.einsum('qe,ke->qk', query_h, key_h, preferred_element_type=jnp.float32)  170 us
    reduce_scatter x1, waiting for transfers between devices, reduce_grads(): lax.psum_scatter(g_ffn_up, ('dp', 'seq'), scatter_dimension=0, tiled=True)  121 us
    reduce_scatter x1, waiting for transfers between devices, reduce_grads(): lax.psum_scatter(g_ffn_down, ('dp', 'seq'), scatter_dimension=0, tiled=True)  120 us
    reduce_scatter x1, waiting for transfers between devices, reduce_grads(): lax.psum_scatter(g_ffn_gate, ('dp', 'seq'), scatter_dimension=0, tiled=True)  120 us
    reduce_scatter x1, waiting for transfers between devices, reduce_grads(): lax.psum_scatter(g_cross_out, ('dp', 'seq'), scatter_dimension=0, tiled=T...  105 us
    reduce_scatter x1, waiting for transfers between devices, reduce_grads(): lax.psum_scatter(g_self_out, ('dp', 'seq'), scatter_dimension=0, tiled=True)  105 us
    reduce_scatter x1, waiting for transfers between devices, reduce_grads(): lax.psum_scatter(g_cross_query, ('dp', 'seq'), scatter_dimension=0, tiled...  104 us
  transfers between devices with their start and end apart: 30, of which 17 were waited for; matrix products, arithmetic and copies ran while one was open for 23% of the time, Pallas kernels for 0%

commit v1 on v0

v1 whole, which is shorter than its diff:
```python
import math

import jax
import jax.numpy as jnp
from jax import lax
from jax.experimental import pallas as pl
from jax.experimental.pallas import tpu as pltpu
from jax.sharding import PartitionSpec as P

D = 768
HEADS = 12
HEAD_DIM = 64
BUCKETS = 32
REACH = 128
TGT_LEN = 512
MEM_DEV = 1024
MICRO = 2
PAIRS = HEADS // 2
LANES = 2 * HEAD_DIM
OWN = MEM_DEV - MEM_DEV // 4
NEXT = MEM_DEV // 2
KEYS = OWN + NEXT
HALF = 256
MASKED = -1e30
NORM_EPS = 1e-06
AXES = ("dp", "seq")
BF = jnp.bfloat16
F32 = jnp.float32


def nn(a, b):
    return lax.dot_general(a, b, (((1,), (0,)), ((), ())), preferred_element_type=F32)


def bucket_limits(buckets, reach):
    exact_count = buckets // 2
    limits = []
    for target in range(exact_count + 1, buckets):
        distance = exact_count
        while (
            exact_count
            + int(
                math.log(distance / exact_count)
                / math.log(reach / exact_count)
                * (buckets - exact_count)
            )
            < target
        ):
            distance += 1
        limits.append(distance)
    return limits


def three_parts(row):
    high = row.astype(BF).astype(F32)
    rest = row - high
    middle = rest.astype(BF).astype(F32)
    return high, middle, rest - middle


def extra_rows(columns, first, parts):
    row_id = lax.broadcasted_iota(jnp.int32, (LANES, columns), 0)
    grid = jnp.where(row_id == 0, first, 0.0)
    for place, part in enumerate(parts):
        grid = jnp.where(row_id == place + 1, part, grid)
    return grid.astype(BF)


def head_rows(stacked, head):
    row_id = lax.broadcasted_iota(jnp.int32, stacked.shape, 0)
    return jnp.where((row_id // HEAD_DIM) == head, stacked, jnp.zeros_like(stacked))


def bias_tiles_kernel(table_ref, tiles_ref):
    head = pl.program_id(0)
    key_id = lax.broadcasted_iota(jnp.int32, (HALF, HALF), 0)
    query_id = lax.broadcasted_iota(jnp.int32, (HALF, HALF), 1)
    limits = bucket_limits(BUCKETS, REACH)
    exact_count = BUCKETS // 2
    for tile in range(2):
        distance = query_id - key_id + tile * HALF
        grid = jnp.full((HALF, HALF), table_ref[head, 0], F32)
        for bucket in range(1, BUCKETS):
            start = bucket if bucket <= exact_count else limits[bucket - exact_count - 1]
            grid = jnp.where(distance >= start, table_ref[head, bucket], grid)
        if tile == 0:
            grid = jnp.where(distance >= 0, grid, MASKED)
        tiles_ref[0, tile] = grid


def bias_tiles(table):
    return pl.pallas_call(
        bias_tiles_kernel,
        grid=(HEADS,),
        in_specs=[pl.BlockSpec(memory_space=pltpu.SMEM)],
        out_specs=pl.BlockSpec((1, 2, HALF, HALF), lambda h: (h, 0, 0, 0)),
        out_shape=jax.ShapeDtypeStruct((HEADS, 2, HALF, HALF), F32),
        name="bias_tiles",
    )(table)


def softmax_columns(scores):
    top = jnp.max(scores, axis=0, keepdims=True)
    weights = jnp.exp(scores - top)
    total = jnp.sum(weights, axis=0, keepdims=True)
    return weights.astype(BF), 1.0 / total, top + jnp.log(total)


def put_lse(lse_ref, rows):
    row_id = lax.broadcasted_iota(jnp.int32, (8, TGT_LEN), 0)
    lse_ref[0] = jnp.where(row_id == 0, rows[0], rows[1])


def cross_forward_kernel(q_ref, ko_ref, kn_ref, vo_ref, vn_ref, mask_ref, o_ref, lse_ref, k_ext):
    k_ext[:OWN, :LANES] = ko_ref[MEM_DEV - OWN :, :]
    k_ext[OWN:, :LANES] = kn_ref[...]
    k_ext[:, LANES:] = mask_ref[0]
    q_t = q_ref[...].T
    v_t = jnp.concatenate([vo_ref[MEM_DEV - OWN :, :], vn_ref[...]], axis=0).T
    ones = extra_rows(TGT_LEN, 1.0, ())
    mixed, lses = [], []
    for head in range(2):
        query = jnp.concatenate([head_rows(q_t, head), ones], axis=0)
        scores = nn(k_ext[...], query)
        weights, inverse, lse = softmax_columns(scores)
        mixed.append(nn(v_t[head * HEAD_DIM : (head + 1) * HEAD_DIM], weights) * inverse)
        lses.append(lse)
    o_ref[...] = jnp.concatenate(mixed, axis=0).T.astype(BF)
    put_lse(lse_ref, lses)


def cross_backward_kernel(
    q_ref, ko_ref, kn_ref, vo_ref, vn_ref, mask_ref, o_ref, do_ref, lse_ref,
    dq_ref, own_ref, next_ref, k_ext, v_ext,
):
    k_ext[:OWN, :LANES] = ko_ref[MEM_DEV - OWN :, :]
    k_ext[OWN:, :LANES] = kn_ref[...]
    k_ext[:, LANES:] = mask_ref[0]
    v_ext[:OWN, :LANES] = vo_ref[MEM_DEV - OWN :, :]
    v_ext[OWN:, :LANES] = vn_ref[...]
    v_ext[:, LANES:] = jnp.ones((KEYS, LANES), BF)
    k_t = k_ext[:, :LANES].T
    q = q_ref[...]
    d_o = do_ref[...]
    q_t = q.T
    do_t = d_o.T
    centre_t = (o_ref[...].astype(F32) * d_o.astype(F32)).T
    dq, dk, dv = [], [], []
    for head in range(2):
        rows = slice(head * HEAD_DIM, (head + 1) * HEAD_DIM)
        lse = lse_ref[0, head : head + 1, :]
        centre = jnp.sum(centre_t[rows], axis=0, keepdims=True)
        query = jnp.concatenate(
            [head_rows(q_t, head), extra_rows(TGT_LEN, 1.0, three_parts(-lse))], axis=0
        )
        grad = jnp.concatenate(
            [head_rows(do_t, head), extra_rows(TGT_LEN, 0.0, three_parts(-centre))], axis=0
        )
        probs = jnp.exp(nn(k_ext[...], query))
        grad_scores = (probs * nn(v_ext[...], grad)).astype(BF)
        dv.append(nn(probs.astype(BF), d_o))
        dk.append(nn(grad_scores, q))
        dq.append(nn(k_t[rows], grad_scores))
    dq_ref[...] = jnp.concatenate(dq, axis=0).T.astype(BF)
    lane = lax.broadcasted_iota(jnp.int32, (KEYS, LANES), 1)
    dk_pair = jnp.where(lane < HEAD_DIM, dk[0], dk[1]).astype(BF)
    dv_pair = jnp.where(lane < HEAD_DIM, dv[0], dv[1]).astype(BF)
    front = jnp.zeros((MEM_DEV - OWN, LANES), BF)
    for place, pair in enumerate((dk_pair, dv_pair)):
        own_ref[place, : MEM_DEV - OWN, :] = front
        own_ref[place, MEM_DEV - OWN :, :] = pair[:OWN]
        next_ref[place] = pair[OWN:]


def self_forward_kernel(q_ref, k_ref, v_ref, tiles_ref, o_ref, lse_ref):
    k = k_ref[...]
    q_t = q_ref[...].T
    v_t = v_ref[...].T
    mixed, lses = [], []
    for head in range(2):
        query = head_rows(q_t, head)
        value = v_t[head * HEAD_DIM : (head + 1) * HEAD_DIM]
        near, far = tiles_ref[head, 0], tiles_ref[head, 1]
        w0, i0, l0 = softmax_columns(nn(k[:HALF], query[:, :HALF]) + near)
        raw = nn(k, query[:, HALF:])
        w1, i1, l1 = softmax_columns(
            jnp.concatenate([raw[:HALF] + far, raw[HALF:] + near], axis=0)
        )
        out0 = nn(value[:, :HALF], w0) * i0
        out1 = nn(value, w1) * i1
        mixed.append(jnp.concatenate([out0, out1], axis=1))
        lses.append(jnp.concatenate([l0, l1], axis=1))
    o_ref[...] = jnp.concatenate(mixed, axis=0).T.astype(BF)
    put_lse(lse_ref, lses)


def self_backward_kernel(
    q_ref, k_ref, v_ref, tiles_ref, o_ref, do_ref, lse_ref,
    dq_ref, dk_ref, dv_ref, near_ref, far_ref, k_ext, v_ext,
):
    row_ext = jnp.ones((TGT_LEN, LANES), BF)
    k_ext[:, :LANES] = k_ref[...]
    k_ext[:, LANES:] = row_ext
    v_ext[:, :LANES] = v_ref[...]
    v_ext[:, LANES:] = row_ext
    k_t = k_ref[...].T
    q = q_ref[...]
    d_o = do_ref[...]
    q_t = q.T
    do_t = d_o.T
    centre_t = (o_ref[...].astype(F32) * d_o.astype(F32)).T
    first = pl.program_id(1) == 0
    dq, dk, dv = [], [], []
    for head in range(2):
        rows = slice(head * HEAD_DIM, (head + 1) * HEAD_DIM)
        lse = lse_ref[0, head : head + 1, :]
        centre = jnp.sum(centre_t[rows], axis=0, keepdims=True)
        query = jnp.concatenate(
            [head_rows(q_t, head), extra_rows(TGT_LEN, 0.0, three_parts(-lse))], axis=0
        )
        grad = jnp.concatenate(
            [head_rows(do_t, head), extra_rows(TGT_LEN, 0.0, three_parts(-centre))], axis=0
        )
        near, far = tiles_ref[head, 0], tiles_ref[head, 1]
        raw0 = nn(k_ext[:HALF, :], query[:, :HALF])
        raw1 = nn(k_ext[...], query[:, HALF:])
        p00 = jnp.exp(raw0 + near)
        p10 = jnp.exp(raw1[:HALF] + far)
        p11 = jnp.exp(raw1[HALF:] + near)
        g0 = nn(v_ext[:HALF, :], grad[:, :HALF])
        g1 = nn(v_ext[...], grad[:, HALF:])
        s00 = p00 * g0
        s10 = p10 * g1[:HALF]
        s11 = p11 * g1[HALF:]
        near_sum, far_sum = s00 + s11, s10

        @pl.when(first)
        def _():
            near_ref[head] = near_sum
            far_ref[head] = far_sum

        @pl.when(jnp.logical_not(first))
        def _():
            near_ref[head] += near_sum
            far_ref[head] += far_sum

        b00, b10, b11 = s00.astype(BF), s10.astype(BF), s11.astype(BF)
        w00, w10, w11 = p00.astype(BF), p10.astype(BF), p11.astype(BF)
        top = jnp.concatenate([w00, w10], axis=1)
        dv.append(jnp.concatenate([nn(top, d_o), nn(w11, d_o[HALF:])], axis=0))
        top = jnp.concatenate([b00, b10], axis=1)
        dk.append(jnp.concatenate([nn(top, q), nn(b11, q[HALF:])], axis=0))
        dq.append(
            jnp.concatenate(
                [
                    nn(k_t[rows, :HALF], b00),
                    nn(k_t[rows], jnp.concatenate([b10, b11], axis=0)),
                ],
                axis=1,
            )
        )
    dq_ref[...] = jnp.concatenate(dq, axis=0).T.astype(BF)
    lane = lax.broadcasted_iota(jnp.int32, (TGT_LEN, LANES), 1)
    dk_ref[...] = jnp.where(lane < HEAD_DIM, dk[0], dk[1]).astype(BF)
    dv_ref[...] = jnp.where(lane < HEAD_DIM, dv[0], dv[1]).astype(BF)


PAIR_GRID = (MICRO, PAIRS)
VMEM_LIMIT = 56 * 1024 * 1024


def params():
    return pltpu.CompilerParams(vmem_limit_bytes=VMEM_LIMIT)


def pair_block(rows, offset=0):
    return pl.BlockSpec((rows, LANES), lambda m, p: (m, p + offset))


LSE_BLOCK = pl.BlockSpec((1, 8, TGT_LEN), lambda m, p: (m * PAIRS + p, 0, 0))
LSE_SHAPE = jax.ShapeDtypeStruct((MICRO * PAIRS, 8, TGT_LEN), F32)
MASK_BLOCK = pl.BlockSpec((1, KEYS, LANES), lambda m, p: (m, 0, 0))
ROWS = MICRO * TGT_LEN


def cross_forward(q, kv_own, kv_next, mask):
    return pl.pallas_call(
        cross_forward_kernel,
        grid=PAIR_GRID,
        in_specs=[
            pair_block(TGT_LEN),
            pair_block(MEM_DEV),
            pair_block(NEXT),
            pair_block(MEM_DEV, PAIRS),
            pair_block(NEXT, PAIRS),
            MASK_BLOCK,
        ],
        out_specs=[pair_block(TGT_LEN), LSE_BLOCK],
        out_shape=[jax.ShapeDtypeStruct((ROWS, D), BF), LSE_SHAPE],
        scratch_shapes=[pltpu.VMEM((KEYS, 2 * LANES), BF)],
        compiler_params=params(),
        name="cross_forward",
    )(q, kv_own, kv_next, kv_own, kv_next, mask)


def cross_backward(q, kv_own, kv_next, mask, o, d_o, lse):
    return pl.pallas_call(
        cross_backward_kernel,
        grid=PAIR_GRID,
        in_specs=[
            pair_block(TGT_LEN),
            pair_block(MEM_DEV),
            pair_block(NEXT),
            pair_block(MEM_DEV, PAIRS),
            pair_block(NEXT, PAIRS),
            MASK_BLOCK,
            pair_block(TGT_LEN),
            pair_block(TGT_LEN),
            LSE_BLOCK,
        ],
        out_specs=[
            pair_block(TGT_LEN),
            pl.BlockSpec((2, MEM_DEV, LANES), lambda m, p: (0, m, p)),
            pl.BlockSpec((2, NEXT, LANES), lambda m, p: (0, m, p)),
        ],
        out_shape=[
            jax.ShapeDtypeStruct((ROWS, D), BF),
            jax.ShapeDtypeStruct((2, MICRO * MEM_DEV, D), BF),
            jax.ShapeDtypeStruct((2, MICRO * NEXT, D), BF),
        ],
        scratch_shapes=[pltpu.VMEM((KEYS, 2 * LANES), BF)] * 2,
        compiler_params=params(),
        name="cross_backward",
    )(q, kv_own, kv_next, kv_own, kv_next, mask, o, d_o, lse)


def swapped(spec):
    index = spec.index_map
    return pl.BlockSpec(spec.block_shape, lambda p, m: index(m, p))


TILE_BLOCK = pl.BlockSpec((2, 2, HALF, HALF), lambda p, m: (p, 0, 0, 0))


def self_forward(qkv, tiles):
    return pl.pallas_call(
        self_forward_kernel,
        grid=(PAIRS, MICRO),
        in_specs=[
            swapped(pair_block(TGT_LEN)),
            swapped(pair_block(TGT_LEN, PAIRS)),
            swapped(pair_block(TGT_LEN, 2 * PAIRS)),
            TILE_BLOCK,
        ],
        out_specs=[swapped(pair_block(TGT_LEN)), swapped(LSE_BLOCK)],
        out_shape=[jax.ShapeDtypeStruct((ROWS, D), BF), LSE_SHAPE],
        compiler_params=params(),
        name="self_forward",
    )(qkv, qkv, qkv, tiles)


def self_backward(qkv, tiles, o, d_o, lse):
    rows = jax.ShapeDtypeStruct((ROWS, D), BF)
    sums = jax.ShapeDtypeStruct((HEADS, HALF, HALF), F32)
    sum_block = pl.BlockSpec((2, HALF, HALF), lambda p, m: (p, 0, 0))
    return pl.pallas_call(
        self_backward_kernel,
        grid=(PAIRS, MICRO),
        in_specs=[
            swapped(pair_block(TGT_LEN)),
            swapped(pair_block(TGT_LEN, PAIRS)),
            swapped(pair_block(TGT_LEN, 2 * PAIRS)),
            TILE_BLOCK,
            swapped(pair_block(TGT_LEN)),
            swapped(pair_block(TGT_LEN)),
            swapped(LSE_BLOCK),
        ],
        out_specs=[swapped(pair_block(TGT_LEN))] * 3 + [sum_block] * 2,
        out_shape=[rows, rows, rows, sums, sums],
        scratch_shapes=[pltpu.VMEM((TGT_LEN, 2 * LANES), BF)] * 2,
        compiler_params=params(),
        name="self_backward",
    )(qkv, qkv, qkv, tiles, o, d_o, lse)


def distance_sums_kernel(near_ref, far_ref, sums_ref):
    near, far = near_ref[0], far_ref[0]
    key_id = lax.broadcasted_iota(jnp.int32, (HALF, HALF), 0)
    query_id = lax.broadcasted_iota(jnp.int32, (HALF, HALF), 1)
    close = (query_id - key_id + HALF) < REACH
    both = near + jnp.where(close, far, 0.0)
    group = both[:8]
    for first in range(8, HALF, 8):
        group = group + pltpu.roll(both[first : first + 8], HALF - first, 1)
    row_id = lax.broadcasted_iota(jnp.int32, (8, HALF), 0)
    turned = group
    for row in range(1, 8):
        turned = jnp.where(row_id == row, pltpu.roll(group, HALF - row, 1), turned)
    by_distance = jnp.sum(turned, axis=0, keepdims=True)
    rest = jnp.sum(jnp.where(close, 0.0, far), axis=0, keepdims=True)
    sums_ref[0] = jnp.where(row_id == 0, by_distance, jnp.where(row_id == 1, rest, 0.0))


def distance_sums(near, far):
    block = pl.BlockSpec((1, HALF, HALF), lambda h: (h, 0, 0))
    return pl.pallas_call(
        distance_sums_kernel,
        grid=(HEADS,),
        in_specs=[block, block],
        out_specs=pl.BlockSpec((1, 8, HALF), lambda h: (h, 0, 0)),
        out_shape=jax.ShapeDtypeStruct((HEADS, 8, HALF), F32),
        name="distance_sums",
    )(near, far)


def table_grad(near, far):
    sums = distance_sums(near, far)
    limits = bucket_limits(BUCKETS, REACH)
    starts = list(range(BUCKETS // 2 + 1)) + limits + [HALF]
    columns = [
        jnp.sum(sums[:, 0, starts[b] : starts[b + 1]], axis=1) for b in range(BUCKETS - 1)
    ]
    columns.append(jnp.sum(sums[:, 0, starts[BUCKETS - 1] :], axis=1) + jnp.sum(sums[:, 1], axis=1))
    return jnp.stack(columns, axis=1)


def key_masks(offsets_row, position):
    shard_ids = jnp.arange(offsets_row.shape[0], dtype=jnp.int32)
    own_start = jnp.sum(jnp.where(shard_ids == position, offsets_row, 0))
    next_start = jnp.sum(jnp.where(shard_ids == position + 1, offsets_row, 0))
    own_valid = jnp.arange(MEM_DEV - OWN, MEM_DEV, dtype=jnp.int32) >= own_start
    next_valid = jnp.arange(NEXT, dtype=jnp.int32) < next_start
    valid = jnp.concatenate([own_valid, next_valid])[:, None]
    lane = jnp.arange(LANES, dtype=jnp.int32)[None, :]
    return jnp.where((lane == 0), jnp.where(valid, 0.0, MASKED), 1.0).astype(BF)


def passed_along(block, distance):
    devices = range(lax.axis_size("seq"))
    route = [(i - distance, i) for i in devices if i - distance in devices]
    return lax.ppermute(block, "seq", route)


def device_bits():
    bits = []
    for axis in AXES:
        count = lax.axis_size(axis).bit_length() - 1
        bits += [(axis, place) for place in reversed(range(count))]
    return bits


def exchange(block, axis, place):
    route = [(i, i ^ (1 << place)) for i in range(lax.axis_size(axis))]
    return lax.ppermute(block, axis, route)


def reduce_rows(partial, order):
    bits = device_bits()
    share = partial.shape[0] >> len(bits)
    held = partial.reshape((2,) * len(bits) + (share, partial.shape[1]))
    left = list(bits)
    for step, bit in enumerate(order):
        axis, place = bit
        dim = left.index(bit)
        left.remove(bit)
        mine = (lax.axis_index(axis) >> place) & 1
        given = lax.dynamic_index_in_dim(held, 1 - mine, dim, keepdims=False)
        kept = lax.dynamic_index_in_dim(held, mine, dim, keepdims=False)
        total = kept.astype(F32) + exchange(given, axis, place).astype(F32)
        held = total if step == len(order) - 1 else total.astype(BF)
    return held


def reduce_orders():
    bits = device_bits()
    core = ("dp", 0)
    across = [bit for bit in bits if bit[0] == "dp" and bit != core]
    along = [bit for bit in bits if bit[0] == "seq" and bit[1] == 0]
    rest = [bit for bit in bits if bit[0] == "seq" and bit[1] > 0]
    return [core] + across + along + rest, [core] + along + across + rest


def reduced(partial):
    first, second = reduce_orders()
    cut = partial.shape[1] // 256 * 128
    return jnp.concatenate(
        [reduce_rows(partial[:, :cut], first), reduce_rows(partial[:, cut:], second)], axis=1
    )


def all_sum(values):
    for axis, place in device_bits():
        values = values + exchange(values, axis, place)
    return values


def project(rows, weight):
    return jnp.dot(rows, weight, preferred_element_type=F32)


def project_back(grads, weight):
    return jnp.einsum("lo,io->li", grads, weight, preferred_element_type=F32)


def weight_grad(rows, grads):
    return jnp.einsum("li,lo->io", rows, grads, preferred_element_type=F32).astype(BF)


def norm_rows(values, gain):
    inverse = lax.rsqrt(jnp.mean(values * values, axis=-1, keepdims=True) + NORM_EPS)
    return (values * inverse * gain).astype(BF), inverse


def norm_back(values, inverse, gain, grads):
    scaled = values * inverse
    gain_grad = jnp.sum(scaled * grads, axis=0)
    weighted = grads * gain
    centre = jnp.mean(scaled * weighted, axis=-1, keepdims=True)
    return inverse * (weighted - scaled * centre), gain_grad


def local(
    decoder_in,
    memory,
    doc_offsets,
    self_query,
    self_key,
    self_value,
    self_out,
    cross_query,
    cross_key,
    cross_value,
    cross_out,
    ffn_gate,
    ffn_up,
    ffn_down,
    norm_self,
    norm_cross,
    norm_ffn,
    bias_table,
    cotangent,
):
    position = lax.axis_index("seq")
    gains = jnp.stack([norm_self, norm_cross, norm_ffn], axis=1)
    gains = jnp.pad(gains, ((0, 0), (0, LANES - 3)))
    early = jnp.concatenate(
        [self_query, self_key, self_value, cross_key, cross_value, gains], axis=1
    )
    late = jnp.concatenate([self_out, cross_query, cross_out, ffn_gate, ffn_up], axis=1)
    early = lax.all_gather(early, AXES, axis=0, tiled=True)
    late = lax.all_gather(late, AXES, axis=0, tiled=True)
    w_down = lax.all_gather(ffn_down, AXES, axis=0, tiled=True)
    w_qkv, w_kv = early[:, : 3 * D], early[:, 3 * D : 5 * D]
    gain_self, gain_cross, gain_ffn = early[:, 5 * D : 5 * D + 3].T.astype(F32)
    w_so, w_cq, w_co = (late[:, i * D : (i + 1) * D] for i in range(3))
    ff = ffn_gate.shape[1]
    w_gate, w_up = late[:, 3 * D : 3 * D + ff], late[:, 3 * D + ff :]

    tiles = bias_tiles(bias_table.astype(F32))
    mask = jnp.stack([key_masks(doc_offsets[m, 0], position) for m in range(MICRO)])
    x = decoder_in.reshape(ROWS, D).astype(F32)
    mem = memory.reshape(MICRO * MEM_DEV, D)
    kv_own = project(mem, w_kv).astype(BF)
    kv_next = passed_along(kv_own.reshape(MICRO, MEM_DEV, 2 * D)[:, :NEXT], -1)
    kv_next = kv_next.reshape(MICRO * NEXT, 2 * D)
    h1, r1 = norm_rows(x, gain_self)
    qkv = project(h1, w_qkv).astype(BF)
    o1, lse1 = self_forward(qkv, tiles)
    x1 = x + project(o1, w_so)
    h2, r2 = norm_rows(x1, gain_cross)
    q2 = project(h2, w_cq).astype(BF)
    o2, lse2 = cross_forward(q2, kv_own, kv_next, mask)
    x2 = x1 + project(o2, w_co)
    h3, r3 = norm_rows(x2, gain_ffn)
    gate = project(h3, w_gate)
    up = project(h3, w_up)
    hidden, gated_back = jax.vjp(
        lambda g, u: jax.nn.gelu(g, approximate=True) * u, gate, up
    )
    hidden = hidden.astype(BF)
    out = (x2 + project(hidden, w_down)).astype(BF)

    dy_low = cotangent.reshape(ROWS, D)
    dy = dy_low.astype(F32)
    d_gate, d_up = gated_back(project_back(dy_low, w_down))
    d_gate, d_up = d_gate.astype(BF), d_up.astype(BF)
    g_down = reduced(weight_grad(hidden, dy_low))
    g_gate_up = reduced(
        jnp.concatenate([weight_grad(h3, d_gate), weight_grad(h3, d_up)], axis=1)
    )
    dh3 = project_back(d_gate, w_gate) + project_back(d_up, w_up)
    dx2, g_norm_ffn = norm_back(x2, r3, gain_ffn, dh3)
    dx2 = dy + dx2
    db2 = dx2.astype(BF)
    do2 = project_back(db2, w_co).astype(BF)
    dq2, dkv_own, dkv_next = cross_backward(q2, kv_own, kv_next, mask, o2, do2, lse2)
    dkv_prev = passed_along(dkv_next, 1).reshape(2, MICRO, NEXT, D)
    dkv = dkv_own.reshape(2, MICRO, MEM_DEV, D)
    dkv = jnp.concatenate(
        [
            (dkv[:, :, :NEXT].astype(F32) + dkv_prev.astype(F32)).astype(BF),
            dkv[:, :, NEXT:],
        ],
        axis=2,
    ).reshape(2, MICRO * MEM_DEV, D)
    grad_memory = project_back(dkv[0], w_kv[:, :D]) + project_back(dkv[1], w_kv[:, D:])
    dx1, g_norm_cross = norm_back(x1, r2, gain_cross, project_back(dq2, w_cq))
    dx1 = dx2 + dx1
    db1 = dx1.astype(BF)
    do1 = project_back(db1, w_so).astype(BF)
    g_cross = reduced(
        jnp.concatenate(
            [
                weight_grad(h2, dq2),
                weight_grad(mem, dkv[0]),
                weight_grad(mem, dkv[1]),
                weight_grad(o2, db2),
            ],
            axis=1,
        )
    )
    dq1, dk1, dv1, near, far = self_backward(qkv, tiles, o1, do1, lse1)
    dh1 = (
        project_back(dq1, w_qkv[:, :D])
        + project_back(dk1, w_qkv[:, D : 2 * D])
        + project_back(dv1, w_qkv[:, 2 * D :])
    )
    dx0, g_norm_self = norm_back(x, r1, gain_self, dh1)
    grad_decoder = (dx1 + dx0).astype(BF)
    g_norms = jnp.stack([g_norm_self, g_norm_cross, g_norm_ffn], axis=1).astype(BF)
    g_self = reduced(
        jnp.concatenate(
            [
                weight_grad(h1, dq1),
                weight_grad(h1, dk1),
                weight_grad(h1, dv1),
                weight_grad(o1, db1),
                jnp.pad(g_norms, ((0, 0), (0, LANES - 3))),
            ],
            axis=1,
        )
    )
    g_table = all_sum(table_grad(near, far))

    def cut(stack, index, width=D):
        return stack[:, index * width : (index + 1) * width]

    return (
        out.reshape(decoder_in.shape),
        grad_decoder.reshape(decoder_in.shape),
        grad_memory.astype(BF).reshape(memory.shape),
        cut(g_self, 0),
        cut(g_self, 1),
        cut(g_self, 2),
        cut(g_self, 3),
        cut(g_cross, 0),
        cut(g_cross, 1),
        cut(g_cross, 2),
        cut(g_cross, 3),
        cut(g_gate_up, 0, ff),
        cut(g_gate_up, 1, ff),
        g_down,
        g_self[:, 4 * D],
        g_self[:, 4 * D + 1],
        g_self[:, 4 * D + 2],
        g_table,
    )


def solution(mesh):
    in_specs = (
        P(None, ("dp", "seq"), None, None),
        P(None, ("dp", "seq"), None, None),
        P(None, "dp", None),
        P(("dp", "seq"), None),
        P(("dp", "seq"), None),
        P(("dp", "seq"), None),
        P(("dp", "seq"), None),
        P(("dp", "seq"), None),
        P(("dp", "seq"), None),
        P(("dp", "seq"), None),
        P(("dp", "seq"), None),
        P(("dp", "seq"), None),
        P(("dp", "seq"), None),
        P(("dp", "seq"), None),
        P(("dp", "seq")),
        P(("dp", "seq")),
        P(("dp", "seq")),
        P(),
        P(None, ("dp", "seq"), None, None),
    )
    out_specs = (
        P(None, ("dp", "seq"), None, None),
        P(None, ("dp", "seq"), None, None),
        P(None, ("dp", "seq"), None, None),
        P(("dp", "seq"), None),
        P(("dp", "seq"), None),
        P(("dp", "seq"), None),
        P(("dp", "seq"), None),
        P(("dp", "seq"), None),
        P(("dp", "seq"), None),
        P(("dp", "seq"), None),
        P(("dp", "seq"), None),
        P(("dp", "seq"), None),
        P(("dp", "seq"), None),
        P(("dp", "seq"), None),
        P(("dp", "seq")),
        P(("dp", "seq")),
        P(("dp", "seq")),
        P(),
    )
    return jax.shard_map(local, mesh=mesh, in_specs=in_specs, out_specs=out_specs, check_vma=False)
```

time: 2570 us -> 803 us (0.31)
  waiting for transfers between devices: 1140 us -> 322 us
  matrix products: 760 us -> 144 us
  local copies, waits for them, and re-layouts: 440 us -> 68.4 us
  Pallas kernels: 0 us -> 134 us
  blocking collectives: 90 us -> 0 us
  starting transfers between devices: 30.6 us -> 56.7 us
    reduce_scatter x9 -> x0, waiting for transfers between devices: 758 us -> none  [the longest x1 121 us: reduce_grads(): lax.psum_scatter(g_ffn_up, ('dp', 'seq'), scatter_dimension=0, tiled=True)]
    dot_general x427 -> x30, matrix products: 760 us -> 144 us  [the longest x8 54.4 us: project(): return jnp.dot(rows, weight, preferred_element_type=F32)]
    unnamed x24 -> x3, waiting for transfers between devices: 216 us -> 0.73 us
    reshape x26 -> x0, local copies, waits for them, and re-layouts: 164 us -> none  [the longest x24 71.2 us: distance_sums(): skewed = padded[:length * (2 * length - 1)].reshape(length, 2 * length - 1)]
    pallas_call x0 -> x6, Pallas kernels: none -> 134 us  [the longest x1 44.6 us: cross_backward(): pl.pallas_call(cross_backward_kernel, grid=PAIR_GRID, in_specs=[pair_bloc...]
    ppermute x8 -> x47, waiting for transfers between devices: 50.2 us -> 160 us  [the longest x45 160 us: exchange(): return lax.ppermute(block, axis, route)]
    unnamed x2 -> x0, blocking collectives: 90 us -> none
    while x78 -> x0, local copies, waits for them, and re-layouts: 81 us -> none
  transfers between devices with their start and end apart: 30 -> 50, of which waited for: 17 -> 26; matrix products, arithmetic and copies ran while one was open for 23% -> 18% of each run, Pallas kernels for 0% -> 3%
where the time goes in v1:
time: 803 us; the launch traced here: 795 us
  waiting for transfers between devices  322 us (40%)
  matrix products  144 us (18%)
  Pallas kernels  134 us (17%)
  local copies, waits for them, and re-layouts  68.4 us (9%)
  starting transfers between devices  56.7 us (7%)
  other arithmetic  53.9 us (7%)
  between operations  15.5 us (2%)
    ppermute x45, waiting for transfers between devices, exchange(): return lax.ppermute(block, axis, route)  160 us
    all_gather x1, waiting for transfers between devices, local(): w_down = lax.all_gather(ffn_down, AXES, axis=0, tiled=True)  56.1 us
    all_gather x1, waiting for transfers between devices, local(): late = lax.all_gather(late, AXES, axis=0, tiled=True)  54.8 us
    dot_general x8, matrix products, project(): return jnp.dot(rows, weight, preferred_element_type=F32)  54.4 us
    ppermute x45, starting transfers between devices, exchange(): return lax.ppermute(block, axis, route)  52.2 us
    dot_general x11, matrix products, project_back(): return jnp.einsum('lo,io->li', grads, weight, preferred_element_type=F32)  50.6 us
    all_gather x1, waiting for transfers between devices, local(): early = lax.all_gather(early, AXES, axis=0, tiled=True)  50.5 us
    pallas_call x1, Pallas kernels, cross_backward(): pl.pallas_call(cross_backward_kernel, grid=PAIR_GRID, in_specs=[pair_bloc...  44.6 us
  transfers between devices with their start and end apart: 50, of which 26 were waited for; matrix products, arithmetic and copies ran while one was open for 18% of the time, Pallas kernels for 3%

profile of v1, /device:TPU:0, one launch (start us, length us, event | category | flops | bytes accessed | tf_op | source)
XLA Modules:
  0.0 795.1 jit_solution(1505782177835933962)
XLA Ops:
  20.9 8.0 %bias_tiles.1.tiles_ref = f32[12,2,256,256]{3,2,1,0:T(8,128)} custom-call(f32[12,32]{1,0:T(8,128)} %convert_element_type.610.table_ref), custom_call_target="tpu_custom_call" | custom-call | tf_op jit(solution)/shard_map/bias_tiles/pallas_call | solution.py:92
  33.6 50.5 %all-gather.4.cloned.1.call-done = bf16[768,3968]{1,0:T(8,128)(2,1)} async-done(((bf16[24,3968]{1,0:T(8,128)(2,1)}), bf16[768,3968]{1,0:T(8,128)(2,1)}) %all-gather.4.cloned.1.call-update) | async-done | bytes 6094864 | tf_op jit(solution)/shard_map/all_gather | solution.py:550
  84.0 6.9 convolution_convert_fusion
  95.9 56.1 %all-gather.8.cloned.1.call-done = bf16[2048,768]{1,0:T(8,128)(2,1)} async-done(((bf16[64,768]{1,0:T(8,128)(2,1)}), bf16[2048,768]{1,0:T(8,128)(2,1)}) %all-gather.8.cloned.1.call-update) | async-done | bytes 3145744 | tf_op jit(solution)/shard_map/all_gather | solution.py:552
  152.0 9.3 %fusion.103 = f32[1024,2048]{1,0:T(8,128)} fusion(bf16[1024,768]{1,0:T(8,128)(2,1)} %bitcast.384, bf16[2048,768]{1,0:T(8,128)(2,1)} %all-gather.8.cloned.1.call-done), kind=kOutput, calls=%fused_computation.313 | convolution fusion | flops 3221225472 | bytes 13107200 | tf_op jit(solution)/shard_map/lo,io->li/dot_general | solution.py:502
  164.5 5.6 convolution_convert_fusion.1.q_ref.k_ref.v_ref
  170.1 17.3 %self_forward.1 = (bf16[1024,768]{1,0:T(8,128)(2,1)}, f32[12,8,512]{2,1,0:T(8,128)}) custom-call(bf16[1024,2304]{1,0:T(8,128)(2,1)} %convolution_convert_fusion.1.q_ref.k_ref.v_ref, bf16[1024,2304]{1,0:T(8,128)(2,1)} %convolution_convert_fusion.1.q_ref.k_ref.v_ref, bf16[1024,2304]{1,0:T(8,128)(2,1)} %convolution_convert_fusion.1.q_ref.k_ref.v_ref, ...), custom_call_target="tpu_custom_call" | custom-call | tf_op jit(solution)/shard_map/self_forward/pallas_call | solution.py:346
  187.4 54.8 %all-gather.6.cloned.1.call-done = bf16[768,6400]{1,0:T(8,128)(2,1)} async-done(((bf16[24,6400]{1,0:T(8,128)(2,1)}), bf16[768,6400]{1,0:T(8,128)(2,1)}) %all-gather.6.cloned.1.call-update) | async-done | bytes 9830416 | tf_op jit(solution)/shard_map/all_gather | solution.py:551
  242.3 3.7 multiply_reduce_fusion.5
  246.0 4.8 convolution_convert_fusion.7.q_ref
  250.8 31.5 %cross_forward.1 = (bf16[1024,768]{1,0:T(8,128)(2,1)}, f32[12,8,512]{2,1,0:T(8,128)}) custom-call(bf16[1024,768]{1,0:T(8,128)(2,1)} %convolution_convert_fusion.7.q_ref, bf16[2048,1536]{1,0:T(8,128)(2,1)} %bitcast.358, bf16[1024,1536]{1,0:T(8,128)(2,1)} %bitcast.8.kn_ref.vn_ref, bf16[2048,1536]{1,0:T(8,128)(2,1)} %bitcast.359, ...), custom_call_target="tpu_custom_call" | custom-call | tf_op jit(solution)/shard_map/cross_forward/pallas_call | solution.py:287
  285.9 8.9 %fusion.26 = f32[1024,2048]{1,0:T(8,128)} fusion(bf16[1024,768]{1,0:T(8,128)(2,1)S(1)} %multiply_convert_fusion.2, bf16[768,6400]{1,0:T(8,128)(2,1)} %all-gather.6.cloned.1.call-done), kind=kOutput, calls=%fused_computation.58 | convolution fusion | flops 3221225472 | bytes 13107200 | tf_op jit(solution)/shard_map/dot_general | solution.py:498
  294.8 16.8 %fusion.6 = (bf16[1024,2048]{1,0:T(8,128)(2,1)}, bf16[1024,2048]{1,0:T(8,128)(2,1)}, bf16[1024,2048]{1,0:T(8,128)(2,1)}) fusion(f32[1024,2048]{1,0:T(8,128)} %fusion.103, f32[1024,2048]{1,0:T(8,128)} %fusion.26, bf16[1024,768]{1,0:T(8,128)(2,1)S(1)} %multiply_convert_fusion.2, bf16[768,6400]{1,0:T(8,128)(2,1)} %all-gather.6.cloned.1.call-done), kind=kOutput, calls=%fused_computation.8 | convolution fusion | flops 3275751424 | bytes 34078720 | tf_op jit(solution)/shard_map/dot_general | solution.py:498
  311.6 6.4 fusion.24
  318.0 6.1 multiply_reduce_fusion
  325.0 4.8 convolution_convert_fusion.6.do_ref
  329.8 44.6 %cross_backward.1 = (bf16[1024,768]{1,0:T(8,128)(2,1)}, bf16[2,2048,768]{2,1,0:T(8,128)(2,1)}, bf16[2,1024,768]{2,1,0:T(8,128)(2,1)}) custom-call(bf16[1024,768]{1,0:T(8,128)(2,1)} %convolution_convert_fusion.7.q_ref, bf16[2048,1536]{1,0:T(8,128)(2,1)} %bitcast.360, bf16[1024,1536]{1,0:T(8,128)(2,1)} %bitcast.8.kn_ref.vn_ref, bf16[2048,1536]{1,0:T(8,128)(2,1)} %bitcast.361, ...), custom_call_target="tpu_custom_call" | custom-call | tf_op jit(solution)/shard_map/cross_backward/pallas_call | solution.py:307
  374.4 3.6 multiply_reduce_fusion.1
  378.8 4.8 convolution_convert_fusion.5.do_ref
  383.6 23.8 %self_backward.1 = (bf16[1024,768]{1,0:T(8,128)(2,1)}, bf16[1024,768]{1,0:T(8,128)(2,1)}, bf16[1024,768]{1,0:T(8,128)(2,1)}, f32[12,256,256]{2,1,0:T(8,128)}, f32[12,256,256]{2,1,0:T(8,128)}) custom-call(bf16[1024,2304]{1,0:T(8,128)(2,1)} %convolution_convert_fusion.1.q_ref.k_ref.v_ref, bf16[1024,2304]{1,0:T(8,128)(2,1)} %convolution_convert_fusion.1.q_ref.k_ref.v_ref, ...), custom_call_target="tpu_custom_call" | custom-call | tf_op jit(solution)/shard_map/self_backward/pallas_call | solution.py:366
  407.4 8.9 %distance_sums.1 = f32[12,8,256]{2,1,0:T(8,128)} custom-call(f32[12,256,256]{2,1,0:T(8,128)} %get-tuple-element.40.near_ref, f32[12,256,256]{2,1,0:T(8,128)} %get-tuple-element.41.far_ref), custom_call_target="tpu_custom_call" | custom-call | tf_op jit(solution)/shard_map/distance_sums/pallas_call | solution.py:406
  432.0 8.0 %convolution_convert_fusion.3 = bf16[768,2048]{1,0:T(8,128)(2,1)} fusion(bf16[1024,768]{1,0:T(8,128)(2,1)} %copy-done.35, bf16[1024,2048]{1,0:T(8,128)(2,1)} %get-tuple-element.120), kind=kOutput, calls=%fused_computation.21 | convolution fusion | flops 3222798336 | bytes 8912896 | tf_op jit(solution)/shard_map/li,lo->io/dot_general | solution.py:506
  440.0 5.3 convolution_convert_fusion.4
  454.7 6.2 convolution_convert_fusion.2
  486.5 4.5 add_convert_fusion.1
  497.4 4.3 copy.61
  504.7 4.5 copy.62
  519.3 3.8 slice.294
  536.8 64.3 %collective-permute-done.34 = bf16[2,2,64,384]{3,2,1,0:T(8,128)(2,1)S(1)} collective-permute-done((bf16[2,2,64,384]{3,2,1,0:T(8,128)(2,1)S(1)}, bf16[2,2,64,384]{3,2,1,0:T(8,128)(2,1)S(1)}, u32[]{:S(2)}, u32[]{:S(2)}) %collective-permute-start.34) | collective-permute-done | bytes 196640 | tf_op jit(solution)/shard_map/ppermute | solution.py:454
  602.7 3.9 collective-permute-start.35
  606.7 4.7 collective-permute-done.35
  612.1 5.7 collective-permute-done.40
  617.9 4.0 collective-permute-done.36
  622.4 3.6 collective-permute-done.41
  635.0 8.3 %collective-permute-done.8 = bf16[2,2,2,24,1664]{4,3,2,1,0:T(8,128)(2,1)S(1)} collective-permute-done((bf16[2,2,2,24,1664]{4,3,2,1,0:T(8,128)(2,1)S(1)}, bf16[2,2,2,24,1664]{4,3,2,1,0:T(8,128)(2,1)S(1)}, u32[]{:S(2)}, u32[]{:S(2)}) %collective-permute-start.8) | collective-permute-done | bytes 639008 | tf_op jit(solution)/shard_map/ppermute | solution.py:454
  643.5 16.7 %collective-permute-done.4 = bf16[2,2,24,1536]{3,2,1,0:T(8,128)(2,1)S(1)} collective-permute-done((bf16[2,2,24,1536]{3,2,1,0:T(8,128)(2,1)S(1)}, bf16[2,2,24,1536]{3,2,1,0:T(8,128)(2,1)S(1)}, u32[]{:S(2)}, u32[]{:S(2)}) %collective-permute-start.4) | collective-permute-done | bytes 294944 | tf_op jit(solution)/shard_map/ppermute | solution.py:454
  660.3 3.3 collective-permute-start.5
  665.0 3.4 collective-permute-done.5
  671.8 3.6 collective-permute-start.10
  681.1 3.9 collective-permute-done.11
  713.3 4.3 copy.64
  720.0 4.6 fusion.44
  726.2 4.3 copy.63
  732.4 5.3 fusion.48
  737.8 5.5 add_convert_fusion
  747.3 13.0 %collective-permute-done.18 = bf16[2,2,2,24,1536]{4,3,2,1,0:T(8,128)(2,1)S(1)} collective-permute-done((bf16[2,2,2,24,1536]{4,3,2,1,0:T(8,128)(2,1)S(1)}, bf16[2,2,2,24,1536]{4,3,2,1,0:T(8,128)(2,1)S(1)}, u32[]{:S(2)}, u32[]{:S(2)}) %collective-permute-start.18) | collective-permute-done | bytes 589856 | tf_op jit(solution)/shard_map/ppermute | solution.py:454
  762.8 5.7 collective-permute-done.19
  771.8 9.2 %collective-permute-done.20 = bf16[2,24,1536]{2,1,0:T(8,128)(2,1)S(1)} collective-permute-done((bf16[2,24,1536]{2,1,0:T(8,128)(2,1)S(1)}, bf16[2,24,1536]{2,1,0:T(8,128)(2,1)S(1)}, u32[]{:S(2)}, u32[]{:S(2)}) %collective-permute-start.20) | collective-permute-done | bytes 147488 | tf_op jit(solution)/shard_map/ppermute | solution.py:454
  (375 shorter events, 188.6 us)
Async XLA Ops:
  7.2 76.8 %all-gather.4.cloned.1.call-start = ((), (), s32[]{:S(2)}) async-start(), calls=%async_computation | async-start | bytes 6285312 | tf_op jit(solution)/shard_map/all_gather | solution.py:550
  12.8 139.3 %all-gather.8.cloned.1.call-start = ((), (), s32[]{:S(2)}) async-start(), calls=%async_computation.2 | async-start | bytes 3244032 | tf_op jit(solution)/shard_map/all_gather | solution.py:552
  13.5 228.7 %all-gather.6.cloned.1.call-start = ((), (), s32[]{:S(2)}) async-start(), calls=%async_computation.1 | async-start | bytes 10137600 | tf_op jit(solution)/shard_map/all_gather | solution.py:551
  94.6 156.2 %collective-permute-start = (bf16[2,512,1536]{2,1,0:T(8,128)(2,1)}, bf16[2,512,1536]{2,1,0:T(8,128)(2,1)}, u32[]{:S(2)}, u32[]{:S(2)}) collective-permute-start(bf16[2,512,1536]{2,1,0:T(8,128)(2,1)} %slice.286), channel_id=1, source_target_pairs={{1,0},{2,1},{3,2},{4,3},{5,4},{6,5},{7,6},{9,8},{10,9},{11,10},{12... | collective-permute-start | bytes 9437192 | tf_op jit(solution)/shard_map/ppermute | solution.py:441
  453.3 39.4 %collective-permute-start.42 = (f32[12,32]{0,1:T(8,128)S(1)}, f32[12,32]{0,1:T(8,128)S(1)}, u32[]{:S(2)}, u32[]{:S(2)}) collective-permute-start(f32[12,32]{0,1:T(8,128)S(1)} %stack.122), channel_id=1, source_target_pairs={{0,16},{8,24},{16,0},{24,8},{1,17},{9,25},{17,1},{25,9},{2,18},{10... | collective-permute-start | bytes 4616 | tf_op jit(solution)/shard_map/ppermute | solution.py:454
  463.4 46.5 %collective-permute-start.32 = (bf16[2,2,2,2,64,384]{5,4,2,1,3,0:T(8,128)(2,1)}, bf16[2,2,2,2,64,384]{5,4,2,1,3,0:T(8,128)(2,1)}, u32[]{:S(2)}, u32[]{:S(2)}) collective-permute-start(bf16[2,2,2,2,64,384]{5,4,2,1,3,0:T(8,128)(2,1)} %bitcast.353), channel_id=1, source_target_pairs={{0,8},{8,0},{16,24},{24,16},{1,9},{9,1},{17,25},{25,17},{2,10},{10... | collective-permute-start | bytes 2359304 | tf_op jit(solution)/shard_map/ppermute | solution.py:454
  465.4 48.5 %collective-permute-start.37 = (bf16[2,2,2,2,64,384]{5,4,2,1,0,3:T(8,128)(2,1)}, bf16[2,2,2,2,64,384]{5,4,2,1,0,3:T(8,128)(2,1)}, u32[]{:S(2)}, u32[]{:S(2)}) collective-permute-start(bf16[2,2,2,2,64,384]{5,4,2,1,0,3:T(8,128)(2,1)} %bitcast.352), channel_id=1, source_target_pairs={{0,8},{8,0},{16,24},{24,16},{1,9},{9,1},{17,25},{25,17},{2,10},{10... | collective-permute-start | bytes 2359304 | tf_op jit(solution)/shard_map/ppermute | solution.py:454
  468.8 158.4 %collective-permute-start.27 = (bf16[2,2,2,2,24,2048]{5,4,2,1,0,3:T(8,128)(2,1)}, bf16[2,2,2,2,24,2048]{5,4,2,1,0,3:T(8,128)(2,1)}, u32[]{:S(2)}, u32[]{:S(2)}) collective-permute-start(bf16[2,2,2,2,24,2048]{5,4,2,1,0,3:T(8,128)(2,1)} %bitcast.350), channel_id=1, source_target_pairs={{0,8},{8,0},{16,24},{24,16},{1,9},{9,1},{17,25},{25,17},{2,10},{10... | collective-permute-start | bytes 4718600 | tf_op jit(solution)/shard_map/ppermute | solution.py:454
  493.9 7.8 collective-permute-start.44
  501.7 7.5 collective-permute-start.45
  509.2 22.6 %collective-permute-start.2 = (bf16[2,2,2,2,24,1536]{5,4,3,2,1,0:T(8,128)(2,1)}, bf16[2,2,2,2,24,1536]{5,4,3,2,1,0:T(8,128)(2,1)}, u32[]{:S(2)}, u32[]{:S(2)}) collective-permute-start(bf16[2,2,2,2,24,1536]{5,4,3,2,1,0:T(8,128)(2,1)} %dynamic-slice_bitcast_fusion.3), channel_id=1, source_target_pairs={{0,8},{8,0},{16,24},{24,16},{1,9},{9,1},{17,25},{25,17},{2,10},{10... | collective-permute-start | bytes 3538952 | tf_op jit(solution)/shard_map/ppermute | solution.py:454
  509.2 13.9 %collective-permute-start.46 = (f32[12,32]{0,1:T(8,128)S(1)}, f32[12,32]{0,1:T(8,128)S(1)}, u32[]{:S(2)}, u32[]{:S(2)}) collective-permute-start(f32[12,32]{0,1:T(8,128)S(1)} %add.435), channel_id=1, source_target_pairs={{0,1},{1,0},{2,3},{3,2},{4,5},{5,4},{6,7},{7,6},{8,9},{9,8},{10,11... | collective-permute-start | bytes 4616 | tf_op jit(solution)/shard_map/ppermute | solution.py:454
  512.4 11.4 %collective-permute-start.33 = (bf16[2,2,2,64,384]{4,3,1,0,2:T(8,128)(2,1)}, bf16[2,2,2,64,384]{4,3,1,0,2:T(8,128)(2,1)S(1)}, u32[]{:S(2)}, u32[]{:S(2)}) collective-permute-start(bf16[2,2,2,64,384]{4,3,1,0,2:T(8,128)(2,1)} %dynamic-slice_bitcast_fusion.11), channel_id=1, source_target_pairs={{0,16},{8,24},{16,0},{24,8},{1,17},{9,25},{17,1},{25,9},{2,18},{10... | collective-permute-start | bytes 1179656 | tf_op jit(solution)/shard_map/ppermute | solution.py:454
  516.2 11.3 %collective-permute-start.38 = (bf16[2,2,2,64,384]{4,3,2,1,0:T(8,128)(2,1)}, bf16[2,2,2,64,384]{4,3,2,1,0:T(8,128)(2,1)}, u32[]{:S(2)}, u32[]{:S(2)}) collective-permute-start(bf16[2,2,2,64,384]{4,3,2,1,0:T(8,128)(2,1)} %dynamic-slice_bitcast_fusion.10), channel_id=1, source_target_pairs={{0,1},{1,0},{2,3},{3,2},{4,5},{5,4},{6,7},{7,6},{8,9},{9,8},{10,11... | collective-permute-start | bytes 1179656 | tf_op jit(solution)/shard_map/ppermute | solution.py:454
  523.1 108.0 %collective-permute-start.22 = (bf16[2,2,2,2,24,2048]{5,4,2,1,3,0:T(8,128)(2,1)}, bf16[2,2,2,2,24,2048]{5,4,2,1,3,0:T(8,128)(2,1)}, u32[]{:S(2)}, u32[]{:S(2)}) collective-permute-start(bf16[2,2,2,2,24,2048]{5,4,2,1,3,0:T(8,128)(2,1)} %bitcast.351), channel_id=1, source_target_pairs={{0,8},{8,0},{16,24},{24,16},{1,9},{9,1},{17,25},{25,17},{2,10},{10... | collective-permute-start | bytes 4718600 | tf_op jit(solution)/shard_map/ppermute | solution.py:454
  523.9 11.9 %collective-permute-start.7 = (bf16[2,2,2,2,24,1664]{5,4,3,2,1,0:T(8,128)(2,1)}, bf16[2,2,2,2,24,1664]{5,4,3,2,1,0:T(8,128)(2,1)S(1)}, u32[]{:S(2)}, u32[]{:S(2)}) collective-permute-start(bf16[2,2,2,2,24,1664]{5,4,3,2,1,0:T(8,128)(2,1)} %dynamic-slice_bitcast_fusion), channel_id=1, source_target_pairs={{0,8},{8,0},{16,24},{24,16},{1,9},{9,1},{17,25},{25,17},{2,10},{10... | collective-permute-start | bytes 3833864 | tf_op jit(solution)/shard_map/ppermute | solution.py:454
  527.4 177.5 %collective-permute-start.1 = (bf16[2,1024,768]{2,1,0:T(8,128)(2,1)}, bf16[2,1024,768]{2,1,0:T(8,128)(2,1)S(1)}, u32[]{:S(2)}, u32[]{:S(2)}) collective-permute-start(bf16[2,1024,768]{2,1,0:T(8,128)(2,1)} %get-tuple-element.39), channel_id=1, source_target_pairs={{0,1},{1,2},{2,3},{3,4},{4,5},{5,6},{6,7},{8,9},{9,10},{10,11},{11... | collective-permute-start | bytes 9437192 | tf_op jit(solution)/shard_map/ppermute | solution.py:441
  531.8 69.3 %collective-permute-start.34 = (bf16[2,2,64,384]{3,2,1,0:T(8,128)(2,1)S(1)}, bf16[2,2,64,384]{3,2,1,0:T(8,128)(2,1)S(1)}, u32[]{:S(2)}, u32[]{:S(2)}) collective-permute-start(bf16[2,2,64,384]{3,2,1,0:T(8,128)(2,1)S(1)} %dynamic-slice_bitcast_fusion.19), channel_id=1, source_target_pairs={{0,1},{1,0},{2,3},{3,2},{4,5},{5,4},{6,7},{7,6},{8,9},{9,8},{10,11... | collective-permute-start | bytes 589832 | tf_op jit(solution)/shard_map/ppermute | solution.py:454
  535.8 66.9 %collective-permute-start.39 = (bf16[2,2,64,384]{3,2,1,0:T(8,128)(2,1)S(1)}, bf16[2,2,64,384]{3,2,1,0:T(8,128)(2,1)S(1)}, u32[]{:S(2)}, u32[]{:S(2)}) collective-permute-start(bf16[2,2,64,384]{3,2,1,0:T(8,128)(2,1)S(1)} %dynamic-slice_bitcast_fusion.18), channel_id=1, source_target_pairs={{0,16},{8,24},{16,0},{24,8},{1,17},{9,25},{17,1},{25,9},{2,18},{10... | collective-permute-start | bytes 589832 | tf_op jit(solution)/shard_map/ppermute | solution.py:454
  601.1 33.6 %collective-permute-start.3 = (bf16[2,2,2,24,1536]{4,3,2,1,0:T(8,128)(2,1)S(1)}, bf16[2,2,2,24,1536]{4,3,2,1,0:T(8,128)(2,1)S(1)}, u32[]{:S(2)}, u32[]{:S(2)}) collective-permute-start(bf16[2,2,2,24,1536]{4,3,2,1,0:T(8,128)(2,1)S(1)} %dynamic-slice_bitcast_fusion.9), channel_id=1, source_target_pairs={{0,16},{8,24},{16,0},{24,8},{1,17},{9,25},{17,1},{25,9},{2,18},{10... | collective-permute-start | bytes 1769480 | tf_op jit(solution)/shard_map/ppermute | solution.py:454
  602.7 8.7 %collective-permute-start.35 = (bf16[2,64,384]{2,1,0:T(8,128)(2,1)S(1)}, bf16[2,64,384]{2,1,0:T(8,128)(2,1)S(1)}, u32[]{:S(2)}, u32[]{:S(2)}) collective-permute-start(bf16[2,64,384]{2,1,0:T(8,128)(2,1)S(1)} %dynamic-slice_bitcast_fusion.27), channel_id=1, source_target_pairs={{0,4},{1,5},{2,6},{3,7},{4,0},{5,1},{6,2},{7,3},{8,12},{9,13},{10,... | collective-permute-start | bytes 294920 | tf_op jit(solution)/shard_map/ppermute | solution.py:454
  611.4 6.4 collective-permute-start.40
  617.8 4.1 collective-permute-start.36
  626.0 17.3 %collective-permute-start.8 = (bf16[2,2,2,24,1664]{4,3,2,1,0:T(8,128)(2,1)S(1)}, bf16[2,2,2,24,1664]{4,3,2,1,0:T(8,128)(2,1)S(1)}, u32[]{:S(2)}, u32[]{:S(2)}) collective-permute-start(bf16[2,2,2,24,1664]{4,3,2,1,0:T(8,128)(2,1)S(1)} %dynamic-slice_bitcast_fusion.6), channel_id=1, source_target_pairs={{0,1},{1,0},{2,3},{3,2},{4,5},{5,4},{6,7},{7,6},{8,9},{9,8},{10,11... | collective-permute-start | bytes 1916936 | tf_op jit(solution)/shard_map/ppermute | solution.py:454
  629.4 46.7 %collective-permute-start.28 = (bf16[2,2,2,24,2048]{4,3,2,1,0:T(8,128)(2,1)S(1)}, bf16[2,2,2,24,2048]{4,3,2,1,0:T(8,128)(2,1)S(1)}, u32[]{:S(2)}, u32[]{:S(2)}) collective-permute-start(bf16[2,2,2,24,2048]{4,3,2,1,0:T(8,128)(2,1)S(1)} %dynamic-slice_bitcast_fusion.4), channel_id=1, source_target_pairs={{0,1},{1,0},{2,3},{3,2},{4,5},{5,4},{6,7},{7,6},{8,9},{9,8},{10,11... | collective-permute-start | bytes 2359304 | tf_op jit(solution)/shard_map/ppermute | solution.py:454
  633.1 44.6 %collective-permute-start.23 = (bf16[2,2,2,24,2048]{4,3,1,0,2:T(8,128)(2,1)S(1)}, bf16[2,2,2,24,2048]{4,3,1,0,2:T(8,128)(2,1)S(1)}, u32[]{:S(2)}, u32[]{:S(2)}) collective-permute-start(bf16[2,2,2,24,2048]{4,3,1,0,2:T(8,128)(2,1)S(1)} %dynamic-slice_bitcast_fusion.5), channel_id=1, source_target_pairs={{0,16},{8,24},{16,0},{24,8},{1,17},{9,25},{17,1},{25,9},{2,18},{10... | collective-permute-start | bytes 2359304 | tf_op jit(solution)/shard_map/ppermute | solution.py:454
  634.9 25.3 %collective-permute-start.4 = (bf16[2,2,24,1536]{3,2,1,0:T(8,128)(2,1)S(1)}, bf16[2,2,24,1536]{3,2,1,0:T(8,128)(2,1)S(1)}, u32[]{:S(2)}, u32[]{:S(2)}) collective-permute-start(bf16[2,2,24,1536]{3,2,1,0:T(8,128)(2,1)S(1)} %dynamic-slice_bitcast_fusion.17), channel_id=1, source_target_pairs={{0,1},{1,0},{2,3},{3,2},{4,5},{5,4},{6,7},{7,6},{8,9},{9,8},{10,11... | collective-permute-start | bytes 884744 | tf_op jit(solution)/shard_map/ppermute | solution.py:454
  660.3 8.1 %collective-permute-start.5 = (bf16[2,24,1536]{2,1,0:T(8,128)(2,1)S(1)}, bf16[2,24,1536]{2,1,0:T(8,128)(2,1)S(1)}, u32[]{:S(2)}, u32[]{:S(2)}) collective-permute-start(bf16[2,24,1536]{2,1,0:T(8,128)(2,1)S(1)} %dynamic-slice_bitcast_fusion.25), channel_id=1, source_target_pairs={{0,4},{1,5},{2,6},{3,7},{4,0},{5,1},{6,2},{7,3},{8,12},{9,13},{10,... | collective-permute-start | bytes 442376 | tf_op jit(solution)/shard_map/ppermute | solution.py:454
  663.7 8.0 %collective-permute-start.9 = (bf16[2,2,24,1664]{3,2,1,0:T(8,128)(2,1)S(1)}, bf16[2,2,24,1664]{3,2,1,0:T(8,128)(2,1)S(1)}, u32[]{:S(2)}, u32[]{:S(2)}) collective-permute-start(bf16[2,2,24,1664]{3,2,1,0:T(8,128)(2,1)S(1)} %dynamic-slice_bitcast_fusion.14), channel_id=1, source_target_pairs={{0,16},{8,24},{16,0},{24,8},{1,17},{9,25},{17,1},{25,9},{2,18},{10... | collective-permute-start | bytes 958472 | tf_op jit(solution)/shard_map/ppermute | solution.py:454
  668.4 7.0 collective-permute-start.6
  671.8 8.6 %collective-permute-start.10 = (bf16[2,24,1664]{2,1,0:T(8,128)(2,1)S(1)}, bf16[2,24,1664]{2,1,0:T(8,128)(2,1)S(1)}, u32[]{:S(2)}, u32[]{:S(2)}) collective-permute-start(bf16[2,24,1664]{2,1,0:T(8,128)(2,1)S(1)} %dynamic-slice_bitcast_fusion.22), channel_id=1, source_target_pairs={{0,4},{1,5},{2,6},{3,7},{4,0},{5,1},{6,2},{7,3},{8,12},{9,13},{10,... | collective-permute-start | bytes 479240 | tf_op jit(solution)/shard_map/ppermute | solution.py:454
  676.4 10.0 %collective-permute-start.29 = (bf16[2,2,24,2048]{3,2,1,0:T(8,128)(2,1)S(1)}, bf16[2,2,24,2048]{3,2,1,0:T(8,128)(2,1)S(1)}, u32[]{:S(2)}, u32[]{:S(2)}) collective-permute-start(bf16[2,2,24,2048]{3,2,1,0:T(8,128)(2,1)S(1)} %dynamic-slice_bitcast_fusion.12), channel_id=1, source_target_pairs={{0,16},{8,24},{16,0},{24,8},{1,17},{9,25},{17,1},{25,9},{2,18},{10... | collective-permute-start | bytes 1179656 | tf_op jit(solution)/shard_map/ppermute | solution.py:454
  680.4 4.5 collective-permute-start.11
  680.6 8.9 %collective-permute-start.24 = (bf16[2,2,24,2048]{3,2,1,0:T(8,128)(2,1)S(1)}, bf16[2,2,24,2048]{3,2,1,0:T(8,128)(2,1)S(1)}, u32[]{:S(2)}, u32[]{:S(2)}) collective-permute-start(bf16[2,2,24,2048]{3,2,1,0:T(8,128)(2,1)S(1)} %dynamic-slice_bitcast_fusion.13), channel_id=1, source_target_pairs={{0,1},{1,0},{2,3},{3,2},{4,5},{5,4},{6,7},{7,6},{8,9},{9,8},{10,11... | collective-permute-start | bytes 1179656 | tf_op jit(solution)/shard_map/ppermute | solution.py:454
  686.5 8.9 %collective-permute-start.30 = (bf16[2,24,2048]{2,1,0:T(8,128)(2,1)S(1)}, bf16[2,24,2048]{2,1,0:T(8,128)(2,1)S(1)}, u32[]{:S(2)}, u32[]{:S(2)}) collective-permute-start(bf16[2,24,2048]{2,1,0:T(8,128)(2,1)S(1)} %dynamic-slice_bitcast_fusion.20), channel_id=1, source_target_pairs={{0,4},{1,5},{2,6},{3,7},{4,0},{5,1},{6,2},{7,3},{8,12},{9,13},{10,... | collective-permute-start | bytes 589832 | tf_op jit(solution)/shard_map/ppermute | solution.py:454
  689.6 9.9 %collective-permute-start.25 = (bf16[2,24,2048]{2,1,0:T(8,128)(2,1)S(1)}, bf16[2,24,2048]{2,1,0:T(8,128)(2,1)S(1)}, u32[]{:S(2)}, u32[]{:S(2)}) collective-permute-start(bf16[2,24,2048]{2,1,0:T(8,128)(2,1)S(1)} %dynamic-slice_bitcast_fusion.21), channel_id=1, source_target_pairs={{0,4},{1,5},{2,6},{3,7},{4,0},{5,1},{6,2},{7,3},{8,12},{9,13},{10,... | collective-permute-start | bytes 589832 | tf_op jit(solution)/shard_map/ppermute | solution.py:454
  695.5 5.6 collective-permute-start.31
  699.6 4.7 collective-permute-start.26
  720.0 23.3 %collective-permute-start.17 = (bf16[2,2,2,2,24,1536]{5,4,3,2,1,0:T(8,128)(2,1)}, bf16[2,2,2,2,24,1536]{5,4,3,2,1,0:T(8,128)(2,1)}, u32[]{:S(2)}, u32[]{:S(2)}) collective-permute-start(bf16[2,2,2,2,24,1536]{5,4,3,2,1,0:T(8,128)(2,1)} %dynamic-slice_bitcast_fusion.1), channel_id=1, source_target_pairs={{0,8},{8,0},{16,24},{24,16},{1,9},{9,1},{17,25},{25,17},{2,10},{10... | collective-permute-start | bytes 3538952 | tf_op jit(solution)/shard_map/ppermute | solution.py:454
  731.9 14.6 %collective-permute-start.12 = (bf16[2,2,2,2,24,1536]{5,4,3,2,1,0:T(8,128)(2,1)S(1)}, bf16[2,2,2,2,24,1536]{5,4,3,2,1,0:T(8,128)(2,1)S(1)}, u32[]{:S(2)}, u32[]{:S(2)}) collective-permute-start(bf16[2,2,2,2,24,1536]{5,4,3,2,1,0:T(8,128)(2,1)S(1)} %dynamic-slice_bitcast_fusion.2), channel_id=1, source_target_pairs={{0,8},{8,0},{16,24},{24,16},{1,9},{9,1},{17,25},{25,17},{2,10},{10... | collective-permute-start | bytes 3538952 | tf_op jit(solution)/shard_map/ppermute | solution.py:454
  745.1 15.2 %collective-permute-start.18 = (bf16[2,2,2,24,1536]{4,3,2,1,0:T(8,128)(2,1)S(1)}, bf16[2,2,2,24,1536]{4,3,2,1,0:T(8,128)(2,1)S(1)}, u32[]{:S(2)}, u32[]{:S(2)}) collective-permute-start(bf16[2,2,2,24,1536]{4,3,2,1,0:T(8,128)(2,1)S(1)} %dynamic-slice_bitcast_fusion.7), channel_id=1, source_target_pairs={{0,1},{1,0},{2,3},{3,2},{4,5},{5,4},{6,7},{7,6},{8,9},{9,8},{10,11... | collective-permute-start | bytes 1769480 | tf_op jit(solution)/shard_map/ppermute | solution.py:454
  746.9 14.9 %collective-permute-start.13 = (bf16[2,2,2,24,1536]{4,3,2,1,0:T(8,128)(2,1)S(1)}, bf16[2,2,2,24,1536]{4,3,2,1,0:T(8,128)(2,1)S(1)}, u32[]{:S(2)}, u32[]{:S(2)}) collective-permute-start(bf16[2,2,2,24,1536]{4,3,2,1,0:T(8,128)(2,1)S(1)} %dynamic-slice_bitcast_fusion.8), channel_id=1, source_target_pairs={{0,16},{8,24},{16,0},{24,8},{1,17},{9,25},{17,1},{25,9},{2,18},{10... | collective-permute-start | bytes 1769480 | tf_op jit(solution)/shard_map/ppermute | solution.py:454
  760.5 8.0 %collective-permute-start.19 = (bf16[2,2,24,1536]{3,2,1,0:T(8,128)(2,1)S(1)}, bf16[2,2,24,1536]{3,2,1,0:T(8,128)(2,1)S(1)}, u32[]{:S(2)}, u32[]{:S(2)}) collective-permute-start(bf16[2,2,24,1536]{3,2,1,0:T(8,128)(2,1)S(1)} %dynamic-slice_bitcast_fusion.15), channel_id=1, source_target_pairs={{0,16},{8,24},{16,0},{24,8},{1,17},{9,25},{17,1},{25,9},{2,18},{10... | collective-permute-start | bytes 884744 | tf_op jit(solution)/shard_map/ppermute | solution.py:454
  761.9 9.0 %collective-permute-start.14 = (bf16[2,2,24,1536]{3,2,1,0:T(8,128)(2,1)S(1)}, bf16[2,2,24,1536]{3,2,1,0:T(8,128)(2,1)S(1)}, u32[]{:S(2)}, u32[]{:S(2)}) collective-permute-start(bf16[2,2,24,1536]{3,2,1,0:T(8,128)(2,1)S(1)} %dynamic-slice_bitcast_fusion.16), channel_id=1, source_target_pairs={{0,1},{1,0},{2,3},{3,2},{4,5},{5,4},{6,7},{7,6},{8,9},{9,8},{10,11... | collective-permute-start | bytes 884744 | tf_op jit(solution)/shard_map/ppermute | solution.py:454
  768.6 12.5 %collective-permute-start.20 = (bf16[2,24,1536]{2,1,0:T(8,128)(2,1)S(1)}, bf16[2,24,1536]{2,1,0:T(8,128)(2,1)S(1)}, u32[]{:S(2)}, u32[]{:S(2)}) collective-permute-start(bf16[2,24,1536]{2,1,0:T(8,128)(2,1)S(1)} %dynamic-slice_bitcast_fusion.23), channel_id=1, source_target_pairs={{0,4},{1,5},{2,6},{3,7},{4,0},{5,1},{6,2},{7,3},{8,12},{9,13},{10,... | collective-permute-start | bytes 442376 | tf_op jit(solution)/shard_map/ppermute | solution.py:454
  771.1 11.9 %collective-permute-start.15 = (bf16[2,24,1536]{2,1,0:T(8,128)(2,1)S(1)}, bf16[2,24,1536]{2,1,0:T(8,128)(2,1)S(1)}, u32[]{:S(2)}, u32[]{:S(2)}) collective-permute-start(bf16[2,24,1536]{2,1,0:T(8,128)(2,1)S(1)} %dynamic-slice_bitcast_fusion.24), channel_id=1, source_target_pairs={{0,4},{1,5},{2,6},{3,7},{4,0},{5,1},{6,2},{7,3},{8,12},{9,13},{10,... | collective-permute-start | bytes 442376 | tf_op jit(solution)/shard_map/ppermute | solution.py:454
  781.1 4.8 collective-permute-start.21
  783.0 4.4 collective-permute-start.16
  (60 other events, 651.1 us)
Sparse Core Ops, SparseCore 0:
  12.9 71.0 all-gather.3
  86.9 65.0 all-gather.7
  155.5 86.7 all-gather.5

commit v2 on v1

v2 whole, which is shorter than its diff:
```python
import functools
import math

import jax
import jax.numpy as jnp
from jax import lax
from jax.experimental import pallas as pl
from jax.experimental.pallas import tpu as pltpu
from jax.sharding import PartitionSpec as P

D = 768
HEADS = 12
HEAD_DIM = 64
BUCKETS = 32
REACH = 128
TGT_LEN = 512
MEM_DEV = 1024
MICRO = 2
PAIRS = HEADS // 2
LANES = 2 * HEAD_DIM
OWN = MEM_DEV - MEM_DEV // 4
NEXT = MEM_DEV // 2
KEYS = OWN + NEXT
HALF = 256
MASKED = -1e30
NORM_EPS = 1e-06
AXES = ("dp", "seq")
ROWS = MICRO * TGT_LEN
BLOCK = 256
WIDE = 256
HALF_COLUMNS = 2048
VMEM_LIMIT = 60 * 1024 * 1024
BF = jnp.bfloat16
F32 = jnp.float32


def nn(a, b):
    return lax.dot_general(a, b, (((1,), (0,)), ((), ())), preferred_element_type=F32)


def bucket_limits(buckets, reach):
    exact_count = buckets // 2
    limits = []
    for target in range(exact_count + 1, buckets):
        distance = exact_count
        while (
            exact_count
            + int(
                math.log(distance / exact_count)
                / math.log(reach / exact_count)
                * (buckets - exact_count)
            )
            < target
        ):
            distance += 1
        limits.append(distance)
    return limits


def three_parts(row):
    high = row.astype(BF).astype(F32)
    rest = row - high
    middle = rest.astype(BF).astype(F32)
    return high, middle, rest - middle


def extra_rows(columns, first, parts):
    row_id = lax.broadcasted_iota(jnp.int32, (LANES, columns), 0)
    grid = jnp.where(row_id == 0, first, 0.0)
    for place, part in enumerate(parts):
        grid = jnp.where(row_id == place + 1, part, grid)
    return grid.astype(BF)


def head_rows(stacked, head):
    row_id = lax.broadcasted_iota(jnp.int32, stacked.shape, 0)
    return jnp.where((row_id // HEAD_DIM) == head, stacked, jnp.zeros_like(stacked))


def nt(a, b):
    return lax.dot_general(a, b, (((1,), (1,)), ((), ())), preferred_element_type=F32)


def params(**options):
    return pltpu.CompilerParams(vmem_limit_bytes=VMEM_LIMIT, **options)


def cost(us):
    return pl.CostEstimate(flops=int(us), bytes_accessed=0, transcendentals=0)


def shape(rows, columns, kind=BF):
    return jax.ShapeDtypeStruct((rows, columns), kind)


def row_block(columns, rows=BLOCK):
    return pl.BlockSpec((rows, columns), lambda i: (i, 0))


def fixed_block(rows, columns):
    return pl.BlockSpec((rows, columns), lambda i: (0, 0))


ANY = pl.BlockSpec(memory_space=pl.ANY)
SMEM = pl.BlockSpec(memory_space=pltpu.SMEM)


def halves_loaded(core_ref, own_ref, other_ref, pieces, sems):
    @pl.when(pl.program_id(0) == 0)
    def _():
        for side in range(2):

            @pl.when(core_ref[0] == side)
            def _():
                halves = (own_ref, other_ref) if side == 0 else (other_ref, own_ref)
                copies = [
                    pltpu.make_async_copy(halves[half].at[:, source], target, sems.at[place])
                    for place, (half, source, target) in enumerate(pieces)
                ]
                for copy in copies:
                    copy.start()
                for copy in copies:
                    copy.wait()


def key_value_pieces(w_kv):
    return [(0, slice(0, 2 * D), w_kv)]


def out_query_pieces(weights):
    return [(side, slice(0, D), weights.at[:, side * D : (side + 1) * D]) for side in range(2)]


def query_pieces(w_qkv):
    cut = HALF_COLUMNS - 2 * D
    return [
        (0, slice(2 * D, HALF_COLUMNS), w_qkv.at[:, :cut]),
        (1, slice(0, 3 * D - cut), w_qkv.at[:, cut:]),
    ]


def normed(values, gain):
    inverse = lax.rsqrt(jnp.mean(values * values, axis=-1, keepdims=True) + NORM_EPS)
    scaled = values * inverse
    return scaled, inverse, (scaled * gain).astype(BF)


def norm_back(values, gain, grads, gain_grad_ref):
    inverse = lax.rsqrt(jnp.mean(values * values, axis=-1, keepdims=True) + NORM_EPS)
    scaled = values * inverse
    add_rows(gain_grad_ref, jnp.sum(scaled * grads, axis=0, keepdims=True))
    weighted = grads * gain
    centre = jnp.mean(scaled * weighted, axis=-1, keepdims=True)
    return inverse * (weighted - scaled * centre)


def add_rows(total_ref, row):
    row_id = lax.broadcasted_iota(jnp.int32, (8, D), 0)
    addend = jnp.where(row_id == 0, row, 0.0)

    @pl.when(pl.program_id(0) == 0)
    def _():
        total_ref[...] = addend

    @pl.when(pl.program_id(0) > 0)
    def _():
        total_ref[...] += addend


def key_value_kernel(core_ref, own_ref, other_ref, rows_ref, kv_ref, w_kv, sems):
    halves_loaded(core_ref, own_ref, other_ref, key_value_pieces(w_kv), sems)
    kv_ref[...] = nn(rows_ref[...], w_kv[...]).astype(BF)


def key_value(core, own, other, rows, steps, index, us):
    return pl.pallas_call(
        key_value_kernel,
        grid=(steps,),
        in_specs=[SMEM, ANY, ANY, pl.BlockSpec((BLOCK, D), index)],
        out_specs=row_block(2 * D),
        out_shape=shape(steps * BLOCK, 2 * D),
        scratch_shapes=[pltpu.VMEM((D, 2 * D), BF), pltpu.SemaphoreType.DMA((1,))],
        compiler_params=params(),
        cost_estimate=cost(us),
        name="key_value",
    )(core, own, other, rows)


def self_inputs_kernel(
    core_ref, own_ref, other_ref, x_ref, h_ref, qkv_ref, gains_ref, w_qkv, gain_columns, sems
):
    first_gain = 5 * D - HALF_COLUMNS
    pieces = query_pieces(w_qkv)
    pieces.append((1, slice(first_gain, first_gain + LANES), gain_columns))
    halves_loaded(core_ref, own_ref, other_ref, pieces, sems)

    @pl.when(pl.program_id(0) == 0)
    def _():
        gains_ref[...] = gain_columns[...].astype(F32).T[:8]

    h_ref[...] = normed(x_ref[...].astype(F32), gains_ref[:1, :])[2]
    qkv_ref[...] = nn(h_ref[...], w_qkv[...]).astype(BF)


def self_inputs(core, own, other, x):
    return pl.pallas_call(
        self_inputs_kernel,
        grid=(ROWS // BLOCK,),
        in_specs=[SMEM, ANY, ANY, row_block(D)],
        out_specs=[row_block(D), row_block(3 * D), fixed_block(8, D)],
        out_shape=[shape(ROWS, D), shape(ROWS, 3 * D), shape(8, D, F32)],
        scratch_shapes=[
            pltpu.VMEM((D, 3 * D), BF),
            pltpu.VMEM((D, LANES), BF),
            pltpu.SemaphoreType.DMA((3,)),
        ],
        compiler_params=params(),
        cost_estimate=cost(6),
        name="self_inputs",
    )(core, own, other, x)


def cross_inputs_kernel(
    core_ref, own_ref, other_ref, gain_ref, x_ref, o_ref, x1_ref, h_ref, q_ref, weights, sems
):
    halves_loaded(core_ref, own_ref, other_ref, out_query_pieces(weights), sems)
    x1 = x_ref[...].astype(F32) + nn(o_ref[...], weights[:, :D])
    x1_ref[...] = x1
    h_ref[...] = normed(x1, gain_ref[1:2, :])[2]
    q_ref[...] = nn(h_ref[...], weights[:, D:]).astype(BF)


def cross_inputs(core, own, other, gain, x, o1):
    return pl.pallas_call(
        cross_inputs_kernel,
        grid=(ROWS // BLOCK,),
        in_specs=[SMEM, ANY, ANY, fixed_block(8, D), row_block(D), row_block(D)],
        out_specs=[row_block(D)] * 3,
        out_shape=[shape(ROWS, D, F32), shape(ROWS, D), shape(ROWS, D)],
        scratch_shapes=[pltpu.VMEM((D, 2 * D), BF), pltpu.SemaphoreType.DMA((2,))],
        compiler_params=params(),
        cost_estimate=cost(5),
        name="cross_inputs",
    )(core, own, other, gain, x, o1)


def ffn_kernel(
    core_ref, late_ref, own_ref, other_ref, gain_ref, x1_ref, o_ref, dy_ref,
    out_ref, h_ref, hidden_ref, dgate_ref, dup_ref, db_ref, dx_ref, do_ref, gain_grad_ref,
    w_out, w_gate, w_up, w_down, sems, down_sems,
):
    width = w_gate.shape[1]
    copies = [
        pltpu.make_async_copy(late_ref.at[:, :D], w_out, sems.at[0]),
        pltpu.make_async_copy(late_ref.at[:, D : D + width], w_gate, sems.at[1]),
        pltpu.make_async_copy(late_ref.at[:, D + width :], w_up, sems.at[2]),
    ]
    first = pl.program_id(0) == 0

    @pl.when(first)
    def _():
        for copy in copies:
            copy.start()

    pieces = [(side, slice(None), w_down.at[:, side * D // 2 : (side + 1) * D // 2]) for side in range(2)]
    halves_loaded(core_ref, own_ref, other_ref, pieces, down_sems)

    def arrived(place):
        @pl.when(first)
        def _():
            copies[place].wait()

    arrived(0)
    x2 = x1_ref[...] + nn(o_ref[...], w_out[...])
    h_ref[...] = normed(x2, gain_ref[2:3, :])[2]
    dy_low = dy_ref[...]
    arrived(1)
    gate = nn(h_ref[...], w_gate[...])
    arrived(2)
    up = nn(h_ref[...], w_up[...])
    d_hidden = nt(dy_low, w_down[...])
    scale = math.sqrt(2.0 / math.pi)
    square = gate * gate
    turn = jnp.tanh(scale * gate * (1.0 + 0.044715 * square))
    half = 0.5 * (1.0 + turn)
    gelu = gate * half
    slope = half + 0.5 * gate * (1.0 - turn * turn) * (scale * (1.0 + 3 * 0.044715 * square))
    hidden_ref[...] = (gelu * up).astype(BF)
    dgate_ref[...] = (d_hidden * up * slope).astype(BF)
    dup_ref[...] = (d_hidden * gelu).astype(BF)
    out_ref[...] = (x2 + nn(hidden_ref[...], w_down[...])).astype(BF)
    dh = nt(dgate_ref[...], w_gate[...]) + nt(dup_ref[...], w_up[...])
    dx = dy_low.astype(F32) + norm_back(x2, gain_ref[2:3, :], dh, gain_grad_ref)
    dx_ref[...] = dx
    db_ref[...] = dx.astype(BF)
    do_ref[...] = nt(db_ref[...], w_out[...]).astype(BF)


def ffn(core, late, own, other, gain, x1, o2, dy):
    width = own.shape[0]
    return pl.pallas_call(
        ffn_kernel,
        grid=(ROWS // BLOCK,),
        in_specs=[SMEM, ANY, ANY, ANY, fixed_block(8, D), row_block(D), row_block(D), row_block(D)],
        out_specs=[
            row_block(D),
            row_block(D),
            row_block(width),
            row_block(width),
            row_block(width),
            row_block(D),
            row_block(D),
            row_block(D),
            fixed_block(8, D),
        ],
        out_shape=[
            shape(ROWS, D),
            shape(ROWS, D),
            shape(ROWS, width),
            shape(ROWS, width),
            shape(ROWS, width),
            shape(ROWS, D),
            shape(ROWS, D, F32),
            shape(ROWS, D),
            shape(8, D, F32),
        ],
        scratch_shapes=[
            pltpu.VMEM((D, D), BF),
            pltpu.VMEM((D, width), BF),
            pltpu.VMEM((D, width), BF),
            pltpu.VMEM((width, D), BF),
            pltpu.SemaphoreType.DMA((3,)),
            pltpu.SemaphoreType.DMA((2,)),
        ],
        compiler_params=params(),
        cost_estimate=cost(30),
        name="ffn",
    )(core, late, own, other, gain, x1, o2, dy)


def self_grads_kernel(
    core_ref, own_ref, other_ref, gain_ref, x1_ref, dx2_ref, dq0_ref, dq1_ref,
    dx1_ref, db_ref, do_ref, gain_grad_ref, weights, sems,
):
    halves_loaded(core_ref, own_ref, other_ref, out_query_pieces(weights), sems)
    low = pl.program_id(0) < TGT_LEN // BLOCK
    dh = nt(jnp.where(low, dq0_ref[...], dq1_ref[...]), weights[:, D:])
    dx1 = dx2_ref[...] + norm_back(x1_ref[...], gain_ref[1:2, :], dh, gain_grad_ref)
    dx1_ref[...] = dx1
    db_ref[...] = dx1.astype(BF)
    do_ref[...] = nt(db_ref[...], weights[:, :D]).astype(BF)


def self_grads(core, own, other, gain, x1, dx2, dq2):
    half = TGT_LEN // BLOCK
    return pl.pallas_call(
        self_grads_kernel,
        grid=(ROWS // BLOCK,),
        in_specs=[
            SMEM,
            ANY,
            ANY,
            fixed_block(8, D),
            row_block(D),
            row_block(D),
            pl.BlockSpec((BLOCK, D), lambda i: (jnp.minimum(i, half - 1), 0)),
            pl.BlockSpec((BLOCK, D), lambda i: (jnp.maximum(i - half, 0), 0)),
        ],
        out_specs=[row_block(D), row_block(D), row_block(D), fixed_block(8, D)],
        out_shape=[shape(ROWS, D, F32), shape(ROWS, D), shape(ROWS, D), shape(8, D, F32)],
        scratch_shapes=[pltpu.VMEM((D, 2 * D), BF), pltpu.SemaphoreType.DMA((2,))],
        compiler_params=params(),
        cost_estimate=cost(5),
        name="self_grads",
    )(core, own, other, gain, x1, dx2, *dq2)


def input_grads_kernel(
    core_ref, own_ref, other_ref, gain_ref, x_ref, dx1_ref, dqkv_ref,
    dx_ref, gain_grad_ref, w_qkv, sems,
):
    halves_loaded(core_ref, own_ref, other_ref, query_pieces(w_qkv), sems)
    dh = (
        nt(dqkv_ref[0], w_qkv[:, :D])
        + nt(dqkv_ref[1], w_qkv[:, D : 2 * D])
        + nt(dqkv_ref[2], w_qkv[:, 2 * D :])
    )
    x = x_ref[...].astype(F32)
    dx_ref[...] = (dx1_ref[...] + norm_back(x, gain_ref[:1, :], dh, gain_grad_ref)).astype(BF)


def input_grads(core, own, other, gain, x, dx1, dqkv):
    return pl.pallas_call(
        input_grads_kernel,
        grid=(ROWS // BLOCK,),
        in_specs=[
            SMEM, ANY, ANY, fixed_block(8, D), row_block(D), row_block(D),
            pl.BlockSpec((3, BLOCK, D), lambda i: (0, i, 0)),
        ],
        out_specs=[row_block(D), fixed_block(8, D)],
        out_shape=[shape(ROWS, D), shape(8, D, F32)],
        scratch_shapes=[pltpu.VMEM((D, 3 * D), BF), pltpu.SemaphoreType.DMA((2,))],
        compiler_params=params(),
        cost_estimate=cost(6),
        name="input_grads",
    )(core, own, other, gain, x, dx1, dqkv)


def memory_grads_kernel(core_ref, own_ref, other_ref, dkv_ref, dm_ref, w_kv, sems):
    halves_loaded(core_ref, own_ref, other_ref, key_value_pieces(w_kv), sems)
    dm_ref[...] = (nt(dkv_ref[0], w_kv[:, :D]) + nt(dkv_ref[1], w_kv[:, D:])).astype(BF)


def memory_grads(core, own, other, dkv):
    rows = dkv.shape[1]
    return pl.pallas_call(
        memory_grads_kernel,
        grid=(rows // BLOCK,),
        in_specs=[SMEM, ANY, ANY, pl.BlockSpec((2, BLOCK, D), lambda i: (0, i, 0))],
        out_specs=row_block(D),
        out_shape=shape(rows, D),
        scratch_shapes=[pltpu.VMEM((D, 2 * D), BF), pltpu.SemaphoreType.DMA((1,))],
        compiler_params=params(),
        cost_estimate=cost(rows / 400),
        name="memory_grads",
    )(core, own, other, dkv)


def stored_by_core(core_ref, grad, give_ref, keep_ref):
    across, _, count = give_ref.shape[0], 2, give_ref.shape[1]
    for side in range(2):

        @pl.when(core_ref[0] == side)
        def _():
            for place in range(across):
                first = place * 2 * count
                here, there = first + side * count, first + (1 - side) * count
                keep_ref[place] = grad[here : here + count].astype(BF)
                give_ref[place] = grad[there : there + count].astype(BF)


def row_grads_kernel(core_ref, rows_ref, grads_ref, give_ref, keep_ref, turned):
    @pl.when(pl.program_id(0) == 0)
    def _():
        turned[...] = rows_ref[...].T

    stored_by_core(core_ref, nn(turned[...], grads_ref[0]), give_ref, keep_ref)


def row_grads(core, rows, grads, across, us):
    units, length = grads.shape[0], grads.shape[1]
    count = D // (2 * across)
    block = pl.BlockSpec((across, count, D), lambda u: (0, 0, u))
    piece = jax.ShapeDtypeStruct((across, count, units * D), BF)
    return pl.pallas_call(
        row_grads_kernel,
        grid=(units,),
        in_specs=[SMEM, fixed_block(length, D), pl.BlockSpec((1, length, D), lambda u: (u, 0, 0))],
        out_specs=[block, block],
        out_shape=[piece, piece],
        scratch_shapes=[pltpu.VMEM((D, length), BF)],
        compiler_params=params(),
        cost_estimate=cost(us),
        name="row_grads",
    )(core, rows, grads)


def pair_grads_kernel(counts, core_ref, *refs):
    give_ref, keep_ref = refs[-2:]
    used = 0
    for place, count in enumerate(counts):
        turned = refs[used][...].T
        length = turned.shape[1] // count
        grad = sum(
            nn(turned[:, part * length : (part + 1) * length], refs[used + 1 + part][...])
            for part in range(count)
        )
        used += 1 + count
        columns = slice(place * D, (place + 1) * D)
        stored_by_core(core_ref, grad, give_ref.at[:, :, columns], keep_ref.at[:, :, columns])


def pair_grads(core, pairs, across):
    count = D // (2 * across)
    piece = jax.ShapeDtypeStruct((across, count, len(pairs) * D), BF)
    whole = pl.BlockSpec(memory_space=pltpu.VMEM)
    flat = [array for rows, grads in pairs for array in (rows,) + tuple(grads)]
    return pl.pallas_call(
        functools.partial(pair_grads_kernel, [len(grads) for _, grads in pairs]),
        in_specs=[SMEM] + [whole] * len(flat),
        out_specs=[whole, whole],
        out_shape=[piece, piece],
        compiler_params=params(),
        cost_estimate=cost(2.5 * len(pairs)),
        name="pair_grads",
    )(core, *flat)


def ffn_weight_grads_kernel(h_ref, hidden_ref, dgate_ref, dup_ref, dy_ref, out_ref):
    unit = pl.program_id(0)
    devices = out_ref.shape[0]
    width = dgate_ref.shape[1]

    def from_columns(grads_ref):
        turned = h_ref[...].T
        share = D // devices
        for first in range(0, width, 2 * WIDE):
            both = [
                nn(turned, grads_ref[:, place : place + WIDE]).reshape(devices, share, WIDE)
                for place in (first, first + WIDE)
            ]
            row = first // WIDE * share
            out_ref[:, row : row + 2 * share, :] = jnp.concatenate(both, axis=1).astype(BF)

    @pl.when(unit == 0)
    def _():
        from_columns(dgate_ref)

    @pl.when(unit == 1)
    def _():
        from_columns(dup_ref)

    @pl.when(unit == 2)
    def _():
        turned = hidden_ref[...].T
        share = width // devices
        for place in range(D // WIDE):
            grad = nn(turned, dy_ref[:, place * WIDE : (place + 1) * WIDE])
            out_ref[:, place * share : (place + 1) * share, :] = grad.reshape(
                devices, share, WIDE
            ).astype(BF)


def ffn_weight_grads(h3, hidden, d_gate, d_up, dy, devices):
    width = hidden.shape[1]
    rows = D * width // WIDE // devices
    return pl.pallas_call(
        ffn_weight_grads_kernel,
        grid=(3,),
        in_specs=[
            fixed_block(ROWS, D),
            fixed_block(ROWS, width),
            fixed_block(ROWS, width),
            fixed_block(ROWS, width),
            fixed_block(ROWS, D),
        ],
        out_specs=pl.BlockSpec((devices, rows, WIDE), lambda u: (0, u, 0)),
        out_shape=jax.ShapeDtypeStruct((devices, 3 * rows, WIDE), BF),
        compiler_params=params(),
        cost_estimate=cost(13),
        name="ffn_weight_grads",
    )(h3, hidden, d_gate, d_up, dy)


def memory_weight_grads_kernel(
    core_ref, mem_ref, next_ref, own0_ref, own1_ref, after0_ref, after1_ref,
    give_ref, keep_ref, turned,
):
    @pl.when(pl.program_id(0) == 0)
    def _():
        for m in range(MICRO):
            turned[:, m * OWN : (m + 1) * OWN] = mem_ref[m, 0, MEM_DEV - OWN :, :].T
        turned[:, MICRO * OWN :] = next_ref[...].T

    grad, used = 0.0, 0
    for part_ref in (own0_ref, own1_ref, after0_ref, after1_ref):
        length = part_ref.shape[1]
        grad = grad + nn(turned[:, used : used + length], part_ref[0])
        used += length
    stored_by_core(core_ref, grad, give_ref, keep_ref)


def memory_weight_grads(core, memory, next_rows, dkv_own, dkv_next, across):
    count = D // (2 * across)
    block = pl.BlockSpec((across, count, D), lambda u: (0, 0, u))
    piece = jax.ShapeDtypeStruct((across, count, 2 * D), BF)
    return pl.pallas_call(
        memory_weight_grads_kernel,
        grid=(2,),
        in_specs=[
            SMEM,
            pl.BlockSpec((MICRO, 1, MEM_DEV, D), lambda u: (0, 0, 0, 0)),
            fixed_block(MICRO * NEXT, D),
        ]
        + [pl.BlockSpec((1, OWN, D), lambda u: (u, 0, 0))] * MICRO
        + [pl.BlockSpec((1, NEXT, D), lambda u: (u, 0, 0))] * MICRO,
        out_specs=[block, block],
        out_shape=[piece, piece],
        scratch_shapes=[pltpu.VMEM((D, MICRO * (OWN + NEXT)), BF)],
        compiler_params=params(),
        cost_estimate=cost(8),
        name="memory_weight_grads",
    )(core, memory, next_rows, *dkv_own, *dkv_next)


def memory_total_kernel(
    core_ref, own_ref, other_ref, dkv0_ref, dkv1_ref, prev0_ref, prev1_ref, dm_ref, w_kv, sems
):
    halves_loaded(core_ref, own_ref, other_ref, key_value_pieces(w_kv), sems)
    low = pl.program_id(0) < 4
    block = pl.program_id(0) % 4
    prev = jnp.where(low, prev0_ref[...], prev1_ref[...])

    @pl.when(block == 0)
    def _():
        dm_ref[...] = prev

    @pl.when(block > 0)
    def _():
        dk, dv = (jnp.where(low, dkv0_ref[place], dkv1_ref[place]) for place in range(2))
        shared = jnp.where(block == 1, prev.astype(F32), 0.0)
        dm_ref[...] = (nt(dk, w_kv[:, :D]) + nt(dv, w_kv[:, D:]) + shared).astype(BF)


def memory_total(core, own, other, dkv, prev):
    def spot(i, m):
        return jnp.clip(i - 4 * m, 0, 3)

    def dkv_block(m):
        return pl.BlockSpec((2, BLOCK, D), lambda i: (0, jnp.maximum(spot(i, m) - 1, 0), 0))

    def prev_block(m):
        return pl.BlockSpec((BLOCK, D), lambda i: (jnp.minimum(spot(i, m), 1), 0))

    return pl.pallas_call(
        memory_total_kernel,
        grid=(MICRO * 4,),
        in_specs=[SMEM, ANY, ANY]
        + [dkv_block(m) for m in range(MICRO)]
        + [prev_block(m) for m in range(MICRO)],
        out_specs=row_block(D),
        out_shape=shape(MICRO * MEM_DEV, D),
        scratch_shapes=[pltpu.VMEM((D, 2 * D), BF), pltpu.SemaphoreType.DMA((1,))],
        compiler_params=params(),
        cost_estimate=cost(7),
        name="memory_total",
    )(core, own, other, *dkv, *prev)


def extras_kernel(share, core_ref, sums_ref, first_ref, second_ref, third_ref, give_ref, keep_ref):
    row_id = lax.broadcasted_iota(jnp.int32, (8, D), 0)
    norms = jnp.zeros((8, D), F32)
    for place, ref in enumerate((first_ref, second_ref, third_ref)):
        norms = jnp.where(row_id == place, ref[:1, :], norms)
    stacked = jnp.concatenate([norms, jnp.zeros((LANES - 8, D), F32)], axis=0).T
    distance = lax.broadcasted_iota(jnp.int32, (HALF, LANES), 0)
    bucket_id = lax.broadcasted_iota(jnp.int32, (HALF, LANES), 1)
    exact_count = BUCKETS // 2
    bucket = jnp.full((HALF, LANES), exact_count, jnp.int32)
    for threshold in bucket_limits(BUCKETS, REACH):
        bucket = bucket + (distance >= threshold).astype(jnp.int32)
    bucket = jnp.where(distance < exact_count, distance, bucket)
    sums = sums_ref[...]
    together = LANES // BUCKETS
    lines = [jnp.zeros((1, LANES), F32) for _ in range(HEADS // together)]
    for part in range(together):
        near_hot = (bucket == bucket_id - part * BUCKETS).astype(F32)
        far_hot = (bucket_id == (part + 1) * BUCKETS - 1).astype(F32)
        table = sum(
            lax.dot_general(
                sums[:, place, :], hot, (((1,), (0,)), ((), ())),
                precision=lax.Precision.HIGHEST, preferred_element_type=F32,
            )
            for place, hot in ((0, near_hot), (1, far_hot))
        )
        for line in range(len(lines)):
            head = line * together + part
            lines[line] = lines[line] + table[head : head + 1]
    row_in_share = lax.broadcasted_iota(jnp.int32, (D, LANES), 0) % share
    tall = jnp.zeros((D, LANES), F32)
    for line, row in enumerate(lines):
        tall = jnp.where(row_in_share == line, row, tall)
    both = jnp.concatenate([stacked, tall], axis=1)
    stored_by_core(core_ref, both, give_ref, keep_ref)


def extras(core, sums, norms, across, share):
    piece = jax.ShapeDtypeStruct((across, D // (2 * across), 2 * LANES), BF)
    whole = pl.BlockSpec(memory_space=pltpu.VMEM)
    return pl.pallas_call(
        functools.partial(extras_kernel, share),
        in_specs=[SMEM] + [whole] * 4,
        out_specs=[whole, whole],
        out_shape=[piece, piece],
        compiler_params=params(),
        cost_estimate=cost(2),
        name="extras",
    )(core, sums, *norms)


def bias_tiles_kernel(table_ref, tiles_ref):
    head = pl.program_id(0)
    key_id = lax.broadcasted_iota(jnp.int32, (HALF, HALF), 0)
    query_id = lax.broadcasted_iota(jnp.int32, (HALF, HALF), 1)
    limits = bucket_limits(BUCKETS, REACH)
    exact_count = BUCKETS // 2
    for tile in range(2):
        distance = query_id - key_id + tile * HALF
        grid = jnp.full((HALF, HALF), table_ref[head, 0], F32)
        for bucket in range(1, BUCKETS):
            start = bucket if bucket <= exact_count else limits[bucket - exact_count - 1]
            grid = jnp.where(distance >= start, table_ref[head, bucket], grid)
        if tile == 0:
            grid = jnp.where(distance >= 0, grid, MASKED)
        tiles_ref[0, tile] = grid


def bias_tiles(table):
    return pl.pallas_call(
        bias_tiles_kernel,
        grid=(HEADS,),
        in_specs=[pl.BlockSpec(memory_space=pltpu.SMEM)],
        out_specs=pl.BlockSpec((1, 2, HALF, HALF), lambda h: (h, 0, 0, 0)),
        out_shape=jax.ShapeDtypeStruct((HEADS, 2, HALF, HALF), F32),
        cost_estimate=cost(8),
        name="bias_tiles",
    )(table)


def softmax_columns(scores):
    top = jnp.max(scores, axis=0, keepdims=True)
    weights = jnp.exp(scores - top)
    total = jnp.sum(weights, axis=0, keepdims=True)
    return weights.astype(BF), 1.0 / total, top + jnp.log(total)


def put_lse(lse_ref, rows):
    row_id = lax.broadcasted_iota(jnp.int32, (8, TGT_LEN), 0)
    lse_ref[0] = jnp.where(row_id == 0, rows[0], rows[1])


def cross_forward_kernel(q_ref, ko_ref, kn_ref, vo_ref, vn_ref, mask_ref, o_ref, lse_ref, k_ext):
    k_ext[:OWN, :LANES] = ko_ref[...]
    k_ext[OWN:, :LANES] = kn_ref[...]
    k_ext[:, LANES:] = mask_ref[0]
    q_t = q_ref[...].T
    v_t = jnp.concatenate([vo_ref[...], vn_ref[...]], axis=0).T
    ones = extra_rows(TGT_LEN, 1.0, ())
    mixed, lses = [], []
    for head in range(2):
        query = jnp.concatenate([head_rows(q_t, head), ones], axis=0)
        scores = nn(k_ext[...], query)
        weights, inverse, lse = softmax_columns(scores)
        mixed.append(nn(v_t[head * HEAD_DIM : (head + 1) * HEAD_DIM], weights) * inverse)
        lses.append(lse)
    o_ref[...] = jnp.concatenate(mixed, axis=0).T.astype(BF)
    put_lse(lse_ref, lses)


def cross_backward_kernel(
    q_ref, ko_ref, kn_ref, vo_ref, vn_ref, mask_ref, o_ref, do_ref, lse_ref,
    dq_ref, own_ref, next_ref, k_ext, v_ext,
):
    k_ext[:OWN, :LANES] = ko_ref[...]
    k_ext[OWN:, :LANES] = kn_ref[...]
    k_ext[:, LANES:] = mask_ref[0]
    v_ext[:OWN, :LANES] = vo_ref[...]
    v_ext[OWN:, :LANES] = vn_ref[...]
    v_ext[:, LANES:] = jnp.ones((KEYS, LANES), BF)
    k_t = k_ext[:, :LANES].T
    q = q_ref[...]
    d_o = do_ref[...]
    q_t = q.T
    do_t = d_o.T
    centre_t = (o_ref[...].astype(F32) * d_o.astype(F32)).T
    dq, dk, dv = [], [], []
    for head in range(2):
        rows = slice(head * HEAD_DIM, (head + 1) * HEAD_DIM)
        lse = lse_ref[0, head : head + 1, :]
        centre = jnp.sum(centre_t[rows], axis=0, keepdims=True)
        query = jnp.concatenate(
            [head_rows(q_t, head), extra_rows(TGT_LEN, 1.0, three_parts(-lse))], axis=0
        )
        grad = jnp.concatenate(
            [head_rows(do_t, head), extra_rows(TGT_LEN, 0.0, three_parts(-centre))], axis=0
        )
        probs = jnp.exp(nn(k_ext[...], query))
        grad_scores = (probs * nn(v_ext[...], grad)).astype(BF)
        dv.append(nn(probs.astype(BF), d_o))
        dk.append(nn(grad_scores, q))
        dq.append(nn(k_t[rows], grad_scores))
    dq_ref[...] = jnp.concatenate(dq, axis=0).T.astype(BF)
    lane = lax.broadcasted_iota(jnp.int32, (KEYS, LANES), 1)
    dk_pair = jnp.where(lane < HEAD_DIM, dk[0], dk[1]).astype(BF)
    dv_pair = jnp.where(lane < HEAD_DIM, dv[0], dv[1]).astype(BF)
    for place, pair in enumerate((dk_pair, dv_pair)):
        own_ref[place] = pair[:OWN]
        next_ref[place] = pair[OWN:]


def self_forward_kernel(q_ref, k_ref, v_ref, tiles_ref, o_ref, lse_ref):
    k = k_ref[...]
    q_t = q_ref[...].T
    v_t = v_ref[...].T
    mixed, lses = [], []
    for head in range(2):
        query = head_rows(q_t, head)
        value = v_t[head * HEAD_DIM : (head + 1) * HEAD_DIM]
        near, far = tiles_ref[head, 0], tiles_ref[head, 1]
        w0, i0, l0 = softmax_columns(nn(k[:HALF], query[:, :HALF]) + near)
        raw = nn(k, query[:, HALF:])
        w1, i1, l1 = softmax_columns(
            jnp.concatenate([raw[:HALF] + far, raw[HALF:] + near], axis=0)
        )
        out0 = nn(value[:, :HALF], w0) * i0
        out1 = nn(value, w1) * i1
        mixed.append(jnp.concatenate([out0, out1], axis=1))
        lses.append(jnp.concatenate([l0, l1], axis=1))
    o_ref[...] = jnp.concatenate(mixed, axis=0).T.astype(BF)
    put_lse(lse_ref, lses)


def distance_sums(near, far):
    key_id = lax.broadcasted_iota(jnp.int32, (HALF, HALF), 0)
    query_id = lax.broadcasted_iota(jnp.int32, (HALF, HALF), 1)
    close = (query_id - key_id + HALF) < REACH
    both = near + jnp.where(close, far, 0.0)
    group = both[:8]
    for first in range(8, HALF, 8):
        group = group + pltpu.roll(both[first : first + 8], HALF - first, 1)
    row_id = lax.broadcasted_iota(jnp.int32, (8, HALF), 0)
    turned = group
    for row in range(1, 8):
        turned = jnp.where(row_id == row, pltpu.roll(group, HALF - row, 1), turned)
    by_distance = jnp.sum(turned, axis=0, keepdims=True)
    rest = jnp.sum(jnp.where(close, 0.0, far), axis=0, keepdims=True)
    return jnp.where(row_id == 0, by_distance, jnp.where(row_id == 1, rest, 0.0))


def self_backward_kernel(
    q_ref, k_ref, v_ref, tiles_ref, o_ref, do_ref, lse_ref,
    dqkv_ref, sums_ref, k_ext, v_ext, near_ref, far_ref,
):
    row_ext = jnp.ones((TGT_LEN, LANES), BF)
    k_ext[:, :LANES] = k_ref[...]
    k_ext[:, LANES:] = row_ext
    v_ext[:, :LANES] = v_ref[...]
    v_ext[:, LANES:] = row_ext
    k_t = k_ref[...].T
    q = q_ref[...]
    d_o = do_ref[...]
    q_t = q.T
    do_t = d_o.T
    centre_t = (o_ref[...].astype(F32) * d_o.astype(F32)).T
    first = pl.program_id(1) == 0
    dq, dk, dv = [], [], []
    for head in range(2):
        rows = slice(head * HEAD_DIM, (head + 1) * HEAD_DIM)
        lse = lse_ref[0, head : head + 1, :]
        centre = jnp.sum(centre_t[rows], axis=0, keepdims=True)
        query = jnp.concatenate(
            [head_rows(q_t, head), extra_rows(TGT_LEN, 0.0, three_parts(-lse))], axis=0
        )
        grad = jnp.concatenate(
            [head_rows(do_t, head), extra_rows(TGT_LEN, 0.0, three_parts(-centre))], axis=0
        )
        near, far = tiles_ref[head, 0], tiles_ref[head, 1]
        raw0 = nn(k_ext[:HALF, :], query[:, :HALF])
        raw1 = nn(k_ext[...], query[:, HALF:])
        p00 = jnp.exp(raw0 + near)
        p10 = jnp.exp(raw1[:HALF] + far)
        p11 = jnp.exp(raw1[HALF:] + near)
        g0 = nn(v_ext[:HALF, :], grad[:, :HALF])
        g1 = nn(v_ext[...], grad[:, HALF:])
        s00 = p00 * g0
        s10 = p10 * g1[:HALF]
        s11 = p11 * g1[HALF:]
        near_sum, far_sum = s00 + s11, s10

        @pl.when(first)
        def _():
            near_ref[head] = near_sum
            far_ref[head] = far_sum

        @pl.when(jnp.logical_not(first))
        def _():
            sums_ref[head] = distance_sums(near_ref[head] + near_sum, far_ref[head] + far_sum)

        b00, b10, b11 = s00.astype(BF), s10.astype(BF), s11.astype(BF)
        w00, w10, w11 = p00.astype(BF), p10.astype(BF), p11.astype(BF)
        top = jnp.concatenate([w00, w10], axis=1)
        dv.append(jnp.concatenate([nn(top, d_o), nn(w11, d_o[HALF:])], axis=0))
        top = jnp.concatenate([b00, b10], axis=1)
        dk.append(jnp.concatenate([nn(top, q), nn(b11, q[HALF:])], axis=0))
        dq.append(
            jnp.concatenate(
                [
                    nn(k_t[rows, :HALF], b00),
                    nn(k_t[rows], jnp.concatenate([b10, b11], axis=0)),
                ],
                axis=1,
            )
        )
    dqkv_ref[0] = jnp.concatenate(dq, axis=0).T.astype(BF)
    lane = lax.broadcasted_iota(jnp.int32, (TGT_LEN, LANES), 1)
    dqkv_ref[1] = jnp.where(lane < HEAD_DIM, dk[0], dk[1]).astype(BF)
    dqkv_ref[2] = jnp.where(lane < HEAD_DIM, dv[0], dv[1]).astype(BF)


PAIR_GRID = (MICRO, PAIRS)


def pair_block(rows, offset=0):
    return pl.BlockSpec((rows, LANES), lambda m, p: (m, p + offset))


LSE_BLOCK = pl.BlockSpec((1, 8, TGT_LEN), lambda m, p: (m * PAIRS + p, 0, 0))
LSE_SHAPE = jax.ShapeDtypeStruct((MICRO * PAIRS, 8, TGT_LEN), F32)
MASK_BLOCK = pl.BlockSpec((1, KEYS, LANES), lambda m, p: (m, 0, 0))


def cross_forward(q, kv_own, kv_next, mask):
    return pl.pallas_call(
        cross_forward_kernel,
        grid=PAIR_GRID,
        in_specs=[
            pair_block(TGT_LEN),
            pair_block(OWN),
            pair_block(NEXT),
            pair_block(OWN, PAIRS),
            pair_block(NEXT, PAIRS),
            MASK_BLOCK,
        ],
        out_specs=[pair_block(TGT_LEN), LSE_BLOCK],
        out_shape=[jax.ShapeDtypeStruct((ROWS, D), BF), LSE_SHAPE],
        scratch_shapes=[pltpu.VMEM((KEYS, 2 * LANES), BF)],
        compiler_params=params(),
        cost_estimate=cost(32),
        name="cross_forward",
    )(q, kv_own, kv_next, kv_own, kv_next, mask)


def cross_backward(m, q, kv_own, kv_next, mask, o, d_o, lse):
    def block(rows, offset=0):
        return pl.BlockSpec((rows, LANES), lambda p: (m, p + offset))

    return pl.pallas_call(
        cross_backward_kernel,
        grid=(PAIRS,),
        in_specs=[
            block(TGT_LEN),
            block(OWN),
            block(NEXT),
            block(OWN, PAIRS),
            block(NEXT, PAIRS),
            pl.BlockSpec((1, KEYS, LANES), lambda p: (m, 0, 0)),
            block(TGT_LEN),
            block(TGT_LEN),
            pl.BlockSpec((1, 8, TGT_LEN), lambda p: (m * PAIRS + p, 0, 0)),
        ],
        out_specs=[
            pl.BlockSpec((TGT_LEN, LANES), lambda p: (0, p)),
            pl.BlockSpec((2, OWN, LANES), lambda p: (0, 0, p)),
            pl.BlockSpec((2, NEXT, LANES), lambda p: (0, 0, p)),
        ],
        out_shape=[
            shape(TGT_LEN, D),
            jax.ShapeDtypeStruct((2, OWN, D), BF),
            jax.ShapeDtypeStruct((2, NEXT, D), BF),
        ],
        scratch_shapes=[pltpu.VMEM((KEYS, 2 * LANES), BF)] * 2,
        compiler_params=params(),
        cost_estimate=cost(22),
        name="cross_backward",
    )(q, kv_own, kv_next, kv_own, kv_next, mask, o, d_o, lse)


def swapped(spec):
    index = spec.index_map
    return pl.BlockSpec(spec.block_shape, lambda p, m: index(m, p))


TILE_BLOCK = pl.BlockSpec((2, 2, HALF, HALF), lambda p, m: (p, 0, 0, 0))


def self_forward(qkv, tiles):
    return pl.pallas_call(
        self_forward_kernel,
        grid=(PAIRS, MICRO),
        in_specs=[
            swapped(pair_block(TGT_LEN)),
            swapped(pair_block(TGT_LEN, PAIRS)),
            swapped(pair_block(TGT_LEN, 2 * PAIRS)),
            TILE_BLOCK,
        ],
        out_specs=[swapped(pair_block(TGT_LEN)), swapped(LSE_BLOCK)],
        out_shape=[jax.ShapeDtypeStruct((ROWS, D), BF), LSE_SHAPE],
        compiler_params=params(),
        cost_estimate=cost(17),
        name="self_forward",
    )(qkv, qkv, qkv, tiles)


def self_backward(qkv, tiles, o, d_o, lse):
    sums = jax.ShapeDtypeStruct((HEADS, 8, HALF), F32)
    return pl.pallas_call(
        self_backward_kernel,
        grid=(PAIRS, MICRO),
        in_specs=[
            swapped(pair_block(TGT_LEN)),
            swapped(pair_block(TGT_LEN, PAIRS)),
            swapped(pair_block(TGT_LEN, 2 * PAIRS)),
            TILE_BLOCK,
            swapped(pair_block(TGT_LEN)),
            swapped(pair_block(TGT_LEN)),
            swapped(LSE_BLOCK),
        ],
        out_specs=[
            pl.BlockSpec((3, TGT_LEN, LANES), lambda p, m: (0, m, p)),
            pl.BlockSpec((2, 8, HALF), lambda p, m: (p, 0, 0)),
        ],
        out_shape=[jax.ShapeDtypeStruct((3, ROWS, D), BF), sums],
        scratch_shapes=[pltpu.VMEM((TGT_LEN, 2 * LANES), BF)] * 2
        + [pltpu.VMEM((2, HALF, HALF), F32)] * 2,
        compiler_params=params(),
        cost_estimate=cost(24),
        name="self_backward",
    )(qkv, qkv, qkv, tiles, o, d_o, lse)


def key_masks(offsets_row, position):
    shard_ids = jnp.arange(offsets_row.shape[0], dtype=jnp.int32)
    own_start = jnp.sum(jnp.where(shard_ids == position, offsets_row, 0))
    next_start = jnp.sum(jnp.where(shard_ids == position + 1, offsets_row, 0))
    own_valid = jnp.arange(MEM_DEV - OWN, MEM_DEV, dtype=jnp.int32) >= own_start
    next_valid = jnp.arange(NEXT, dtype=jnp.int32) < next_start
    valid = jnp.concatenate([own_valid, next_valid])[:, None]
    lane = jnp.arange(LANES, dtype=jnp.int32)[None, :]
    return jnp.where((lane == 0), jnp.where(valid, 0.0, MASKED), 1.0).astype(BF)


def passed_along(block, distance):
    devices = range(lax.axis_size("seq"))
    route = [(i - distance, i) for i in devices if i - distance in devices]
    return lax.ppermute(block, "seq", route)


def device_bits():
    bits = []
    for axis in AXES:
        count = lax.axis_size(axis).bit_length() - 1
        bits += [(axis, place) for place in reversed(range(count))]
    return bits


def bit_groups():
    bits = device_bits()
    core = ("dp", 0)
    low = (lax.axis_size("seq").bit_length() - 1) // 2
    plane = [b for b in bits if b != core and (b[0] == "dp" or b[1] < low)]
    column = [b for b in bits if b[0] == "seq" and b[1] >= low]
    return [core], plane, column


def mine(bit):
    axis, place = bit
    return (lax.axis_index(axis) >> place) & 1


def flips(group):
    for mask in range(1, 1 << len(group)):
        yield [(mask >> place) & 1 for place in range(len(group))]


def exchange(block, group, flip):
    mask = 0
    for (axis, place), turned in zip(group, flip):
        stride = lax.axis_size("seq") if axis == "dp" else 1
        mask ^= turned * stride << place
    count = lax.axis_size("dp") * lax.axis_size("seq")
    return lax.ppermute(block, AXES, [(i, i ^ mask) for i in range(count)])


def gather_stage(held, dims, group, fillers=()):
    order = device_bits()
    joined = sorted(dims + group, key=order.index)
    tail = held.shape[len(dims) :]
    spot = tuple(1 if bit in group else 2 for bit in joined) + tail
    turns = [[0] * len(group)] + list(flips(group))
    pieces = [held] + [exchange(held, group, flip) for flip in turns[1:]]
    pieces, fillers = tied(pieces, fillers)
    result = jnp.zeros((2,) * len(joined) + tail, held.dtype)
    for flip, piece in zip(turns, pieces):
        start = [mine(bit) ^ flip[group.index(bit)] if bit in group else 0 for bit in joined]
        result = lax.dynamic_update_slice(result, piece.reshape(spot), start + [0] * len(tail))
    return result, joined, fillers


def paired_halves(shard, core):
    halves = shard.reshape(shard.shape[0], 2, -1)
    here = lax.dynamic_index_in_dim(halves, core, 1, keepdims=False)
    there = lax.dynamic_index_in_dim(halves, 1 - core, 1, keepdims=False)
    received = exchange(there, bit_groups()[0], [1])
    return jnp.stack([jnp.where(core == 0, here, received), jnp.where(core == 0, received, here)])


def both_halves(held):
    own = held.reshape(-1, held.shape[-1])
    return own, exchange(own, bit_groups()[0], [1])


def gather_bits(held, dims, group):
    for bit in reversed(group):
        held, dims, _ = gather_stage(held, dims, [bit])
    return held, dims, ()


def tree_sum(terms):
    terms = [term.astype(F32) for term in terms]
    while len(terms) > 1:
        terms = [
            terms[place] + terms[place + 1] if place + 1 < len(terms) else terms[place]
            for place in range(0, len(terms), 2)
        ]
    return terms[0]


def picked(array, dims, group, flip):
    left = list(dims)
    for bit, turned in zip(group, flip):
        place = left.index(bit)
        left.remove(bit)
        array = lax.dynamic_index_in_dim(array, mine(bit) ^ turned, place, keepdims=False)
    return array


def scatter_parts(bundles, dims, group):
    def part(flip):
        sums = [
            tree_sum([picked(term, dims, group, flip) for term in terms]).astype(BF)
            for terms in bundles
        ]
        return jnp.concatenate(sums, axis=-1) if len(sums) > 1 else sums[0]

    return [part([0] * len(group))] + [part(flip) for flip in flips(group)]


def scattered(parts, group):
    sent = [exchange(part, group, flip) for part, flip in zip(parts[1:], flips(group))]
    return parts[:1] + sent


def core_stage(give, keep):
    core, _, _ = bit_groups()
    dims = [bit for bit in device_bits() if bit not in core]
    received = exchange(give, core, [1])
    split = (2,) * len(dims) + (give.shape[0] * give.shape[1] >> len(dims), give.shape[2])
    return [keep.reshape(split), received.reshape(split)]


def without(dims, group):
    return [bit for bit in dims if bit not in group]


def passed_along(block, distance):
    devices = range(lax.axis_size("seq"))
    route = [(i - distance, i) for i in devices if i - distance in devices]
    return lax.ppermute(block, "seq", route)


def ffn_grads(h3, hidden, d_gate, d_up, dy, later):
    devices = lax.axis_size("dp") * lax.axis_size("seq")
    width = hidden.shape[1]
    if D // devices % 8 or width // devices % 16:
        total = [
            lax.psum_scatter(
                lax.dot_general(
                    rows, grads, (((0,), (0,)), ((), ())), preferred_element_type=F32
                ),
                AXES,
                scatter_dimension=0,
                tiled=True,
            )
            for rows, grads in ((h3, d_gate), (h3, d_up), (hidden, dy))
        ]
        return total, later
    partial = ffn_weight_grads(h3, hidden, d_gate, d_up, dy, devices)
    later, partial = tied(later, partial)
    return lax.psum_scatter(partial, AXES, scatter_dimension=0, tiled=True), later


def ffn_columns(total, share, width):
    if isinstance(total, (list, tuple)):
        return total
    total = total[0].astype(F32)
    rows = share * width // WIDE

    def columns(first, height):
        block = total[first : first + rows].reshape(-1, height, WIDE)
        return block.transpose(1, 0, 2).reshape(height, -1)

    return columns(0, share), columns(rows, share), columns(2 * rows, rows * WIDE // D)


def tied(values, parts):
    values, parts = lax.optimization_barrier((values, parts))
    return values, parts


def local(
    decoder_in,
    memory,
    doc_offsets,
    self_query,
    self_key,
    self_value,
    self_out,
    cross_query,
    cross_key,
    cross_value,
    cross_out,
    ffn_gate,
    ffn_up,
    ffn_down,
    norm_self,
    norm_cross,
    norm_ffn,
    bias_table,
    cotangent,
):
    position = lax.axis_index("seq")
    core = lax.axis_index("dp") & 1
    core_id = core.reshape(1).astype(jnp.int32)
    across = lax.axis_size("dp") // 2
    share = self_query.shape[0]
    core_bits, plane, column = bit_groups()

    gains = jnp.stack([norm_self, norm_cross, norm_ffn], axis=1)
    gains = jnp.pad(gains, ((0, 0), (0, 2 * LANES - 3)))
    first = jnp.concatenate(
        [cross_key, cross_value, self_query, self_key, self_value, gains], axis=1
    )
    second = jnp.concatenate([self_out, cross_query], axis=1)
    late = jnp.concatenate([cross_out, ffn_gate, ffn_up], axis=1)
    first = paired_halves(first, core)
    first, dims, _ = gather_stage(first, core_bits, column)
    first, second, ffn_down, doc_offsets, memory, bias_table = lax.optimization_barrier(
        (first, second, ffn_down, doc_offsets, memory, bias_table)
    )
    second = paired_halves(second, core)
    third = paired_halves(ffn_down, core)
    tiles = bias_tiles(bias_table.astype(F32))
    mask = jnp.stack([key_masks(doc_offsets[m, 0], position) for m in range(MICRO)])
    next_rows = memory[:, 0, :NEXT]
    second, _, _ = gather_bits(second, core_bits, column)
    first, _, (second, third, tiles, mask, next_rows) = gather_stage(
        first, dims, plane, (second, third, tiles, mask, next_rows)
    )
    own, other = both_halves(first)
    late = lax.all_gather(late, AXES, axis=0, tiled=True)
    x = decoder_in.reshape(ROWS, D)
    dy = cotangent.reshape(ROWS, D)
    mem = memory.reshape(MICRO * MEM_DEV, D)
    next_rows = passed_along(next_rows, -1).reshape(MICRO * NEXT, D)

    x, second = tied(x, second)
    h1, qkv, gains = self_inputs(core_id, own, other, x)
    o1, lse1 = self_forward(qkv, tiles)
    mem, o1 = tied(mem, o1)
    kv_own = key_value(
        core_id, own, other, mem, MICRO * OWN // BLOCK, lambda i: (i + i // 3 + 1, 0), 6
    )
    second, _, (o1, kv_own, next_rows) = gather_stage(
        second, dims, plane, (o1, kv_own, next_rows)
    )
    own_b, other_b = both_halves(second)
    next_rows, third, own_b = lax.optimization_barrier((next_rows, third, own_b))
    kv_next = key_value(
        core_id, own, other, next_rows, MICRO * NEXT // BLOCK, lambda i: (i, 0), 4
    )
    o1, kv_next = tied(o1, kv_next)
    x1, h2, q2 = cross_inputs(core_id, own_b, other_b, gains, x, o1)
    third, _, q2 = gather_stage(third, core_bits, column, q2)
    o2, lse2 = cross_forward(q2, kv_own, kv_next, mask)
    third, _, o2 = gather_stage(third, dims, plane, o2)
    own_c, other_c = both_halves(third)
    out, h3, hidden, d_gate, d_up, db2, dx2, do2, g_norm_ffn = ffn(
        core_id, late, own_c, other_c, gains, x1, o2, dy
    )
    ffn_total, do2 = ffn_grads(h3, hidden, d_gate, d_up, dy, do2)
    dims = without(device_bits(), core_bits)
    arguments = (q2, kv_own, kv_next, mask, o2, do2, lse2)
    results, arrived = [], []
    for m in range(MICRO):
        dq_m, own_m, next_m = cross_backward(m, *arguments)
        dm_m = memory_grads(core_id, own, other, next_m)
        if m + 1 < MICRO:
            arguments, dm_m = tied(arguments, dm_m)
        results.append((dq_m, own_m, next_m))
        if arrived:
            dm_m, arrived[-1] = tied(dm_m, arrived[-1])
        arrived.append(passed_along(dm_m, 1))
    dq2, dkv_own, dkv_next = zip(*results)
    dkv_own, dkv_next, dm_m = lax.optimization_barrier((dkv_own, dkv_next, dm_m))
    pair_terms = core_stage(*pair_grads(core_id, [(o2, (db2,)), (h2, dq2)], across))
    give, keep = memory_weight_grads(core_id, memory, next_rows, dkv_own, dkv_next, across)
    dq2, give = tied(dq2, give)
    memory_terms = core_stage(give, keep)
    dx1, db1, do1, g_norm_cross = self_grads(core_id, own_b, other_b, gains, x1, dx2, dq2)
    (db1, do1), arrived[-1], pair_terms, memory_terms = lax.optimization_barrier(
        ((db1, do1), arrived[-1], pair_terms, memory_terms)
    )
    out_terms = core_stage(*pair_grads(core_id, [(o1, (db1,))], across))
    cross_parts = scatter_parts([pair_terms, memory_terms, out_terms], dims, plane)
    do1, cross_parts = tied(do1, cross_parts)
    cross_terms = scattered(cross_parts, plane)
    dqkv, sums = self_backward(qkv, tiles, o1, do1, lse1)
    give, keep = row_grads(core_id, h1, dqkv, across, 5)
    (dqkv, cross_terms, ffn_total), give = tied((dqkv, cross_terms, ffn_total), give)
    self_terms = core_stage(give, keep)
    cross_parts = scatter_parts([cross_terms], without(dims, plane), column)
    dqkv, cross_parts = tied(dqkv, cross_parts)
    cross_terms = scattered(cross_parts, column)
    grad_decoder, g_norm_self = input_grads(core_id, own, other, gains, x, dx1, dqkv)
    extra_terms = core_stage(
        *extras(core_id, sums, [g_norm_self, g_norm_cross, g_norm_ffn], across, share)
    )
    self_terms, extra_terms, cross_terms = lax.optimization_barrier(
        (self_terms, extra_terms, cross_terms)
    )
    self_parts = scatter_parts([self_terms, extra_terms], dims, plane)
    dkv_own, self_parts = tied(dkv_own, self_parts)
    self_terms = scattered(self_parts, plane)
    grad_memory = memory_total(core_id, own, other, dkv_own, arrived)
    grad_memory, self_terms = tied(grad_memory, self_terms)
    self_parts = scatter_parts([self_terms], without(dims, plane), column)
    g_self = tree_sum(scattered(self_parts, column))
    g_cross = tree_sum(cross_terms)
    g_gate, g_up, g_down = ffn_columns(ffn_total, share, ffn_gate.shape[1])

    table = g_self[: HEADS * BUCKETS // LANES, 3 * D + LANES :].reshape(HEADS, BUCKETS)

    def cut(stack, index):
        return stack[:, index * D : (index + 1) * D]

    return (
        out.reshape(decoder_in.shape),
        grad_decoder.reshape(decoder_in.shape),
        grad_memory.reshape(memory.shape),
        cut(g_self, 0),
        cut(g_self, 1),
        cut(g_self, 2),
        cut(g_cross, 4),
        cut(g_cross, 1),
        cut(g_cross, 2),
        cut(g_cross, 3),
        cut(g_cross, 0),
        g_gate,
        g_up,
        g_down,
        g_self[:, 3 * D],
        g_self[:, 3 * D + 1],
        g_self[:, 3 * D + 2],
        table,
    )


def solution(mesh):
    in_specs = (
        P(None, ("dp", "seq"), None, None),
        P(None, ("dp", "seq"), None, None),
        P(None, "dp", None),
        P(("dp", "seq"), None),
        P(("dp", "seq"), None),
        P(("dp", "seq"), None),
        P(("dp", "seq"), None),
        P(("dp", "seq"), None),
        P(("dp", "seq"), None),
        P(("dp", "seq"), None),
        P(("dp", "seq"), None),
        P(("dp", "seq"), None),
        P(("dp", "seq"), None),
        P(("dp", "seq"), None),
        P(("dp", "seq")),
        P(("dp", "seq")),
        P(("dp", "seq")),
        P(),
        P(None, ("dp", "seq"), None, None),
    )
    out_specs = (
        P(None, ("dp", "seq"), None, None),
        P(None, ("dp", "seq"), None, None),
        P(None, ("dp", "seq"), None, None),
        P(("dp", "seq"), None),
        P(("dp", "seq"), None),
        P(("dp", "seq"), None),
        P(("dp", "seq"), None),
        P(("dp", "seq"), None),
        P(("dp", "seq"), None),
        P(("dp", "seq"), None),
        P(("dp", "seq"), None),
        P(("dp", "seq"), None),
        P(("dp", "seq"), None),
        P(("dp", "seq"), None),
        P(("dp", "seq")),
        P(("dp", "seq")),
        P(("dp", "seq")),
        P(),
    )
    return jax.shard_map(local, mesh=mesh, in_specs=in_specs, out_specs=out_specs, check_vma=False)
```

time: 803 us -> 503 us (0.63)
  waiting for transfers between devices: 322 us -> 83 us
  Pallas kernels: 134 us -> 302 us
  matrix products: 144 us -> 0 us
  local copies, waits for them, and re-layouts: 68.4 us -> 28.5 us
  other arithmetic: 53.9 us -> 15.5 us
    pallas_call x2 -> x18, Pallas kernels: 53.5 us -> 219 us  [the longest x2 46.5 us: cross_backward(): pl.pallas_call(cross_backward_kernel, grid=(PAIRS,), in_specs=[block(TGT_...]
    dot_general x30 -> x0, matrix products: 144 us -> none  [the longest x8 54.4 us: project(): return jnp.dot(rows, weight, preferred_element_type=F32)]
    all_gather x2 -> x0, waiting for transfers between devices: 107 us -> none  [the longest x1 56.1 us: local(): w_down = lax.all_gather(ffn_down, AXES, axis=0, tiled=True)]
    ppermute x45 -> x40, waiting for transfers between devices: 160 us -> 71.1 us  [exchange(): return lax.ppermute(block, AXES, [(i, i ^ mask) for i in range(count)])]
    all_gather x1, waiting for transfers between devices: 54.8 us -> 0.01 us  [local(): late = lax.all_gather(late, AXES, axis=0, tiled=True)]
    concatenate x6 -> x1, local copies, waits for them, and re-layouts: 18.2 us -> 0.01 us  [local(): jnp.concatenate([cross_key, cross_value, self_query, self_key, self_value...]
    convert_element_type x37 -> x7, other arithmetic: 20.5 us -> 4.24 us  [part(): tree_sum([picked(term, dims, group, flip) for term in terms]).astype(BF)]
    reduce_sum x13 -> x0, other arithmetic: 15 us -> none  [the longest x10 11.1 us: table_grad(): jnp.sum(sums[:, 0, starts[b]:starts[b + 1]], axis=1)]
  transfers between devices with their start and end apart: 50 -> 45, of which waited for: 26 -> 15; matrix products, arithmetic and copies ran while one was open for 18% -> 6% of each run, Pallas kernels for 3% -> 49%
where the time goes in v2:
time: 503 us; the launch traced here: 497 us
  Pallas kernels  302 us (60%)
  waiting for transfers between devices  83 us (17%)
  starting transfers between devices  52.4 us (10%)
  local copies, waits for them, and re-layouts  28.5 us (6%)
  other arithmetic  15.5 us (3%)
  between operations  15.4 us (3%)
    ppermute x40, waiting for transfers between devices, exchange(): return lax.ppermute(block, AXES, [(i, i ^ mask) for i in range(count)])  71.1 us
    pallas_call x2, Pallas kernels, cross_backward(): pl.pallas_call(cross_backward_kernel, grid=(PAIRS,), in_specs=[block(TGT_...  46.5 us
    ppermute x40, starting transfers between devices, exchange(): return lax.ppermute(block, AXES, [(i, i ^ mask) for i in range(count)])  43.9 us
    pallas_call x1, Pallas kernels, ffn(): pl.pallas_call(ffn_kernel, grid=(ROWS // BLOCK,), in_specs=[SMEM, ANY, AN...  39.4 us
    pallas_call x1, Pallas kernels, cross_forward(): pl.pallas_call(cross_forward_kernel, grid=PAIR_GRID, in_specs=[pair_block...  31.6 us
    pallas_call x1, Pallas kernels, self_backward(): pl.pallas_call(self_backward_kernel, grid=(PAIRS, MICRO), in_specs=[swapp...  25.8 us
    pallas_call x1, Pallas kernels, ffn_weight_grads(): pl.pallas_call(ffn_weight_grads_kernel, grid=(3,), in_specs=[fixed_block(...  18.1 us
    pallas_call x1, Pallas kernels, self_forward(): pl.pallas_call(self_forward_kernel, grid=(PAIRS, MICRO), in_specs=[swappe...  17.5 us
  transfers between devices with their start and end apart: 45, of which 15 were waited for; matrix products, arithmetic and copies ran while one was open for 6% of the time, Pallas kernels for 49%

profile of v2, /device:TPU:0, one launch (start us, length us, event | category | flops | bytes accessed | tf_op | source)
XLA Modules:
  0.0 496.7 jit_solution(7328801630115481111)
XLA Ops:
  14.6 4.7 collective-permute-start.3
  20.0 5.2 %collective-permute-done.3 = bf16[2,24,2048]{2,1,0:T(8,128)(2,1)S(1)} collective-permute-done((bf16[2,24,2048]{2,1,0:T(8,128)(2,1)S(1)}, bf16[2,24,2048]{2,1,0:T(8,128)(2,1)S(1)}, u32[]{:S(2)}, u32[]{:S(2)}) %collective-permute-start.3) | collective-permute-done | bytes 196640 | tf_op jit(solution)/shard_map/ppermute | solution.py:1071
  25.1 6.0 %collective-permute-done.2 = bf16[2,24,2048]{2,1,0:T(8,128)(2,1)S(1)} collective-permute-done((bf16[2,24,2048]{2,1,0:T(8,128)(2,1)S(1)}, bf16[2,24,2048]{2,1,0:T(8,128)(2,1)S(1)}, u32[]{:S(2)}, u32[]{:S(2)}) %collective-permute-start.2) | collective-permute-done | bytes 196640 | tf_op jit(solution)/shard_map/ppermute | solution.py:1071
  31.2 10.0 %collective-permute-done.1 = bf16[2,24,2048]{2,1,0:T(8,128)(2,1)S(1)} collective-permute-done((bf16[2,24,2048]{2,1,0:T(8,128)(2,1)S(1)}, bf16[2,24,2048]{2,1,0:T(8,128)(2,1)S(1)}, u32[]{:S(2)}, u32[]{:S(2)}) %collective-permute-start.1) | collective-permute-done | bytes 196640 | tf_op jit(solution)/shard_map/ppermute | solution.py:1071
  44.9 2.6 collective-permute-start.6
  57.6 7.9 %bias_tiles.1.tiles_ref = f32[12,2,256,256]{3,2,1,0:T(8,128)} custom-call(f32[12,32]{1,0:T(8,128)} %convert_element_type.509.table_ref), custom_call_target="tpu_custom_call" | custom-call | flops 8 | tf_op jit(solution)/shard_map/bias_tiles/pallas_call | solution.py:709
  65.6 3.5 collective-permute-start.9
  69.1 9.8 %collective-permute-done.9 = bf16[2,2,24,768]{3,2,1,0:T(8,128)(2,1)S(1)} collective-permute-done((bf16[2,2,24,768]{3,2,1,0:T(8,128)(2,1)S(1)}, bf16[2,2,24,768]{3,2,1,0:T(8,128)(2,1)S(1)}, u32[]{:S(2)}, u32[]{:S(2)}) %collective-permute-start.9) | collective-permute-done | bytes 147488 | tf_op jit(solution)/shard_map/ppermute | solution.py:1071
  78.9 6.5 %collective-permute-done.5 = bf16[2,2,2,24,2048]{4,3,2,1,0:T(8,128)(2,1)} collective-permute-done((bf16[2,2,2,24,2048]{4,3,2,1,0:T(8,128)(2,1)}, bf16[2,2,2,24,2048]{4,3,2,1,0:T(8,128)(2,1)}, u32[]{:S(2)}, u32[]{:S(2)}) %collective-permute-start.5) | collective-permute-done | bytes 786464 | tf_op jit(solution)/shard_map/ppermute | solution.py:1071
  85.4 5.1 %collective-permute-done.4 = bf16[2,2,2,24,2048]{4,3,2,1,0:T(8,128)(2,1)} collective-permute-done((bf16[2,2,2,24,2048]{4,3,2,1,0:T(8,128)(2,1)}, bf16[2,2,2,24,2048]{4,3,2,1,0:T(8,128)(2,1)}, u32[]{:S(2)}, u32[]{:S(2)}) %collective-permute-start.4) | collective-permute-done | bytes 786464 | tf_op jit(solution)/shard_map/ppermute | solution.py:1071
  95.8 1.6 collective-permute-start.15
  97.4 4.5 collective-permute-start.13
  102.5 1.7 copy-done.1
  104.2 9.0 %self_inputs.1 = (bf16[1024,768]{1,0:T(8,128)(2,1)}, bf16[1024,2304]{1,0:T(8,128)(2,1)}, f32[8,768]{1,0:T(8,128)}) custom-call(s32[1]{0:T(128)} %bitcast.core_ref, bf16[768,2048]{1,0:T(8,128)(2,1)} %bitcast.258, bf16[768,2048]{1,0:T(8,128)(2,1)} %copy-done.1, bf16[1024,768]{1,0:T(8,128)(2,1)} %bitcast.266), custom_call_target="tpu_custom_call" | custom-call | flops 6 | tf_op jit(solution)/shard_map/self_inputs/pallas_call | solution.py:206
  113.3 17.5 %self_forward.1 = (bf16[1024,768]{1,0:T(8,128)(2,1)}, f32[12,8,512]{2,1,0:T(8,128)}) custom-call(bf16[1024,2304]{1,0:T(8,128)(2,1)} %get-tuple-element.193.q_ref.k_ref.v_ref, bf16[1024,2304]{1,0:T(8,128)(2,1)} %get-tuple-element.193.q_ref.k_ref.v_ref, bf16[1024,2304]{1,0:T(8,128)(2,1)} %get-tuple-element.193.q_ref.k_ref.v_ref, ...), custom_call_target="tpu_custom_call" | custom-call | flops 17 | tf_op jit(solution)/shard_map/self_forward/pallas_call | solution.py:977
  130.7 9.4 %key_value.2.ko_ref.vo_ref = bf16[1536,1536]{1,0:T(8,128)(2,1)} custom-call(s32[1]{0:T(128)} %bitcast.core_ref, bf16[768,2048]{1,0:T(8,128)(2,1)} %bitcast.259, bf16[768,2048]{1,0:T(8,128)(2,1)} %copy-done.1, bf16[2048,768]{1,0:T(8,128)(2,1)} %bitcast.265), custom_call_target="tpu_custom_call" | custom-call | flops 6 | tf_op jit(solution)/shard_map/key_value/pallas_call | solution.py:176
  140.2 7.3 %collective-permute-done.12 = bf16[2,2,2,24,768]{4,3,2,1,0:T(8,128)(2,1)S(1)} collective-permute-done((bf16[2,2,2,24,768]{4,3,2,1,0:T(8,128)(2,1)S(1)}, bf16[2,2,2,24,768]{4,3,2,1,0:T(8,128)(2,1)S(1)}, u32[]{:S(2)}, u32[]{:S(2)}) %collective-permute-start.12) | collective-permute-done | bytes 294944 | tf_op jit(solution)/shard_map/ppermute | solution.py:1071
  148.8 3.4 collective-permute-start.18
  153.3 7.3 %key_value.3.kn_ref.vn_ref = bf16[1024,1536]{1,0:T(8,128)(2,1)} custom-call(s32[1]{0:T(128)} %bitcast.core_ref, bf16[768,2048]{1,0:T(8,128)(2,1)} %bitcast.260, bf16[768,2048]{1,0:T(8,128)(2,1)} %copy-done.1, bf16[1024,768]{1,0:T(8,128)(2,1)} %bitcast.38.rows_ref.next_ref), custom_call_target="tpu_custom_call" | custom-call | flops 4 | tf_op jit(solution)/shard_map/key_value/pallas_call | solution.py:176
  161.6 8.4 %cross_inputs.1 = (f32[1024,768]{1,0:T(8,128)}, bf16[1024,768]{1,0:T(8,128)(2,1)}, bf16[1024,768]{1,0:T(8,128)(2,1)}) custom-call(s32[1]{0:T(128)} %bitcast.core_ref, bf16[768,768]{1,0:T(8,128)(2,1)} %bitcast.270, bf16[768,768]{1,0:T(8,128)(2,1)} %copy-done.5, f32[8,768]{1,0:T(8,128)} %get-tuple-element.207.gain_ref, bf16[1024,768]{1,0:T(8,128)(2,1)} %bitcast.267, ...), custom_call_target="tpu_custom_call" | custom-call | flops 5 | tf_op jit(solution)/shard_map/cross_inputs/pallas_call | solution.py:234
  170.2 2.7 collective-permute-start.22
  173.9 31.6 %cross_forward.1 = (bf16[1024,768]{1,0:T(8,128)(2,1)}, f32[12,8,512]{2,1,0:T(8,128)}) custom-call(bf16[1024,768]{1,0:T(8,128)(2,1)} %get-tuple-element.238.q_ref, bf16[1536,1536]{1,0:T(8,128)(2,1)} %key_value.2.ko_ref.vo_ref, bf16[1024,1536]{1,0:T(8,128)(2,1)} %key_value.3.kn_ref.vn_ref, bf16[1536,1536]{1,0:T(8,128)(2,1)} %key_value.2.ko_ref.vo_ref, ...), custom_call_target="tpu_custom_call" | custom-call | flops 32 | tf_op jit(solution)/shard_map/cross_forward/pallas_call | solution.py:913
  206.2 3.4 collective-permute-done.23.other_ref
  210.8 39.4 %ffn.1 = (bf16[1024,768]{1,0:T(8,128)(2,1)}, bf16[1024,768]{1,0:T(8,128)(2,1)}, bf16[1024,2048]{1,0:T(8,128)(2,1)}, bf16[1024,2048]{1,0:T(8,128)(2,1)}, bf16[102...) custom-call(s32[1]{0:T(128)} %bitcast.core_ref, ...), custom_call_target="tpu_custom_call" | custom-call | flops 30 | tf_op jit(solution)/shard_map/ffn/pallas_call | solution.py:301
  250.1 18.1 %ffn_weight_grads.1 = bf16[32,576,256]{2,1,0:T(8,128)(2,1)} custom-call(bf16[1024,768]{1,0:T(8,128)(2,1)} %get-tuple-element.230.h_ref, bf16[1024,2048]{1,0:T(8,128)(2,1)} %get-tuple-element.231.hidden_ref, bf16[1024,2048]{1,0:T(8,128)(2,1)} %get-tuple-element.232.dgate_ref, bf16[1024,2048]{1,0:T(8,128)(2,1)} %get-tuple-element.233.dup_ref, ...), custom_call_target="tpu_custom_call" | custom-call | flops 13 | tf_op jit(solution)/shard_map/ffn_weight_grads/pallas_call | solution.py:537
  268.2 23.1 %cross_backward.2 = (bf16[512,768]{1,0:T(8,128)(2,1)}, bf16[2,768,768]{2,1,0:T(8,128)(2,1)}, bf16[2,512,768]{2,1,0:T(8,128)(2,1)}) custom-call(bf16[1024,768]{1,0:T(8,128)(2,1)} %get-tuple-element.238.q_ref, bf16[1536,1536]{1,0:T(8,128)(2,1)} %key_value.2.ko_ref.vo_ref, bf16[1024,1536]{1,0:T(8,128)(2,1)} %key_value.3.kn_ref.vn_ref, ...), custom_call_target="tpu_custom_call" | custom-call | flops 22 | tf_op jit(solution)/shard_map/cross_backward/pallas_call | solution.py:937
  291.3 5.4 %memory_grads.2 = bf16[512,768]{1,0:T(8,128)(2,1)} custom-call(s32[1]{0:T(128)} %bitcast.core_ref, bf16[768,2048]{1,0:T(8,128)(2,1)} %bitcast.261, bf16[768,2048]{1,0:T(8,128)(2,1)} %copy-done.1, bf16[2,512,768]{2,1,0:T(8,128)(2,1)} %get-tuple-element.253.dkv_ref.after0_ref), custom_call_target="tpu_custom_call" | custom-call | flops 1 | tf_op jit(solution)/shard_map/memory_grads/pallas_call | solution.py:416
  296.7 3.0 collective-permute-start.24
  299.8 23.4 %cross_backward.3 = (bf16[512,768]{1,0:T(8,128)(2,1)}, bf16[2,768,768]{2,1,0:T(8,128)(2,1)}, bf16[2,512,768]{2,1,0:T(8,128)(2,1)}) custom-call(bf16[1024,768]{1,0:T(8,128)(2,1)} %get-tuple-element.238.q_ref, bf16[1536,1536]{1,0:T(8,128)(2,1)} %key_value.2.ko_ref.vo_ref, bf16[1024,1536]{1,0:T(8,128)(2,1)} %key_value.3.kn_ref.vn_ref, ...), custom_call_target="tpu_custom_call" | custom-call | flops 22 | tf_op jit(solution)/shard_map/cross_backward/pallas_call | solution.py:937
  323.2 8.1 %pair_grads.2 = (bf16[2,192,1536]{2,1,0:T(8,128)(2,1)}, bf16[2,192,1536]{2,1,0:T(8,128)(2,1)}) custom-call(s32[1]{0:T(128)} %bitcast.core_ref, bf16[1024,768]{1,0:T(8,128)(2,1)} %get-tuple-element.242.o_ref.refs_0_, bf16[1024,768]{1,0:T(8,128)(2,1)} %get-tuple-element.261.refs_1_, bf16[1024,768]{1,0:T(8,128)(2,1)} %get-tuple-element.262.refs_2_, ...), custom_call_target="tpu_custom_call" | custom-call | flops 5 | tf_op jit(solution)/shard_map/pair_grads/pallas_call | solution.py:488
  331.2 5.3 %memory_grads.3 = bf16[512,768]{1,0:T(8,128)(2,1)} custom-call(s32[1]{0:T(128)} %bitcast.core_ref, bf16[768,2048]{1,0:T(8,128)(2,1)} %bitcast.262, bf16[768,2048]{1,0:T(8,128)(2,1)} %copy-done.1, bf16[2,512,768]{2,1,0:T(8,128)(2,1)} %get-tuple-element.254.dkv_ref.after1_ref), custom_call_target="tpu_custom_call" | custom-call | flops 1 | tf_op jit(solution)/shard_map/memory_grads/pallas_call | solution.py:416
  336.6 13.6 %memory_weight_grads.1 = (bf16[2,192,1536]{2,1,0:T(8,128)(2,1)}, bf16[2,192,1536]{2,1,0:T(8,128)(2,1)}) custom-call(s32[1]{0:T(128)} %bitcast.core_ref, bf16[2,1,1024,768]{3,2,1,0:T(8,128)(2,1)} %mem_ref, bf16[1024,768]{1,0:T(8,128)(2,1)} %bitcast.38.rows_ref.next_ref, bf16[2,768,768]{2,1,0:T(8,128)(2,1)} %get-tuple-element.308.own0_ref.dkv0_ref, ...), custom_call_target="tpu_custom_call" | custom-call | flops 8 | tf_op jit(solution)/shard_map/memory_weight_grads/pallas_call | solution.py:577
  350.8 3.9 collective-permute-start.25
  354.7 10.9 %self_grads.1 = (f32[1024,768]{1,0:T(8,128)}, bf16[1024,768]{1,0:T(8,128)(2,1)}, bf16[1024,768]{1,0:T(8,128)(2,1)}, f32[8,768]{1,0:T(8,128)}) custom-call(s32[1]{0:T(128)} %bitcast.core_ref, bf16[768,768]{1,0:T(8,128)(2,1)} %bitcast.271, bf16[768,768]{1,0:T(8,128)(2,1)} %copy-done.5, f32[8,768]{1,0:T(8,128)} %get-tuple-element.207.gain_ref, ...), custom_call_target="tpu_custom_call" | custom-call | flops 5 | tf_op jit(solution)/shard_map/self_grads/pallas_call | solution.py:356
  365.6 11.9 %collective-permute-done.25.prev1_ref = bf16[512,768]{1,0:T(8,128)(2,1)} collective-permute-done((bf16[512,768]{1,0:T(8,128)(2,1)S(1)}, bf16[512,768]{1,0:T(8,128)(2,1)}, u32[]{:S(2)}, u32[]{:S(2)}) %collective-permute-start.25) | collective-permute-done | bytes 786464 | tf_op jit(solution)/shard_map/ppermute | solution.py:1158
  377.5 4.6 pair_grads.3
  387.0 2.6 collective-permute-start.30
  389.8 25.8 %self_backward.1 = (bf16[3,1024,768]{2,1,0:T(8,128)(2,1)}, f32[12,8,256]{2,1,0:T(8,128)}) custom-call(bf16[1024,2304]{1,0:T(8,128)(2,1)} %get-tuple-element.193.q_ref.k_ref.v_ref, bf16[1024,2304]{1,0:T(8,128)(2,1)} %get-tuple-element.193.q_ref.k_ref.v_ref, bf16[1024,2304]{1,0:T(8,128)(2,1)} %get-tuple-element.193.q_ref.k_ref.v_ref, ...), custom_call_target="tpu_custom_call" | custom-call | flops 24 | tf_op jit(solution)/shard_map/self_backward/pallas_call | solution.py:996
  415.6 8.3 %row_grads.1 = (bf16[2,192,2304]{2,1,0:T(8,128)(2,1)}, bf16[2,192,2304]{2,1,0:T(8,128)(2,1)}) custom-call(s32[1]{0:T(128)} %bitcast.core_ref, bf16[1024,768]{1,0:T(8,128)(2,1)} %get-tuple-element.283.rows_ref, bf16[3,1024,768]{2,1,0:T(8,128)(2,1)} %get-tuple-element.290.grads_ref.dqkv_ref), custom_call_target="tpu_custom_call" | custom-call | flops 5 | tf_op jit(solution)/shard_map/row_grads/pallas_call | solution.py:455
  425.0 2.6 fusion.16
  427.6 3.5 collective-permute-start.34
  432.6 10.8 %input_grads.1 = (bf16[1024,768]{1,0:T(8,128)(2,1)}, f32[8,768]{1,0:T(8,128)}) custom-call(s32[1]{0:T(128)} %bitcast.core_ref, bf16[768,2048]{1,0:T(8,128)(2,1)} %bitcast.263, bf16[768,2048]{1,0:T(8,128)(2,1)} %copy-done.1, f32[8,768]{1,0:T(8,128)} %get-tuple-element.207.gain_ref, bf16[1024,768]{1,0:T(8,128)(2,1)} %bitcast.268, ...), custom_call_target="tpu_custom_call" | custom-call | flops 6 | tf_op jit(solution)/shard_map/input_grads/pallas_call | solution.py:393
  443.3 2.6 extras.1
  450.6 1.9 collective-permute-start.38
  453.0 11.6 %memory_total.1 = bf16[2048,768]{1,0:T(8,128)(2,1)} custom-call(s32[1]{0:T(128)} %bitcast.core_ref, bf16[768,2048]{1,0:T(8,128)(2,1)} %bitcast.264, bf16[768,2048]{1,0:T(8,128)(2,1)} %copy-done.1, bf16[2,768,768]{2,1,0:T(8,128)(2,1)} %get-tuple-element.308.own0_ref.dkv0_ref, bf16[2,768,768]{2,1,0:T(8,128)(2,1)} %get-tuple-element.309.own1_ref.dkv1_ref, ...), custom_call_target="tpu_custom_call" | custom-call | flops 7 | tf_op jit(solution)/shard_map/memory_total/pallas_call | solution.py:625
  465.7 8.2 %collective-permute-done.38 = bf16[2,2,24,2560]{3,2,1,0:T(8,128)(2,1)S(1)} collective-permute-done((bf16[2,2,24,2560]{3,2,1,0:T(8,128)(2,1)S(1)}, bf16[2,2,24,2560]{3,2,1,0:T(8,128)(2,1)S(1)}, u32[]{:S(2)}, u32[]{:S(2)}) %collective-permute-start.38) | collective-permute-done | bytes 491552 | tf_op jit(solution)/shard_map/ppermute | solution.py:1071
  475.0 2.1 collective-permute-start.40
  479.3 6.9 %collective-permute-done.40 = bf16[24,2560]{1,0:T(8,128)(2,1)S(1)} collective-permute-done((bf16[24,2560]{1,0:T(8,128)(2,1)S(1)}, bf16[24,2560]{1,0:T(8,128)(2,1)S(1)}, u32[]{:S(2)}, u32[]{:S(2)}) %collective-permute-start.40) | collective-permute-done | bytes 122912 | tf_op jit(solution)/shard_map/ppermute | solution.py:1071
  (209 shorter events, 55.1 us)
Async XLA Ops:
  7.2 202.4 %all-gather.2.cloned.1.call-start = ((), (), s32[]{:S(2)}) async-start(), calls=%async_computation.1 | async-start | bytes 7704576 | tf_op jit(solution)/shard_map/all_gather | solution.py:1250
  12.6 1.9 collective-permute-start
  13.9 410.2 %reduce-scatter.2.cloned.1.call-start = ((), (), s32[]{:S(2)}) async-start(), calls=%async_computation.2 | async-start | bytes 9732096 | tf_op jit(solution)/shard_map/reduce_scatter | solution.py:1179
  14.6 33.9 %copy-start.23 = (bf16[12,32]{1,0:T(8,128)(2,1)S(1)}, bf16[12,32]{1,0:T(8,128)(2,1)}, u32[]{:S(2)}) copy-start(bf16[12,32]{1,0:T(8,128)(2,1)} %param.36) | copy-start | bytes 2308
  14.6 34.7 %copy-start.19 = (bf16[64,768]{1,0:T(8,128)(2,1)S(1)}, bf16[64,768]{1,0:T(8,128)(2,1)}, u32[]{:S(2)}) copy-start(bf16[64,768]{1,0:T(8,128)(2,1)} %param.32) | copy-start | bytes 294916
  14.6 10.5 %collective-permute-start.3 = (bf16[2,24,2048]{2,1,0:T(8,128)(2,1)S(1)}, bf16[2,24,2048]{2,1,0:T(8,128)(2,1)S(1)}, u32[]{:S(2)}, u32[]{:S(2)}) collective-permute-start(bf16[2,24,2048]{2,1,0:T(8,128)(2,1)S(1)} %pad_maximum_fusion.10), channel_id=1, source_target_pairs={{0,6},{1,7},{2,4},{3,5},{4,2},{5,3},{6,0},{7,1},{8,14},{9,15},{10,... | collective-permute-start | bytes 589832 | tf_op jit(solution)/shard_map/ppermute | solution.py:1071
  19.3 11.9 %collective-permute-start.2 = (bf16[2,24,2048]{2,1,0:T(8,128)(2,1)S(1)}, bf16[2,24,2048]{2,1,0:T(8,128)(2,1)S(1)}, u32[]{:S(2)}, u32[]{:S(2)}) collective-permute-start(bf16[2,24,2048]{2,1,0:T(8,128)(2,1)S(1)} %pad_maximum_fusion.10), channel_id=1, source_target_pairs={{0,2},{1,3},{2,0},{3,1},{4,6},{5,7},{6,4},{7,5},{8,10},{9,11},{10,... | collective-permute-start | bytes 589832 | tf_op jit(solution)/shard_map/ppermute | solution.py:1071
  19.3 21.9 %collective-permute-start.1 = (bf16[2,24,2048]{2,1,0:T(8,128)(2,1)S(1)}, bf16[2,24,2048]{2,1,0:T(8,128)(2,1)S(1)}, u32[]{:S(2)}, u32[]{:S(2)}) collective-permute-start(bf16[2,24,2048]{2,1,0:T(8,128)(2,1)S(1)} %pad_maximum_fusion.10), channel_id=1, source_target_pairs={{0,4},{1,5},{2,6},{3,7},{4,0},{5,1},{6,2},{7,3},{8,12},{9,13},{10,... | collective-permute-start | bytes 589832 | tf_op jit(solution)/shard_map/ppermute | solution.py:1071
  44.9 34.0 %collective-permute-start.6 = (bf16[2,2,2,24,2048]{4,3,2,1,0:T(8,128)(2,1)}, bf16[2,2,2,24,2048]{4,3,2,1,0:T(8,128)(2,1)}, u32[]{:S(2)}, u32[]{:S(2)}) collective-permute-start(bf16[2,2,2,24,2048]{4,3,2,1,0:T(8,128)(2,1)} %bitcast_dynamic-update-slice_fusion.12), channel_id=1, source_target_pairs={{0,17},{1,16},{2,19},{3,18},{4,21},{5,20},{6,23},{7,22},{8,25},{9,... | collective-permute-start | bytes 2359304 | tf_op jit(solution)/shard_map/ppermute | solution.py:1071
  47.5 37.9 %collective-permute-start.5 = (bf16[2,2,2,24,2048]{4,3,2,1,0:T(8,128)(2,1)}, bf16[2,2,2,24,2048]{4,3,2,1,0:T(8,128)(2,1)}, u32[]{:S(2)}, u32[]{:S(2)}) collective-permute-start(bf16[2,2,2,24,2048]{4,3,2,1,0:T(8,128)(2,1)} %bitcast_dynamic-update-slice_fusion.12), channel_id=1, source_target_pairs={{0,1},{1,0},{2,3},{3,2},{4,5},{5,4},{6,7},{7,6},{8,9},{9,8},{10,11... | collective-permute-start | bytes 2359304 | tf_op jit(solution)/shard_map/ppermute | solution.py:1071
  47.9 42.6 %collective-permute-start.4 = (bf16[2,2,2,24,2048]{4,3,2,1,0:T(8,128)(2,1)}, bf16[2,2,2,24,2048]{4,3,2,1,0:T(8,128)(2,1)}, u32[]{:S(2)}, u32[]{:S(2)}) collective-permute-start(bf16[2,2,2,24,2048]{4,3,2,1,0:T(8,128)(2,1)} %bitcast_dynamic-update-slice_fusion.12), channel_id=1, source_target_pairs={{0,16},{1,17},{2,18},{3,19},{4,20},{5,21},{6,22},{7,23},{8,24},{9,... | collective-permute-start | bytes 2359304 | tf_op jit(solution)/shard_map/ppermute | solution.py:1071
  49.2 6.5 %collective-permute-start.7 = (bf16[24,768]{1,0:T(8,128)(2,1)S(1)}, bf16[24,768]{1,0:T(8,128)(2,1)}, u32[]{:S(2)}, u32[]{:S(2)}) collective-permute-start(bf16[24,768]{1,0:T(8,128)(2,1)S(1)} %bitcast.296), channel_id=1, source_target_pairs={{0,8},{1,9},{2,10},{3,11},{4,12},{5,13},{6,14},{7,15},{8,0},{9,1},... | collective-permute-start | bytes 110600 | tf_op jit(solution)/shard_map/ppermute | solution.py:1071
  49.6 19.5 %collective-permute-start.10 = (bf16[64,384]{1,0:T(8,128)(2,1)S(1)}, bf16[64,384]{1,0:T(8,128)(2,1)S(1)}, u32[]{:S(2)}, u32[]{:S(2)}) collective-permute-start(bf16[64,384]{1,0:T(8,128)(2,1)S(1)} %bitcast.295), channel_id=1, source_target_pairs={{0,8},{1,9},{2,10},{3,11},{4,12},{5,13},{6,14},{7,15},{8,0},{9,1},... | collective-permute-start | bytes 147464 | tf_op jit(solution)/shard_map/ppermute | solution.py:1071
  56.6 8.9 %collective-permute-start.8 = (bf16[2,24,768]{2,1,0:T(8,128)(2,1)S(1)}, bf16[2,24,768]{2,1,0:T(8,128)(2,1)S(1)}, u32[]{:S(2)}, u32[]{:S(2)}) collective-permute-start(bf16[2,24,768]{2,1,0:T(8,128)(2,1)S(1)} %pad_maximum_fusion.13), channel_id=1, source_target_pairs={{0,2},{1,3},{2,0},{3,1},{4,6},{5,7},{6,4},{7,5},{8,10},{9,11},{10,... | collective-permute-start | bytes 221192 | tf_op jit(solution)/shard_map/ppermute | solution.py:1071
  65.6 13.3 %collective-permute-start.9 = (bf16[2,2,24,768]{3,2,1,0:T(8,128)(2,1)S(1)}, bf16[2,2,24,768]{3,2,1,0:T(8,128)(2,1)S(1)}, u32[]{:S(2)}, u32[]{:S(2)}) collective-permute-start(bf16[2,2,24,768]{3,2,1,0:T(8,128)(2,1)S(1)} %bitcast_dynamic-update-slice_fusion.22), channel_id=1, source_target_pairs={{0,4},{1,5},{2,6},{3,7},{4,0},{5,1},{6,2},{7,3},{8,12},{9,13},{10,... | collective-permute-start | bytes 442376 | tf_op jit(solution)/shard_map/ppermute | solution.py:1071
  95.8 6.8 %collective-permute-start.14 = (bf16[768,2048]{1,0:T(8,128)(2,1)S(1)}, bf16[768,2048]{1,0:T(8,128)(2,1)S(1)}, u32[]{:S(2)}, u32[]{:S(2)}) collective-permute-start(bf16[768,2048]{1,0:T(8,128)(2,1)S(1)} %bitcast.257), channel_id=1, source_target_pairs={{0,8},{1,9},{2,10},{3,11},{4,12},{5,13},{6,14},{7,15},{8,0},{9,1},... | collective-permute-start | bytes 9437192 | tf_op jit(solution)/shard_map/ppermute | solution.py:1071
  95.8 51.7 %collective-permute-start.15 = (bf16[2,512,768]{2,1,0:T(8,128)(2,1)}, bf16[2,512,768]{2,1,0:T(8,128)(2,1)}, u32[]{:S(2)}, u32[]{:S(2)}) collective-permute-start(bf16[2,512,768]{2,1,0:T(8,128)(2,1)} %slice_bitcast_fusion), channel_id=1, source_target_pairs={{1,0},{2,1},{3,2},{4,3},{5,4},{6,5},{7,6},{9,8},{10,9},{11,10},{12... | collective-permute-start | bytes 4718600 | tf_op jit(solution)/shard_map/ppermute | solution.py:1158
  97.4 42.8 %collective-permute-start.13 = (bf16[2,2,2,24,768]{4,3,2,1,0:T(8,128)(2,1)S(1)}, bf16[2,2,2,24,768]{4,3,2,1,0:T(8,128)(2,1)S(1)}, u32[]{:S(2)}, u32[]{:S(2)}) collective-permute-start(bf16[2,2,2,24,768]{4,3,2,1,0:T(8,128)(2,1)S(1)} %bitcast_dynamic-update-slice_fusion.17), channel_id=1, source_target_pairs={{0,17},{1,16},{2,19},{3,18},{4,21},{5,20},{6,23},{7,22},{8,25},{9,... | collective-permute-start | bytes 884744 | tf_op jit(solution)/shard_map/ppermute | solution.py:1071
  101.9 45.6 %collective-permute-start.12 = (bf16[2,2,2,24,768]{4,3,2,1,0:T(8,128)(2,1)S(1)}, bf16[2,2,2,24,768]{4,3,2,1,0:T(8,128)(2,1)S(1)}, u32[]{:S(2)}, u32[]{:S(2)}) collective-permute-start(bf16[2,2,2,24,768]{4,3,2,1,0:T(8,128)(2,1)S(1)} %bitcast_dynamic-update-slice_fusion.17), channel_id=1, source_target_pairs={{0,1},{1,0},{2,3},{3,2},{4,5},{5,4},{6,7},{7,6},{8,9},{9,8},{10,11... | collective-permute-start | bytes 884744 | tf_op jit(solution)/shard_map/ppermute | solution.py:1071
  101.9 45.6 %collective-permute-start.11 = (bf16[2,2,2,24,768]{4,3,2,1,0:T(8,128)(2,1)S(1)}, bf16[2,2,2,24,768]{4,3,2,1,0:T(8,128)(2,1)}, u32[]{:S(2)}, u32[]{:S(2)}) collective-permute-start(bf16[2,2,2,24,768]{4,3,2,1,0:T(8,128)(2,1)S(1)} %bitcast_dynamic-update-slice_fusion.17), channel_id=1, source_target_pairs={{0,16},{1,17},{2,18},{3,19},{4,20},{5,21},{6,22},{7,23},{8,24},{9,... | collective-permute-start | bytes 884744 | tf_op jit(solution)/shard_map/ppermute | solution.py:1071
  148.7 11.9 %collective-permute-start.19 = (bf16[768,768]{1,0:T(8,128)(2,1)S(1)}, bf16[768,768]{1,0:T(8,128)(2,1)S(1)}, u32[]{:S(2)}, u32[]{:S(2)}) collective-permute-start(bf16[768,768]{1,0:T(8,128)(2,1)S(1)} %bitcast.269), channel_id=1, source_target_pairs={{0,8},{1,9},{2,10},{3,11},{4,12},{5,13},{6,14},{7,15},{8,0},{9,1},... | collective-permute-start | bytes 3538952 | tf_op jit(solution)/shard_map/ppermute | solution.py:1071
  148.8 21.2 %collective-permute-start.18 = (bf16[2,64,384]{2,1,0:T(8,128)(2,1)S(1)}, bf16[2,64,384]{2,1,0:T(8,128)(2,1)S(1)}, u32[]{:S(2)}, u32[]{:S(2)}) collective-permute-start(bf16[2,64,384]{2,1,0:T(8,128)(2,1)S(1)} %pad_maximum_fusion.11), channel_id=1, source_target_pairs={{0,6},{1,7},{2,4},{3,5},{4,2},{5,3},{6,0},{7,1},{8,14},{9,15},{10,... | collective-permute-start | bytes 294920 | tf_op jit(solution)/shard_map/ppermute | solution.py:1071
  152.2 17.8 %collective-permute-start.17 = (bf16[2,64,384]{2,1,0:T(8,128)(2,1)S(1)}, bf16[2,64,384]{2,1,0:T(8,128)(2,1)S(1)}, u32[]{:S(2)}, u32[]{:S(2)}) collective-permute-start(bf16[2,64,384]{2,1,0:T(8,128)(2,1)S(1)} %pad_maximum_fusion.11), channel_id=1, source_target_pairs={{0,2},{1,3},{2,0},{3,1},{4,6},{5,7},{6,4},{7,5},{8,10},{9,11},{10,... | collective-permute-start | bytes 294920 | tf_op jit(solution)/shard_map/ppermute | solution.py:1071
  152.2 17.8 %collective-permute-start.16 = (bf16[2,64,384]{2,1,0:T(8,128)(2,1)S(1)}, bf16[2,64,384]{2,1,0:T(8,128)(2,1)S(1)}, u32[]{:S(2)}, u32[]{:S(2)}) collective-permute-start(bf16[2,64,384]{2,1,0:T(8,128)(2,1)S(1)} %pad_maximum_fusion.11), channel_id=1, source_target_pairs={{0,4},{1,5},{2,6},{3,7},{4,0},{5,1},{6,2},{7,3},{8,12},{9,13},{10,... | collective-permute-start | bytes 294920 | tf_op jit(solution)/shard_map/ppermute | solution.py:1071
  170.2 35.4 %collective-permute-start.22 = (bf16[2,2,2,64,384]{4,3,2,1,0:T(8,128)(2,1)S(1)}, bf16[2,2,2,64,384]{4,3,2,1,0:T(8,128)(2,1)S(1)}, u32[]{:S(2)}, u32[]{:S(2)}) collective-permute-start(bf16[2,2,2,64,384]{4,3,2,1,0:T(8,128)(2,1)S(1)} %bitcast_dynamic-update-slice_fusion.18), channel_id=1, source_target_pairs={{0,17},{1,16},{2,19},{3,18},{4,21},{5,20},{6,23},{7,22},{8,25},{9,... | collective-permute-start | bytes 1179656 | tf_op jit(solution)/shard_map/ppermute | solution.py:1071
  172.9 32.6 %collective-permute-start.21 = (bf16[2,2,2,64,384]{4,3,2,1,0:T(8,128)(2,1)S(1)}, bf16[2,2,2,64,384]{4,3,2,1,0:T(8,128)(2,1)S(1)}, u32[]{:S(2)}, u32[]{:S(2)}) collective-permute-start(bf16[2,2,2,64,384]{4,3,2,1,0:T(8,128)(2,1)S(1)} %bitcast_dynamic-update-slice_fusion.18), channel_id=1, source_target_pairs={{0,1},{1,0},{2,3},{3,2},{4,5},{5,4},{6,7},{7,6},{8,9},{9,8},{10,11... | collective-permute-start | bytes 1179656 | tf_op jit(solution)/shard_map/ppermute | solution.py:1071
  173.9 31.6 %collective-permute-start.20 = (bf16[2,2,2,64,384]{4,3,2,1,0:T(8,128)(2,1)S(1)}, bf16[2,2,2,64,384]{4,3,2,1,0:T(8,128)(2,1)S(1)}, u32[]{:S(2)}, u32[]{:S(2)}) collective-permute-start(bf16[2,2,2,64,384]{4,3,2,1,0:T(8,128)(2,1)S(1)} %bitcast_dynamic-update-slice_fusion.18), channel_id=1, source_target_pairs={{0,16},{1,17},{2,18},{3,19},{4,20},{5,21},{6,22},{7,23},{8,24},{9,... | collective-permute-start | bytes 1179656 | tf_op jit(solution)/shard_map/ppermute | solution.py:1071
  206.1 3.5 collective-permute-start.23
  296.7 39.8 %collective-permute-start.24 = (bf16[512,768]{1,0:T(8,128)(2,1)}, bf16[512,768]{1,0:T(8,128)(2,1)S(1)}, u32[]{:S(2)}, u32[]{:S(2)}) collective-permute-start(bf16[512,768]{1,0:T(8,128)(2,1)} %memory_grads.2), channel_id=1, source_target_pairs={{0,1},{1,2},{2,3},{3,4},{4,5},{5,6},{6,7},{8,9},{9,10},{10,11},{11... | collective-permute-start | bytes 2359304 | tf_op jit(solution)/shard_map/ppermute | solution.py:1158
  331.2 34.3 %collective-permute-start.26 = (bf16[2,192,1536]{2,1,0:T(8,128)(2,1)}, bf16[2,192,1536]{2,1,0:T(8,128)(2,1)S(1)}, u32[]{:S(2)}, u32[]{:S(2)}) collective-permute-start(bf16[2,192,1536]{2,1,0:T(8,128)(2,1)} %get-tuple-element.264), channel_id=1, source_target_pairs={{0,8},{1,9},{2,10},{3,11},{4,12},{5,13},{6,14},{7,15},{8,0},{9,1},... | collective-permute-start | bytes 3538952 | tf_op jit(solution)/shard_map/ppermute | solution.py:1071
  350.2 27.3 %collective-permute-start.27 = (bf16[2,192,1536]{2,1,0:T(8,128)(2,1)}, bf16[2,192,1536]{2,1,0:T(8,128)(2,1)S(1)}, u32[]{:S(2)}, u32[]{:S(2)}) collective-permute-start(bf16[2,192,1536]{2,1,0:T(8,128)(2,1)} %get-tuple-element.266), channel_id=1, source_target_pairs={{0,8},{1,9},{2,10},{3,11},{4,12},{5,13},{6,14},{7,15},{8,0},{9,1},... | collective-permute-start | bytes 3538952 | tf_op jit(solution)/shard_map/ppermute | solution.py:1071
  350.8 26.7 %collective-permute-start.25 = (bf16[512,768]{1,0:T(8,128)(2,1)S(1)}, bf16[512,768]{1,0:T(8,128)(2,1)}, u32[]{:S(2)}, u32[]{:S(2)}) collective-permute-start(bf16[512,768]{1,0:T(8,128)(2,1)S(1)} %copy-done.12), channel_id=1, source_target_pairs={{0,1},{1,2},{2,3},{3,4},{4,5},{5,6},{6,7},{8,9},{9,10},{10,11},{11... | collective-permute-start | bytes 2359304 | tf_op jit(solution)/shard_map/ppermute | solution.py:1158
  382.0 2.2 collective-permute-start.28
  385.6 38.3 %collective-permute-start.29 = (bf16[2,2,24,3840]{3,2,1,0:T(8,128)(2,1)S(1)}, bf16[2,2,24,3840]{3,2,1,0:T(8,128)(2,1)S(1)}, u32[]{:S(2)}, u32[]{:S(2)}) collective-permute-start(bf16[2,2,24,3840]{3,2,1,0:T(8,128)(2,1)S(1)} %pad_maximum_fusion.1), channel_id=1, source_target_pairs={{0,16},{1,17},{2,18},{3,19},{4,20},{5,21},{6,22},{7,23},{8,24},{9,... | collective-permute-start | bytes 2211848 | tf_op jit(solution)/shard_map/ppermute | solution.py:1071
  387.0 36.9 %collective-permute-start.30 = (bf16[2,2,24,3840]{3,2,1,0:T(8,128)(2,1)}, bf16[2,2,24,3840]{3,2,1,0:T(8,128)(2,1)}, u32[]{:S(2)}, u32[]{:S(2)}) collective-permute-start(bf16[2,2,24,3840]{3,2,1,0:T(8,128)(2,1)} %pad_maximum_fusion.2), channel_id=1, source_target_pairs={{0,1},{1,0},{2,3},{3,2},{4,5},{5,4},{6,7},{7,6},{8,9},{9,8},{10,11... | collective-permute-start | bytes 2211848 | tf_op jit(solution)/shard_map/ppermute | solution.py:1071
  389.6 34.5 %collective-permute-start.31 = (bf16[2,2,24,3840]{3,2,1,0:T(8,128)(2,1)S(1)}, bf16[2,2,24,3840]{3,2,1,0:T(8,128)(2,1)S(1)}, u32[]{:S(2)}, u32[]{:S(2)}) collective-permute-start(bf16[2,2,24,3840]{3,2,1,0:T(8,128)(2,1)S(1)} %pad_maximum_fusion.3), channel_id=1, source_target_pairs={{0,17},{1,16},{2,19},{3,18},{4,21},{5,20},{6,23},{7,22},{8,25},{9,... | collective-permute-start | bytes 2211848 | tf_op jit(solution)/shard_map/ppermute | solution.py:1071
  425.0 23.3 %collective-permute-start.32 = (bf16[2,192,2304]{2,1,0:T(8,128)(2,1)}, bf16[2,192,2304]{2,1,0:T(8,128)(2,1)S(1)}, u32[]{:S(2)}, u32[]{:S(2)}) collective-permute-start(bf16[2,192,2304]{2,1,0:T(8,128)(2,1)} %get-tuple-element.293), channel_id=1, source_target_pairs={{0,8},{1,9},{2,10},{3,11},{4,12},{5,13},{6,14},{7,15},{8,0},{9,1},... | collective-permute-start | bytes 5308424 | tf_op jit(solution)/shard_map/ppermute | solution.py:1071
  427.6 20.6 %collective-permute-start.34 = (bf16[24,3840]{1,0:T(8,128)(2,1)}, bf16[24,3840]{1,0:T(8,128)(2,1)}, u32[]{:S(2)}, u32[]{:S(2)}) collective-permute-start(bf16[24,3840]{1,0:T(8,128)(2,1)} %get-tuple-element.301), channel_id=1, source_target_pairs={{0,4},{1,5},{2,6},{3,7},{4,0},{5,1},{6,2},{7,3},{8,12},{9,13},{10,... | collective-permute-start | bytes 552968 | tf_op jit(solution)/shard_map/ppermute | solution.py:1071
  431.1 17.1 %collective-permute-start.35 = (bf16[24,3840]{1,0:T(8,128)(2,1)}, bf16[24,3840]{1,0:T(8,128)(2,1)}, u32[]{:S(2)}, u32[]{:S(2)}) collective-permute-start(bf16[24,3840]{1,0:T(8,128)(2,1)} %get-tuple-element.302), channel_id=1, source_target_pairs={{0,2},{1,3},{2,0},{3,1},{4,6},{5,7},{6,4},{7,5},{8,10},{9,11},{10,... | collective-permute-start | bytes 552968 | tf_op jit(solution)/shard_map/ppermute | solution.py:1071
  431.1 17.1 %collective-permute-start.36 = (bf16[24,3840]{1,0:T(8,128)(2,1)}, bf16[24,3840]{1,0:T(8,128)(2,1)}, u32[]{:S(2)}, u32[]{:S(2)}) collective-permute-start(bf16[24,3840]{1,0:T(8,128)(2,1)} %get-tuple-element.303), channel_id=1, source_target_pairs={{0,6},{1,7},{2,4},{3,5},{4,2},{5,3},{6,0},{7,1},{8,14},{9,15},{10,... | collective-permute-start | bytes 552968 | tf_op jit(solution)/shard_map/ppermute | solution.py:1071
  445.9 2.3 collective-permute-start.33
  449.4 15.1 %copy-start.13 = (bf16[24,3840]{1,0:T(8,128)(2,1)S(1)}, bf16[24,3840]{1,0:T(8,128)(2,1)}, u32[]{:S(2)}) copy-start(bf16[24,3840]{1,0:T(8,128)(2,1)} %get-tuple-element.321) | copy-start | bytes 552964
  449.4 16.3 %collective-permute-start.37 = (bf16[2,2,24,2560]{3,2,1,0:T(8,128)(2,1)S(1)}, bf16[2,2,24,2560]{3,2,1,0:T(8,128)(2,1)S(1)}, u32[]{:S(2)}, u32[]{:S(2)}) collective-permute-start(bf16[2,2,24,2560]{3,2,1,0:T(8,128)(2,1)S(1)} %pad_maximum_fusion.6), channel_id=1, source_target_pairs={{0,16},{1,17},{2,18},{3,19},{4,20},{5,21},{6,22},{7,23},{8,24},{9,... | collective-permute-start | bytes 1474568 | tf_op jit(solution)/shard_map/ppermute | solution.py:1071
  450.6 23.3 %collective-permute-start.38 = (bf16[2,2,24,2560]{3,2,1,0:T(8,128)(2,1)S(1)}, bf16[2,2,24,2560]{3,2,1,0:T(8,128)(2,1)S(1)}, u32[]{:S(2)}, u32[]{:S(2)}) collective-permute-start(bf16[2,2,24,2560]{3,2,1,0:T(8,128)(2,1)S(1)} %pad_maximum_fusion.7), channel_id=1, source_target_pairs={{0,1},{1,0},{2,3},{3,2},{4,5},{5,4},{6,7},{7,6},{8,9},{9,8},{10,11... | collective-permute-start | bytes 1474568 | tf_op jit(solution)/shard_map/ppermute | solution.py:1071
  452.5 22.3 %collective-permute-start.39 = (bf16[2,2,24,2560]{3,2,1,0:T(8,128)(2,1)S(1)}, bf16[2,2,24,2560]{3,2,1,0:T(8,128)(2,1)S(1)}, u32[]{:S(2)}, u32[]{:S(2)}) collective-permute-start(bf16[2,2,24,2560]{3,2,1,0:T(8,128)(2,1)S(1)} %pad_maximum_fusion.8), channel_id=1, source_target_pairs={{0,17},{1,16},{2,19},{3,18},{4,21},{5,20},{6,23},{7,22},{8,25},{9,... | collective-permute-start | bytes 1474568 | tf_op jit(solution)/shard_map/ppermute | solution.py:1071
  475.0 11.1 %collective-permute-start.40 = (bf16[24,2560]{1,0:T(8,128)(2,1)S(1)}, bf16[24,2560]{1,0:T(8,128)(2,1)S(1)}, u32[]{:S(2)}, u32[]{:S(2)}) collective-permute-start(bf16[24,2560]{1,0:T(8,128)(2,1)S(1)} %get-tuple-element.403), channel_id=1, source_target_pairs={{0,4},{1,5},{2,6},{3,7},{4,0},{5,1},{6,2},{7,3},{8,12},{9,13},{10,... | collective-permute-start | bytes 368648 | tf_op jit(solution)/shard_map/ppermute | solution.py:1071
  477.1 9.1 %collective-permute-start.42 = (bf16[24,2560]{1,0:T(8,128)(2,1)S(1)}, bf16[24,2560]{1,0:T(8,128)(2,1)S(1)}, u32[]{:S(2)}, u32[]{:S(2)}) collective-permute-start(bf16[24,2560]{1,0:T(8,128)(2,1)S(1)} %get-tuple-element.404), channel_id=1, source_target_pairs={{0,6},{1,7},{2,4},{3,5},{4,2},{5,3},{6,0},{7,1},{8,14},{9,15},{10,... | collective-permute-start | bytes 368648 | tf_op jit(solution)/shard_map/ppermute | solution.py:1071
  478.0 9.2 %collective-permute-start.41 = (bf16[24,2560]{1,0:T(8,128)(2,1)S(1)}, bf16[24,2560]{1,0:T(8,128)(2,1)S(1)}, u32[]{:S(2)}, u32[]{:S(2)}) collective-permute-start(bf16[24,2560]{1,0:T(8,128)(2,1)S(1)} %get-tuple-element.405), channel_id=1, source_target_pairs={{0,2},{1,3},{2,0},{3,1},{4,6},{5,7},{6,4},{7,5},{8,10},{9,11},{10,... | collective-permute-start | bytes 368648 | tf_op jit(solution)/shard_map/ppermute | solution.py:1071
  (22 other events, 135.9 us)
Sparse Core Ops, SparseCore 0:
  14.0 112.7 all-gather.1
  268.4 144.2 reduce-scatter.1

commit v3 on v2

--- a/solution.py
+++ b/solution.py
@@ -28,8 +28,10 @@
 ROWS = MICRO * TGT_LEN
 BLOCK = 256
 WIDE = 256
+SMALL_SCORE = 59.0
+FFN_CHUNK = 1024
 HALF_COLUMNS = 2048
-VMEM_LIMIT = 60 * 1024 * 1024
+VMEM_LIMIT = 52 * 1024 * 1024
 BF = jnp.bfloat16
 F32 = jnp.float32
 
@@ -77,6 +79,10 @@
     return jnp.where((row_id // HEAD_DIM) == head, stacked, jnp.zeros_like(stacked))
 
 
+def far(array):
+    return pltpu.with_memory_space_constraint(array, pltpu.HBM)
+
+
 def nt(a, b):
     return lax.dot_general(a, b, (((1,), (1,)), ((), ())), preferred_element_type=F32)
 
@@ -167,9 +173,27 @@
         total_ref[...] += addend
 
 
-def key_value_kernel(core_ref, own_ref, other_ref, rows_ref, kv_ref, w_kv, sems):
+def keep_largest(total_ref, values):
+    head = lax.broadcasted_iota(jnp.int32, (D, LANES), 0) // HEAD_DIM
+    lane = lax.broadcasted_iota(jnp.int32, (D, LANES), 1)
+    hot = jnp.where(head == lane, 1.0, 0.0).astype(BF)
+    values = values.astype(F32)
+    squares = nn((values * values).astype(BF), hot)
+    row = jnp.broadcast_to(jnp.max(squares, axis=0, keepdims=True), (8, LANES))
+
+    @pl.when(pl.program_id(0) == 0)
+    def _():
+        total_ref[...] = row
+
+    @pl.when(pl.program_id(0) > 0)
+    def _():
+        total_ref[...] = jnp.maximum(total_ref[...], row)
+
+
+def key_value_kernel(core_ref, own_ref, other_ref, rows_ref, kv_ref, size_ref, w_kv, sems):
     halves_loaded(core_ref, own_ref, other_ref, key_value_pieces(w_kv), sems)
     kv_ref[...] = nn(rows_ref[...], w_kv[...]).astype(BF)
+    keep_largest(size_ref, kv_ref[:, :D])
 
 
 def key_value(core, own, other, rows, steps, index, us):
@@ -177,8 +201,8 @@
         key_value_kernel,
         grid=(steps,),
         in_specs=[SMEM, ANY, ANY, pl.BlockSpec((BLOCK, D), index)],
-        out_specs=row_block(2 * D),
-        out_shape=shape(steps * BLOCK, 2 * D),
+        out_specs=[row_block(2 * D), fixed_block(8, LANES)],
+        out_shape=[shape(steps * BLOCK, 2 * D), shape(8, LANES, F32)],
         scratch_shapes=[pltpu.VMEM((D, 2 * D), BF), pltpu.SemaphoreType.DMA((1,))],
         compiler_params=params(),
         cost_estimate=cost(us),
@@ -221,13 +245,15 @@
 
 
 def cross_inputs_kernel(
-    core_ref, own_ref, other_ref, gain_ref, x_ref, o_ref, x1_ref, h_ref, q_ref, weights, sems
+    core_ref, own_ref, other_ref, gain_ref, x_ref, o_ref,
+    x1_ref, h_ref, q_ref, size_ref, weights, sems,
 ):
     halves_loaded(core_ref, own_ref, other_ref, out_query_pieces(weights), sems)
     x1 = x_ref[...].astype(F32) + nn(o_ref[...], weights[:, :D])
     x1_ref[...] = x1
     h_ref[...] = normed(x1, gain_ref[1:2, :])[2]
     q_ref[...] = nn(h_ref[...], weights[:, D:]).astype(BF)
+    keep_largest(size_ref, q_ref[...])
 
 
 def cross_inputs(core, own, other, gain, x, o1):
@@ -235,8 +261,8 @@
         cross_inputs_kernel,
         grid=(ROWS // BLOCK,),
         in_specs=[SMEM, ANY, ANY, fixed_block(8, D), row_block(D), row_block(D)],
-        out_specs=[row_block(D)] * 3,
-        out_shape=[shape(ROWS, D, F32), shape(ROWS, D), shape(ROWS, D)],
+        out_specs=[row_block(D)] * 3 + [fixed_block(8, LANES)],
+        out_shape=[shape(ROWS, D, F32), shape(ROWS, D), shape(ROWS, D), shape(8, LANES, F32)],
         scratch_shapes=[pltpu.VMEM((D, 2 * D), BF), pltpu.SemaphoreType.DMA((2,))],
         compiler_params=params(),
         cost_estimate=cost(5),
@@ -246,24 +272,35 @@
 
 def ffn_kernel(
     core_ref, late_ref, own_ref, other_ref, gain_ref, x1_ref, o_ref, dy_ref,
-    out_ref, h_ref, hidden_ref, dgate_ref, dup_ref, db_ref, dx_ref, do_ref, gain_grad_ref,
-    w_out, w_gate, w_up, w_down, sems, down_sems,
+    out_ref, h_ref, acts_ref, db_ref, dx_ref, do_ref, gain_grad_ref,
+    w_out, w_gate, w_up, w_down, sems,
 ):
     width = w_gate.shape[1]
+    first = pl.program_id(0) == 0
     copies = [
         pltpu.make_async_copy(late_ref.at[:, :D], w_out, sems.at[0]),
         pltpu.make_async_copy(late_ref.at[:, D : D + width], w_gate, sems.at[1]),
         pltpu.make_async_copy(late_ref.at[:, D + width :], w_up, sems.at[2]),
     ]
-    first = pl.program_id(0) == 0
+
+    def down_copies(side):
+        halves = (own_ref, other_ref) if side == 0 else (other_ref, own_ref)
+        columns = [slice(half * D // 2, (half + 1) * D // 2) for half in range(2)]
+        return [
+            pltpu.make_async_copy(halves[half], w_down.at[:, columns[half]], sems.at[3 + half])
+            for half in range(2)
+        ]
 
     @pl.when(first)
     def _():
         for copy in copies:
             copy.start()
-
-    pieces = [(side, slice(None), w_down.at[:, side * D // 2 : (side + 1) * D // 2]) for side in range(2)]
-    halves_loaded(core_ref, own_ref, other_ref, pieces, down_sems)
+        for side in range(2):
+
+            @pl.when(core_ref[0] == side)
+            def _():
+                for copy in down_copies(side):
+                    copy.start()
 
     def arrived(place):
         @pl.when(first)
@@ -275,21 +312,40 @@
     h_ref[...] = normed(x2, gain_ref[2:3, :])[2]
     dy_low = dy_ref[...]
     arrived(1)
-    gate = nn(h_ref[...], w_gate[...])
     arrived(2)
-    up = nn(h_ref[...], w_up[...])
-    d_hidden = nt(dy_low, w_down[...])
+
+    @pl.when(first)
+    def _():
+        for side in range(2):
+
+            @pl.when(core_ref[0] == side)
+            def _():
+                for copy in down_copies(side):
+                    copy.wait()
+
     scale = math.sqrt(2.0 / math.pi)
-    square = gate * gate
-    turn = jnp.tanh(scale * gate * (1.0 + 0.044715 * square))
-    half = 0.5 * (1.0 + turn)
-    gelu = gate * half
-    slope = half + 0.5 * gate * (1.0 - turn * turn) * (scale * (1.0 + 3 * 0.044715 * square))
-    hidden_ref[...] = (gelu * up).astype(BF)
-    dgate_ref[...] = (d_hidden * up * slope).astype(BF)
-    dup_ref[...] = (d_hidden * gelu).astype(BF)
-    out_ref[...] = (x2 + nn(hidden_ref[...], w_down[...])).astype(BF)
-    dh = nt(dgate_ref[...], w_gate[...]) + nt(dup_ref[...], w_up[...])
+    out, dh = x2, 0.0
+    h = h_ref[...]
+    for start in range(0, width, FFN_CHUNK):
+        part = slice(start, start + FFN_CHUNK)
+        gate = nn(h, w_gate[:, part])
+        up = nn(h, w_up[:, part])
+        d_hidden = nt(dy_low, w_down[part, :])
+        square = gate * gate
+        turn = jnp.tanh(gate * (scale + (scale * 0.044715) * square))
+        half = 0.5 + 0.5 * turn
+        gelu = gate * half
+        bend = gate * (0.5 * scale + (0.5 * scale * 3 * 0.044715) * square)
+        slope = half + (1.0 - turn * turn) * bend
+        hidden = (gelu * up).astype(BF)
+        d_gate = (d_hidden * up * slope).astype(BF)
+        d_up = (d_hidden * gelu).astype(BF)
+        acts_ref[0, :, part] = d_gate
+        acts_ref[1, :, part] = d_up
+        acts_ref[2, :, part] = hidden
+        out = out + nn(hidden, w_down[part, :])
+        dh = dh + nt(d_gate, w_gate[:, part]) + nt(d_up, w_up[:, part])
+    out_ref[...] = out.astype(BF)
     dx = dy_low.astype(F32) + norm_back(x2, gain_ref[2:3, :], dh, gain_grad_ref)
     dx_ref[...] = dx
     db_ref[...] = dx.astype(BF)
@@ -305,9 +361,7 @@
         out_specs=[
             row_block(D),
             row_block(D),
-            row_block(width),
-            row_block(width),
-            row_block(width),
+            pl.BlockSpec((3, BLOCK, width), lambda i: (0, i, 0)),
             row_block(D),
             row_block(D),
             row_block(D),
@@ -316,9 +370,7 @@
         out_shape=[
             shape(ROWS, D),
             shape(ROWS, D),
-            shape(ROWS, width),
-            shape(ROWS, width),
-            shape(ROWS, width),
+            jax.ShapeDtypeStruct((3, ROWS, width), BF),
             shape(ROWS, D),
             shape(ROWS, D, F32),
             shape(ROWS, D),
@@ -329,13 +381,12 @@
             pltpu.VMEM((D, width), BF),
             pltpu.VMEM((D, width), BF),
             pltpu.VMEM((width, D), BF),
-            pltpu.SemaphoreType.DMA((3,)),
-            pltpu.SemaphoreType.DMA((2,)),
+            pltpu.SemaphoreType.DMA((5,)),
         ],
         compiler_params=params(),
         cost_estimate=cost(30),
         name="ffn",
-    )(core, late, own, other, gain, x1, o2, dy)
+    )(core, far(late), far(own), far(other), gain, far(x1), o2, far(dy))
 
 
 def self_grads_kernel(
@@ -372,7 +423,7 @@
         compiler_params=params(),
         cost_estimate=cost(5),
         name="self_grads",
-    )(core, own, other, gain, x1, dx2, *dq2)
+    )(core, far(own), far(other), gain, far(x1), far(dx2), *dq2)
 
 
 def input_grads_kernel(
@@ -403,7 +454,7 @@
         compiler_params=params(),
         cost_estimate=cost(6),
         name="input_grads",
-    )(core, own, other, gain, x, dx1, dqkv)
+    )(core, far(own), far(other), gain, far(x), dx1, dqkv)
 
 
 def memory_grads_kernel(core_ref, own_ref, other_ref, dkv_ref, dm_ref, w_kv, sems):
@@ -496,33 +547,25 @@
     )(core, *flat)
 
 
-def ffn_weight_grads_kernel(h_ref, hidden_ref, dgate_ref, dup_ref, dy_ref, out_ref):
-    unit = pl.program_id(0)
+def ffn_weight_grads_kernel(h_ref, acts_ref, dy_ref, out_ref):
     devices = out_ref.shape[0]
-    width = dgate_ref.shape[1]
-
-    def from_columns(grads_ref):
+    width = acts_ref.shape[2]
+
+    @pl.when(pl.program_id(0) < 2)
+    def _():
         turned = h_ref[...].T
         share = D // devices
         for first in range(0, width, 2 * WIDE):
             both = [
-                nn(turned, grads_ref[:, place : place + WIDE]).reshape(devices, share, WIDE)
+                nn(turned, acts_ref[0, :, place : place + WIDE]).reshape(devices, share, WIDE)
                 for place in (first, first + WIDE)
             ]
             row = first // WIDE * share
             out_ref[:, row : row + 2 * share, :] = jnp.concatenate(both, axis=1).astype(BF)
 
-    @pl.when(unit == 0)
-    def _():
-        from_columns(dgate_ref)
-
-    @pl.when(unit == 1)
-    def _():
-        from_columns(dup_ref)
-
-    @pl.when(unit == 2)
-    def _():
-        turned = hidden_ref[...].T
+    @pl.when(pl.program_id(0) == 2)
+    def _():
+        turned = acts_ref[0].T
         share = width // devices
         for place in range(D // WIDE):
             grad = nn(turned, dy_ref[:, place * WIDE : (place + 1) * WIDE])
@@ -531,17 +574,15 @@
             ).astype(BF)
 
 
-def ffn_weight_grads(h3, hidden, d_gate, d_up, dy, devices):
-    width = hidden.shape[1]
+def ffn_weight_grads(h3, acts, dy, devices):
+    width = acts.shape[2]
     rows = D * width // WIDE // devices
     return pl.pallas_call(
         ffn_weight_grads_kernel,
         grid=(3,),
         in_specs=[
             fixed_block(ROWS, D),
-            fixed_block(ROWS, width),
-            fixed_block(ROWS, width),
-            fixed_block(ROWS, width),
+            pl.BlockSpec((1, ROWS, width), lambda u: (u, 0, 0)),
             fixed_block(ROWS, D),
         ],
         out_specs=pl.BlockSpec((devices, rows, WIDE), lambda u: (0, u, 0)),
@@ -549,7 +590,7 @@
         compiler_params=params(),
         cost_estimate=cost(13),
         name="ffn_weight_grads",
-    )(h3, hidden, d_gate, d_up, dy)
+    )(h3, far(acts), far(dy))
 
 
 def memory_weight_grads_kernel(
@@ -593,48 +634,39 @@
     )(core, memory, next_rows, *dkv_own, *dkv_next)
 
 
-def memory_total_kernel(
-    core_ref, own_ref, other_ref, dkv0_ref, dkv1_ref, prev0_ref, prev1_ref, dm_ref, w_kv, sems
-):
+def memory_total_kernel(core_ref, own_ref, other_ref, dkv_ref, prev_ref, dm_ref, w_kv, sems):
     halves_loaded(core_ref, own_ref, other_ref, key_value_pieces(w_kv), sems)
-    low = pl.program_id(0) < 4
-    block = pl.program_id(0) % 4
-    prev = jnp.where(low, prev0_ref[...], prev1_ref[...])
+    block = pl.program_id(0)
 
     @pl.when(block == 0)
     def _():
-        dm_ref[...] = prev
+        dm_ref[...] = prev_ref[...]
 
     @pl.when(block > 0)
     def _():
-        dk, dv = (jnp.where(low, dkv0_ref[place], dkv1_ref[place]) for place in range(2))
-        shared = jnp.where(block == 1, prev.astype(F32), 0.0)
-        dm_ref[...] = (nt(dk, w_kv[:, :D]) + nt(dv, w_kv[:, D:]) + shared).astype(BF)
+        grads = nt(dkv_ref[0], w_kv[:, :D]) + nt(dkv_ref[1], w_kv[:, D:])
+        shared = jnp.where(block == 1, prev_ref[...].astype(F32), 0.0)
+        dm_ref[...] = (grads + shared).astype(BF)
 
 
 def memory_total(core, own, other, dkv, prev):
-    def spot(i, m):
-        return jnp.clip(i - 4 * m, 0, 3)
-
-    def dkv_block(m):
-        return pl.BlockSpec((2, BLOCK, D), lambda i: (0, jnp.maximum(spot(i, m) - 1, 0), 0))
-
-    def prev_block(m):
-        return pl.BlockSpec((BLOCK, D), lambda i: (jnp.minimum(spot(i, m), 1), 0))
-
     return pl.pallas_call(
         memory_total_kernel,
-        grid=(MICRO * 4,),
-        in_specs=[SMEM, ANY, ANY]
-        + [dkv_block(m) for m in range(MICRO)]
-        + [prev_block(m) for m in range(MICRO)],
+        grid=(MEM_DEV // BLOCK,),
+        in_specs=[
+            SMEM,
+            ANY,
+            ANY,
+            pl.BlockSpec((2, BLOCK, D), lambda i: (0, jnp.maximum(i - 1, 0), 0)),
+            pl.BlockSpec((BLOCK, D), lambda i: (jnp.minimum(i, 1), 0)),
+        ],
         out_specs=row_block(D),
-        out_shape=shape(MICRO * MEM_DEV, D),
+        out_shape=shape(MEM_DEV, D),
         scratch_shapes=[pltpu.VMEM((D, 2 * D), BF), pltpu.SemaphoreType.DMA((1,))],
         compiler_params=params(),
-        cost_estimate=cost(7),
+        cost_estimate=cost(4),
         name="memory_total",
-    )(core, own, other, *dkv, *prev)
+    )(core, own, other, dkv, prev)
 
 
 def extras_kernel(share, core_ref, sums_ref, first_ref, second_ref, third_ref, give_ref, keep_ref):
@@ -729,22 +761,44 @@
     lse_ref[0] = jnp.where(row_id == 0, rows[0], rows[1])
 
 
-def cross_forward_kernel(q_ref, ko_ref, kn_ref, vo_ref, vn_ref, mask_ref, o_ref, lse_ref, k_ext):
-    k_ext[:OWN, :LANES] = ko_ref[...]
-    k_ext[OWN:, :LANES] = kn_ref[...]
-    k_ext[:, LANES:] = mask_ref[0]
-    q_t = q_ref[...].T
-    v_t = jnp.concatenate([vo_ref[...], vn_ref[...]], axis=0).T
-    ones = extra_rows(TGT_LEN, 1.0, ())
-    mixed, lses = [], []
-    for head in range(2):
-        query = jnp.concatenate([head_rows(q_t, head), ones], axis=0)
-        scores = nn(k_ext[...], query)
-        weights, inverse, lse = softmax_columns(scores)
-        mixed.append(nn(v_t[head * HEAD_DIM : (head + 1) * HEAD_DIM], weights) * inverse)
-        lses.append(lse)
-    o_ref[...] = jnp.concatenate(mixed, axis=0).T.astype(BF)
-    put_lse(lse_ref, lses)
+def attended(scores, value, small):
+    top = 0.0 if small else jnp.max(scores, axis=0, keepdims=True)
+    weights = jnp.exp(scores if small else scores - top).astype(BF)
+    both = nn(value, weights)
+    total = both[HEAD_DIM : HEAD_DIM + 1]
+    return both[:HEAD_DIM] * (1.0 / total), top + jnp.log(total)
+
+
+def cross_forward_kernel(
+    small_ref, q_ref, ko_ref, kn_ref, vo_ref, vn_ref, mask_ref, o_ref, lse_ref, k_ext
+):
+    def run(small):
+        k_ext[:OWN, :LANES] = ko_ref[...]
+        k_ext[OWN:, :LANES] = kn_ref[...]
+        k_ext[:, LANES:] = mask_ref[0]
+        q_t = q_ref[...].T
+        v_t = jnp.concatenate([vo_ref[...], vn_ref[...]], axis=0).T
+        ones = extra_rows(TGT_LEN, 1.0, ())
+        rows_of_ones = jnp.ones((16, KEYS), BF)
+        scores = [
+            nn(k_ext[...], jnp.concatenate([head_rows(q_t, head), ones], axis=0))
+            for head in range(2)
+        ]
+        values = [
+            jnp.concatenate([v_t[head * HEAD_DIM : (head + 1) * HEAD_DIM], rows_of_ones], axis=0)
+            for head in range(2)
+        ]
+        mixed, lses = zip(*[attended(scores[head], values[head], small) for head in range(2)])
+        o_ref[...] = jnp.concatenate(mixed, axis=0).T.astype(BF)
+        put_lse(lse_ref, lses)
+
+    @pl.when(small_ref[0] == 1)
+    def _():
+        run(True)
+
+    @pl.when(small_ref[0] != 1)
+    def _():
+        run(False)
 
 
 def cross_backward_kernel(
@@ -909,11 +963,12 @@
 MASK_BLOCK = pl.BlockSpec((1, KEYS, LANES), lambda m, p: (m, 0, 0))
 
 
-def cross_forward(q, kv_own, kv_next, mask):
+def cross_forward(small, q, kv_own, kv_next, mask):
     return pl.pallas_call(
         cross_forward_kernel,
         grid=PAIR_GRID,
         in_specs=[
+            SMEM,
             pair_block(TGT_LEN),
             pair_block(OWN),
             pair_block(NEXT),
@@ -927,7 +982,7 @@
         compiler_params=params(),
         cost_estimate=cost(32),
         name="cross_forward",
-    )(q, kv_own, kv_next, kv_own, kv_next, mask)
+    )(small, q, kv_own, kv_next, kv_own, kv_next, mask)
 
 
 def cross_backward(m, q, kv_own, kv_next, mask, o, d_o, lse):
@@ -962,7 +1017,7 @@
         compiler_params=params(),
         cost_estimate=cost(22),
         name="cross_backward",
-    )(q, kv_own, kv_next, kv_own, kv_next, mask, o, d_o, lse)
+    )(*map(far, (q, kv_own, kv_next, kv_own, kv_next, mask, o, d_o, lse)))
 
 
 def swapped(spec):
@@ -1158,9 +1213,9 @@
     return lax.ppermute(block, "seq", route)
 
 
-def ffn_grads(h3, hidden, d_gate, d_up, dy, later):
+def ffn_grads(h3, acts, dy, later):
     devices = lax.axis_size("dp") * lax.axis_size("seq")
-    width = hidden.shape[1]
+    width = acts.shape[2]
     if D // devices % 8 or width // devices % 16:
         total = [
             lax.psum_scatter(
@@ -1171,10 +1226,10 @@
                 scatter_dimension=0,
                 tiled=True,
             )
-            for rows, grads in ((h3, d_gate), (h3, d_up), (hidden, dy))
+            for rows, grads in ((h3, acts[0]), (h3, acts[1]), (acts[2], dy))
         ]
         return total, later
-    partial = ffn_weight_grads(h3, hidden, d_gate, d_up, dy, devices)
+    partial = ffn_weight_grads(h3, acts, dy, devices)
     later, partial = tied(later, partial)
     return lax.psum_scatter(partial, AXES, scatter_dimension=0, tiled=True), later
 
@@ -1242,10 +1297,13 @@
     tiles = bias_tiles(bias_table.astype(F32))
     mask = jnp.stack([key_masks(doc_offsets[m, 0], position) for m in range(MICRO)])
     next_rows = memory[:, 0, :NEXT]
-    second, _, _ = gather_bits(second, core_bits, column)
-    first, _, (second, third, tiles, mask, next_rows) = gather_stage(
-        first, dims, plane, (second, third, tiles, mask, next_rows)
+    narrow = second.reshape(2, 2 * share, -1)
+    second, _, _ = gather_bits(jnp.concatenate([narrow, third], axis=1), core_bits, column)
+    first, _, (second, tiles, mask, next_rows, late) = gather_stage(
+        first, dims, plane, (second, tiles, mask, next_rows, late)
     )
+    third = second[..., 2 * share :, :]
+    second = second[..., : 2 * share, :].reshape(third.shape[:-2] + (share, D))
     own, other = both_halves(first)
     late = lax.all_gather(late, AXES, axis=0, tiled=True)
     x = decoder_in.reshape(ROWS, D)
@@ -1257,7 +1315,7 @@
     h1, qkv, gains = self_inputs(core_id, own, other, x)
     o1, lse1 = self_forward(qkv, tiles)
     mem, o1 = tied(mem, o1)
-    kv_own = key_value(
+    kv_own, own_size = key_value(
         core_id, own, other, mem, MICRO * OWN // BLOCK, lambda i: (i + i // 3 + 1, 0), 6
     )
     second, _, (o1, kv_own, next_rows) = gather_stage(
@@ -1265,19 +1323,20 @@
     )
     own_b, other_b = both_halves(second)
     next_rows, third, own_b = lax.optimization_barrier((next_rows, third, own_b))
-    kv_next = key_value(
+    kv_next, next_size = key_value(
         core_id, own, other, next_rows, MICRO * NEXT // BLOCK, lambda i: (i, 0), 4
     )
     o1, kv_next = tied(o1, kv_next)
-    x1, h2, q2 = cross_inputs(core_id, own_b, other_b, gains, x, o1)
-    third, _, q2 = gather_stage(third, core_bits, column, q2)
-    o2, lse2 = cross_forward(q2, kv_own, kv_next, mask)
+    x1, h2, q2, query_size = cross_inputs(core_id, own_b, other_b, gains, x, o1)
+    largest = jnp.max(query_size[:1] * jnp.maximum(own_size[:1], next_size[:1]))
+    small = (largest <= SMALL_SCORE**2).astype(jnp.int32).reshape(1)
+    o2, lse2 = cross_forward(small, q2, kv_own, kv_next, mask)
     third, _, o2 = gather_stage(third, dims, plane, o2)
     own_c, other_c = both_halves(third)
-    out, h3, hidden, d_gate, d_up, db2, dx2, do2, g_norm_ffn = ffn(
+    out, h3, acts, db2, dx2, do2, g_norm_ffn = ffn(
         core_id, late, own_c, other_c, gains, x1, o2, dy
     )
-    ffn_total, do2 = ffn_grads(h3, hidden, d_gate, d_up, dy, do2)
+    ffn_total, do2 = ffn_grads(h3, acts, dy, do2)
     dims = without(device_bits(), core_bits)
     arguments = (q2, kv_own, kv_next, mask, o2, do2, lse2)
     results, arrived = [], []
@@ -1297,35 +1356,56 @@
     dq2, give = tied(dq2, give)
     memory_terms = core_stage(give, keep)
     dx1, db1, do1, g_norm_cross = self_grads(core_id, own_b, other_b, gains, x1, dx2, dq2)
-    (db1, do1), arrived[-1], pair_terms, memory_terms = lax.optimization_barrier(
-        ((db1, do1), arrived[-1], pair_terms, memory_terms)
+    (db1, do1), pair_terms, memory_terms = lax.optimization_barrier(
+        ((db1, do1), pair_terms, memory_terms)
     )
     out_terms = core_stage(*pair_grads(core_id, [(o1, (db1,))], across))
     cross_parts = scatter_parts([pair_terms, memory_terms, out_terms], dims, plane)
     do1, cross_parts = tied(do1, cross_parts)
     cross_terms = scattered(cross_parts, plane)
     dqkv, sums = self_backward(qkv, tiles, o1, do1, lse1)
+    dqkv, arrived[-1] = tied(dqkv, arrived[-1])
     give, keep = row_grads(core_id, h1, dqkv, across, 5)
-    (dqkv, cross_terms, ffn_total), give = tied((dqkv, cross_terms, ffn_total), give)
+    dqkv, give, cross_terms = lax.optimization_barrier((dqkv, give, cross_terms))
     self_terms = core_stage(give, keep)
-    cross_parts = scatter_parts([cross_terms], without(dims, plane), column)
+    left = without(dims, plane)
+    high, low = column[:1], column[1:]
+    cross_parts = scatter_parts([cross_terms], left, high)
     dqkv, cross_parts = tied(dqkv, cross_parts)
-    cross_terms = scattered(cross_parts, column)
+    cross_terms = scattered(cross_parts, high)
     grad_decoder, g_norm_self = input_grads(core_id, own, other, gains, x, dx1, dqkv)
-    extra_terms = core_stage(
-        *extras(core_id, sums, [g_norm_self, g_norm_cross, g_norm_ffn], across, share)
+    g_norm_self, cross_terms, self_terms = lax.optimization_barrier(
+        (g_norm_self, cross_terms, self_terms)
     )
-    self_terms, extra_terms, cross_terms = lax.optimization_barrier(
-        (self_terms, extra_terms, cross_terms)
+    self_parts = scatter_parts([self_terms], dims, plane)
+    cross_parts = scatter_parts([cross_terms], low, low)
+    give, keep = extras(core_id, sums, [g_norm_self, g_norm_cross, g_norm_ffn], across, share)
+    dkv_own, cross_parts, self_parts, give = lax.optimization_barrier(
+        (dkv_own, cross_parts, self_parts, give)
     )
-    self_parts = scatter_parts([self_terms, extra_terms], dims, plane)
-    dkv_own, self_parts = tied(dkv_own, self_parts)
     self_terms = scattered(self_parts, plane)
-    grad_memory = memory_total(core_id, own, other, dkv_own, arrived)
-    grad_memory, self_terms = tied(grad_memory, self_terms)
-    self_parts = scatter_parts([self_terms], without(dims, plane), column)
+    extra_terms = core_stage(give, keep)
+    cross_terms = scattered(cross_parts, low)
+    totals = [memory_total(core_id, own, other, dkv_own[0], arrived[0])]
+    totals[0], extra_terms = tied(totals[0], extra_terms)
+    extra_left = list(dims)
+    for bit in plane:
+        extra_parts = scatter_parts([extra_terms], extra_left, [bit])
+        extra_left.remove(bit)
+        if len(totals) == 1:
+            dkv_own, extra_parts = tied(dkv_own, extra_parts)
+        extra_terms = scattered(extra_parts, [bit])
+        if len(totals) == 1:
+            totals.append(memory_total(core_id, own, other, dkv_own[1], arrived[1]))
+            totals[1], extra_terms = tied(totals[1], extra_terms)
+    totals, self_terms, extra_terms = lax.optimization_barrier((totals, self_terms, extra_terms))
+    self_parts = scatter_parts([self_terms, extra_terms], left, column)
+    self_parts, cross_terms, ffn_total = lax.optimization_barrier(
+        (self_parts, cross_terms, ffn_total)
+    )
     g_self = tree_sum(scattered(self_parts, column))
     g_cross = tree_sum(cross_terms)
+    grad_memory = jnp.stack(totals)
     g_gate, g_up, g_down = ffn_columns(ffn_total, share, ffn_gate.shape[1])
 
     table = g_self[: HEADS * BUCKETS // LANES, 3 * D + LANES :].reshape(HEADS, BUCKETS)

time: 503 us -> 478 us (0.950)
  Pallas kernels: 302 us -> 278 us
  waiting for transfers between devices: 83 us -> 62.8 us
  starting transfers between devices: 52.4 us -> 68.2 us
    ppermute x40 -> x38, starting transfers between devices: 43.9 us -> 57.4 us  [exchange(): return lax.ppermute(block, AXES, [(i, i ^ mask) for i in range(count)])]
    ppermute x3, waiting for transfers between devices: 11.9 us -> 0.01 us  [passed_along(): return lax.ppermute(block, 'seq', route)]
    pallas_call x2 -> x3, Pallas kernels: 43.2 us -> 32 us  [the longest x1 18.9 us: cross_forward(): pl.pallas_call(cross_forward_kernel, grid=PAIR_GRID, in_specs=[SMEM, pair...]
    ppermute x40 -> x38, waiting for transfers between devices: 71.1 us -> 62.7 us  [exchange(): return lax.ppermute(block, AXES, [(i, i ^ mask) for i in range(count)])]
    unnamed x60 -> x62, local copies, waits for them, and re-layouts: 11 us -> 10.1 us
  transfers between devices with their start and end apart: 45 -> 43, of which waited for: 15 -> 13; matrix products, arithmetic and copies ran while one was open for 6% -> 7% of each run, Pallas kernels for 49% -> 48%
where the time goes in v3:
time: 478 us; the launch traced here: 472 us
  Pallas kernels  278 us (58%)
  starting transfers between devices  68.2 us (14%)
  waiting for transfers between devices  62.8 us (13%)
  local copies, waits for them, and re-layouts  31.7 us (7%)
  between operations  15.9 us (3%)
  other arithmetic  14.9 us (3%)
    ppermute x38, waiting for transfers between devices, exchange(): return lax.ppermute(block, AXES, [(i, i ^ mask) for i in range(count)])  62.7 us
    ppermute x38, starting transfers between devices, exchange(): return lax.ppermute(block, AXES, [(i, i ^ mask) for i in range(count)])  57.4 us
    pallas_call x2, Pallas kernels, cross_backward(): pl.pallas_call(cross_backward_kernel, grid=(PAIRS,), in_specs=[block(TGT_...  47 us
    pallas_call x1, Pallas kernels, ffn(): pl.pallas_call(ffn_kernel, grid=(ROWS // BLOCK,), in_specs=[SMEM, ANY, AN...  35.5 us
    pallas_call x1, Pallas kernels, self_backward(): pl.pallas_call(self_backward_kernel, grid=(PAIRS, MICRO), in_specs=[swapp...  26 us
    pallas_call x1, Pallas kernels, cross_forward(): pl.pallas_call(cross_forward_kernel, grid=PAIR_GRID, in_specs=[SMEM, pair...  18.9 us
    pallas_call x1, Pallas kernels, self_forward(): pl.pallas_call(self_forward_kernel, grid=(PAIRS, MICRO), in_specs=[swappe...  16.6 us
    pallas_call x2, Pallas kernels, key_value(): pl.pallas_call(key_value_kernel, grid=(steps,), in_specs=[SMEM, ANY, ANY,...  16.3 us
  transfers between devices with their start and end apart: 43, of which 13 were waited for; matrix products, arithmetic and copies ran while one was open for 7% of the time, Pallas kernels for 48%

profile of v3, /device:TPU:0, one launch (start us, length us, event | category | flops | bytes accessed | tf_op | source)
XLA Modules:
  0.0 471.8 jit_solution(6093672304029961903)
XLA Ops:
  14.2 4.0 collective-permute-start.1
  19.8 8.5 %collective-permute-done.1 = bf16[2,24,2048]{2,1,0:T(8,128)(2,1)S(1)} collective-permute-done((bf16[2,24,2048]{2,1,0:T(8,128)(2,1)S(1)}, bf16[2,24,2048]{2,1,0:T(8,128)(2,1)S(1)}, u32[]{:S(2)}, u32[]{:S(2)}) %collective-permute-start.1) | collective-permute-done | bytes 196640 | tf_op jit(solution)/shard_map/ppermute | solution.py:1126
  28.3 4.7 %collective-permute-done.3 = bf16[2,24,2048]{2,1,0:T(8,128)(2,1)S(1)} collective-permute-done((bf16[2,24,2048]{2,1,0:T(8,128)(2,1)S(1)}, bf16[2,24,2048]{2,1,0:T(8,128)(2,1)S(1)}, u32[]{:S(2)}, u32[]{:S(2)}) %collective-permute-start.3) | collective-permute-done | bytes 196640 | tf_op jit(solution)/shard_map/ppermute | solution.py:1126
  41.4 3.8 collective-permute-start.9
  46.2 3.5 collective-permute-done.9
  49.9 3.7 collective-permute-start.10
  53.7 7.9 %bias_tiles.1.tiles_ref = f32[12,2,256,256]{3,2,1,0:T(8,128)} custom-call(f32[12,32]{1,0:T(8,128)} %convert_element_type.544.table_ref), custom_call_target="tpu_custom_call" | custom-call | flops 8 | tf_op jit(solution)/shard_map/bias_tiles/pallas_call | solution.py:741
  61.6 2.7 slice_bitcast_fusion
  64.3 4.2 collective-permute-done.10
  73.3 2.1 bitcast_dynamic-update-slice_fusion.1
  75.4 2.1 bitcast_dynamic-update-slice_fusion
  77.5 2.1 bitcast_dynamic-update-slice_fusion.3
  82.8 2.6 collective-permute-start.12
  85.6 9.0 %self_inputs.1 = (bf16[1024,768]{1,0:T(8,128)(2,1)S(1)}, bf16[1024,2304]{1,0:T(8,128)(2,1)}, f32[8,768]{1,0:T(8,128)S(1)}) custom-call(s32[1]{0:T(128)} %bitcast.core_ref, bf16[768,2048]{1,0:T(8,128)(2,1)} %bitcast.35.own_ref, bf16[768,2048]{1,0:T(8,128)(2,1)} %collective-permute-done.14.other_ref, bf16[1024,768]{1,0:T(8,128)(2,1)} %bitcast.252), custom_call_target="tpu_custom_call" | custom-call | flops 6 | tf_op jit(solution)/shard_map/self_inputs/pallas_call | solution.py:230
  95.8 16.6 %self_forward.1 = (bf16[1024,768]{1,0:T(8,128)(2,1)S(1)}, f32[12,8,512]{2,1,0:T(8,128)S(1)}) custom-call(bf16[1024,2304]{1,0:T(8,128)(2,1)} %get-tuple-element.209.q_ref.k_ref.v_ref, bf16[1024,2304]{1,0:T(8,128)(2,1)} %get-tuple-element.209.q_ref.k_ref.v_ref, bf16[1024,2304]{1,0:T(8,128)(2,1)} %get-tuple-element.209.q_ref.k_ref.v_ref, ...), custom_call_target="tpu_custom_call" | custom-call | flops 17 | tf_op jit(solution)/shard_map/self_forward/pallas_call | solution.py:1032
  113.6 10.0 %key_value.2 = (bf16[1536,1536]{1,0:T(8,128)(2,1)}, f32[8,128]{1,0:T(8,128)S(1)}) custom-call(s32[1]{0:T(128)} %bitcast.core_ref, bf16[768,2048]{1,0:T(8,128)(2,1)} %bitcast.35.own_ref, bf16[768,2048]{1,0:T(8,128)(2,1)} %collective-permute-done.14.other_ref, bf16[2048,768]{1,0:T(8,128)(2,1)} %bitcast.251), custom_call_target="tpu_custom_call" | custom-call | flops 6 | tf_op jit(solution)/shard_map/key_value/pallas_call | solution.py:200
  123.7 12.5 %collective-permute-done.12 = bf16[2,2,2,24,768]{4,3,2,1,0:T(8,128)(2,1)S(1)} collective-permute-done((bf16[2,2,2,24,768]{4,3,2,1,0:T(8,128)(2,1)S(1)}, bf16[2,2,2,24,768]{4,3,2,1,0:T(8,128)(2,1)S(1)}, u32[]{:S(2)}, u32[]{:S(2)}) %collective-permute-start.12) | collective-permute-done | bytes 294944 | tf_op jit(solution)/shard_map/ppermute | solution.py:1126
  137.8 7.5 %collective-permute-start.17 = (bf16[2,2,2,64,384]{4,3,2,1,0:T(8,128)(2,1)S(1)}, bf16[2,2,2,64,384]{4,3,2,1,0:T(8,128)(2,1)}, u32[]{:S(2)}, u32[]{:S(2)}) collective-permute-start(bf16[2,2,2,64,384]{4,3,2,1,0:T(8,128)(2,1)S(1)} %slice.76), channel_id=1, source_target_pairs={{0,1},{1,0},{2,3},{3,2},{4,5},{5,4},{6,7},{7,6},{8,9},{9,8},{10,11... | collective-permute-start | bytes 1179656 | tf_op jit(solution)/shard_map/ppermute | solution.py:1126
  145.3 6.3 %key_value.3 = (bf16[1024,1536]{1,0:T(8,128)(2,1)}, f32[8,128]{1,0:T(8,128)S(1)}) custom-call(s32[1]{0:T(128)} %bitcast.core_ref, bf16[768,2048]{1,0:T(8,128)(2,1)} %bitcast.35.own_ref, bf16[768,2048]{1,0:T(8,128)(2,1)} %collective-permute-done.14.other_ref, bf16[1024,768]{1,0:T(8,128)(2,1)S(1)} %bitcast.247), custom_call_target="tpu_custom_call" | custom-call | flops 4 | tf_op jit(solution)/shard_map/key_value/pallas_call | solution.py:200
  152.6 9.3 %cross_inputs.1 = (f32[1024,768]{1,0:T(8,128)}, bf16[1024,768]{1,0:T(8,128)(2,1)}, bf16[1024,768]{1,0:T(8,128)(2,1)}, f32[8,128]{1,0:T(8,128)S(1)}) custom-call(s32[1]{0:T(128)} %bitcast.core_ref, bf16[768,768]{1,0:T(8,128)(2,1)S(1)} %bitcast.245, bf16[768,768]{1,0:T(8,128)(2,1)} %copy-done.13, f32[8,768]{1,0:T(8,128)S(1)} %get-tuple-element.223.gain_ref, ...), custom_call_target="tpu_custom_call" | custom-call | flops 5 | tf_op jit(solution)/shard_map/cross_inputs/pallas_call | solution.py:260
  163.2 18.9 %cross_forward.1 = (bf16[1024,768]{1,0:T(8,128)(2,1)}, f32[12,8,512]{2,1,0:T(8,128)S(1)}) custom-call(s32[1]{0:T(128)} %bitcast.45.small_ref, bf16[1024,768]{1,0:T(8,128)(2,1)} %get-tuple-element.251.q_ref, bf16[1536,1536]{1,0:T(8,128)(2,1)} %get-tuple-element.252.ko_ref.vo_ref, bf16[1024,1536]{1,0:T(8,128)(2,1)} %get-tuple-element.253.kn_ref.vn_ref, ...), custom_call_target="tpu_custom_call" | custom-call | flops 32 | tf_op jit(solution)/shard_map/cross_forward/pallas_call | solution.py:967
  184.8 8.7 %collective-permute-start.20 = (bf16[2048,384]{1,0:T(8,128)(2,1)S(1)}, bf16[2048,384]{1,0:T(8,128)(2,1)S(1)}, u32[]{:S(2)}, u32[]{:S(2)}) collective-permute-start(bf16[2048,384]{1,0:T(8,128)(2,1)S(1)} %bitcast.259), channel_id=1, source_target_pairs={{0,8},{1,9},{2,10},{3,11},{4,12},{5,13},{6,14},{7,15},{8,0},{9,1},... | collective-permute-start | bytes 4718600 | tf_op jit(solution)/shard_map/ppermute | solution.py:1126
  193.5 3.0 collective-permute-done.20.other_ref
  197.7 35.5 %ffn.1 = (bf16[1024,768]{1,0:T(8,128)(2,1)}, bf16[1024,768]{1,0:T(8,128)(2,1)S(1)}, bf16[3,1024,2048]{2,1,0:T(8,128)(2,1)}, bf16[1024,768]{1,0:T(8,128)(2,1)}, f...) custom-call(s32[1]{0:T(128)} %bitcast.core_ref, ...), custom_call_target="tpu_custom_call" | custom-call | flops 30 | tf_op jit(solution)/shard_map/ffn/pallas_call | solution.py:357
  233.2 14.9 %ffn_weight_grads.1 = bf16[32,576,256]{2,1,0:T(8,128)(2,1)} custom-call(bf16[1024,768]{1,0:T(8,128)(2,1)S(1)} %get-tuple-element.245.h_ref, bf16[3,1024,2048]{2,1,0:T(8,128)(2,1)} %get-tuple-element.246.acts_ref, bf16[1024,768]{1,0:T(8,128)(2,1)} %bitcast.258), custom_call_target="tpu_custom_call" | custom-call | flops 13 | tf_op jit(solution)/shard_map/ffn_weight_grads/pallas_call | solution.py:580
  248.1 23.5 %cross_backward.2 = (bf16[512,768]{1,0:T(8,128)(2,1)S(1)}, bf16[2,768,768]{2,1,0:T(8,128)(2,1)}, bf16[2,512,768]{2,1,0:T(8,128)(2,1)}) custom-call(bf16[1024,768]{1,0:T(8,128)(2,1)} %get-tuple-element.251.q_ref, bf16[1536,1536]{1,0:T(8,128)(2,1)} %get-tuple-element.252.ko_ref.vo_ref, bf16[1024,1536]{1,0:T(8,128)(2,1)} %get-tuple-element.253.kn_ref.vn_ref, ...), custom_call_target="tpu_custom_call" | custom-call | flops 22 | tf_op jit(solution)/shard_map/cross_backward/pallas_call | solution.py:992
  271.7 4.7 memory_grads.2
  276.4 3.9 collective-permute-start.21
  280.3 23.5 %cross_backward.3 = (bf16[512,768]{1,0:T(8,128)(2,1)S(1)}, bf16[2,768,768]{2,1,0:T(8,128)(2,1)}, bf16[2,512,768]{2,1,0:T(8,128)(2,1)}) custom-call(bf16[1024,768]{1,0:T(8,128)(2,1)} %get-tuple-element.251.q_ref, bf16[1536,1536]{1,0:T(8,128)(2,1)} %get-tuple-element.252.ko_ref.vo_ref, bf16[1024,1536]{1,0:T(8,128)(2,1)} %get-tuple-element.253.kn_ref.vn_ref, ...), custom_call_target="tpu_custom_call" | custom-call | flops 22 | tf_op jit(solution)/shard_map/cross_backward/pallas_call | solution.py:992
  303.8 7.7 %pair_grads.2 = (bf16[2,192,1536]{2,1,0:T(8,128)(2,1)}, bf16[2,192,1536]{2,1,0:T(8,128)(2,1)}) custom-call(s32[1]{0:T(128)} %bitcast.core_ref, bf16[1024,768]{1,0:T(8,128)(2,1)} %get-tuple-element.255.o_ref.refs_0_, bf16[1024,768]{1,0:T(8,128)(2,1)} %get-tuple-element.274.refs_1_, bf16[1024,768]{1,0:T(8,128)(2,1)} %get-tuple-element.275.refs_2_, ...), custom_call_target="tpu_custom_call" | custom-call | flops 5 | tf_op jit(solution)/shard_map/pair_grads/pallas_call | solution.py:539
  311.5 4.9 %memory_grads.3 = bf16[512,768]{1,0:T(8,128)(2,1)S(1)} custom-call(s32[1]{0:T(128)} %bitcast.core_ref, bf16[768,2048]{1,0:T(8,128)(2,1)} %bitcast.35.own_ref, bf16[768,2048]{1,0:T(8,128)(2,1)} %collective-permute-done.14.other_ref, bf16[2,512,768]{2,1,0:T(8,128)(2,1)} %get-tuple-element.267.dkv_ref.after1_ref), custom_call_target="tpu_custom_call" | custom-call | flops 1 | tf_op jit(solution)/shard_map/memory_grads/pallas_call | solution.py:467
  316.4 13.3 %memory_weight_grads.1 = (bf16[2,192,1536]{2,1,0:T(8,128)(2,1)}, bf16[2,192,1536]{2,1,0:T(8,128)(2,1)}) custom-call(s32[1]{0:T(128)} %bitcast.core_ref, bf16[2,1,1024,768]{3,2,1,0:T(8,128)(2,1)} %mem_ref, bf16[1024,768]{1,0:T(8,128)(2,1)} %bitcast.248, bf16[2,768,768]{2,1,0:T(8,128)(2,1)} %get-tuple-element.319.own0_ref.dkv_ref, ...), custom_call_target="tpu_custom_call" | custom-call | flops 8 | tf_op jit(solution)/shard_map/memory_weight_grads/pallas_call | solution.py:618
  330.2 5.0 %collective-permute-start.25 = (bf16[512,768]{1,0:T(8,128)(2,1)S(1)}, bf16[512,768]{1,0:T(8,128)(2,1)S(1)}, u32[]{:S(2)}, u32[]{:S(2)}) collective-permute-start(bf16[512,768]{1,0:T(8,128)(2,1)S(1)} %memory_grads.3), channel_id=1, source_target_pairs={{0,1},{1,2},{2,3},{3,4},{4,5},{5,6},{6,7},{8,9},{9,10},{10,11},{11... | collective-permute-start | bytes 2359304 | tf_op jit(solution)/shard_map/ppermute | solution.py:1213
  335.2 9.9 %self_grads.1 = (f32[1024,768]{1,0:T(8,128)}, bf16[1024,768]{1,0:T(8,128)(2,1)}, bf16[1024,768]{1,0:T(8,128)(2,1)}, f32[8,768]{1,0:T(8,128)S(1)}) custom-call(s32[1]{0:T(128)} %bitcast.core_ref, bf16[768,768]{1,0:T(8,128)(2,1)} %bitcast.246, bf16[768,768]{1,0:T(8,128)(2,1)} %copy-done.13, f32[8,768]{1,0:T(8,128)S(1)} %get-tuple-element.223.gain_ref, ...), custom_call_target="tpu_custom_call" | custom-call | flops 5 | tf_op jit(solution)/shard_map/self_grads/pallas_call | solution.py:407
  345.2 3.7 pair_grads.3
  356.2 26.0 %self_backward.1 = (bf16[3,1024,768]{2,1,0:T(8,128)(2,1)}, f32[12,8,256]{2,1,0:T(8,128)S(1)}) custom-call(bf16[1024,2304]{1,0:T(8,128)(2,1)} %get-tuple-element.209.q_ref.k_ref.v_ref, bf16[1024,2304]{1,0:T(8,128)(2,1)} %get-tuple-element.209.q_ref.k_ref.v_ref, bf16[1024,2304]{1,0:T(8,128)(2,1)} %get-tuple-element.209.q_ref.k_ref.v_ref, ...), custom_call_target="tpu_custom_call" | custom-call | flops 24 | tf_op jit(solution)/shard_map/self_backward/pallas_call | solution.py:1051
  382.2 7.9 %row_grads.1 = (bf16[2,192,2304]{2,1,0:T(8,128)(2,1)}, bf16[2,192,2304]{2,1,0:T(8,128)(2,1)}) custom-call(s32[1]{0:T(128)} %bitcast.core_ref, bf16[1024,768]{1,0:T(8,128)(2,1)S(1)} %copy-done.6, bf16[3,1024,768]{2,1,0:T(8,128)(2,1)} %get-tuple-element.303.grads_ref.dqkv_ref), custom_call_target="tpu_custom_call" | custom-call | flops 5 | tf_op jit(solution)/shard_map/row_grads/pallas_call | solution.py:506
  390.1 4.2 collective-permute-done.27
  394.7 4.4 collective-permute-start.29
  399.1 10.8 %input_grads.1 = (bf16[1024,768]{1,0:T(8,128)(2,1)}, f32[8,768]{1,0:T(8,128)S(1)}) custom-call(s32[1]{0:T(128)} %bitcast.core_ref, bf16[768,2048]{1,0:T(8,128)(2,1)} %bitcast.35.own_ref, bf16[768,2048]{1,0:T(8,128)(2,1)} %collective-permute-done.14.other_ref, f32[8,768]{1,0:T(8,128)S(1)} %get-tuple-element.223.gain_ref, bf16[1024,768]{1,0:T(8,128)(2,1)} %bitcast.254, ...), custom_call_target="tpu_custom_call" | custom-call | flops 6 | tf_op jit(solution)/shard_map/input_grads/pallas_call | solution.py:444
  410.0 6.3 %collective-permute-done.29 = bf16[2,24,3840]{2,1,0:T(8,128)(2,1)S(1)} collective-permute-done((bf16[2,24,3840]{2,1,0:T(8,128)(2,1)S(1)}, bf16[2,24,3840]{2,1,0:T(8,128)(2,1)S(1)}, u32[]{:S(2)}, u32[]{:S(2)}) %collective-permute-start.29) | collective-permute-done | bytes 368672 | tf_op jit(solution)/shard_map/ppermute | solution.py:1126
  419.0 2.3 collective-permute-start.35
  421.3 6.6 %memory_total.2 = bf16[1024,768]{1,0:T(8,128)(2,1)} custom-call(s32[1]{0:T(128)} %bitcast.core_ref, bf16[768,2048]{1,0:T(8,128)(2,1)} %bitcast.35.own_ref, bf16[768,2048]{1,0:T(8,128)(2,1)} %collective-permute-done.14.other_ref, bf16[2,768,768]{2,1,0:T(8,128)(2,1)} %get-tuple-element.319.own0_ref.dkv_ref, bf16[512,768]{1,0:T(8,128)(2,1)S(1)} %collective-permute-done.21.prev_ref), custom_call_target="tpu_custom_call" | custom-call | flops 4 | tf_op jit(solution)/shard_map/memory_total/pallas_call | solution.py:653
  428.4 6.6 %memory_total.3 = bf16[1024,768]{1,0:T(8,128)(2,1)} custom-call(s32[1]{0:T(128)} %bitcast.core_ref, bf16[768,2048]{1,0:T(8,128)(2,1)} %bitcast.35.own_ref, bf16[768,2048]{1,0:T(8,128)(2,1)} %collective-permute-done.14.other_ref, bf16[2,768,768]{2,1,0:T(8,128)(2,1)} %get-tuple-element.327.own1_ref.dkv_ref, bf16[512,768]{1,0:T(8,128)(2,1)S(1)} %collective-permute-done.25.prev_ref), custom_call_target="tpu_custom_call" | custom-call | flops 4 | tf_op jit(solution)/shard_map/memory_total/pallas_call | solution.py:653
  435.0 6.9 %collective-permute-done.32 = bf16[2,2,2,24,256]{4,3,1,0,2:T(8,128)(2,1)S(1)} collective-permute-done((bf16[2,2,2,24,256]{4,3,1,0,2:T(8,128)(2,1)S(1)}, bf16[2,2,2,24,256]{4,3,1,0,2:T(8,128)(2,1)S(1)}, u32[]{:S(2)}, u32[]{:S(2)}) %collective-permute-start.32) | collective-permute-done | bytes 98336 | tf_op jit(solution)/shard_map/ppermute | solution.py:1126
  442.8 3.3 collective-permute-done.36
  452.2 2.3 collective-permute-start.39
  458.8 3.8 collective-permute-done.38
  (212 shorter events, 60.2 us)
Async XLA Ops:
  7.2 189.3 %all-gather.2.cloned.1.call-start = ((), (), s32[]{:S(2)}) async-start(), calls=%async_computation.1 | async-start | bytes 7704576 | tf_op jit(solution)/shard_map/all_gather | solution.py:1308
  12.6 1.5 collective-permute-start
  14.2 22.9 %copy-start.20 = (bf16[64,768]{1,0:T(8,128)(2,1)S(1)}, bf16[64,768]{1,0:T(8,128)(2,1)}, u32[]{:S(2)}) copy-start(bf16[64,768]{1,0:T(8,128)(2,1)} %param.32) | copy-start | bytes 294916
  14.2 14.1 %collective-permute-start.1 = (bf16[2,24,2048]{2,1,0:T(8,128)(2,1)S(1)}, bf16[2,24,2048]{2,1,0:T(8,128)(2,1)S(1)}, u32[]{:S(2)}, u32[]{:S(2)}) collective-permute-start(bf16[2,24,2048]{2,1,0:T(8,128)(2,1)S(1)} %pad_maximum_fusion.6), channel_id=1, source_target_pairs={{0,4},{1,5},{2,6},{3,7},{4,0},{5,1},{6,2},{7,3},{8,12},{9,13},{10,... | collective-permute-start | bytes 589832 | tf_op jit(solution)/shard_map/ppermute | solution.py:1126
  18.2 10.1 %collective-permute-start.2 = (bf16[2,24,2048]{2,1,0:T(8,128)(2,1)S(1)}, bf16[2,24,2048]{2,1,0:T(8,128)(2,1)S(1)}, u32[]{:S(2)}, u32[]{:S(2)}) collective-permute-start(bf16[2,24,2048]{2,1,0:T(8,128)(2,1)S(1)} %pad_maximum_fusion.6), channel_id=1, source_target_pairs={{0,2},{1,3},{2,0},{3,1},{4,6},{5,7},{6,4},{7,5},{8,10},{9,11},{10,... | collective-permute-start | bytes 589832 | tf_op jit(solution)/shard_map/ppermute | solution.py:1126
  19.8 13.3 %collective-permute-start.3 = (bf16[2,24,2048]{2,1,0:T(8,128)(2,1)S(1)}, bf16[2,24,2048]{2,1,0:T(8,128)(2,1)S(1)}, u32[]{:S(2)}, u32[]{:S(2)}) collective-permute-start(bf16[2,24,2048]{2,1,0:T(8,128)(2,1)S(1)} %pad_maximum_fusion.6), channel_id=1, source_target_pairs={{0,6},{1,7},{2,4},{3,5},{4,2},{5,3},{6,0},{7,1},{8,14},{9,15},{10,... | collective-permute-start | bytes 589832 | tf_op jit(solution)/shard_map/ppermute | solution.py:1126
  33.3 35.4 %collective-permute-start.4 = (bf16[2,2,2,24,2048]{4,3,2,1,0:T(8,128)(2,1)S(1)}, bf16[2,2,2,24,2048]{4,3,2,1,0:T(8,128)(2,1)}, u32[]{:S(2)}, u32[]{:S(2)}) collective-permute-start(bf16[2,2,2,24,2048]{4,3,2,1,0:T(8,128)(2,1)S(1)} %bitcast_dynamic-update-slice_fusion.14), channel_id=1, source_target_pairs={{0,16},{1,17},{2,18},{3,19},{4,20},{5,21},{6,22},{7,23},{8,24},{9,... | collective-permute-start | bytes 2359304 | tf_op jit(solution)/shard_map/ppermute | solution.py:1126
  34.8 35.4 %collective-permute-start.5 = (bf16[2,2,2,24,2048]{4,3,2,1,0:T(8,128)(2,1)S(1)}, bf16[2,2,2,24,2048]{4,3,2,1,0:T(8,128)(2,1)}, u32[]{:S(2)}, u32[]{:S(2)}) collective-permute-start(bf16[2,2,2,24,2048]{4,3,2,1,0:T(8,128)(2,1)S(1)} %bitcast_dynamic-update-slice_fusion.14), channel_id=1, source_target_pairs={{0,1},{1,0},{2,3},{3,2},{4,5},{5,4},{6,7},{7,6},{8,9},{9,8},{10,11... | collective-permute-start | bytes 2359304 | tf_op jit(solution)/shard_map/ppermute | solution.py:1126
  36.4 33.9 %collective-permute-start.6 = (bf16[2,2,2,24,2048]{4,3,2,1,0:T(8,128)(2,1)S(1)}, bf16[2,2,2,24,2048]{4,3,2,1,0:T(8,128)(2,1)}, u32[]{:S(2)}, u32[]{:S(2)}) collective-permute-start(bf16[2,2,2,24,2048]{4,3,2,1,0:T(8,128)(2,1)S(1)} %bitcast_dynamic-update-slice_fusion.14), channel_id=1, source_target_pairs={{0,17},{1,16},{2,19},{3,18},{4,21},{5,20},{6,23},{7,22},{8,25},{9,... | collective-permute-start | bytes 2359304 | tf_op jit(solution)/shard_map/ppermute | solution.py:1126
  37.0 4.2 collective-permute-start.7
  37.4 4.0 collective-permute-start.8
  41.4 8.4 %collective-permute-start.9 = (bf16[2,112,384]{2,1,0:T(8,128)(2,1)S(1)}, bf16[2,112,384]{2,1,0:T(8,128)(2,1)S(1)}, u32[]{:S(2)}, u32[]{:S(2)}) collective-permute-start(bf16[2,112,384]{2,1,0:T(8,128)(2,1)S(1)} %maximum_maximum_fusion), channel_id=1, source_target_pairs={{0,2},{1,3},{2,0},{3,1},{4,6},{5,7},{6,4},{7,5},{8,10},{9,11},{10,... | collective-permute-start | bytes 516104 | tf_op jit(solution)/shard_map/ppermute | solution.py:1126
  49.9 18.6 %collective-permute-start.10 = (bf16[2,2,112,384]{3,2,1,0:T(8,128)(2,1)S(1)}, bf16[2,2,112,384]{3,2,1,0:T(8,128)(2,1)S(1)}, u32[]{:S(2)}, u32[]{:S(2)}) collective-permute-start(bf16[2,2,112,384]{3,2,1,0:T(8,128)(2,1)S(1)} %bitcast_dynamic-update-slice_fusion.18), channel_id=1, source_target_pairs={{0,4},{1,5},{2,6},{3,7},{4,0},{5,1},{6,2},{7,3},{8,12},{9,13},{10,... | collective-permute-start | bytes 1032200 | tf_op jit(solution)/shard_map/ppermute | solution.py:1126
  53.7 109.5 %copy-start.3 = (bf16[2,1280,128]{2,1,0:T(8,128)(2,1)}, bf16[2,1280,128]{2,1,0:T(8,128)(2,1)S(1)}, u32[]{:S(2)}) copy-start(bf16[2,1280,128]{2,1,0:T(8,128)(2,1)S(1)} %pad_maximum_fusion.4.mask_ref) | copy-start | bytes 1966084
  70.2 380.1 %reduce-scatter.2.cloned.1.call-start = ((), (), s32[]{:S(2)}) async-start(), calls=%async_computation.2 | async-start | bytes 9732096 | tf_op jit(solution)/shard_map/reduce_scatter | solution.py:1234
  79.6 6.1 %collective-permute-start.14 = (bf16[768,2048]{1,0:T(8,128)(2,1)}, bf16[768,2048]{1,0:T(8,128)(2,1)}, u32[]{:S(2)}, u32[]{:S(2)}) collective-permute-start(bf16[768,2048]{1,0:T(8,128)(2,1)} %bitcast.35.own_ref), channel_id=1, source_target_pairs={{0,8},{1,9},{2,10},{3,11},{4,12},{5,13},{6,14},{7,15},{8,0},{9,1},... | collective-permute-start | bytes 9437192 | tf_op jit(solution)/shard_map/ppermute | solution.py:1126
  79.6 56.5 %collective-permute-start.15 = (bf16[2,512,768]{2,1,0:T(8,128)(2,1)}, bf16[2,512,768]{2,1,0:T(8,128)(2,1)S(1)}, u32[]{:S(2)}, u32[]{:S(2)}) collective-permute-start(bf16[2,512,768]{2,1,0:T(8,128)(2,1)} %slice_bitcast_fusion), channel_id=1, source_target_pairs={{1,0},{2,1},{3,2},{4,3},{5,4},{6,5},{7,6},{9,8},{10,9},{11,10},{12... | collective-permute-start | bytes 4718600 | tf_op jit(solution)/shard_map/ppermute | solution.py:1213
  81.5 42.2 %collective-permute-start.11 = (bf16[2,2,2,24,768]{4,3,2,1,0:T(8,128)(2,1)S(1)}, bf16[2,2,2,24,768]{4,3,2,1,0:T(8,128)(2,1)S(1)}, u32[]{:S(2)}, u32[]{:S(2)}) collective-permute-start(bf16[2,2,2,24,768]{4,3,2,1,0:T(8,128)(2,1)S(1)} %reshape.611), channel_id=1, source_target_pairs={{0,16},{1,17},{2,18},{3,19},{4,20},{5,21},{6,22},{7,23},{8,24},{9,... | collective-permute-start | bytes 884744 | tf_op jit(solution)/shard_map/ppermute | solution.py:1126
  82.8 53.3 %collective-permute-start.12 = (bf16[2,2,2,24,768]{4,3,2,1,0:T(8,128)(2,1)S(1)}, bf16[2,2,2,24,768]{4,3,2,1,0:T(8,128)(2,1)S(1)}, u32[]{:S(2)}, u32[]{:S(2)}) collective-permute-start(bf16[2,2,2,24,768]{4,3,2,1,0:T(8,128)(2,1)S(1)} %reshape.611), channel_id=1, source_target_pairs={{0,1},{1,0},{2,3},{3,2},{4,5},{5,4},{6,7},{7,6},{8,9},{9,8},{10,11... | collective-permute-start | bytes 884744 | tf_op jit(solution)/shard_map/ppermute | solution.py:1126
  85.4 50.7 %collective-permute-start.13 = (bf16[2,2,2,24,768]{4,3,2,1,0:T(8,128)(2,1)S(1)}, bf16[2,2,2,24,768]{4,3,2,1,0:T(8,128)(2,1)S(1)}, u32[]{:S(2)}, u32[]{:S(2)}) collective-permute-start(bf16[2,2,2,24,768]{4,3,2,1,0:T(8,128)(2,1)S(1)} %reshape.611), channel_id=1, source_target_pairs={{0,17},{1,16},{2,19},{3,18},{4,21},{5,20},{6,23},{7,22},{8,25},{9,... | collective-permute-start | bytes 884744 | tf_op jit(solution)/shard_map/ppermute | solution.py:1126
  136.4 15.2 %copy-start.2 = (bf16[2,2,2,2,2,24,768]{6,5,4,3,2,1,0:T(8,128)(2,1)}, bf16[2,2,2,2,2,24,768]{6,5,4,3,2,1,0:T(8,128)(2,1)S(1)}, u32[]{:S(2)}) copy-start(bf16[2,2,2,2,2,24,768]{6,5,4,3,2,1,0:T(8,128)(2,1)S(1)} %bitcast_dynamic-update-slice_fusion.13) | copy-start | bytes 3538948
  136.4 15.2 %collective-permute-start.19 = (bf16[768,768]{1,0:T(8,128)(2,1)S(1)}, bf16[768,768]{1,0:T(8,128)(2,1)S(1)}, u32[]{:S(2)}, u32[]{:S(2)}) collective-permute-start(bf16[768,768]{1,0:T(8,128)(2,1)S(1)} %bitcast.244), channel_id=1, source_target_pairs={{0,8},{1,9},{2,10},{3,11},{4,12},{5,13},{6,14},{7,15},{8,0},{9,1},... | collective-permute-start | bytes 3538952 | tf_op jit(solution)/shard_map/ppermute | solution.py:1126
  136.5 45.5 %collective-permute-start.16 = (bf16[2,2,2,64,384]{4,3,2,1,0:T(8,128)(2,1)S(1)}, bf16[2,2,2,64,384]{4,3,2,1,0:T(8,128)(2,1)S(1)}, u32[]{:S(2)}, u32[]{:S(2)}) collective-permute-start(bf16[2,2,2,64,384]{4,3,2,1,0:T(8,128)(2,1)S(1)} %slice.76), channel_id=1, source_target_pairs={{0,16},{1,17},{2,18},{3,19},{4,20},{5,21},{6,22},{7,23},{8,24},{9,... | collective-permute-start | bytes 1179656 | tf_op jit(solution)/shard_map/ppermute | solution.py:1126
  137.8 44.2 %collective-permute-start.17 = (bf16[2,2,2,64,384]{4,3,2,1,0:T(8,128)(2,1)S(1)}, bf16[2,2,2,64,384]{4,3,2,1,0:T(8,128)(2,1)}, u32[]{:S(2)}, u32[]{:S(2)}) collective-permute-start(bf16[2,2,2,64,384]{4,3,2,1,0:T(8,128)(2,1)S(1)} %slice.76), channel_id=1, source_target_pairs={{0,1},{1,0},{2,3},{3,2},{4,5},{5,4},{6,7},{7,6},{8,9},{9,8},{10,11... | collective-permute-start | bytes 1179656 | tf_op jit(solution)/shard_map/ppermute | solution.py:1126
  145.3 36.7 %collective-permute-start.18 = (bf16[2,2,2,64,384]{4,3,2,1,0:T(8,128)(2,1)S(1)}, bf16[2,2,2,64,384]{4,3,2,1,0:T(8,128)(2,1)}, u32[]{:S(2)}, u32[]{:S(2)}) collective-permute-start(bf16[2,2,2,64,384]{4,3,2,1,0:T(8,128)(2,1)S(1)} %slice.76), channel_id=1, source_target_pairs={{0,17},{1,16},{2,19},{3,18},{4,21},{5,20},{6,23},{7,22},{8,25},{9,... | collective-permute-start | bytes 1179656 | tf_op jit(solution)/shard_map/ppermute | solution.py:1126
  184.8 11.7 %collective-permute-start.20 = (bf16[2048,384]{1,0:T(8,128)(2,1)S(1)}, bf16[2048,384]{1,0:T(8,128)(2,1)S(1)}, u32[]{:S(2)}, u32[]{:S(2)}) collective-permute-start(bf16[2048,384]{1,0:T(8,128)(2,1)S(1)} %bitcast.259), channel_id=1, source_target_pairs={{0,8},{1,9},{2,10},{3,11},{4,12},{5,13},{6,14},{7,15},{8,0},{9,1},... | collective-permute-start | bytes 4718600 | tf_op jit(solution)/shard_map/ppermute | solution.py:1126
  276.4 40.1 %collective-permute-start.21 = (bf16[512,768]{1,0:T(8,128)(2,1)S(1)}, bf16[512,768]{1,0:T(8,128)(2,1)S(1)}, u32[]{:S(2)}, u32[]{:S(2)}) collective-permute-start(bf16[512,768]{1,0:T(8,128)(2,1)S(1)} %memory_grads.2), channel_id=1, source_target_pairs={{0,1},{1,2},{2,3},{3,4},{4,5},{5,6},{6,7},{8,9},{9,10},{10,11},{11... | collective-permute-start | bytes 2359304 | tf_op jit(solution)/shard_map/ppermute | solution.py:1213
  311.5 33.7 %collective-permute-start.22 = (bf16[2,192,1536]{2,1,0:T(8,128)(2,1)}, bf16[2,192,1536]{2,1,0:T(8,128)(2,1)}, u32[]{:S(2)}, u32[]{:S(2)}) collective-permute-start(bf16[2,192,1536]{2,1,0:T(8,128)(2,1)} %get-tuple-element.277), channel_id=1, source_target_pairs={{0,8},{1,9},{2,10},{3,11},{4,12},{5,13},{6,14},{7,15},{8,0},{9,1},... | collective-permute-start | bytes 3538952 | tf_op jit(solution)/shard_map/ppermute | solution.py:1126
  329.7 15.5 %collective-permute-start.23 = (bf16[2,192,1536]{2,1,0:T(8,128)(2,1)}, bf16[2,192,1536]{2,1,0:T(8,128)(2,1)}, u32[]{:S(2)}, u32[]{:S(2)}) collective-permute-start(bf16[2,192,1536]{2,1,0:T(8,128)(2,1)} %get-tuple-element.279), channel_id=1, source_target_pairs={{0,8},{1,9},{2,10},{3,11},{4,12},{5,13},{6,14},{7,15},{8,0},{9,1},... | collective-permute-start | bytes 3538952 | tf_op jit(solution)/shard_map/ppermute | solution.py:1126
  330.2 52.0 %collective-permute-start.25 = (bf16[512,768]{1,0:T(8,128)(2,1)S(1)}, bf16[512,768]{1,0:T(8,128)(2,1)S(1)}, u32[]{:S(2)}, u32[]{:S(2)}) collective-permute-start(bf16[512,768]{1,0:T(8,128)(2,1)S(1)} %memory_grads.3), channel_id=1, source_target_pairs={{0,1},{1,2},{2,3},{3,4},{4,5},{5,6},{6,7},{8,9},{9,10},{10,11},{11... | collective-permute-start | bytes 2359304 | tf_op jit(solution)/shard_map/ppermute | solution.py:1213
  348.9 3.3 collective-permute-start.24
  352.6 37.5 %collective-permute-start.26 = (bf16[2,2,24,3840]{3,2,1,0:T(8,128)(2,1)S(1)}, bf16[2,2,24,3840]{3,2,1,0:T(8,128)(2,1)S(1)}, u32[]{:S(2)}, u32[]{:S(2)}) collective-permute-start(bf16[2,2,24,3840]{3,2,1,0:T(8,128)(2,1)S(1)} %pad_maximum_fusion.1), channel_id=1, source_target_pairs={{0,16},{1,17},{2,18},{3,19},{4,20},{5,21},{6,22},{7,23},{8,24},{9,... | collective-permute-start | bytes 2211848 | tf_op jit(solution)/shard_map/ppermute | solution.py:1126
  353.4 40.9 %collective-permute-start.27 = (bf16[2,2,24,3840]{3,2,1,0:T(8,128)(2,1)S(1)}, bf16[2,2,24,3840]{3,2,1,0:T(8,128)(2,1)S(1)}, u32[]{:S(2)}, u32[]{:S(2)}) collective-permute-start(bf16[2,2,24,3840]{3,2,1,0:T(8,128)(2,1)S(1)} %pad_maximum_fusion.2), channel_id=1, source_target_pairs={{0,1},{1,0},{2,3},{3,2},{4,5},{5,4},{6,7},{7,6},{8,9},{9,8},{10,11... | collective-permute-start | bytes 2211848 | tf_op jit(solution)/shard_map/ppermute | solution.py:1126
  354.5 39.8 %collective-permute-start.28 = (bf16[2,2,24,3840]{3,2,1,0:T(8,128)(2,1)S(1)}, bf16[2,2,24,3840]{3,2,1,0:T(8,128)(2,1)S(1)}, u32[]{:S(2)}, u32[]{:S(2)}) collective-permute-start(bf16[2,2,24,3840]{3,2,1,0:T(8,128)(2,1)S(1)} %pad_maximum_fusion.3), channel_id=1, source_target_pairs={{0,17},{1,16},{2,19},{3,18},{4,21},{5,20},{6,23},{7,22},{8,25},{9,... | collective-permute-start | bytes 2211848 | tf_op jit(solution)/shard_map/ppermute | solution.py:1126
  356.2 26.0 %copy-start.6 = (bf16[1024,768]{1,0:T(8,128)(2,1)S(1)}, bf16[1024,768]{1,0:T(8,128)(2,1)}, u32[]{:S(2)}) copy-start(bf16[1024,768]{1,0:T(8,128)(2,1)} %copy-done.5) | copy-start | bytes 4718596
  394.3 22.0 %collective-permute-start.30 = (bf16[2,192,2304]{2,1,0:T(8,128)(2,1)}, bf16[2,192,2304]{2,1,0:T(8,128)(2,1)S(1)}, u32[]{:S(2)}, u32[]{:S(2)}) collective-permute-start(bf16[2,192,2304]{2,1,0:T(8,128)(2,1)} %get-tuple-element.309), channel_id=1, source_target_pairs={{0,8},{1,9},{2,10},{3,11},{4,12},{5,13},{6,14},{7,15},{8,0},{9,1},... | collective-permute-start | bytes 5308424 | tf_op jit(solution)/shard_map/ppermute | solution.py:1126
  394.7 21.6 %collective-permute-start.29 = (bf16[2,24,3840]{2,1,0:T(8,128)(2,1)S(1)}, bf16[2,24,3840]{2,1,0:T(8,128)(2,1)S(1)}, u32[]{:S(2)}, u32[]{:S(2)}) collective-permute-start(bf16[2,24,3840]{2,1,0:T(8,128)(2,1)S(1)} %get-tuple-element.307), channel_id=1, source_target_pairs={{0,4},{1,5},{2,6},{3,7},{4,0},{5,1},{6,2},{7,3},{8,12},{9,13},{10,... | collective-permute-start | bytes 1105928 | tf_op jit(solution)/shard_map/ppermute | solution.py:1126
  399.1 18.0 %copy-start.14 = (bf16[2,192,2304]{2,1,0:T(8,128)(2,1)S(1)}, bf16[2,192,2304]{2,1,0:T(8,128)(2,1)}, u32[]{:S(2)}) copy-start(bf16[2,192,2304]{2,1,0:T(8,128)(2,1)} %get-tuple-element.308) | copy-start | bytes 5308420
  417.6 10.2 %collective-permute-start.31 = (bf16[2,192,256]{2,1,0:T(8,128)(2,1)S(1)}, bf16[2,192,256]{2,1,0:T(8,128)(2,1)S(1)}, u32[]{:S(2)}, u32[]{:S(2)}) collective-permute-start(bf16[2,192,256]{2,1,0:T(8,128)(2,1)S(1)} %get-tuple-element.322), channel_id=1, source_target_pairs={{0,8},{1,9},{2,10},{3,11},{4,12},{5,13},{6,14},{7,15},{8,0},{9,1},... | collective-permute-start | bytes 589832 | tf_op jit(solution)/shard_map/ppermute | solution.py:1126
  417.7 28.4 %collective-permute-start.33 = (bf16[2,2,24,2304]{3,2,1,0:T(8,128)(2,1)S(1)}, bf16[2,2,24,2304]{3,2,1,0:T(8,128)(2,1)S(1)}, u32[]{:S(2)}, u32[]{:S(2)}) collective-permute-start(bf16[2,2,24,2304]{3,2,1,0:T(8,128)(2,1)S(1)} %get-tuple-element.333), channel_id=1, source_target_pairs={{0,16},{1,17},{2,18},{3,19},{4,20},{5,21},{6,22},{7,23},{8,24},{9,... | collective-permute-start | bytes 1327112 | tf_op jit(solution)/shard_map/ppermute | solution.py:1126
  418.2 27.9 %collective-permute-start.34 = (bf16[2,2,24,2304]{3,2,1,0:T(8,128)(2,1)S(1)}, bf16[2,2,24,2304]{3,2,1,0:T(8,128)(2,1)}, u32[]{:S(2)}, u32[]{:S(2)}) collective-permute-start(bf16[2,2,24,2304]{3,2,1,0:T(8,128)(2,1)S(1)} %get-tuple-element.334), channel_id=1, source_target_pairs={{0,1},{1,0},{2,3},{3,2},{4,5},{5,4},{6,7},{7,6},{8,9},{9,8},{10,11... | collective-permute-start | bytes 1327112 | tf_op jit(solution)/shard_map/ppermute | solution.py:1126
  419.0 27.1 %collective-permute-start.35 = (bf16[2,2,24,2304]{3,2,1,0:T(8,128)(2,1)S(1)}, bf16[2,2,24,2304]{3,2,1,0:T(8,128)(2,1)}, u32[]{:S(2)}, u32[]{:S(2)}) collective-permute-start(bf16[2,2,24,2304]{3,2,1,0:T(8,128)(2,1)S(1)} %get-tuple-element.335), channel_id=1, source_target_pairs={{0,17},{1,16},{2,19},{3,18},{4,21},{5,20},{6,23},{7,22},{8,25},{9,... | collective-permute-start | bytes 1327112 | tf_op jit(solution)/shard_map/ppermute | solution.py:1126
  427.9 14.0 %collective-permute-start.32 = (bf16[2,2,2,24,256]{4,3,1,0,2:T(8,128)(2,1)S(1)}, bf16[2,2,2,24,256]{4,3,1,0,2:T(8,128)(2,1)S(1)}, u32[]{:S(2)}, u32[]{:S(2)}) collective-permute-start(bf16[2,2,2,24,256]{4,3,1,0,2:T(8,128)(2,1)S(1)} %get-tuple-element.330), channel_id=1, source_target_pairs={{0,16},{1,17},{2,18},{3,19},{4,20},{5,21},{6,22},{7,23},{8,24},{9,... | collective-permute-start | bytes 294920 | tf_op jit(solution)/shard_map/ppermute | solution.py:1126
  441.9 4.2 collective-permute-start.36
  442.8 7.6 %collective-permute-start.37 = (bf16[24,3840]{1,0:T(8,128)(2,1)S(1)}, bf16[24,3840]{1,0:T(8,128)(2,1)S(1)}, u32[]{:S(2)}, u32[]{:S(2)}) collective-permute-start(bf16[24,3840]{1,0:T(8,128)(2,1)S(1)} %get-tuple-element.347), channel_id=1, source_target_pairs={{0,2},{1,3},{2,0},{3,1},{4,6},{5,7},{6,4},{7,5},{8,10},{9,11},{10,... | collective-permute-start | bytes 552968 | tf_op jit(solution)/shard_map/ppermute | solution.py:1126
  452.2 10.4 %collective-permute-start.38 = (bf16[24,2560]{1,0:T(8,128)(2,1)S(1)}, bf16[24,2560]{1,0:T(8,128)(2,1)S(1)}, u32[]{:S(2)}, u32[]{:S(2)}) collective-permute-start(bf16[24,2560]{1,0:T(8,128)(2,1)S(1)} %pad_maximum_fusion.8), channel_id=1, source_target_pairs={{0,4},{1,5},{2,6},{3,7},{4,0},{5,1},{6,2},{7,3},{8,12},{9,13},{10,... | collective-permute-start | bytes 368648 | tf_op jit(solution)/shard_map/ppermute | solution.py:1126
  452.2 10.4 %collective-permute-start.39 = (bf16[24,2560]{1,0:T(8,128)(2,1)S(1)}, bf16[24,2560]{1,0:T(8,128)(2,1)S(1)}, u32[]{:S(2)}, u32[]{:S(2)}) collective-permute-start(bf16[24,2560]{1,0:T(8,128)(2,1)S(1)} %pad_maximum_fusion.9), channel_id=1, source_target_pairs={{0,2},{1,3},{2,0},{3,1},{4,6},{5,7},{6,4},{7,5},{8,10},{9,11},{10,... | collective-permute-start | bytes 368648 | tf_op jit(solution)/shard_map/ppermute | solution.py:1126
  454.6 8.0 %collective-permute-start.40 = (bf16[24,2560]{1,0:T(8,128)(2,1)S(1)}, bf16[24,2560]{1,0:T(8,128)(2,1)S(1)}, u32[]{:S(2)}, u32[]{:S(2)}) collective-permute-start(bf16[24,2560]{1,0:T(8,128)(2,1)S(1)} %pad_maximum_fusion.10), channel_id=1, source_target_pairs={{0,6},{1,7},{2,4},{3,5},{4,2},{5,3},{6,0},{7,1},{8,14},{9,15},{10,... | collective-permute-start | bytes 368648 | tf_op jit(solution)/shard_map/ppermute | solution.py:1126
  (21 other events, 108.3 us)
Sparse Core Ops, SparseCore 0:
  70.4 98.4 all-gather.1
  248.2 151.6 reduce-scatter.1

commit v4 on v3

--- a/solution.py
+++ b/solution.py
@@ -718,6 +718,61 @@
         cost_estimate=cost(2),
         name="extras",
     )(core, sums, *norms)
+
+
+def packed_kernel(core_ref, *refs):
+    here_ref, there_ref = refs[-2:]
+    joined = jnp.concatenate([ref[...] for ref in refs[:-2]], axis=1)
+    halves = joined[:, :HALF_COLUMNS], joined[:, HALF_COLUMNS:]
+    for side in range(2):
+
+        @pl.when(core_ref[0] == side)
+        def _():
+            here_ref[...] = halves[side]
+            there_ref[...] = halves[1 - side]
+
+
+def packed(core, parts):
+    whole = pl.BlockSpec(memory_space=pltpu.VMEM)
+    piece = shape(parts[0].shape[0], HALF_COLUMNS)
+    return pl.pallas_call(
+        packed_kernel,
+        in_specs=[SMEM] + [whole] * len(parts),
+        out_specs=[whole, whole],
+        out_shape=[piece, piece],
+        compiler_params=params(),
+        cost_estimate=cost(1),
+        name="packed",
+    )(core, *parts)
+
+
+def assembled_kernel(place_ref, *refs):
+    out_ref = refs[-1]
+    for step, piece_ref in enumerate(refs[:-1]):
+
+        @pl.when(pl.program_id(0) == step)
+        def _():
+            out_ref[0, :, 0] = piece_ref[...]
+
+
+def assembled(place, pieces):
+    count, rows, columns = pieces[0].shape
+    return pl.pallas_call(
+        assembled_kernel,
+        grid_spec=pltpu.PrefetchScalarGridSpec(
+            num_scalar_prefetch=1,
+            grid=(4,),
+            in_specs=[pl.BlockSpec((count, rows, columns), lambda i, place: (0, 0, 0))] * 4,
+            out_specs=pl.BlockSpec(
+                (1, count, 1, rows, columns),
+                lambda i, place: (place[0] ^ (i // 2), 0, place[1] ^ (i % 2), 0, 0),
+            ),
+        ),
+        out_shape=jax.ShapeDtypeStruct((2, count, 2, rows, columns), BF),
+        compiler_params=params(),
+        cost_estimate=cost(3),
+        name="assembled",
+    )(place, *pieces)
 
 
 def bias_tiles_kernel(table_ref, tiles_ref):
@@ -1134,6 +1189,11 @@
     turns = [[0] * len(group)] + list(flips(group))
     pieces = [held] + [exchange(held, group, flip) for flip in turns[1:]]
     pieces, fillers = tied(pieces, fillers)
+    if len(group) == 2 and joined[0] == group[0] and joined[-1] == group[1] and tail[0] % 8 == 0:
+        place = jnp.stack([mine(bit) for bit in group]).astype(jnp.int32)
+        order = [turns.index([first, last]) for first in range(2) for last in range(2)]
+        flat = [pieces[turn].reshape((-1,) + tail) for turn in order]
+        return assembled(place, flat).reshape((2,) * len(joined) + tail), joined, fillers
     result = jnp.zeros((2,) * len(joined) + tail, held.dtype)
     for flip, piece in zip(turns, pieces):
         start = [mine(bit) ^ flip[group.index(bit)] if bit in group else 0 for bit in joined]
@@ -1145,6 +1205,10 @@
     halves = shard.reshape(shard.shape[0], 2, -1)
     here = lax.dynamic_index_in_dim(halves, core, 1, keepdims=False)
     there = lax.dynamic_index_in_dim(halves, 1 - core, 1, keepdims=False)
+    return swapped_halves(here, there, core)
+
+
+def swapped_halves(here, there, core):
     received = exchange(there, bit_groups()[0], [1])
     return jnp.stack([jnp.where(core == 0, here, received), jnp.where(core == 0, received, here)])
 
@@ -1282,12 +1346,12 @@
 
     gains = jnp.stack([norm_self, norm_cross, norm_ffn], axis=1)
     gains = jnp.pad(gains, ((0, 0), (0, 2 * LANES - 3)))
-    first = jnp.concatenate(
-        [cross_key, cross_value, self_query, self_key, self_value, gains], axis=1
+    first = packed(
+        core_id, [cross_key, cross_value, self_query, self_key, self_value, gains]
     )
     second = jnp.concatenate([self_out, cross_query], axis=1)
     late = jnp.concatenate([cross_out, ffn_gate, ffn_up], axis=1)
-    first = paired_halves(first, core)
+    first = swapped_halves(*first, core)
     first, dims, _ = gather_stage(first, core_bits, column)
     first, second, ffn_down, doc_offsets, memory, bias_table = lax.optimization_barrier(
         (first, second, ffn_down, doc_offsets, memory, bias_table)
@@ -1374,20 +1438,19 @@
     dqkv, cross_parts = tied(dqkv, cross_parts)
     cross_terms = scattered(cross_parts, high)
     grad_decoder, g_norm_self = input_grads(core_id, own, other, gains, x, dx1, dqkv)
-    g_norm_self, cross_terms, self_terms = lax.optimization_barrier(
-        (g_norm_self, cross_terms, self_terms)
-    )
+    g_norm_self, self_terms = tied(g_norm_self, self_terms)
     self_parts = scatter_parts([self_terms], dims, plane)
-    cross_parts = scatter_parts([cross_terms], low, low)
     give, keep = extras(core_id, sums, [g_norm_self, g_norm_cross, g_norm_ffn], across, share)
-    dkv_own, cross_parts, self_parts, give = lax.optimization_barrier(
-        (dkv_own, cross_parts, self_parts, give)
-    )
+    dkv_own, self_parts, give = lax.optimization_barrier((dkv_own, self_parts, give))
     self_terms = scattered(self_parts, plane)
     extra_terms = core_stage(give, keep)
+    totals = [memory_total(core_id, own, other, dkv_own[0], arrived[0])]
+    totals[0], extra_terms, cross_terms = lax.optimization_barrier(
+        (totals[0], extra_terms, cross_terms)
+    )
+    cross_parts = scatter_parts([cross_terms], low, low)
+    dkv_own, cross_parts = tied(dkv_own, cross_parts)
     cross_terms = scattered(cross_parts, low)
-    totals = [memory_total(core_id, own, other, dkv_own[0], arrived[0])]
-    totals[0], extra_terms = tied(totals[0], extra_terms)
     extra_left = list(dims)
     for bit in plane:
         extra_parts = scatter_parts([extra_terms], extra_left, [bit])

time: 478 us -> 465 us (0.973)
  Pallas kernels: 278 us -> 297 us
  starting transfers between devices: 68.2 us -> 53.5 us
  local copies, waits for them, and re-layouts: 31.7 us -> 22.2 us
  waiting for transfers between devices: 62.8 us -> 54.8 us
    ppermute x38, starting transfers between devices: 57.4 us -> 44.4 us  [exchange(): return lax.ppermute(block, AXES, [(i, i ^ mask) for i in range(count)])]
    ppermute x38, waiting for transfers between devices: 62.7 us -> 52 us  [exchange(): return lax.ppermute(block, AXES, [(i, i ^ mask) for i in range(count)])]
    pallas_call x0 -> x4, Pallas kernels: none -> 10.1 us  [the longest x3 10.1 us: assembled(): pl.pallas_call(assembled_kernel, grid_spec=pltpu.PrefetchScalarGridSpec(n...]
    pallas_call x1, Pallas kernels: 18.9 us -> 27.5 us  [cross_forward(): pl.pallas_call(cross_forward_kernel, grid=PAIR_GRID, in_specs=[SMEM, pair...]
    dynamic_update_slice x20 -> x8, local copies, waits for them, and re-layouts: 9.84 us -> 1.26 us  [gather_stage(): lax.dynamic_update_slice(result, piece.reshape(spot), start + [0] * len(t...]
    unnamed x62 -> x61, local copies, waits for them, and re-layouts: 10.1 us -> 10.3 us
  transfers between devices with their start and end apart: 43 -> 43, of which waited for: 13 -> 12; matrix products, arithmetic and copies ran while one was open for 7% -> 5% of each run, Pallas kernels for 48% -> 54%
where the time goes in v4:
time: 465 us; the launch traced here: 460 us
  Pallas kernels  297 us (64%)
  waiting for transfers between devices  54.8 us (12%)
  starting transfers between devices  53.5 us (12%)
  local copies, waits for them, and re-layouts  22.2 us (5%)
  other arithmetic  16.2 us (3%)
  between operations  15.9 us (3%)
    ppermute x38, waiting for transfers between devices, exchange(): return lax.ppermute(block, AXES, [(i, i ^ mask) for i in range(count)])  52 us
    pallas_call x2, Pallas kernels, cross_backward(): pl.pallas_call(cross_backward_kernel, grid=(PAIRS,), in_specs=[block(TGT_...  47 us
    ppermute x38, starting transfers between devices, exchange(): return lax.ppermute(block, AXES, [(i, i ^ mask) for i in range(count)])  44.4 us
    pallas_call x1, Pallas kernels, ffn(): pl.pallas_call(ffn_kernel, grid=(ROWS // BLOCK,), in_specs=[SMEM, ANY, AN...  35.8 us
    pallas_call x1, Pallas kernels, cross_forward(): pl.pallas_call(cross_forward_kernel, grid=PAIR_GRID, in_specs=[SMEM, pair...  27.5 us
    pallas_call x1, Pallas kernels, self_backward(): pl.pallas_call(self_backward_kernel, grid=(PAIRS, MICRO), in_specs=[swapp...  26.1 us
    pallas_call x1, Pallas kernels, self_forward(): pl.pallas_call(self_forward_kernel, grid=(PAIRS, MICRO), in_specs=[swappe...  16.5 us
    pallas_call x2, Pallas kernels, key_value(): pl.pallas_call(key_value_kernel, grid=(steps,), in_specs=[SMEM, ANY, ANY,...  16.3 us
  transfers between devices with their start and end apart: 43, of which 12 were waited for; matrix products, arithmetic and copies ran while one was open for 5% of the time, Pallas kernels for 54%

profile of v4, /device:TPU:0, one launch (start us, length us, event | category | flops | bytes accessed | tf_op | source)
XLA Modules:
  0.0 459.7 jit_solution(18240997399673025613)
XLA Ops:
  14.2 3.7 collective-permute-start.1
  20.2 7.7 %collective-permute-done.1 = bf16[2,24,2048]{2,1,0:T(8,128)(2,1)S(1)} collective-permute-done((bf16[2,24,2048]{2,1,0:T(8,128)(2,1)S(1)}, bf16[2,24,2048]{2,1,0:T(8,128)(2,1)S(1)}, u32[]{:S(2)}, u32[]{:S(2)}) %collective-permute-start.1) | collective-permute-done | bytes 196640 | tf_op jit(solution)/shard_map/ppermute | solution.py:1181
  27.9 5.1 %collective-permute-done.3 = bf16[2,24,2048]{2,1,0:T(8,128)(2,1)S(1)} collective-permute-done((bf16[2,24,2048]{2,1,0:T(8,128)(2,1)S(1)}, bf16[2,24,2048]{2,1,0:T(8,128)(2,1)S(1)}, u32[]{:S(2)}, u32[]{:S(2)}) %collective-permute-start.3) | collective-permute-done | bytes 196640 | tf_op jit(solution)/shard_map/ppermute | solution.py:1181
  41.4 3.8 collective-permute-start.9
  46.2 3.5 collective-permute-done.9
  49.9 3.7 collective-permute-start.10
  53.7 8.0 %bias_tiles.1.tiles_ref = f32[12,2,256,256]{3,2,1,0:T(8,128)} custom-call(f32[12,32]{1,0:T(8,128)} %convert_element_type.544.table_ref), custom_call_target="tpu_custom_call" | custom-call | flops 8 | tf_op jit(solution)/shard_map/bias_tiles/pallas_call | solution.py:796
  61.7 2.7 slice_bitcast_fusion
  64.3 4.2 collective-permute-done.10
  70.8 4.1 assembled.3
  79.1 2.6 collective-permute-start.12
  81.8 9.0 %self_inputs.1 = (bf16[1024,768]{1,0:T(8,128)(2,1)S(1)}, bf16[1024,2304]{1,0:T(8,128)(2,1)}, f32[8,768]{1,0:T(8,128)S(1)}) custom-call(s32[1]{0:T(128)} %bitcast.core_ref, bf16[768,2048]{1,0:T(8,128)(2,1)} %bitcast.220, bf16[768,2048]{1,0:T(8,128)(2,1)} %collective-permute-done.14.other_ref, bf16[1024,768]{1,0:T(8,128)(2,1)} %bitcast.229), custom_call_target="tpu_custom_call" | custom-call | flops 6 | tf_op jit(solution)/shard_map/self_inputs/pallas_call | solution.py:230
  92.0 16.5 %self_forward.1 = (bf16[1024,768]{1,0:T(8,128)(2,1)S(1)}, f32[12,8,512]{2,1,0:T(8,128)S(1)}) custom-call(bf16[1024,2304]{1,0:T(8,128)(2,1)} %get-tuple-element.214.q_ref.k_ref.v_ref, bf16[1024,2304]{1,0:T(8,128)(2,1)} %get-tuple-element.214.q_ref.k_ref.v_ref, bf16[1024,2304]{1,0:T(8,128)(2,1)} %get-tuple-element.214.q_ref.k_ref.v_ref, ...), custom_call_target="tpu_custom_call" | custom-call | flops 17 | tf_op jit(solution)/shard_map/self_forward/pallas_call | solution.py:1087
  109.7 10.0 %key_value.2 = (bf16[1536,1536]{1,0:T(8,128)(2,1)}, f32[8,128]{1,0:T(8,128)S(1)}) custom-call(s32[1]{0:T(128)} %bitcast.core_ref, bf16[768,2048]{1,0:T(8,128)(2,1)} %bitcast.221, bf16[768,2048]{1,0:T(8,128)(2,1)} %collective-permute-done.14.other_ref, bf16[2048,768]{1,0:T(8,128)(2,1)} %bitcast.228), custom_call_target="tpu_custom_call" | custom-call | flops 6 | tf_op jit(solution)/shard_map/key_value/pallas_call | solution.py:200
  119.8 9.6 %collective-permute-done.12 = bf16[2,2,2,24,768]{4,3,2,1,0:T(8,128)(2,1)S(1)} collective-permute-done((bf16[2,2,2,24,768]{4,3,2,1,0:T(8,128)(2,1)S(1)}, bf16[2,2,2,24,768]{4,3,2,1,0:T(8,128)(2,1)S(1)}, u32[]{:S(2)}, u32[]{:S(2)}) %collective-permute-start.12) | collective-permute-done | bytes 294944 | tf_op jit(solution)/shard_map/ppermute | solution.py:1181
  129.4 2.3 assembled.4
  133.4 2.5 collective-permute-start.17
  136.6 6.3 %key_value.3 = (bf16[1024,1536]{1,0:T(8,128)(2,1)}, f32[8,128]{1,0:T(8,128)S(1)}) custom-call(s32[1]{0:T(128)} %bitcast.core_ref, bf16[768,2048]{1,0:T(8,128)(2,1)} %bitcast.222, bf16[768,2048]{1,0:T(8,128)(2,1)} %collective-permute-done.14.other_ref, bf16[1024,768]{1,0:T(8,128)(2,1)S(1)} %bitcast.209), custom_call_target="tpu_custom_call" | custom-call | flops 4 | tf_op jit(solution)/shard_map/key_value/pallas_call | solution.py:200
  143.9 9.3 %cross_inputs.1 = (f32[1024,768]{1,0:T(8,128)}, bf16[1024,768]{1,0:T(8,128)(2,1)}, bf16[1024,768]{1,0:T(8,128)(2,1)}, f32[8,128]{1,0:T(8,128)S(1)}) custom-call(s32[1]{0:T(128)} %bitcast.core_ref, bf16[768,768]{1,0:T(8,128)(2,1)S(1)} %bitcast.208, bf16[768,768]{1,0:T(8,128)(2,1)} %copy-done.17, f32[8,768]{1,0:T(8,128)S(1)} %get-tuple-element.228.gain_ref, ...), custom_call_target="tpu_custom_call" | custom-call | flops 5 | tf_op jit(solution)/shard_map/cross_inputs/pallas_call | solution.py:260
  154.4 27.5 %cross_forward.1 = (bf16[1024,768]{1,0:T(8,128)(2,1)}, f32[12,8,512]{2,1,0:T(8,128)S(1)}) custom-call(s32[1]{0:T(128)} %bitcast.41.small_ref, bf16[1024,768]{1,0:T(8,128)(2,1)} %get-tuple-element.256.q_ref, bf16[1536,1536]{1,0:T(8,128)(2,1)} %get-tuple-element.257.ko_ref.vo_ref, bf16[1024,1536]{1,0:T(8,128)(2,1)} %get-tuple-element.258.kn_ref.vn_ref, ...), custom_call_target="tpu_custom_call" | custom-call | flops 32 | tf_op jit(solution)/shard_map/cross_forward/pallas_call | solution.py:1022
  182.6 3.7 assembled.5
  186.3 3.6 collective-permute-done.20.other_ref
  189.9 2.7 all-gather.2.cloned.1.call-done.late_ref
  192.7 35.8 %ffn.1 = (bf16[1024,768]{1,0:T(8,128)(2,1)}, bf16[1024,768]{1,0:T(8,128)(2,1)S(1)}, bf16[3,1024,2048]{2,1,0:T(8,128)(2,1)}, bf16[1024,768]{1,0:T(8,128)(2,1)}, f...) custom-call(s32[1]{0:T(128)} %bitcast.core_ref, ...), custom_call_target="tpu_custom_call" | custom-call | flops 30 | tf_op jit(solution)/shard_map/ffn/pallas_call | solution.py:357
  228.5 14.9 %ffn_weight_grads.1 = bf16[32,576,256]{2,1,0:T(8,128)(2,1)} custom-call(bf16[1024,768]{1,0:T(8,128)(2,1)S(1)} %get-tuple-element.250.h_ref, bf16[3,1024,2048]{2,1,0:T(8,128)(2,1)} %get-tuple-element.251.acts_ref, bf16[1024,768]{1,0:T(8,128)(2,1)} %bitcast.235), custom_call_target="tpu_custom_call" | custom-call | flops 13 | tf_op jit(solution)/shard_map/ffn_weight_grads/pallas_call | solution.py:580
  243.4 23.5 %cross_backward.2 = (bf16[512,768]{1,0:T(8,128)(2,1)S(1)}, bf16[2,768,768]{2,1,0:T(8,128)(2,1)}, bf16[2,512,768]{2,1,0:T(8,128)(2,1)}) custom-call(bf16[1024,768]{1,0:T(8,128)(2,1)} %get-tuple-element.256.q_ref, bf16[1536,1536]{1,0:T(8,128)(2,1)} %get-tuple-element.257.ko_ref.vo_ref, bf16[1024,1536]{1,0:T(8,128)(2,1)} %get-tuple-element.258.kn_ref.vn_ref, ...), custom_call_target="tpu_custom_call" | custom-call | flops 22 | tf_op jit(solution)/shard_map/cross_backward/pallas_call | solution.py:1047
  266.9 4.7 %memory_grads.2 = bf16[512,768]{1,0:T(8,128)(2,1)S(1)} custom-call(s32[1]{0:T(128)} %bitcast.core_ref, bf16[768,2048]{1,0:T(8,128)(2,1)} %bitcast.223, bf16[768,2048]{1,0:T(8,128)(2,1)} %collective-permute-done.14.other_ref, bf16[2,512,768]{2,1,0:T(8,128)(2,1)} %get-tuple-element.271.dkv_ref.after0_ref), custom_call_target="tpu_custom_call" | custom-call | flops 1 | tf_op jit(solution)/shard_map/memory_grads/pallas_call | solution.py:467
  271.6 3.5 collective-permute-start.21
  275.1 23.5 %cross_backward.3 = (bf16[512,768]{1,0:T(8,128)(2,1)S(1)}, bf16[2,768,768]{2,1,0:T(8,128)(2,1)}, bf16[2,512,768]{2,1,0:T(8,128)(2,1)}) custom-call(bf16[1024,768]{1,0:T(8,128)(2,1)} %get-tuple-element.256.q_ref, bf16[1536,1536]{1,0:T(8,128)(2,1)} %get-tuple-element.257.ko_ref.vo_ref, bf16[1024,1536]{1,0:T(8,128)(2,1)} %get-tuple-element.258.kn_ref.vn_ref, ...), custom_call_target="tpu_custom_call" | custom-call | flops 22 | tf_op jit(solution)/shard_map/cross_backward/pallas_call | solution.py:1047
  298.6 7.7 %pair_grads.2 = (bf16[2,192,1536]{2,1,0:T(8,128)(2,1)}, bf16[2,192,1536]{2,1,0:T(8,128)(2,1)}) custom-call(s32[1]{0:T(128)} %bitcast.core_ref, bf16[1024,768]{1,0:T(8,128)(2,1)} %get-tuple-element.260.o_ref.refs_0_, bf16[1024,768]{1,0:T(8,128)(2,1)} %get-tuple-element.279.refs_1_, bf16[1024,768]{1,0:T(8,128)(2,1)} %get-tuple-element.280.refs_2_, ...), custom_call_target="tpu_custom_call" | custom-call | flops 5 | tf_op jit(solution)/shard_map/pair_grads/pallas_call | solution.py:539
  306.3 4.7 %memory_grads.3 = bf16[512,768]{1,0:T(8,128)(2,1)S(1)} custom-call(s32[1]{0:T(128)} %bitcast.core_ref, bf16[768,2048]{1,0:T(8,128)(2,1)} %bitcast.224, bf16[768,2048]{1,0:T(8,128)(2,1)} %collective-permute-done.14.other_ref, bf16[2,512,768]{2,1,0:T(8,128)(2,1)} %get-tuple-element.272.dkv_ref.after1_ref), custom_call_target="tpu_custom_call" | custom-call | flops 1 | tf_op jit(solution)/shard_map/memory_grads/pallas_call | solution.py:467
  311.0 13.3 %memory_weight_grads.1 = (bf16[2,192,1536]{2,1,0:T(8,128)(2,1)}, bf16[2,192,1536]{2,1,0:T(8,128)(2,1)}) custom-call(s32[1]{0:T(128)} %bitcast.core_ref, bf16[2,1,1024,768]{3,2,1,0:T(8,128)(2,1)} %mem_ref, bf16[1024,768]{1,0:T(8,128)(2,1)} %bitcast.210, bf16[2,768,768]{2,1,0:T(8,128)(2,1)} %get-tuple-element.320.own0_ref.dkv_ref, ...), custom_call_target="tpu_custom_call" | custom-call | flops 8 | tf_op jit(solution)/shard_map/memory_weight_grads/pallas_call | solution.py:618
  324.9 4.0 collective-permute-start.25
  328.9 9.8 %self_grads.1 = (f32[1024,768]{1,0:T(8,128)}, bf16[1024,768]{1,0:T(8,128)(2,1)}, bf16[1024,768]{1,0:T(8,128)(2,1)}, f32[8,768]{1,0:T(8,128)S(1)}) custom-call(s32[1]{0:T(128)} %bitcast.core_ref, bf16[768,768]{1,0:T(8,128)(2,1)} %bitcast.207, bf16[768,768]{1,0:T(8,128)(2,1)} %copy-done.17, f32[8,768]{1,0:T(8,128)S(1)} %get-tuple-element.228.gain_ref, ...), custom_call_target="tpu_custom_call" | custom-call | flops 5 | tf_op jit(solution)/shard_map/self_grads/pallas_call | solution.py:407
  338.8 3.5 pair_grads.3
  349.7 26.1 %self_backward.1 = (bf16[3,1024,768]{2,1,0:T(8,128)(2,1)}, f32[12,8,256]{2,1,0:T(8,128)S(1)}) custom-call(bf16[1024,2304]{1,0:T(8,128)(2,1)} %get-tuple-element.214.q_ref.k_ref.v_ref, bf16[1024,2304]{1,0:T(8,128)(2,1)} %get-tuple-element.214.q_ref.k_ref.v_ref, bf16[1024,2304]{1,0:T(8,128)(2,1)} %get-tuple-element.214.q_ref.k_ref.v_ref, ...), custom_call_target="tpu_custom_call" | custom-call | flops 24 | tf_op jit(solution)/shard_map/self_backward/pallas_call | solution.py:1106
  375.8 7.9 %row_grads.1 = (bf16[2,192,2304]{2,1,0:T(8,128)(2,1)}, bf16[2,192,2304]{2,1,0:T(8,128)(2,1)}) custom-call(s32[1]{0:T(128)} %bitcast.core_ref, bf16[1024,768]{1,0:T(8,128)(2,1)S(1)} %copy-done.6, bf16[3,1024,768]{2,1,0:T(8,128)(2,1)} %get-tuple-element.308.grads_ref.dqkv_ref), custom_call_target="tpu_custom_call" | custom-call | flops 5 | tf_op jit(solution)/shard_map/row_grads/pallas_call | solution.py:506
  383.7 4.2 collective-permute-done.27
  388.4 4.0 collective-permute-start.31
  392.4 10.8 %input_grads.1 = (bf16[1024,768]{1,0:T(8,128)(2,1)}, f32[8,768]{1,0:T(8,128)S(1)}) custom-call(s32[1]{0:T(128)} %bitcast.core_ref, bf16[768,2048]{1,0:T(8,128)(2,1)} %bitcast.225, bf16[768,2048]{1,0:T(8,128)(2,1)} %collective-permute-done.14.other_ref, f32[8,768]{1,0:T(8,128)S(1)} %get-tuple-element.228.gain_ref, bf16[1024,768]{1,0:T(8,128)(2,1)} %bitcast.231, ...), custom_call_target="tpu_custom_call" | custom-call | flops 6 | tf_op jit(solution)/shard_map/input_grads/pallas_call | solution.py:444
  405.7 2.1 collective-permute-start.33
  409.3 6.6 %memory_total.2 = bf16[1024,768]{1,0:T(8,128)(2,1)} custom-call(s32[1]{0:T(128)} %bitcast.core_ref, bf16[768,2048]{1,0:T(8,128)(2,1)} %bitcast.226, bf16[768,2048]{1,0:T(8,128)(2,1)} %collective-permute-done.14.other_ref, bf16[2,768,768]{2,1,0:T(8,128)(2,1)} %get-tuple-element.320.own0_ref.dkv_ref, bf16[512,768]{1,0:T(8,128)(2,1)S(1)} %collective-permute-done.21.prev_ref), custom_call_target="tpu_custom_call" | custom-call | flops 4 | tf_op jit(solution)/shard_map/memory_total/pallas_call | solution.py:653
  416.1 2.1 collective-permute-start.32
  418.1 6.6 %memory_total.3 = bf16[1024,768]{1,0:T(8,128)(2,1)} custom-call(s32[1]{0:T(128)} %bitcast.core_ref, bf16[768,2048]{1,0:T(8,128)(2,1)} %bitcast.227, bf16[768,2048]{1,0:T(8,128)(2,1)} %collective-permute-done.14.other_ref, bf16[2,768,768]{2,1,0:T(8,128)(2,1)} %get-tuple-element.333.own1_ref.dkv_ref, bf16[512,768]{1,0:T(8,128)(2,1)S(1)} %collective-permute-done.25.prev_ref), custom_call_target="tpu_custom_call" | custom-call | flops 4 | tf_op jit(solution)/shard_map/memory_total/pallas_call | solution.py:653
  424.7 5.6 %collective-permute-done.32 = bf16[2,2,2,24,256]{4,3,1,0,2:T(8,128)(2,1)S(1)} collective-permute-done((bf16[2,2,2,24,256]{4,3,1,0,2:T(8,128)(2,1)S(1)}, bf16[2,2,2,24,256]{4,3,1,0,2:T(8,128)(2,1)S(1)}, u32[]{:S(2)}, u32[]{:S(2)}) %collective-permute-start.32) | collective-permute-done | bytes 98336 | tf_op jit(solution)/shard_map/ppermute | solution.py:1181
  430.5 4.0 collective-permute-done.36
  441.9 2.7 collective-permute-start.40
  446.8 3.6 collective-permute-done.38
  (200 shorter events, 56.3 us)
Async XLA Ops:
  7.2 12.3 %copy-start.26 = (bf16[24,768]{1,0:T(8,128)(2,1)S(1)}, bf16[24,768]{1,0:T(8,128)(2,1)}, u32[]{:S(2)}) copy-start(bf16[24,768]{1,0:T(8,128)(2,1)} %param.26) | copy-start | bytes 110596
  7.2 185.5 %all-gather.2.cloned.1.call-start = ((), (), s32[]{:S(2)}) async-start(), calls=%async_computation.1 | async-start | bytes 7704576 | tf_op jit(solution)/shard_map/all_gather | solution.py:1372
  11.9 2.2 collective-permute-start
  14.2 23.0 %copy-start.25 = (bf16[64,768]{1,0:T(8,128)(2,1)S(1)}, bf16[64,768]{1,0:T(8,128)(2,1)}, u32[]{:S(2)}) copy-start(bf16[64,768]{1,0:T(8,128)(2,1)} %param.32) | copy-start | bytes 294916
  14.2 13.7 %collective-permute-start.1 = (bf16[2,24,2048]{2,1,0:T(8,128)(2,1)S(1)}, bf16[2,24,2048]{2,1,0:T(8,128)(2,1)S(1)}, u32[]{:S(2)}, u32[]{:S(2)}) collective-permute-start(bf16[2,24,2048]{2,1,0:T(8,128)(2,1)S(1)} %pad_maximum_fusion.6), channel_id=1, source_target_pairs={{0,4},{1,5},{2,6},{3,7},{4,0},{5,1},{6,2},{7,3},{8,12},{9,13},{10,... | collective-permute-start | bytes 589832 | tf_op jit(solution)/shard_map/ppermute | solution.py:1181
  17.9 10.0 %collective-permute-start.2 = (bf16[2,24,2048]{2,1,0:T(8,128)(2,1)S(1)}, bf16[2,24,2048]{2,1,0:T(8,128)(2,1)S(1)}, u32[]{:S(2)}, u32[]{:S(2)}) collective-permute-start(bf16[2,24,2048]{2,1,0:T(8,128)(2,1)S(1)} %pad_maximum_fusion.6), channel_id=1, source_target_pairs={{0,2},{1,3},{2,0},{3,1},{4,6},{5,7},{6,4},{7,5},{8,10},{9,11},{10,... | collective-permute-start | bytes 589832 | tf_op jit(solution)/shard_map/ppermute | solution.py:1181
  19.5 13.6 %collective-permute-start.3 = (bf16[2,24,2048]{2,1,0:T(8,128)(2,1)S(1)}, bf16[2,24,2048]{2,1,0:T(8,128)(2,1)S(1)}, u32[]{:S(2)}, u32[]{:S(2)}) collective-permute-start(bf16[2,24,2048]{2,1,0:T(8,128)(2,1)S(1)} %pad_maximum_fusion.6), channel_id=1, source_target_pairs={{0,6},{1,7},{2,4},{3,5},{4,2},{5,3},{6,0},{7,1},{8,14},{9,15},{10,... | collective-permute-start | bytes 589832 | tf_op jit(solution)/shard_map/ppermute | solution.py:1181
  33.2 12.4 %copy-start.27 = (bf16[12,32]{1,0:T(8,128)(2,1)S(1)}, bf16[12,32]{1,0:T(8,128)(2,1)}, u32[]{:S(2)}) copy-start(bf16[12,32]{1,0:T(8,128)(2,1)} %param.36) | copy-start | bytes 2308
  33.3 36.4 %collective-permute-start.4 = (bf16[2,2,2,24,2048]{4,3,2,1,0:T(8,128)(2,1)S(1)}, bf16[2,2,2,24,2048]{4,3,2,1,0:T(8,128)(2,1)S(1)}, u32[]{:S(2)}, u32[]{:S(2)}) collective-permute-start(bf16[2,2,2,24,2048]{4,3,2,1,0:T(8,128)(2,1)S(1)} %bitcast_dynamic-update-slice_fusion.2), channel_id=1, source_target_pairs={{0,16},{1,17},{2,18},{3,19},{4,20},{5,21},{6,22},{7,23},{8,24},{9,... | collective-permute-start | bytes 2359304 | tf_op jit(solution)/shard_map/ppermute | solution.py:1181
  34.8 35.6 %collective-permute-start.5 = (bf16[2,2,2,24,2048]{4,3,2,1,0:T(8,128)(2,1)S(1)}, bf16[2,2,2,24,2048]{4,3,2,1,0:T(8,128)(2,1)S(1)}, u32[]{:S(2)}, u32[]{:S(2)}) collective-permute-start(bf16[2,2,2,24,2048]{4,3,2,1,0:T(8,128)(2,1)S(1)} %bitcast_dynamic-update-slice_fusion.2), channel_id=1, source_target_pairs={{0,1},{1,0},{2,3},{3,2},{4,5},{5,4},{6,7},{7,6},{8,9},{9,8},{10,11... | collective-permute-start | bytes 2359304 | tf_op jit(solution)/shard_map/ppermute | solution.py:1181
  36.4 34.2 %collective-permute-start.6 = (bf16[2,2,2,24,2048]{4,3,2,1,0:T(8,128)(2,1)S(1)}, bf16[2,2,2,24,2048]{4,3,2,1,0:T(8,128)(2,1)}, u32[]{:S(2)}, u32[]{:S(2)}) collective-permute-start(bf16[2,2,2,24,2048]{4,3,2,1,0:T(8,128)(2,1)S(1)} %bitcast_dynamic-update-slice_fusion.2), channel_id=1, source_target_pairs={{0,17},{1,16},{2,19},{3,18},{4,21},{5,20},{6,23},{7,22},{8,25},{9,... | collective-permute-start | bytes 2359304 | tf_op jit(solution)/shard_map/ppermute | solution.py:1181
  37.0 4.2 collective-permute-start.7
  37.4 4.0 collective-permute-start.8
  41.4 8.4 %collective-permute-start.9 = (bf16[2,112,384]{2,1,0:T(8,128)(2,1)S(1)}, bf16[2,112,384]{2,1,0:T(8,128)(2,1)S(1)}, u32[]{:S(2)}, u32[]{:S(2)}) collective-permute-start(bf16[2,112,384]{2,1,0:T(8,128)(2,1)S(1)} %maximum_maximum_fusion), channel_id=1, source_target_pairs={{0,2},{1,3},{2,0},{3,1},{4,6},{5,7},{6,4},{7,5},{8,10},{9,11},{10,... | collective-permute-start | bytes 516104 | tf_op jit(solution)/shard_map/ppermute | solution.py:1181
  49.9 18.6 %collective-permute-start.10 = (bf16[2,2,112,384]{3,2,1,0:T(8,128)(2,1)S(1)}, bf16[2,2,112,384]{3,2,1,0:T(8,128)(2,1)}, u32[]{:S(2)}, u32[]{:S(2)}) collective-permute-start(bf16[2,2,112,384]{3,2,1,0:T(8,128)(2,1)S(1)} %bitcast_dynamic-update-slice_fusion.6), channel_id=1, source_target_pairs={{0,4},{1,5},{2,6},{3,7},{4,0},{5,1},{6,2},{7,3},{8,12},{9,13},{10,... | collective-permute-start | bytes 1032200 | tf_op jit(solution)/shard_map/ppermute | solution.py:1181
  53.7 100.7 %copy-start.3 = (bf16[2,1280,128]{2,1,0:T(8,128)(2,1)}, bf16[2,1280,128]{2,1,0:T(8,128)(2,1)S(1)}, u32[]{:S(2)}) copy-start(bf16[2,1280,128]{2,1,0:T(8,128)(2,1)S(1)} %pad_maximum_fusion.4.mask_ref) | copy-start | bytes 1966084
  70.6 367.8 %reduce-scatter.2.cloned.1.call-start = ((), (), s32[]{:S(2)}) async-start(), calls=%async_computation.2 | async-start | bytes 9732096 | tf_op jit(solution)/shard_map/reduce_scatter | solution.py:1298
  74.9 6.9 %collective-permute-start.14 = (bf16[768,2048]{1,0:T(8,128)(2,1)}, bf16[768,2048]{1,0:T(8,128)(2,1)}, u32[]{:S(2)}, u32[]{:S(2)}) collective-permute-start(bf16[768,2048]{1,0:T(8,128)(2,1)} %bitcast.219), channel_id=1, source_target_pairs={{0,8},{1,9},{2,10},{3,11},{4,12},{5,13},{6,14},{7,15},{8,0},{9,1},... | collective-permute-start | bytes 9437192 | tf_op jit(solution)/shard_map/ppermute | solution.py:1181
  74.9 54.5 %collective-permute-start.15 = (bf16[2,512,768]{2,1,0:T(8,128)(2,1)}, bf16[2,512,768]{2,1,0:T(8,128)(2,1)S(1)}, u32[]{:S(2)}, u32[]{:S(2)}) collective-permute-start(bf16[2,512,768]{2,1,0:T(8,128)(2,1)} %slice_bitcast_fusion), channel_id=1, source_target_pairs={{1,0},{2,1},{3,2},{4,3},{5,4},{6,5},{7,6},{9,8},{10,9},{11,10},{12... | collective-permute-start | bytes 4718600 | tf_op jit(solution)/shard_map/ppermute | solution.py:1277
  77.6 42.2 %collective-permute-start.11 = (bf16[2,2,2,24,768]{4,3,2,1,0:T(8,128)(2,1)S(1)}, bf16[2,2,2,24,768]{4,3,2,1,0:T(8,128)(2,1)S(1)}, u32[]{:S(2)}, u32[]{:S(2)}) collective-permute-start(bf16[2,2,2,24,768]{4,3,2,1,0:T(8,128)(2,1)S(1)} %reshape.598), channel_id=1, source_target_pairs={{0,16},{1,17},{2,18},{3,19},{4,20},{5,21},{6,22},{7,23},{8,24},{9,... | collective-permute-start | bytes 884744 | tf_op jit(solution)/shard_map/ppermute | solution.py:1181
  79.1 50.3 %collective-permute-start.12 = (bf16[2,2,2,24,768]{4,3,2,1,0:T(8,128)(2,1)S(1)}, bf16[2,2,2,24,768]{4,3,2,1,0:T(8,128)(2,1)S(1)}, u32[]{:S(2)}, u32[]{:S(2)}) collective-permute-start(bf16[2,2,2,24,768]{4,3,2,1,0:T(8,128)(2,1)S(1)} %reshape.598), channel_id=1, source_target_pairs={{0,1},{1,0},{2,3},{3,2},{4,5},{5,4},{6,7},{7,6},{8,9},{9,8},{10,11... | collective-permute-start | bytes 884744 | tf_op jit(solution)/shard_map/ppermute | solution.py:1181
  81.8 47.6 %collective-permute-start.13 = (bf16[2,2,2,24,768]{4,3,2,1,0:T(8,128)(2,1)S(1)}, bf16[2,2,2,24,768]{4,3,2,1,0:T(8,128)(2,1)S(1)}, u32[]{:S(2)}, u32[]{:S(2)}) collective-permute-start(bf16[2,2,2,24,768]{4,3,2,1,0:T(8,128)(2,1)S(1)} %reshape.598), channel_id=1, source_target_pairs={{0,17},{1,16},{2,19},{3,18},{4,21},{5,20},{6,23},{7,22},{8,25},{9,... | collective-permute-start | bytes 884744 | tf_op jit(solution)/shard_map/ppermute | solution.py:1181
  131.7 11.2 %collective-permute-start.19 = (bf16[768,768]{1,0:T(8,128)(2,1)}, bf16[768,768]{1,0:T(8,128)(2,1)S(1)}, u32[]{:S(2)}, u32[]{:S(2)}) collective-permute-start(bf16[768,768]{1,0:T(8,128)(2,1)} %bitcast.206), channel_id=1, source_target_pairs={{0,8},{1,9},{2,10},{3,11},{4,12},{5,13},{6,14},{7,15},{8,0},{9,1},... | collective-permute-start | bytes 3538952 | tf_op jit(solution)/shard_map/ppermute | solution.py:1181
  132.5 50.1 %collective-permute-start.16 = (bf16[2,2,2,64,384]{4,3,2,1,0:T(8,128)(2,1)}, bf16[2,2,2,64,384]{4,3,2,1,0:T(8,128)(2,1)}, u32[]{:S(2)}, u32[]{:S(2)}) collective-permute-start(bf16[2,2,2,64,384]{4,3,2,1,0:T(8,128)(2,1)} %slice.76), channel_id=1, source_target_pairs={{0,16},{1,17},{2,18},{3,19},{4,20},{5,21},{6,22},{7,23},{8,24},{9,... | collective-permute-start | bytes 1179656 | tf_op jit(solution)/shard_map/ppermute | solution.py:1181
  133.4 49.1 %collective-permute-start.17 = (bf16[2,2,2,64,384]{4,3,2,1,0:T(8,128)(2,1)}, bf16[2,2,2,64,384]{4,3,2,1,0:T(8,128)(2,1)}, u32[]{:S(2)}, u32[]{:S(2)}) collective-permute-start(bf16[2,2,2,64,384]{4,3,2,1,0:T(8,128)(2,1)} %slice.76), channel_id=1, source_target_pairs={{0,1},{1,0},{2,3},{3,2},{4,5},{5,4},{6,7},{7,6},{8,9},{9,8},{10,11... | collective-permute-start | bytes 1179656 | tf_op jit(solution)/shard_map/ppermute | solution.py:1181
  136.0 46.6 %collective-permute-start.18 = (bf16[2,2,2,64,384]{4,3,2,1,0:T(8,128)(2,1)}, bf16[2,2,2,64,384]{4,3,2,1,0:T(8,128)(2,1)}, u32[]{:S(2)}, u32[]{:S(2)}) collective-permute-start(bf16[2,2,2,64,384]{4,3,2,1,0:T(8,128)(2,1)} %slice.76), channel_id=1, source_target_pairs={{0,17},{1,16},{2,19},{3,18},{4,21},{5,20},{6,23},{7,22},{8,25},{9,... | collective-permute-start | bytes 1179656 | tf_op jit(solution)/shard_map/ppermute | solution.py:1181
  186.3 3.6 collective-permute-start.20
  271.6 39.4 %collective-permute-start.21 = (bf16[512,768]{1,0:T(8,128)(2,1)S(1)}, bf16[512,768]{1,0:T(8,128)(2,1)S(1)}, u32[]{:S(2)}, u32[]{:S(2)}) collective-permute-start(bf16[512,768]{1,0:T(8,128)(2,1)S(1)} %memory_grads.2), channel_id=1, source_target_pairs={{0,1},{1,2},{2,3},{3,4},{4,5},{5,6},{6,7},{8,9},{9,10},{10,11},{11... | collective-permute-start | bytes 2359304 | tf_op jit(solution)/shard_map/ppermute | solution.py:1277
  306.3 32.5 %collective-permute-start.22 = (bf16[2,192,1536]{2,1,0:T(8,128)(2,1)}, bf16[2,192,1536]{2,1,0:T(8,128)(2,1)}, u32[]{:S(2)}, u32[]{:S(2)}) collective-permute-start(bf16[2,192,1536]{2,1,0:T(8,128)(2,1)} %get-tuple-element.282), channel_id=1, source_target_pairs={{0,8},{1,9},{2,10},{3,11},{4,12},{5,13},{6,14},{7,15},{8,0},{9,1},... | collective-permute-start | bytes 3538952 | tf_op jit(solution)/shard_map/ppermute | solution.py:1181
  324.3 14.4 %collective-permute-start.23 = (bf16[2,192,1536]{2,1,0:T(8,128)(2,1)}, bf16[2,192,1536]{2,1,0:T(8,128)(2,1)}, u32[]{:S(2)}, u32[]{:S(2)}) collective-permute-start(bf16[2,192,1536]{2,1,0:T(8,128)(2,1)} %get-tuple-element.284), channel_id=1, source_target_pairs={{0,8},{1,9},{2,10},{3,11},{4,12},{5,13},{6,14},{7,15},{8,0},{9,1},... | collective-permute-start | bytes 3538952 | tf_op jit(solution)/shard_map/ppermute | solution.py:1181
  324.9 50.9 %collective-permute-start.25 = (bf16[512,768]{1,0:T(8,128)(2,1)S(1)}, bf16[512,768]{1,0:T(8,128)(2,1)S(1)}, u32[]{:S(2)}, u32[]{:S(2)}) collective-permute-start(bf16[512,768]{1,0:T(8,128)(2,1)S(1)} %memory_grads.3), channel_id=1, source_target_pairs={{0,1},{1,2},{2,3},{3,4},{4,5},{5,6},{6,7},{8,9},{9,10},{10,11},{11... | collective-permute-start | bytes 2359304 | tf_op jit(solution)/shard_map/ppermute | solution.py:1277
  342.3 3.4 collective-permute-start.24
  346.1 37.6 %collective-permute-start.26 = (bf16[2,2,24,3840]{3,2,1,0:T(8,128)(2,1)S(1)}, bf16[2,2,24,3840]{3,2,1,0:T(8,128)(2,1)S(1)}, u32[]{:S(2)}, u32[]{:S(2)}) collective-permute-start(bf16[2,2,24,3840]{3,2,1,0:T(8,128)(2,1)S(1)} %pad_maximum_fusion.1), channel_id=1, source_target_pairs={{0,16},{1,17},{2,18},{3,19},{4,20},{5,21},{6,22},{7,23},{8,24},{9,... | collective-permute-start | bytes 2211848 | tf_op jit(solution)/shard_map/ppermute | solution.py:1181
  347.3 40.6 %collective-permute-start.27 = (bf16[2,2,24,3840]{3,2,1,0:T(8,128)(2,1)S(1)}, bf16[2,2,24,3840]{3,2,1,0:T(8,128)(2,1)S(1)}, u32[]{:S(2)}, u32[]{:S(2)}) collective-permute-start(bf16[2,2,24,3840]{3,2,1,0:T(8,128)(2,1)S(1)} %pad_maximum_fusion.2), channel_id=1, source_target_pairs={{0,1},{1,0},{2,3},{3,2},{4,5},{5,4},{6,7},{7,6},{8,9},{9,8},{10,11... | collective-permute-start | bytes 2211848 | tf_op jit(solution)/shard_map/ppermute | solution.py:1181
  348.6 39.4 %collective-permute-start.28 = (bf16[2,2,24,3840]{3,2,1,0:T(8,128)(2,1)S(1)}, bf16[2,2,24,3840]{3,2,1,0:T(8,128)(2,1)S(1)}, u32[]{:S(2)}, u32[]{:S(2)}) collective-permute-start(bf16[2,2,24,3840]{3,2,1,0:T(8,128)(2,1)S(1)} %pad_maximum_fusion.3), channel_id=1, source_target_pairs={{0,17},{1,16},{2,19},{3,18},{4,21},{5,20},{6,23},{7,22},{8,25},{9,... | collective-permute-start | bytes 2211848 | tf_op jit(solution)/shard_map/ppermute | solution.py:1181
  349.7 26.1 %copy-start.6 = (bf16[1024,768]{1,0:T(8,128)(2,1)S(1)}, bf16[1024,768]{1,0:T(8,128)(2,1)}, u32[]{:S(2)}) copy-start(bf16[1024,768]{1,0:T(8,128)(2,1)} %copy-done.5) | copy-start | bytes 4718596
  388.0 15.3 %collective-permute-start.29 = (bf16[2,192,2304]{2,1,0:T(8,128)(2,1)}, bf16[2,192,2304]{2,1,0:T(8,128)(2,1)S(1)}, u32[]{:S(2)}, u32[]{:S(2)}) collective-permute-start(bf16[2,192,2304]{2,1,0:T(8,128)(2,1)} %get-tuple-element.312), channel_id=1, source_target_pairs={{0,8},{1,9},{2,10},{3,11},{4,12},{5,13},{6,14},{7,15},{8,0},{9,1},... | collective-permute-start | bytes 5308424 | tf_op jit(solution)/shard_map/ppermute | solution.py:1181
  388.4 27.5 %collective-permute-start.31 = (bf16[2,24,3840]{2,1,0:T(8,128)(2,1)S(1)}, bf16[2,24,3840]{2,1,0:T(8,128)(2,1)S(1)}, u32[]{:S(2)}, u32[]{:S(2)}) collective-permute-start(bf16[2,24,3840]{2,1,0:T(8,128)(2,1)S(1)} %get-tuple-element.325), channel_id=1, source_target_pairs={{0,4},{1,5},{2,6},{3,7},{4,0},{5,1},{6,2},{7,3},{8,12},{9,13},{10,... | collective-permute-start | bytes 1105928 | tf_op jit(solution)/shard_map/ppermute | solution.py:1181
  405.4 10.4 %collective-permute-start.30 = (bf16[2,192,256]{2,1,0:T(8,128)(2,1)S(1)}, bf16[2,192,256]{2,1,0:T(8,128)(2,1)S(1)}, u32[]{:S(2)}, u32[]{:S(2)}) collective-permute-start(bf16[2,192,256]{2,1,0:T(8,128)(2,1)S(1)} %get-tuple-element.323), channel_id=1, source_target_pairs={{0,8},{1,9},{2,10},{3,11},{4,12},{5,13},{6,14},{7,15},{8,0},{9,1},... | collective-permute-start | bytes 589832 | tf_op jit(solution)/shard_map/ppermute | solution.py:1181
  405.7 28.8 %collective-permute-start.33 = (bf16[2,2,24,2304]{3,2,1,0:T(8,128)(2,1)}, bf16[2,2,24,2304]{3,2,1,0:T(8,128)(2,1)S(1)}, u32[]{:S(2)}, u32[]{:S(2)}) collective-permute-start(bf16[2,2,24,2304]{3,2,1,0:T(8,128)(2,1)} %get-tuple-element.339), channel_id=1, source_target_pairs={{0,16},{1,17},{2,18},{3,19},{4,20},{5,21},{6,22},{7,23},{8,24},{9,... | collective-permute-start | bytes 1327112 | tf_op jit(solution)/shard_map/ppermute | solution.py:1181
  407.8 26.7 %collective-permute-start.34 = (bf16[2,2,24,2304]{3,2,1,0:T(8,128)(2,1)}, bf16[2,2,24,2304]{3,2,1,0:T(8,128)(2,1)S(1)}, u32[]{:S(2)}, u32[]{:S(2)}) collective-permute-start(bf16[2,2,24,2304]{3,2,1,0:T(8,128)(2,1)} %get-tuple-element.340), channel_id=1, source_target_pairs={{0,1},{1,0},{2,3},{3,2},{4,5},{5,4},{6,7},{7,6},{8,9},{9,8},{10,11... | collective-permute-start | bytes 1327112 | tf_op jit(solution)/shard_map/ppermute | solution.py:1181
  407.8 26.7 %collective-permute-start.35 = (bf16[2,2,24,2304]{3,2,1,0:T(8,128)(2,1)}, bf16[2,2,24,2304]{3,2,1,0:T(8,128)(2,1)S(1)}, u32[]{:S(2)}, u32[]{:S(2)}) collective-permute-start(bf16[2,2,24,2304]{3,2,1,0:T(8,128)(2,1)} %get-tuple-element.341), channel_id=1, source_target_pairs={{0,17},{1,16},{2,19},{3,18},{4,21},{5,20},{6,23},{7,22},{8,25},{9,... | collective-permute-start | bytes 1327112 | tf_op jit(solution)/shard_map/ppermute | solution.py:1181
  416.1 14.3 %collective-permute-start.32 = (bf16[2,2,2,24,256]{4,3,1,0,2:T(8,128)(2,1)S(1)}, bf16[2,2,2,24,256]{4,3,1,0,2:T(8,128)(2,1)S(1)}, u32[]{:S(2)}, u32[]{:S(2)}) collective-permute-start(bf16[2,2,2,24,256]{4,3,1,0,2:T(8,128)(2,1)S(1)} %get-tuple-element.336), channel_id=1, source_target_pairs={{0,16},{1,17},{2,18},{3,19},{4,20},{5,21},{6,22},{7,23},{8,24},{9,... | collective-permute-start | bytes 294920 | tf_op jit(solution)/shard_map/ppermute | solution.py:1181
  430.4 4.2 collective-permute-start.36
  430.5 7.9 %collective-permute-start.37 = (bf16[24,3840]{1,0:T(8,128)(2,1)S(1)}, bf16[24,3840]{1,0:T(8,128)(2,1)S(1)}, u32[]{:S(2)}, u32[]{:S(2)}) collective-permute-start(bf16[24,3840]{1,0:T(8,128)(2,1)S(1)} %get-tuple-element.353), channel_id=1, source_target_pairs={{0,2},{1,3},{2,0},{3,1},{4,6},{5,7},{6,4},{7,5},{8,10},{9,11},{10,... | collective-permute-start | bytes 552968 | tf_op jit(solution)/shard_map/ppermute | solution.py:1181
  440.3 10.2 %collective-permute-start.38 = (bf16[24,2560]{1,0:T(8,128)(2,1)S(1)}, bf16[24,2560]{1,0:T(8,128)(2,1)S(1)}, u32[]{:S(2)}, u32[]{:S(2)}) collective-permute-start(bf16[24,2560]{1,0:T(8,128)(2,1)S(1)} %pad_maximum_fusion.8), channel_id=1, source_target_pairs={{0,4},{1,5},{2,6},{3,7},{4,0},{5,1},{6,2},{7,3},{8,12},{9,13},{10,... | collective-permute-start | bytes 368648 | tf_op jit(solution)/shard_map/ppermute | solution.py:1181
  440.3 10.1 %collective-permute-start.39 = (bf16[24,2560]{1,0:T(8,128)(2,1)S(1)}, bf16[24,2560]{1,0:T(8,128)(2,1)S(1)}, u32[]{:S(2)}, u32[]{:S(2)}) collective-permute-start(bf16[24,2560]{1,0:T(8,128)(2,1)S(1)} %pad_maximum_fusion.9), channel_id=1, source_target_pairs={{0,2},{1,3},{2,0},{3,1},{4,6},{5,7},{6,4},{7,5},{8,10},{9,11},{10,... | collective-permute-start | bytes 368648 | tf_op jit(solution)/shard_map/ppermute | solution.py:1181
  441.9 8.5 %collective-permute-start.40 = (bf16[24,2560]{1,0:T(8,128)(2,1)S(1)}, bf16[24,2560]{1,0:T(8,128)(2,1)S(1)}, u32[]{:S(2)}, u32[]{:S(2)}) collective-permute-start(bf16[24,2560]{1,0:T(8,128)(2,1)S(1)} %pad_maximum_fusion.10), channel_id=1, source_target_pairs={{0,6},{1,7},{2,4},{3,5},{4,2},{5,3},{6,0},{7,1},{8,14},{9,15},{10,... | collective-permute-start | bytes 368648 | tf_op jit(solution)/shard_map/ppermute | solution.py:1181
  (24 other events, 84.9 us)
Sparse Core Ops, SparseCore 0:
  70.7 121.8 all-gather.1
  243.5 150.5 reduce-scatter.1

commit v5 on v4

--- a/solution.py
+++ b/solution.py
@@ -802,13 +802,6 @@
         cost_estimate=cost(8),
         name="bias_tiles",
     )(table)
-
-
-def softmax_columns(scores):
-    top = jnp.max(scores, axis=0, keepdims=True)
-    weights = jnp.exp(scores - top)
-    total = jnp.sum(weights, axis=0, keepdims=True)
-    return weights.astype(BF), 1.0 / total, top + jnp.log(total)
 
 
 def put_lse(lse_ref, rows):
@@ -901,18 +894,18 @@
     k = k_ref[...]
     q_t = q_ref[...].T
     v_t = v_ref[...].T
+    rows_of_ones = jnp.ones((16, TGT_LEN), BF)
+    queries = [head_rows(q_t, head) for head in range(2)]
+    raws = [(nn(k[:HALF], query[:, :HALF]), nn(k, query[:, HALF:])) for query in queries]
     mixed, lses = [], []
     for head in range(2):
-        query = head_rows(q_t, head)
-        value = v_t[head * HEAD_DIM : (head + 1) * HEAD_DIM]
+        rows = slice(head * HEAD_DIM, (head + 1) * HEAD_DIM)
+        value = jnp.concatenate([v_t[rows], rows_of_ones], axis=0)
         near, far = tiles_ref[head, 0], tiles_ref[head, 1]
-        w0, i0, l0 = softmax_columns(nn(k[:HALF], query[:, :HALF]) + near)
-        raw = nn(k, query[:, HALF:])
-        w1, i1, l1 = softmax_columns(
-            jnp.concatenate([raw[:HALF] + far, raw[HALF:] + near], axis=0)
-        )
-        out0 = nn(value[:, :HALF], w0) * i0
-        out1 = nn(value, w1) * i1
+        first, raw = raws[head]
+        out0, l0 = attended(first + near, value[:, :HALF], False)
+        scores = jnp.concatenate([raw[:HALF] + far, raw[HALF:] + near], axis=0)
+        out1, l1 = attended(scores, value, False)
         mixed.append(jnp.concatenate([out0, out1], axis=1))
         lses.append(jnp.concatenate([l0, l1], axis=1))
     o_ref[...] = jnp.concatenate(mixed, axis=0).T.astype(BF)

time: 465 us -> 465 us (level)
  transfers between devices with their start and end apart: 43 -> 43, of which waited for: 12 -> 12; matrix products, arithmetic and copies ran while one was open for 5% -> 5% of each run, Pallas kernels for 54% -> 53%
where the time goes in v5:
time: 465 us; the launch traced here: 460 us
  Pallas kernels  296 us (64%)
  waiting for transfers between devices  55.9 us (12%)
  starting transfers between devices  53.5 us (12%)
  local copies, waits for them, and re-layouts  22.2 us (5%)
  other arithmetic  16.2 us (3%)
  between operations  15.9 us (3%)
    ppermute x38, waiting for transfers between devices, exchange(): return lax.ppermute(block, AXES, [(i, i ^ mask) for i in range(count)])  53.2 us
    pallas_call x2, Pallas kernels, cross_backward(): pl.pallas_call(cross_backward_kernel, grid=(PAIRS,), in_specs=[block(TGT_...  47 us
    ppermute x38, starting transfers between devices, exchange(): return lax.ppermute(block, AXES, [(i, i ^ mask) for i in range(count)])  44.4 us
    pallas_call x1, Pallas kernels, ffn(): pl.pallas_call(ffn_kernel, grid=(ROWS // BLOCK,), in_specs=[SMEM, ANY, AN...  35.8 us
    pallas_call x1, Pallas kernels, cross_forward(): pl.pallas_call(cross_forward_kernel, grid=PAIR_GRID, in_specs=[SMEM, pair...  27.5 us
    pallas_call x1, Pallas kernels, self_backward(): pl.pallas_call(self_backward_kernel, grid=(PAIRS, MICRO), in_specs=[swapp...  26.1 us
    pallas_call x2, Pallas kernels, key_value(): pl.pallas_call(key_value_kernel, grid=(steps,), in_specs=[SMEM, ANY, ANY,...  16.3 us
    pallas_call x1, Pallas kernels, self_forward(): pl.pallas_call(self_forward_kernel, grid=(PAIRS, MICRO), in_specs=[swappe...  15.4 us
  transfers between devices with their start and end apart: 43, of which 12 were waited for; matrix products, arithmetic and copies ran while one was open for 5% of the time, Pallas kernels for 53%

profile of v5, /device:TPU:0, one launch (start us, length us, event | category | flops | bytes accessed | tf_op | source)
XLA Modules:
  0.0 459.7 jit_solution(6197868110221789327)
XLA Ops:
  14.2 3.7 collective-permute-start.1
  20.2 7.7 %collective-permute-done.1 = bf16[2,24,2048]{2,1,0:T(8,128)(2,1)S(1)} collective-permute-done((bf16[2,24,2048]{2,1,0:T(8,128)(2,1)S(1)}, bf16[2,24,2048]{2,1,0:T(8,128)(2,1)S(1)}, u32[]{:S(2)}, u32[]{:S(2)}) %collective-permute-start.1) | collective-permute-done | bytes 196640 | tf_op jit(solution)/shard_map/ppermute | solution.py:1174
  27.9 5.1 %collective-permute-done.3 = bf16[2,24,2048]{2,1,0:T(8,128)(2,1)S(1)} collective-permute-done((bf16[2,24,2048]{2,1,0:T(8,128)(2,1)S(1)}, bf16[2,24,2048]{2,1,0:T(8,128)(2,1)S(1)}, u32[]{:S(2)}, u32[]{:S(2)}) %collective-permute-start.3) | collective-permute-done | bytes 196640 | tf_op jit(solution)/shard_map/ppermute | solution.py:1174
  41.4 3.8 collective-permute-start.9
  46.2 3.5 collective-permute-done.9
  49.9 3.7 collective-permute-start.10
  53.7 8.0 %bias_tiles.1.tiles_ref = f32[12,2,256,256]{3,2,1,0:T(8,128)} custom-call(f32[12,32]{1,0:T(8,128)} %convert_element_type.544.table_ref), custom_call_target="tpu_custom_call" | custom-call | flops 8 | tf_op jit(solution)/shard_map/bias_tiles/pallas_call | solution.py:796
  61.7 2.7 slice_bitcast_fusion
  64.3 4.2 collective-permute-done.10
  70.8 4.1 assembled.3
  79.1 2.6 collective-permute-start.12
  81.8 9.0 %self_inputs.1 = (bf16[1024,768]{1,0:T(8,128)(2,1)S(1)}, bf16[1024,2304]{1,0:T(8,128)(2,1)}, f32[8,768]{1,0:T(8,128)S(1)}) custom-call(s32[1]{0:T(128)} %bitcast.core_ref, bf16[768,2048]{1,0:T(8,128)(2,1)} %bitcast.220, bf16[768,2048]{1,0:T(8,128)(2,1)} %collective-permute-done.14.other_ref, bf16[1024,768]{1,0:T(8,128)(2,1)} %bitcast.229), custom_call_target="tpu_custom_call" | custom-call | flops 6 | tf_op jit(solution)/shard_map/self_inputs/pallas_call | solution.py:230
  92.0 15.4 %self_forward.1 = (bf16[1024,768]{1,0:T(8,128)(2,1)S(1)}, f32[12,8,512]{2,1,0:T(8,128)S(1)}) custom-call(bf16[1024,2304]{1,0:T(8,128)(2,1)} %get-tuple-element.214.q_ref.k_ref.v_ref, bf16[1024,2304]{1,0:T(8,128)(2,1)} %get-tuple-element.214.q_ref.k_ref.v_ref, bf16[1024,2304]{1,0:T(8,128)(2,1)} %get-tuple-element.214.q_ref.k_ref.v_ref, ...), custom_call_target="tpu_custom_call" | custom-call | flops 17 | tf_op jit(solution)/shard_map/self_forward/pallas_call | solution.py:1080
  108.6 10.0 %key_value.2 = (bf16[1536,1536]{1,0:T(8,128)(2,1)}, f32[8,128]{1,0:T(8,128)S(1)}) custom-call(s32[1]{0:T(128)} %bitcast.core_ref, bf16[768,2048]{1,0:T(8,128)(2,1)} %bitcast.221, bf16[768,2048]{1,0:T(8,128)(2,1)} %collective-permute-done.14.other_ref, bf16[2048,768]{1,0:T(8,128)(2,1)} %bitcast.228), custom_call_target="tpu_custom_call" | custom-call | flops 6 | tf_op jit(solution)/shard_map/key_value/pallas_call | solution.py:200
  118.7 10.7 %collective-permute-done.12 = bf16[2,2,2,24,768]{4,3,2,1,0:T(8,128)(2,1)S(1)} collective-permute-done((bf16[2,2,2,24,768]{4,3,2,1,0:T(8,128)(2,1)S(1)}, bf16[2,2,2,24,768]{4,3,2,1,0:T(8,128)(2,1)S(1)}, u32[]{:S(2)}, u32[]{:S(2)}) %collective-permute-start.12) | collective-permute-done | bytes 294944 | tf_op jit(solution)/shard_map/ppermute | solution.py:1174
  129.4 2.3 assembled.4
  133.4 2.5 collective-permute-start.17
  136.6 6.3 %key_value.3 = (bf16[1024,1536]{1,0:T(8,128)(2,1)}, f32[8,128]{1,0:T(8,128)S(1)}) custom-call(s32[1]{0:T(128)} %bitcast.core_ref, bf16[768,2048]{1,0:T(8,128)(2,1)} %bitcast.222, bf16[768,2048]{1,0:T(8,128)(2,1)} %collective-permute-done.14.other_ref, bf16[1024,768]{1,0:T(8,128)(2,1)S(1)} %bitcast.209), custom_call_target="tpu_custom_call" | custom-call | flops 4 | tf_op jit(solution)/shard_map/key_value/pallas_call | solution.py:200
  143.9 9.3 %cross_inputs.1 = (f32[1024,768]{1,0:T(8,128)}, bf16[1024,768]{1,0:T(8,128)(2,1)}, bf16[1024,768]{1,0:T(8,128)(2,1)}, f32[8,128]{1,0:T(8,128)S(1)}) custom-call(s32[1]{0:T(128)} %bitcast.core_ref, bf16[768,768]{1,0:T(8,128)(2,1)S(1)} %bitcast.208, bf16[768,768]{1,0:T(8,128)(2,1)} %copy-done.17, f32[8,768]{1,0:T(8,128)S(1)} %get-tuple-element.228.gain_ref, ...), custom_call_target="tpu_custom_call" | custom-call | flops 5 | tf_op jit(solution)/shard_map/cross_inputs/pallas_call | solution.py:260
  154.4 27.5 %cross_forward.1 = (bf16[1024,768]{1,0:T(8,128)(2,1)}, f32[12,8,512]{2,1,0:T(8,128)S(1)}) custom-call(s32[1]{0:T(128)} %bitcast.41.small_ref, bf16[1024,768]{1,0:T(8,128)(2,1)} %get-tuple-element.256.q_ref, bf16[1536,1536]{1,0:T(8,128)(2,1)} %get-tuple-element.257.ko_ref.vo_ref, bf16[1024,1536]{1,0:T(8,128)(2,1)} %get-tuple-element.258.kn_ref.vn_ref, ...), custom_call_target="tpu_custom_call" | custom-call | flops 32 | tf_op jit(solution)/shard_map/cross_forward/pallas_call | solution.py:1015
  182.6 3.7 assembled.5
  186.3 3.6 collective-permute-done.20.other_ref
  189.9 2.7 all-gather.2.cloned.1.call-done.late_ref
  192.7 35.8 %ffn.1 = (bf16[1024,768]{1,0:T(8,128)(2,1)}, bf16[1024,768]{1,0:T(8,128)(2,1)S(1)}, bf16[3,1024,2048]{2,1,0:T(8,128)(2,1)}, bf16[1024,768]{1,0:T(8,128)(2,1)}, f...) custom-call(s32[1]{0:T(128)} %bitcast.core_ref, ...), custom_call_target="tpu_custom_call" | custom-call | flops 30 | tf_op jit(solution)/shard_map/ffn/pallas_call | solution.py:357
  228.5 14.9 %ffn_weight_grads.1 = bf16[32,576,256]{2,1,0:T(8,128)(2,1)} custom-call(bf16[1024,768]{1,0:T(8,128)(2,1)S(1)} %get-tuple-element.250.h_ref, bf16[3,1024,2048]{2,1,0:T(8,128)(2,1)} %get-tuple-element.251.acts_ref, bf16[1024,768]{1,0:T(8,128)(2,1)} %bitcast.235), custom_call_target="tpu_custom_call" | custom-call | flops 13 | tf_op jit(solution)/shard_map/ffn_weight_grads/pallas_call | solution.py:580
  243.4 23.5 %cross_backward.2 = (bf16[512,768]{1,0:T(8,128)(2,1)S(1)}, bf16[2,768,768]{2,1,0:T(8,128)(2,1)}, bf16[2,512,768]{2,1,0:T(8,128)(2,1)}) custom-call(bf16[1024,768]{1,0:T(8,128)(2,1)} %get-tuple-element.256.q_ref, bf16[1536,1536]{1,0:T(8,128)(2,1)} %get-tuple-element.257.ko_ref.vo_ref, bf16[1024,1536]{1,0:T(8,128)(2,1)} %get-tuple-element.258.kn_ref.vn_ref, ...), custom_call_target="tpu_custom_call" | custom-call | flops 22 | tf_op jit(solution)/shard_map/cross_backward/pallas_call | solution.py:1040
  266.9 4.7 %memory_grads.2 = bf16[512,768]{1,0:T(8,128)(2,1)S(1)} custom-call(s32[1]{0:T(128)} %bitcast.core_ref, bf16[768,2048]{1,0:T(8,128)(2,1)} %bitcast.223, bf16[768,2048]{1,0:T(8,128)(2,1)} %collective-permute-done.14.other_ref, bf16[2,512,768]{2,1,0:T(8,128)(2,1)} %get-tuple-element.271.dkv_ref.after0_ref), custom_call_target="tpu_custom_call" | custom-call | flops 1 | tf_op jit(solution)/shard_map/memory_grads/pallas_call | solution.py:467
  271.6 3.4 collective-permute-start.21
  275.1 23.5 %cross_backward.3 = (bf16[512,768]{1,0:T(8,128)(2,1)S(1)}, bf16[2,768,768]{2,1,0:T(8,128)(2,1)}, bf16[2,512,768]{2,1,0:T(8,128)(2,1)}) custom-call(bf16[1024,768]{1,0:T(8,128)(2,1)} %get-tuple-element.256.q_ref, bf16[1536,1536]{1,0:T(8,128)(2,1)} %get-tuple-element.257.ko_ref.vo_ref, bf16[1024,1536]{1,0:T(8,128)(2,1)} %get-tuple-element.258.kn_ref.vn_ref, ...), custom_call_target="tpu_custom_call" | custom-call | flops 22 | tf_op jit(solution)/shard_map/cross_backward/pallas_call | solution.py:1040
  298.6 7.7 %pair_grads.2 = (bf16[2,192,1536]{2,1,0:T(8,128)(2,1)}, bf16[2,192,1536]{2,1,0:T(8,128)(2,1)}) custom-call(s32[1]{0:T(128)} %bitcast.core_ref, bf16[1024,768]{1,0:T(8,128)(2,1)} %get-tuple-element.260.o_ref.refs_0_, bf16[1024,768]{1,0:T(8,128)(2,1)} %get-tuple-element.279.refs_1_, bf16[1024,768]{1,0:T(8,128)(2,1)} %get-tuple-element.280.refs_2_, ...), custom_call_target="tpu_custom_call" | custom-call | flops 5 | tf_op jit(solution)/shard_map/pair_grads/pallas_call | solution.py:539
  306.3 4.7 %memory_grads.3 = bf16[512,768]{1,0:T(8,128)(2,1)S(1)} custom-call(s32[1]{0:T(128)} %bitcast.core_ref, bf16[768,2048]{1,0:T(8,128)(2,1)} %bitcast.224, bf16[768,2048]{1,0:T(8,128)(2,1)} %collective-permute-done.14.other_ref, bf16[2,512,768]{2,1,0:T(8,128)(2,1)} %get-tuple-element.272.dkv_ref.after1_ref), custom_call_target="tpu_custom_call" | custom-call | flops 1 | tf_op jit(solution)/shard_map/memory_grads/pallas_call | solution.py:467
  311.0 13.3 %memory_weight_grads.1 = (bf16[2,192,1536]{2,1,0:T(8,128)(2,1)}, bf16[2,192,1536]{2,1,0:T(8,128)(2,1)}) custom-call(s32[1]{0:T(128)} %bitcast.core_ref, bf16[2,1,1024,768]{3,2,1,0:T(8,128)(2,1)} %mem_ref, bf16[1024,768]{1,0:T(8,128)(2,1)} %bitcast.210, bf16[2,768,768]{2,1,0:T(8,128)(2,1)} %get-tuple-element.320.own0_ref.dkv_ref, ...), custom_call_target="tpu_custom_call" | custom-call | flops 8 | tf_op jit(solution)/shard_map/memory_weight_grads/pallas_call | solution.py:618
  324.9 4.0 collective-permute-start.25
  328.9 9.8 %self_grads.1 = (f32[1024,768]{1,0:T(8,128)}, bf16[1024,768]{1,0:T(8,128)(2,1)}, bf16[1024,768]{1,0:T(8,128)(2,1)}, f32[8,768]{1,0:T(8,128)S(1)}) custom-call(s32[1]{0:T(128)} %bitcast.core_ref, bf16[768,768]{1,0:T(8,128)(2,1)} %bitcast.207, bf16[768,768]{1,0:T(8,128)(2,1)} %copy-done.17, f32[8,768]{1,0:T(8,128)S(1)} %get-tuple-element.228.gain_ref, ...), custom_call_target="tpu_custom_call" | custom-call | flops 5 | tf_op jit(solution)/shard_map/self_grads/pallas_call | solution.py:407
  338.7 3.5 pair_grads.3
  349.7 26.1 %self_backward.1 = (bf16[3,1024,768]{2,1,0:T(8,128)(2,1)}, f32[12,8,256]{2,1,0:T(8,128)S(1)}) custom-call(bf16[1024,2304]{1,0:T(8,128)(2,1)} %get-tuple-element.214.q_ref.k_ref.v_ref, bf16[1024,2304]{1,0:T(8,128)(2,1)} %get-tuple-element.214.q_ref.k_ref.v_ref, bf16[1024,2304]{1,0:T(8,128)(2,1)} %get-tuple-element.214.q_ref.k_ref.v_ref, ...), custom_call_target="tpu_custom_call" | custom-call | flops 24 | tf_op jit(solution)/shard_map/self_backward/pallas_call | solution.py:1099
  375.8 7.9 %row_grads.1 = (bf16[2,192,2304]{2,1,0:T(8,128)(2,1)}, bf16[2,192,2304]{2,1,0:T(8,128)(2,1)}) custom-call(s32[1]{0:T(128)} %bitcast.core_ref, bf16[1024,768]{1,0:T(8,128)(2,1)S(1)} %copy-done.6, bf16[3,1024,768]{2,1,0:T(8,128)(2,1)} %get-tuple-element.308.grads_ref.dqkv_ref), custom_call_target="tpu_custom_call" | custom-call | flops 5 | tf_op jit(solution)/shard_map/row_grads/pallas_call | solution.py:506
  383.7 4.2 collective-permute-done.27
  388.4 4.0 collective-permute-start.31
  392.4 10.8 %input_grads.1 = (bf16[1024,768]{1,0:T(8,128)(2,1)}, f32[8,768]{1,0:T(8,128)S(1)}) custom-call(s32[1]{0:T(128)} %bitcast.core_ref, bf16[768,2048]{1,0:T(8,128)(2,1)} %bitcast.225, bf16[768,2048]{1,0:T(8,128)(2,1)} %collective-permute-done.14.other_ref, f32[8,768]{1,0:T(8,128)S(1)} %get-tuple-element.228.gain_ref, bf16[1024,768]{1,0:T(8,128)(2,1)} %bitcast.231, ...), custom_call_target="tpu_custom_call" | custom-call | flops 6 | tf_op jit(solution)/shard_map/input_grads/pallas_call | solution.py:444
  405.7 2.1 collective-permute-start.33
  409.3 6.6 %memory_total.2 = bf16[1024,768]{1,0:T(8,128)(2,1)} custom-call(s32[1]{0:T(128)} %bitcast.core_ref, bf16[768,2048]{1,0:T(8,128)(2,1)} %bitcast.226, bf16[768,2048]{1,0:T(8,128)(2,1)} %collective-permute-done.14.other_ref, bf16[2,768,768]{2,1,0:T(8,128)(2,1)} %get-tuple-element.320.own0_ref.dkv_ref, bf16[512,768]{1,0:T(8,128)(2,1)S(1)} %collective-permute-done.21.prev_ref), custom_call_target="tpu_custom_call" | custom-call | flops 4 | tf_op jit(solution)/shard_map/memory_total/pallas_call | solution.py:653
  416.1 2.1 collective-permute-start.32
  418.1 6.6 %memory_total.3 = bf16[1024,768]{1,0:T(8,128)(2,1)} custom-call(s32[1]{0:T(128)} %bitcast.core_ref, bf16[768,2048]{1,0:T(8,128)(2,1)} %bitcast.227, bf16[768,2048]{1,0:T(8,128)(2,1)} %collective-permute-done.14.other_ref, bf16[2,768,768]{2,1,0:T(8,128)(2,1)} %get-tuple-element.333.own1_ref.dkv_ref, bf16[512,768]{1,0:T(8,128)(2,1)S(1)} %collective-permute-done.25.prev_ref), custom_call_target="tpu_custom_call" | custom-call | flops 4 | tf_op jit(solution)/shard_map/memory_total/pallas_call | solution.py:653
  424.7 5.6 %collective-permute-done.32 = bf16[2,2,2,24,256]{4,3,1,0,2:T(8,128)(2,1)S(1)} collective-permute-done((bf16[2,2,2,24,256]{4,3,1,0,2:T(8,128)(2,1)S(1)}, bf16[2,2,2,24,256]{4,3,1,0,2:T(8,128)(2,1)S(1)}, u32[]{:S(2)}, u32[]{:S(2)}) %collective-permute-start.32) | collective-permute-done | bytes 98336 | tf_op jit(solution)/shard_map/ppermute | solution.py:1174
  430.5 4.0 collective-permute-done.36
  441.9 2.7 collective-permute-start.40
  446.8 3.6 collective-permute-done.38
  (200 shorter events, 56.3 us)
Async XLA Ops:
  7.2 185.5 %all-gather.2.cloned.1.call-start = ((), (), s32[]{:S(2)}) async-start(), calls=%async_computation.1 | async-start | bytes 7704576 | tf_op jit(solution)/shard_map/all_gather | solution.py:1365
  11.9 2.2 collective-permute-start
  14.2 23.0 %copy-start.25 = (bf16[64,768]{1,0:T(8,128)(2,1)S(1)}, bf16[64,768]{1,0:T(8,128)(2,1)}, u32[]{:S(2)}) copy-start(bf16[64,768]{1,0:T(8,128)(2,1)} %param.32) | copy-start | bytes 294916
  14.2 13.7 %collective-permute-start.1 = (bf16[2,24,2048]{2,1,0:T(8,128)(2,1)S(1)}, bf16[2,24,2048]{2,1,0:T(8,128)(2,1)S(1)}, u32[]{:S(2)}, u32[]{:S(2)}) collective-permute-start(bf16[2,24,2048]{2,1,0:T(8,128)(2,1)S(1)} %pad_maximum_fusion.6), channel_id=1, source_target_pairs={{0,4},{1,5},{2,6},{3,7},{4,0},{5,1},{6,2},{7,3},{8,12},{9,13},{10,... | collective-permute-start | bytes 589832 | tf_op jit(solution)/shard_map/ppermute | solution.py:1174
  17.9 10.0 %collective-permute-start.2 = (bf16[2,24,2048]{2,1,0:T(8,128)(2,1)S(1)}, bf16[2,24,2048]{2,1,0:T(8,128)(2,1)S(1)}, u32[]{:S(2)}, u32[]{:S(2)}) collective-permute-start(bf16[2,24,2048]{2,1,0:T(8,128)(2,1)S(1)} %pad_maximum_fusion.6), channel_id=1, source_target_pairs={{0,2},{1,3},{2,0},{3,1},{4,6},{5,7},{6,4},{7,5},{8,10},{9,11},{10,... | collective-permute-start | bytes 589832 | tf_op jit(solution)/shard_map/ppermute | solution.py:1174
  19.5 13.6 %collective-permute-start.3 = (bf16[2,24,2048]{2,1,0:T(8,128)(2,1)S(1)}, bf16[2,24,2048]{2,1,0:T(8,128)(2,1)S(1)}, u32[]{:S(2)}, u32[]{:S(2)}) collective-permute-start(bf16[2,24,2048]{2,1,0:T(8,128)(2,1)S(1)} %pad_maximum_fusion.6), channel_id=1, source_target_pairs={{0,6},{1,7},{2,4},{3,5},{4,2},{5,3},{6,0},{7,1},{8,14},{9,15},{10,... | collective-permute-start | bytes 589832 | tf_op jit(solution)/shard_map/ppermute | solution.py:1174
  33.2 12.4 %copy-start.27 = (bf16[12,32]{1,0:T(8,128)(2,1)S(1)}, bf16[12,32]{1,0:T(8,128)(2,1)}, u32[]{:S(2)}) copy-start(bf16[12,32]{1,0:T(8,128)(2,1)} %param.36) | copy-start | bytes 2308
  33.3 36.4 %collective-permute-start.4 = (bf16[2,2,2,24,2048]{4,3,2,1,0:T(8,128)(2,1)S(1)}, bf16[2,2,2,24,2048]{4,3,2,1,0:T(8,128)(2,1)S(1)}, u32[]{:S(2)}, u32[]{:S(2)}) collective-permute-start(bf16[2,2,2,24,2048]{4,3,2,1,0:T(8,128)(2,1)S(1)} %bitcast_dynamic-update-slice_fusion.2), channel_id=1, source_target_pairs={{0,16},{1,17},{2,18},{3,19},{4,20},{5,21},{6,22},{7,23},{8,24},{9,... | collective-permute-start | bytes 2359304 | tf_op jit(solution)/shard_map/ppermute | solution.py:1174
  34.8 35.6 %collective-permute-start.5 = (bf16[2,2,2,24,2048]{4,3,2,1,0:T(8,128)(2,1)S(1)}, bf16[2,2,2,24,2048]{4,3,2,1,0:T(8,128)(2,1)S(1)}, u32[]{:S(2)}, u32[]{:S(2)}) collective-permute-start(bf16[2,2,2,24,2048]{4,3,2,1,0:T(8,128)(2,1)S(1)} %bitcast_dynamic-update-slice_fusion.2), channel_id=1, source_target_pairs={{0,1},{1,0},{2,3},{3,2},{4,5},{5,4},{6,7},{7,6},{8,9},{9,8},{10,11... | collective-permute-start | bytes 2359304 | tf_op jit(solution)/shard_map/ppermute | solution.py:1174
  36.4 34.2 %collective-permute-start.6 = (bf16[2,2,2,24,2048]{4,3,2,1,0:T(8,128)(2,1)S(1)}, bf16[2,2,2,24,2048]{4,3,2,1,0:T(8,128)(2,1)}, u32[]{:S(2)}, u32[]{:S(2)}) collective-permute-start(bf16[2,2,2,24,2048]{4,3,2,1,0:T(8,128)(2,1)S(1)} %bitcast_dynamic-update-slice_fusion.2), channel_id=1, source_target_pairs={{0,17},{1,16},{2,19},{3,18},{4,21},{5,20},{6,23},{7,22},{8,25},{9,... | collective-permute-start | bytes 2359304 | tf_op jit(solution)/shard_map/ppermute | solution.py:1174
  37.0 4.2 collective-permute-start.7
  37.4 4.0 collective-permute-start.8
  41.4 8.4 %collective-permute-start.9 = (bf16[2,112,384]{2,1,0:T(8,128)(2,1)S(1)}, bf16[2,112,384]{2,1,0:T(8,128)(2,1)S(1)}, u32[]{:S(2)}, u32[]{:S(2)}) collective-permute-start(bf16[2,112,384]{2,1,0:T(8,128)(2,1)S(1)} %maximum_maximum_fusion), channel_id=1, source_target_pairs={{0,2},{1,3},{2,0},{3,1},{4,6},{5,7},{6,4},{7,5},{8,10},{9,11},{10,... | collective-permute-start | bytes 516104 | tf_op jit(solution)/shard_map/ppermute | solution.py:1174
  49.9 18.6 %collective-permute-start.10 = (bf16[2,2,112,384]{3,2,1,0:T(8,128)(2,1)S(1)}, bf16[2,2,112,384]{3,2,1,0:T(8,128)(2,1)}, u32[]{:S(2)}, u32[]{:S(2)}) collective-permute-start(bf16[2,2,112,384]{3,2,1,0:T(8,128)(2,1)S(1)} %bitcast_dynamic-update-slice_fusion.6), channel_id=1, source_target_pairs={{0,4},{1,5},{2,6},{3,7},{4,0},{5,1},{6,2},{7,3},{8,12},{9,13},{10,... | collective-permute-start | bytes 1032200 | tf_op jit(solution)/shard_map/ppermute | solution.py:1174
  53.7 100.7 %copy-start.3 = (bf16[2,1280,128]{2,1,0:T(8,128)(2,1)}, bf16[2,1280,128]{2,1,0:T(8,128)(2,1)S(1)}, u32[]{:S(2)}) copy-start(bf16[2,1280,128]{2,1,0:T(8,128)(2,1)S(1)} %pad_maximum_fusion.4.mask_ref) | copy-start | bytes 1966084
  70.6 367.8 %reduce-scatter.2.cloned.1.call-start = ((), (), s32[]{:S(2)}) async-start(), calls=%async_computation.2 | async-start | bytes 9732096 | tf_op jit(solution)/shard_map/reduce_scatter | solution.py:1291
  74.9 6.9 %collective-permute-start.14 = (bf16[768,2048]{1,0:T(8,128)(2,1)}, bf16[768,2048]{1,0:T(8,128)(2,1)}, u32[]{:S(2)}, u32[]{:S(2)}) collective-permute-start(bf16[768,2048]{1,0:T(8,128)(2,1)} %bitcast.219), channel_id=1, source_target_pairs={{0,8},{1,9},{2,10},{3,11},{4,12},{5,13},{6,14},{7,15},{8,0},{9,1},... | collective-permute-start | bytes 9437192 | tf_op jit(solution)/shard_map/ppermute | solution.py:1174
  74.9 54.5 %collective-permute-start.15 = (bf16[2,512,768]{2,1,0:T(8,128)(2,1)}, bf16[2,512,768]{2,1,0:T(8,128)(2,1)S(1)}, u32[]{:S(2)}, u32[]{:S(2)}) collective-permute-start(bf16[2,512,768]{2,1,0:T(8,128)(2,1)} %slice_bitcast_fusion), channel_id=1, source_target_pairs={{1,0},{2,1},{3,2},{4,3},{5,4},{6,5},{7,6},{9,8},{10,9},{11,10},{12... | collective-permute-start | bytes 4718600 | tf_op jit(solution)/shard_map/ppermute | solution.py:1270
  77.6 41.1 %collective-permute-start.11 = (bf16[2,2,2,24,768]{4,3,2,1,0:T(8,128)(2,1)S(1)}, bf16[2,2,2,24,768]{4,3,2,1,0:T(8,128)(2,1)S(1)}, u32[]{:S(2)}, u32[]{:S(2)}) collective-permute-start(bf16[2,2,2,24,768]{4,3,2,1,0:T(8,128)(2,1)S(1)} %reshape.598), channel_id=1, source_target_pairs={{0,16},{1,17},{2,18},{3,19},{4,20},{5,21},{6,22},{7,23},{8,24},{9,... | collective-permute-start | bytes 884744 | tf_op jit(solution)/shard_map/ppermute | solution.py:1174
  79.1 50.3 %collective-permute-start.12 = (bf16[2,2,2,24,768]{4,3,2,1,0:T(8,128)(2,1)S(1)}, bf16[2,2,2,24,768]{4,3,2,1,0:T(8,128)(2,1)S(1)}, u32[]{:S(2)}, u32[]{:S(2)}) collective-permute-start(bf16[2,2,2,24,768]{4,3,2,1,0:T(8,128)(2,1)S(1)} %reshape.598), channel_id=1, source_target_pairs={{0,1},{1,0},{2,3},{3,2},{4,5},{5,4},{6,7},{7,6},{8,9},{9,8},{10,11... | collective-permute-start | bytes 884744 | tf_op jit(solution)/shard_map/ppermute | solution.py:1174
  81.8 47.6 %collective-permute-start.13 = (bf16[2,2,2,24,768]{4,3,2,1,0:T(8,128)(2,1)S(1)}, bf16[2,2,2,24,768]{4,3,2,1,0:T(8,128)(2,1)S(1)}, u32[]{:S(2)}, u32[]{:S(2)}) collective-permute-start(bf16[2,2,2,24,768]{4,3,2,1,0:T(8,128)(2,1)S(1)} %reshape.598), channel_id=1, source_target_pairs={{0,17},{1,16},{2,19},{3,18},{4,21},{5,20},{6,23},{7,22},{8,25},{9,... | collective-permute-start | bytes 884744 | tf_op jit(solution)/shard_map/ppermute | solution.py:1174
  118.7 13.0 %copy-start.19 = (bf16[2,2,2,112,384]{4,3,2,1,0:T(8,128)(2,1)S(1)}, bf16[2,2,2,112,384]{4,3,2,1,0:T(8,128)(2,1)}, u32[]{:S(2)}) copy-start(bf16[2,2,2,112,384]{4,3,2,1,0:T(8,128)(2,1)} %copy-done.18) | copy-start | bytes 2064388
  131.7 11.2 %collective-permute-start.19 = (bf16[768,768]{1,0:T(8,128)(2,1)}, bf16[768,768]{1,0:T(8,128)(2,1)S(1)}, u32[]{:S(2)}, u32[]{:S(2)}) collective-permute-start(bf16[768,768]{1,0:T(8,128)(2,1)} %bitcast.206), channel_id=1, source_target_pairs={{0,8},{1,9},{2,10},{3,11},{4,12},{5,13},{6,14},{7,15},{8,0},{9,1},... | collective-permute-start | bytes 3538952 | tf_op jit(solution)/shard_map/ppermute | solution.py:1174
  132.5 50.1 %collective-permute-start.16 = (bf16[2,2,2,64,384]{4,3,2,1,0:T(8,128)(2,1)}, bf16[2,2,2,64,384]{4,3,2,1,0:T(8,128)(2,1)}, u32[]{:S(2)}, u32[]{:S(2)}) collective-permute-start(bf16[2,2,2,64,384]{4,3,2,1,0:T(8,128)(2,1)} %slice.76), channel_id=1, source_target_pairs={{0,16},{1,17},{2,18},{3,19},{4,20},{5,21},{6,22},{7,23},{8,24},{9,... | collective-permute-start | bytes 1179656 | tf_op jit(solution)/shard_map/ppermute | solution.py:1174
  133.4 49.1 %collective-permute-start.17 = (bf16[2,2,2,64,384]{4,3,2,1,0:T(8,128)(2,1)}, bf16[2,2,2,64,384]{4,3,2,1,0:T(8,128)(2,1)}, u32[]{:S(2)}, u32[]{:S(2)}) collective-permute-start(bf16[2,2,2,64,384]{4,3,2,1,0:T(8,128)(2,1)} %slice.76), channel_id=1, source_target_pairs={{0,1},{1,0},{2,3},{3,2},{4,5},{5,4},{6,7},{7,6},{8,9},{9,8},{10,11... | collective-permute-start | bytes 1179656 | tf_op jit(solution)/shard_map/ppermute | solution.py:1174
  136.0 46.6 %collective-permute-start.18 = (bf16[2,2,2,64,384]{4,3,2,1,0:T(8,128)(2,1)}, bf16[2,2,2,64,384]{4,3,2,1,0:T(8,128)(2,1)}, u32[]{:S(2)}, u32[]{:S(2)}) collective-permute-start(bf16[2,2,2,64,384]{4,3,2,1,0:T(8,128)(2,1)} %slice.76), channel_id=1, source_target_pairs={{0,17},{1,16},{2,19},{3,18},{4,21},{5,20},{6,23},{7,22},{8,25},{9,... | collective-permute-start | bytes 1179656 | tf_op jit(solution)/shard_map/ppermute | solution.py:1174
  186.3 3.6 collective-permute-start.20
  271.6 39.4 %collective-permute-start.21 = (bf16[512,768]{1,0:T(8,128)(2,1)S(1)}, bf16[512,768]{1,0:T(8,128)(2,1)S(1)}, u32[]{:S(2)}, u32[]{:S(2)}) collective-permute-start(bf16[512,768]{1,0:T(8,128)(2,1)S(1)} %memory_grads.2), channel_id=1, source_target_pairs={{0,1},{1,2},{2,3},{3,4},{4,5},{5,6},{6,7},{8,9},{9,10},{10,11},{11... | collective-permute-start | bytes 2359304 | tf_op jit(solution)/shard_map/ppermute | solution.py:1270
  306.3 32.4 %collective-permute-start.22 = (bf16[2,192,1536]{2,1,0:T(8,128)(2,1)}, bf16[2,192,1536]{2,1,0:T(8,128)(2,1)}, u32[]{:S(2)}, u32[]{:S(2)}) collective-permute-start(bf16[2,192,1536]{2,1,0:T(8,128)(2,1)} %get-tuple-element.282), channel_id=1, source_target_pairs={{0,8},{1,9},{2,10},{3,11},{4,12},{5,13},{6,14},{7,15},{8,0},{9,1},... | collective-permute-start | bytes 3538952 | tf_op jit(solution)/shard_map/ppermute | solution.py:1174
  324.4 14.4 %collective-permute-start.23 = (bf16[2,192,1536]{2,1,0:T(8,128)(2,1)}, bf16[2,192,1536]{2,1,0:T(8,128)(2,1)}, u32[]{:S(2)}, u32[]{:S(2)}) collective-permute-start(bf16[2,192,1536]{2,1,0:T(8,128)(2,1)} %get-tuple-element.284), channel_id=1, source_target_pairs={{0,8},{1,9},{2,10},{3,11},{4,12},{5,13},{6,14},{7,15},{8,0},{9,1},... | collective-permute-start | bytes 3538952 | tf_op jit(solution)/shard_map/ppermute | solution.py:1174
  324.9 50.9 %collective-permute-start.25 = (bf16[512,768]{1,0:T(8,128)(2,1)S(1)}, bf16[512,768]{1,0:T(8,128)(2,1)S(1)}, u32[]{:S(2)}, u32[]{:S(2)}) collective-permute-start(bf16[512,768]{1,0:T(8,128)(2,1)S(1)} %memory_grads.3), channel_id=1, source_target_pairs={{0,1},{1,2},{2,3},{3,4},{4,5},{5,6},{6,7},{8,9},{9,10},{10,11},{11... | collective-permute-start | bytes 2359304 | tf_op jit(solution)/shard_map/ppermute | solution.py:1270
  342.3 3.4 collective-permute-start.24
  346.1 37.6 %collective-permute-start.26 = (bf16[2,2,24,3840]{3,2,1,0:T(8,128)(2,1)S(1)}, bf16[2,2,24,3840]{3,2,1,0:T(8,128)(2,1)S(1)}, u32[]{:S(2)}, u32[]{:S(2)}) collective-permute-start(bf16[2,2,24,3840]{3,2,1,0:T(8,128)(2,1)S(1)} %pad_maximum_fusion.1), channel_id=1, source_target_pairs={{0,16},{1,17},{2,18},{3,19},{4,20},{5,21},{6,22},{7,23},{8,24},{9,... | collective-permute-start | bytes 2211848 | tf_op jit(solution)/shard_map/ppermute | solution.py:1174
  347.3 40.6 %collective-permute-start.27 = (bf16[2,2,24,3840]{3,2,1,0:T(8,128)(2,1)S(1)}, bf16[2,2,24,3840]{3,2,1,0:T(8,128)(2,1)S(1)}, u32[]{:S(2)}, u32[]{:S(2)}) collective-permute-start(bf16[2,2,24,3840]{3,2,1,0:T(8,128)(2,1)S(1)} %pad_maximum_fusion.2), channel_id=1, source_target_pairs={{0,1},{1,0},{2,3},{3,2},{4,5},{5,4},{6,7},{7,6},{8,9},{9,8},{10,11... | collective-permute-start | bytes 2211848 | tf_op jit(solution)/shard_map/ppermute | solution.py:1174
  348.6 39.4 %collective-permute-start.28 = (bf16[2,2,24,3840]{3,2,1,0:T(8,128)(2,1)S(1)}, bf16[2,2,24,3840]{3,2,1,0:T(8,128)(2,1)S(1)}, u32[]{:S(2)}, u32[]{:S(2)}) collective-permute-start(bf16[2,2,24,3840]{3,2,1,0:T(8,128)(2,1)S(1)} %pad_maximum_fusion.3), channel_id=1, source_target_pairs={{0,17},{1,16},{2,19},{3,18},{4,21},{5,20},{6,23},{7,22},{8,25},{9,... | collective-permute-start | bytes 2211848 | tf_op jit(solution)/shard_map/ppermute | solution.py:1174
  349.7 26.1 %copy-start.6 = (bf16[1024,768]{1,0:T(8,128)(2,1)S(1)}, bf16[1024,768]{1,0:T(8,128)(2,1)}, u32[]{:S(2)}) copy-start(bf16[1024,768]{1,0:T(8,128)(2,1)} %copy-done.5) | copy-start | bytes 4718596
  388.0 15.3 %collective-permute-start.29 = (bf16[2,192,2304]{2,1,0:T(8,128)(2,1)}, bf16[2,192,2304]{2,1,0:T(8,128)(2,1)S(1)}, u32[]{:S(2)}, u32[]{:S(2)}) collective-permute-start(bf16[2,192,2304]{2,1,0:T(8,128)(2,1)} %get-tuple-element.312), channel_id=1, source_target_pairs={{0,8},{1,9},{2,10},{3,11},{4,12},{5,13},{6,14},{7,15},{8,0},{9,1},... | collective-permute-start | bytes 5308424 | tf_op jit(solution)/shard_map/ppermute | solution.py:1174
  388.4 27.5 %collective-permute-start.31 = (bf16[2,24,3840]{2,1,0:T(8,128)(2,1)S(1)}, bf16[2,24,3840]{2,1,0:T(8,128)(2,1)S(1)}, u32[]{:S(2)}, u32[]{:S(2)}) collective-permute-start(bf16[2,24,3840]{2,1,0:T(8,128)(2,1)S(1)} %get-tuple-element.325), channel_id=1, source_target_pairs={{0,4},{1,5},{2,6},{3,7},{4,0},{5,1},{6,2},{7,3},{8,12},{9,13},{10,... | collective-permute-start | bytes 1105928 | tf_op jit(solution)/shard_map/ppermute | solution.py:1174
  405.4 10.4 %collective-permute-start.30 = (bf16[2,192,256]{2,1,0:T(8,128)(2,1)S(1)}, bf16[2,192,256]{2,1,0:T(8,128)(2,1)S(1)}, u32[]{:S(2)}, u32[]{:S(2)}) collective-permute-start(bf16[2,192,256]{2,1,0:T(8,128)(2,1)S(1)} %get-tuple-element.323), channel_id=1, source_target_pairs={{0,8},{1,9},{2,10},{3,11},{4,12},{5,13},{6,14},{7,15},{8,0},{9,1},... | collective-permute-start | bytes 589832 | tf_op jit(solution)/shard_map/ppermute | solution.py:1174
  405.7 28.8 %collective-permute-start.33 = (bf16[2,2,24,2304]{3,2,1,0:T(8,128)(2,1)}, bf16[2,2,24,2304]{3,2,1,0:T(8,128)(2,1)S(1)}, u32[]{:S(2)}, u32[]{:S(2)}) collective-permute-start(bf16[2,2,24,2304]{3,2,1,0:T(8,128)(2,1)} %get-tuple-element.339), channel_id=1, source_target_pairs={{0,16},{1,17},{2,18},{3,19},{4,20},{5,21},{6,22},{7,23},{8,24},{9,... | collective-permute-start | bytes 1327112 | tf_op jit(solution)/shard_map/ppermute | solution.py:1174
  407.8 26.7 %collective-permute-start.34 = (bf16[2,2,24,2304]{3,2,1,0:T(8,128)(2,1)}, bf16[2,2,24,2304]{3,2,1,0:T(8,128)(2,1)S(1)}, u32[]{:S(2)}, u32[]{:S(2)}) collective-permute-start(bf16[2,2,24,2304]{3,2,1,0:T(8,128)(2,1)} %get-tuple-element.340), channel_id=1, source_target_pairs={{0,1},{1,0},{2,3},{3,2},{4,5},{5,4},{6,7},{7,6},{8,9},{9,8},{10,11... | collective-permute-start | bytes 1327112 | tf_op jit(solution)/shard_map/ppermute | solution.py:1174
  407.8 26.7 %collective-permute-start.35 = (bf16[2,2,24,2304]{3,2,1,0:T(8,128)(2,1)}, bf16[2,2,24,2304]{3,2,1,0:T(8,128)(2,1)S(1)}, u32[]{:S(2)}, u32[]{:S(2)}) collective-permute-start(bf16[2,2,24,2304]{3,2,1,0:T(8,128)(2,1)} %get-tuple-element.341), channel_id=1, source_target_pairs={{0,17},{1,16},{2,19},{3,18},{4,21},{5,20},{6,23},{7,22},{8,25},{9,... | collective-permute-start | bytes 1327112 | tf_op jit(solution)/shard_map/ppermute | solution.py:1174
  416.1 14.3 %collective-permute-start.32 = (bf16[2,2,2,24,256]{4,3,1,0,2:T(8,128)(2,1)S(1)}, bf16[2,2,2,24,256]{4,3,1,0,2:T(8,128)(2,1)S(1)}, u32[]{:S(2)}, u32[]{:S(2)}) collective-permute-start(bf16[2,2,2,24,256]{4,3,1,0,2:T(8,128)(2,1)S(1)} %get-tuple-element.336), channel_id=1, source_target_pairs={{0,16},{1,17},{2,18},{3,19},{4,20},{5,21},{6,22},{7,23},{8,24},{9,... | collective-permute-start | bytes 294920 | tf_op jit(solution)/shard_map/ppermute | solution.py:1174
  430.4 4.2 collective-permute-start.36
  430.5 7.9 %collective-permute-start.37 = (bf16[24,3840]{1,0:T(8,128)(2,1)S(1)}, bf16[24,3840]{1,0:T(8,128)(2,1)S(1)}, u32[]{:S(2)}, u32[]{:S(2)}) collective-permute-start(bf16[24,3840]{1,0:T(8,128)(2,1)S(1)} %get-tuple-element.353), channel_id=1, source_target_pairs={{0,2},{1,3},{2,0},{3,1},{4,6},{5,7},{6,4},{7,5},{8,10},{9,11},{10,... | collective-permute-start | bytes 552968 | tf_op jit(solution)/shard_map/ppermute | solution.py:1174
  440.3 10.2 %collective-permute-start.38 = (bf16[24,2560]{1,0:T(8,128)(2,1)S(1)}, bf16[24,2560]{1,0:T(8,128)(2,1)S(1)}, u32[]{:S(2)}, u32[]{:S(2)}) collective-permute-start(bf16[24,2560]{1,0:T(8,128)(2,1)S(1)} %pad_maximum_fusion.8), channel_id=1, source_target_pairs={{0,4},{1,5},{2,6},{3,7},{4,0},{5,1},{6,2},{7,3},{8,12},{9,13},{10,... | collective-permute-start | bytes 368648 | tf_op jit(solution)/shard_map/ppermute | solution.py:1174
  440.3 10.1 %collective-permute-start.39 = (bf16[24,2560]{1,0:T(8,128)(2,1)S(1)}, bf16[24,2560]{1,0:T(8,128)(2,1)S(1)}, u32[]{:S(2)}, u32[]{:S(2)}) collective-permute-start(bf16[24,2560]{1,0:T(8,128)(2,1)S(1)} %pad_maximum_fusion.9), channel_id=1, source_target_pairs={{0,2},{1,3},{2,0},{3,1},{4,6},{5,7},{6,4},{7,5},{8,10},{9,11},{10,... | collective-permute-start | bytes 368648 | tf_op jit(solution)/shard_map/ppermute | solution.py:1174
  441.9 8.5 %collective-permute-start.40 = (bf16[24,2560]{1,0:T(8,128)(2,1)S(1)}, bf16[24,2560]{1,0:T(8,128)(2,1)S(1)}, u32[]{:S(2)}, u32[]{:S(2)}) collective-permute-start(bf16[24,2560]{1,0:T(8,128)(2,1)S(1)} %pad_maximum_fusion.10), channel_id=1, source_target_pairs={{0,6},{1,7},{2,4},{3,5},{4,2},{5,3},{6,0},{7,1},{8,14},{9,15},{10,... | collective-permute-start | bytes 368648 | tf_op jit(solution)/shard_map/ppermute | solution.py:1174
  (24 other events, 85.3 us)
Sparse Core Ops, SparseCore 0:
  70.7 121.8 all-gather.1
  243.5 150.5 reduce-scatter.1
